TPU v7x, 32 devices: a whole 2x2x4 slice. The times are simulated.
32 devices in a mesh: leaf: 16 (over z, y, core), oct: 2 (over x).
Axes of the slice: x: 2, y: 2, z: 4, core: 2. Of those that a mesh axis runs over, the one named last changes fastest.
Arguments:
- children: bfloat16 [1024, 4096], P(('leaf', 'oct')), may hold values from -6 to 6
- child_slot: int32 [128, 8], P('leaf', 'oct'), may hold values from 0 to 31, as said below
- two_scale: bfloat16 [32, 32], replicated, may hold values from -1 to 1
- factors: bfloat16 [27, 30720], replicated, may hold values from -0.5390625 to 0.5390625
- disp_kind: int32 [128, 4], P(('leaf', 'oct')), may hold values from 0 to 26
- target_leaf: int32 [128, 4, 1], P(('leaf', 'oct')), may hold values from 0 to 15; in each aligned block of 16 rows (0 to 15, 16 to 31, ..., all dimensions but the last counted through in order) at most 2 rows name the same one
- target_node: int32 [128, 4], P(('leaf', 'oct')), may hold values from 0 to 3
Outputs:
- octant_out: bfloat16 [64, 8, 4096], P('leaf', 'oct')
Inputs may be any that keep to these rules, and one draw needn't show every extreme that they name: Over the parents of one subtree and the octants held by one device along oct, child_slot takes every value exactly once. `target_leaf`: of the 16 entries of one device, at most 2 name the same subtree; some device reaches 2.
All inputs are finite; a program needn't handle non-finite values.
Results may differ from a plain program's by a relative error of at most 0.018.
Values may be sent and summed in bfloat16 or wider, within the bound.
No kernel may reach another device: no remote copies, remote signals or barrier semaphores. Data moves between devices by JAX's collectives and lax.ppermute only.
A program may use at most 64 MiB of HBM per device.

v0:
```python
import jax
import jax.numpy as jnp
from jax import lax
from jax.sharding import PartitionSpec as P

TGT_DEV = 2


def filter_blocks(block_batch, filter_halfset):
    half_edge = filter_halfset.shape[2]
    count_batch = block_batch.shape[0]
    split_blocks = block_batch.reshape(count_batch, 2, 2, 2, half_edge, half_edge, half_edge)
    first_pass = jnp.einsum(
        "nijlpsr,aip->najlsr", split_blocks, filter_halfset, preferred_element_type=jnp.float32
    ).astype(jnp.bfloat16)
    second_sweep = jnp.einsum(
        "najlsr,bjs->nablr", first_pass, filter_halfset, preferred_element_type=jnp.float32
    ).astype(jnp.bfloat16)
    return jnp.einsum(
        "qyixz,wxz->qyiw", second_sweep, filter_halfset, preferred_element_type=jnp.float32
    ).astype(jnp.bfloat16)


def unfilter_blocks(cube_batch, filter_halfset):
    half_edge = filter_halfset.shape[2]
    count_batch = cube_batch.shape[0]
    first_pass = jnp.einsum(
        "nabc,aip->nipbc", cube_batch, filter_halfset, preferred_element_type=jnp.float32
    ).astype(jnp.bfloat16)
    second_sweep = jnp.einsum(
        "nipbc,bjs->nipjsc", first_pass, filter_halfset, preferred_element_type=jnp.float32
    ).astype(jnp.bfloat16)
    third_sweep = jnp.einsum(
        "xmezhw,wbf->xmezhbf", second_sweep, filter_halfset, preferred_element_type=jnp.float32
    ).astype(jnp.bfloat16)
    ordered = jnp.transpose(third_sweep, (0, 1, 3, 5, 2, 4, 6))
    return ordered.reshape(count_batch, 8, half_edge * half_edge * half_edge)


def apply_parent(parent_item):
    parent_cube, factor_rows = parent_item
    edge_len = parent_cube.shape[0]
    factor_set = factor_rows.reshape(factor_rows.shape[0], 3, -1, edge_len, edge_len)
    section_z = jnp.einsum(
        "abc,ktdc->ktabd", parent_cube, factor_set[:, 2], preferred_element_type=jnp.float32
    ).astype(jnp.bfloat16)
    section_y = jnp.einsum(
        "ktabd,kteb->ktaed", section_z, factor_set[:, 1], preferred_element_type=jnp.float32
    ).astype(jnp.bfloat16)
    summed = jnp.einsum(
        "ktaed,ktfa->kfed", section_y, factor_set[:, 0], preferred_element_type=jnp.float32
    ).astype(jnp.bfloat16)
    return summed.reshape(summed.shape[0], -1)


def local(children, child_slot, two_scale, factors, disp_kind, target_leaf, target_node):
    oct_count = lax.axis_size("oct")
    leaf_count = lax.axis_size("leaf")
    edge_len = two_scale.shape[0]
    half_edge = edge_len // 2
    cube_len = edge_len * edge_len * edge_len
    filter_halfset = two_scale.reshape(edge_len, 2, half_edge)
    picked_blocks = children[child_slot]
    octant_blocks = lax.all_to_all(picked_blocks, "oct", split_axis=0, concat_axis=1, tiled=True)
    parent_blocks = filter_blocks(octant_blocks, filter_halfset)
    kind_factors = factors[disp_kind]
    contributions = lax.map(apply_parent, (parent_blocks, kind_factors))
    flat_rows = contributions.reshape(-1, cube_len)
    row_total = flat_rows.shape[0]
    leaf_numbers = target_leaf.reshape(-1)
    node_numbers = target_node.reshape(-1)
    slot_count = max(2, (2 * row_total + leaf_count - 1) // leaf_count)
    row_order = jnp.arange(row_total, dtype=jnp.int32)
    earlier_same = (leaf_numbers[:, None] == leaf_numbers[None, :]) & (
        row_order[None, :] < row_order[:, None]
    )
    slot_rank = jnp.sum(earlier_same.astype(jnp.int32), axis=1)
    slot_index = leaf_numbers * slot_count + slot_rank
    slot_chooser = (
        jnp.arange(leaf_count * slot_count, dtype=jnp.int32)[:, None] == slot_index[None, :]
    )
    packed_rows = jnp.dot(
        slot_chooser.astype(jnp.bfloat16), flat_rows, preferred_element_type=jnp.float32
    ).astype(jnp.bfloat16)
    packed_ids = jnp.sum(jnp.where(slot_chooser, node_numbers[None, :] + 1, 0), axis=1) - 1
    arrived, arrived_ids = (
        lax.all_to_all(
            packed_rows.reshape(leaf_count, slot_count, cube_len),
            "leaf",
            split_axis=0,
            concat_axis=0,
            tiled=True,
        ),
        lax.all_to_all(
            packed_ids.reshape(leaf_count, slot_count),
            "leaf",
            split_axis=0,
            concat_axis=0,
            tiled=True,
        ),
    )
    node_count = TGT_DEV * oct_count
    node_select = (
        jnp.arange(node_count, dtype=jnp.int32)[:, None] == arrived_ids.reshape(-1)[None, :]
    ).astype(jnp.bfloat16)
    partial_totals = jnp.dot(
        node_select, arrived.reshape(-1, cube_len), preferred_element_type=jnp.float32
    )
    node_share = lax.psum_scatter(
        partial_totals.astype(jnp.bfloat16), "oct", scatter_dimension=0, tiled=True
    )
    child_blocks = unfilter_blocks(
        node_share.reshape(-1, edge_len, edge_len, edge_len), filter_halfset
    )
    return lax.all_to_all(child_blocks, "oct", split_axis=1, concat_axis=0, tiled=True)


def solution(mesh):
    placed = (
        P(("leaf", "oct"), None),
        P("leaf", "oct"),
        P(),
        P(),
        P(("leaf", "oct"), None),
        P(("leaf", "oct"), None, None),
        P(("leaf", "oct"), None),
    )
    return jax.shard_map(
        local, mesh=mesh, in_specs=placed, out_specs=P("leaf", "oct", None), check_vma=False
    )
```

profile of v0, /device:TPU:0, one launch (start us, length us, event | category | flops | bytes accessed | tf_op | source)
XLA Modules:
  0.0 290.3 jit_solution(3368793012803245433)
XLA Ops:
  6.5 0.8 compare_select_fusion
  7.5 1.9 gather_fusion.1
  9.5 0.8 reshape.85
  10.3 4.2 %all-to-all-start.1 = ((bf16[8,4,4096]{2,1,0:T(4,128)(2,1)}), bf16[8,4,4096]{2,1,0:T(4,128)(2,1)S(1)}, u32[]{:S(2)}, u32[]{:S(2)}) async-start(bf16[8,4,4096]{2,1,0:T(4,128)(2,1)} %reshape.85), calls=%async_computation.1 | async-start | bytes 524288 | tf_op jit(solution)/shard_map/all_to_all | solution.py:64
  14.7 1.2 gather_fusion
  15.9 1.4 reshape.77
  17.3 0.5 broadcast.60
  17.8 0.6 reduce.6
  18.5 0.2 convert_reduce_fusion
  18.8 0.1 select_reduce_fusion
  18.9 0.7 sub.7
  19.6 0.8 all-to-all-done.1
  20.4 6.2 %all-to-all-start = ((s32[16,1,2]{2,1,0:T(1,128)}), s32[16,1,2]{2,1,0:T(1,128)S(1)}, u32[]{:S(2)}, u32[]{:S(2)}) async-start(s32[16,1,2]{2,1,0:T(1,128)} %bitcast.16), calls=%async_computation | async-start | bytes 16384 | tf_op jit(solution)/shard_map/all_to_all | solution.py:94
  26.6 2.6 reshape.110
  29.1 2.3 fusion.22
  31.4 4.2 %copy.90 = bf16[4,32,2,2,16,16]{4,5,2,3,1,0:T(8,128)(2,1)} copy(bf16[4,32,2,2,16,16]{1,5,4,3,2,0:T(8,128)(2,1)S(1)} %fusion.22) | data formatting | bytes 524288 | tf_op jit(solution)/shard_map/convert_element_type | solution.py:15
  35.7 4.0 %bitcast_convert_fusion.1 = bf16[4,32,32,32]{3,2,1,0:T(8,128)(2,1)} fusion(bf16[32,2,16,1,1]{0,2,1,4,3:T(8,128)(2,1)S(1)} %bitcast.138, bf16[4,32,2,2,16,16]{4,5,2,3,1,0:T(8,128)(2,1)} %copy.90, bf16[32,2,16,1,1,1]{0,2,1,5,4,3:T(8,128)(2,1)S(1)} %bitcast.137), kind=kOutput, calls=%fused_computation.20 | convolution fusion | flops 17039360 | bytes 528384 | tf_op jit(solution)/shard_map/qyixz,wxz->qyiw/dot_general | solution.py:19
  39.7 138.1 %while.10 = (s32[]{:T(128)}, bf16[4,4,32768]{2,1,0:T(4,128)(2,1)}, bf16[4,4,30720]{2,1,0:T(4,128)(2,1)}, bf16[4,32,32,32]{3,2,1,0:T(8,128)(2,1)}, s32[]{:T(128)}) while((s32[]{:T(128)}, bf16[4,4,32768]{2,1,0:T(4,128)(2,1)}, bf16[4,4,30720]{2,1,0:T(4,128)(2,1)}, bf16[4,32,32,32]{3,2,1,0:T(8,128)(2,1)}, s32[]{:T(128)}) %tuple.18), condition=%wide.region_3.4_spmd, body=%wide.region_2.3_spmd.sunk | while | flops 254410752 | bytes 9307201 | solution.py:67
  39.7 1.0 constant_dynamic-slice_fusion.3
  40.7 0.5 reshape.130
  41.3 21.9 %convert_bitcast_fusion.2 = bf16[4,10,32,32,32]{4,3,2,1,0:T(8,128)(2,1)} fusion(bf16[4,3,10,32,32]{4,3,2,1,0:T(8,128)(2,1)S(1)} %reshape.130, bf16[4,32,32,32]{3,2,1,0:T(8,128)(2,1)} %get-tuple-element.74, s32[]{:T(128)} %get-tuple-element.66), kind=kOutput, calls=%fused_computation.6.clone.1 | convolution fusion | flops 170393600 | bytes 3539456 | tf_op jit(solution)/shard_map/while/body/eval_jaxpr/ktabd,kteb->ktaed/dot_general | solution.py:47
  63.1 8.8 %bitcast_convert_fusion.5 = bf16[4,32,32,32]{3,1,2,0:T(8,128)(2,1)S(1)} fusion(bf16[4,10,32,32,32]{4,3,2,1,0:T(8,128)(2,1)} %convert_bitcast_fusion.2, bf16[4,3,10,32,32]{4,3,2,1,0:T(8,128)(2,1)S(1)} %reshape.130), kind=kOutput, calls=%fused_computation.9.clone.1 | convolution fusion | flops 84017152 | bytes 3211264 | tf_op jit(solution)/shard_map/while/body/eval_jaxpr/ktaed,ktfa->kfed/dot_general | solution.py:50
  72.0 0.4 copy.140
  72.4 1.1 broadcast_in_dim.38
  73.4 0.8 constant_dynamic-update-slice_fusion.2
  74.2 1.0 constant_dynamic-slice_fusion.3
  75.2 0.5 reshape.130
  75.8 21.9 %convert_bitcast_fusion.2 = bf16[4,10,32,32,32]{4,3,2,1,0:T(8,128)(2,1)} fusion(bf16[4,3,10,32,32]{4,3,2,1,0:T(8,128)(2,1)S(1)} %reshape.130, bf16[4,32,32,32]{3,2,1,0:T(8,128)(2,1)} %get-tuple-element.74, s32[]{:T(128)} %get-tuple-element.66), kind=kOutput, calls=%fused_computation.6.clone.1 | convolution fusion | flops 170393600 | bytes 3539456 | tf_op jit(solution)/shard_map/while/body/eval_jaxpr/ktabd,kteb->ktaed/dot_general | solution.py:47
  97.7 8.8 %bitcast_convert_fusion.5 = bf16[4,32,32,32]{3,1,2,0:T(8,128)(2,1)S(1)} fusion(bf16[4,10,32,32,32]{4,3,2,1,0:T(8,128)(2,1)} %convert_bitcast_fusion.2, bf16[4,3,10,32,32]{4,3,2,1,0:T(8,128)(2,1)S(1)} %reshape.130), kind=kOutput, calls=%fused_computation.9.clone.1 | convolution fusion | flops 84017152 | bytes 3211264 | tf_op jit(solution)/shard_map/while/body/eval_jaxpr/ktaed,ktfa->kfed/dot_general | solution.py:50
  106.5 0.4 copy.140
  106.9 1.1 broadcast_in_dim.38
  108.0 0.8 constant_dynamic-update-slice_fusion.2
  108.7 1.0 constant_dynamic-slice_fusion.3
  109.8 0.5 reshape.130
  110.3 21.9 %convert_bitcast_fusion.2 = bf16[4,10,32,32,32]{4,3,2,1,0:T(8,128)(2,1)} fusion(bf16[4,3,10,32,32]{4,3,2,1,0:T(8,128)(2,1)S(1)} %reshape.130, bf16[4,32,32,32]{3,2,1,0:T(8,128)(2,1)} %get-tuple-element.74, s32[]{:T(128)} %get-tuple-element.66), kind=kOutput, calls=%fused_computation.6.clone.1 | convolution fusion | flops 170393600 | bytes 3539456 | tf_op jit(solution)/shard_map/while/body/eval_jaxpr/ktabd,kteb->ktaed/dot_general | solution.py:47
  132.2 8.8 %bitcast_convert_fusion.5 = bf16[4,32,32,32]{3,1,2,0:T(8,128)(2,1)S(1)} fusion(bf16[4,10,32,32,32]{4,3,2,1,0:T(8,128)(2,1)} %convert_bitcast_fusion.2, bf16[4,3,10,32,32]{4,3,2,1,0:T(8,128)(2,1)S(1)} %reshape.130), kind=kOutput, calls=%fused_computation.9.clone.1 | convolution fusion | flops 84017152 | bytes 3211264 | tf_op jit(solution)/shard_map/while/body/eval_jaxpr/ktaed,ktfa->kfed/dot_general | solution.py:50
  141.0 0.4 copy.140
  141.4 1.1 broadcast_in_dim.38
  142.5 0.8 constant_dynamic-update-slice_fusion.2
  143.3 1.0 constant_dynamic-slice_fusion.3
  144.3 0.5 reshape.130
  144.9 21.9 %convert_bitcast_fusion.2 = bf16[4,10,32,32,32]{4,3,2,1,0:T(8,128)(2,1)} fusion(bf16[4,3,10,32,32]{4,3,2,1,0:T(8,128)(2,1)S(1)} %reshape.130, bf16[4,32,32,32]{3,2,1,0:T(8,128)(2,1)} %get-tuple-element.74, s32[]{:T(128)} %get-tuple-element.66), kind=kOutput, calls=%fused_computation.6.clone.1 | convolution fusion | flops 170393600 | bytes 3539456 | tf_op jit(solution)/shard_map/while/body/eval_jaxpr/ktabd,kteb->ktaed/dot_general | solution.py:47
  166.7 8.8 %bitcast_convert_fusion.5 = bf16[4,32,32,32]{3,1,2,0:T(8,128)(2,1)S(1)} fusion(bf16[4,10,32,32,32]{4,3,2,1,0:T(8,128)(2,1)} %convert_bitcast_fusion.2, bf16[4,3,10,32,32]{4,3,2,1,0:T(8,128)(2,1)S(1)} %reshape.130), kind=kOutput, calls=%fused_computation.9.clone.1 | convolution fusion | flops 84017152 | bytes 3211264 | tf_op jit(solution)/shard_map/while/body/eval_jaxpr/ktaed,ktfa->kfed/dot_general | solution.py:50
  175.5 0.4 copy.140
  176.0 1.1 broadcast_in_dim.38
  177.0 0.8 constant_dynamic-update-slice_fusion.2
  177.8 1.4 reshape.71
  179.2 2.2 convolution_convert_fusion
  181.3 4.4 %reshape.72 = bf16[16,2,32768]{2,1,0:T(2,128)(2,1)} reshape(bf16[32,32768]{1,0:T(8,128)(2,1)} %convolution_convert_fusion) | data formatting | bytes 4194304 | tf_op jit(solution)/shard_map/reshape | solution.py:88
  185.7 6.1 %all-to-all-start.2 = ((bf16[16,2,32768]{2,1,0:T(2,128)(2,1)}), bf16[16,2,32768]{2,1,0:T(2,128)(2,1)}, u32[]{:S(2)}, u32[]{:S(2)}) async-start(bf16[16,2,32768]{2,1,0:T(2,128)(2,1)} %reshape.72), calls=%async_computation.2 | async-start | bytes 4194304 | tf_op jit(solution)/shard_map/all_to_all | solution.py:87
  191.8 0.6 reduce.7
  192.6 40.4 %all-to-all-done.2 = bf16[16,2,32768]{2,1,0:T(2,128)(2,1)} async-done(((bf16[16,2,32768]{2,1,0:T(2,128)(2,1)}), bf16[16,2,32768]{2,1,0:T(2,128)(2,1)}, u32[]{:S(2)}, u32[]{:S(2)}) %all-to-all-start.2) | async-done | bytes 2097184 | tf_op jit(solution)/shard_map/all_to_all | solution.py:87
  232.9 4.1 %reshape.73 = bf16[32,32768]{1,0:T(8,128)(2,1)} reshape(bf16[16,2,32768]{2,1,0:T(2,128)(2,1)} %all-to-all-done.2) | data formatting | bytes 4194304 | tf_op jit(solution)/shard_map/reshape | solution.py:107
  237.1 2.7 convolution_convert_fusion.1
  239.8 0.6 dynamic-slice
  241.0 28.8 %all-reduce.3.cloned.1.call-done = bf16[4,32768]{1,0:T(4,128)(2,1)} async-done(((bf16[4,32768]{1,0:T(4,128)(2,1)}), bf16[4,32768]{1,0:T(4,128)(2,1)}) %all-reduce.3.cloned.1.call-update) | async-done | bytes 262160
  269.9 1.1 constant_dynamic-slice_fusion.1
  270.9 0.3 reshape.74
  271.2 0.3 fusion.26
  271.5 0.6 fusion.21
  272.1 1.2 copy.117
  273.4 2.5 reshape.111
  275.9 6.8 %all_to_all.44 = bf16[2,8,4096]{2,0,1:T(2,128)(2,1)S(1)} all-to-all(bf16[2,8,4096]{2,0,1:T(2,128)(2,1)S(1)} %reshape.111), channel_id=1, replica_groups=mesh['leaf'=16,'oct'=2] {'oct'}, dimensions={1} | all-to-all | bytes 262144 | tf_op jit(solution)/shard_map/all_to_all | solution.py:115
  282.7 0.8 copy.95
  (29 shorter events, 0.7 us)
Async XLA Ops:
  6.5 8.1 %copy-start = (bf16[27,30720]{1,0:T(8,128)(2,1)S(1)}, bf16[27,30720]{1,0:T(8,128)(2,1)}, u32[]{:S(2)}) copy-start(bf16[27,30720]{1,0:T(8,128)(2,1)} %param.12) | copy-start | bytes 4976644
  6.5 8.0 %copy-start.1 = (bf16[32,32]{1,0:T(8,128)(2,1)S(1)}, bf16[32,32]{1,0:T(8,128)(2,1)}, u32[]{:S(2)}) copy-start(bf16[32,32]{1,0:T(8,128)(2,1)} %param.11) | copy-start | bytes 6148
  6.5 8.0 %copy-start.2 = (s32[4,4]{1,0:T(4,128)S(1)}, s32[4,4]{1,0:T(4,128)}, u32[]{:S(2)}) copy-start(s32[4,4]{1,0:T(4,128)} %param.13) | copy-start | bytes 196
  10.3 10.1 %all-to-all-start.1 = ((bf16[8,4,4096]{2,1,0:T(4,128)(2,1)}), bf16[8,4,4096]{2,1,0:T(4,128)(2,1)S(1)}, u32[]{:S(2)}, u32[]{:S(2)}) async-start(bf16[8,4,4096]{2,1,0:T(4,128)(2,1)} %reshape.85), calls=%async_computation.1 | async-start | bytes 524288 | tf_op jit(solution)/shard_map/all_to_all | solution.py:64
  14.7 3.1 %copy-start.3 = (s32[4,4,1]{1,2,0:T(1,128)S(1)}, s32[4,4,1]{1,2,0:T(1,128)}, u32[]{:S(2)}) copy-start(s32[4,4,1]{1,2,0:T(1,128)} %param.14) | copy-start | bytes 196
  14.7 4.0 %copy-start.4 = (s32[4,4]{1,0:T(4,128)S(1)}, s32[4,4]{1,0:T(4,128)}, u32[]{:S(2)}) copy-start(s32[4,4]{1,0:T(4,128)} %param.15) | copy-start | bytes 196
  20.4 165.4 %all-to-all-start = ((s32[16,1,2]{2,1,0:T(1,128)}), s32[16,1,2]{2,1,0:T(1,128)S(1)}, u32[]{:S(2)}, u32[]{:S(2)}) async-start(s32[16,1,2]{2,1,0:T(1,128)} %bitcast.16), calls=%async_computation | async-start | bytes 16384 | tf_op jit(solution)/shard_map/all_to_all | solution.py:94
  185.7 47.2 %all-to-all-start.2 = ((bf16[16,2,32768]{2,1,0:T(2,128)(2,1)}), bf16[16,2,32768]{2,1,0:T(2,128)(2,1)}, u32[]{:S(2)}, u32[]{:S(2)}) async-start(bf16[16,2,32768]{2,1,0:T(2,128)(2,1)} %reshape.72), calls=%async_computation.2 | async-start | bytes 4194304 | tf_op jit(solution)/shard_map/all_to_all | solution.py:87
  191.8 78.1 %all-reduce.3.cloned.1.call-start = ((), (), s32[]{:S(2)}) async-start(), calls=%async_computation.4 | async-start | bytes 524288
  237.1 2.7 copy-start.5
Sparse Core Ops, SparseCore 0:
  239.9 29.9 all-reduce.2
where the time goes:
time: 291 us; the launch traced here: 290 us
  matrix products  135 us (46%)
  waiting for transfers between devices  70 us (24%)
  local copies, waits for them, and re-layouts  45.5 us (16%)
  starting transfers between devices  16.5 us (6%)
  between operations  14.2 us (5%)
  blocking collectives  6.85 us (2%)
    dot_general x4, matrix products, apply_parent(): jnp.einsum('ktabd,kteb->ktaed', section_z, factor_set[:, 1], preferred_el...  87.5 us
    all_to_all x1, waiting for transfers between devices, local(): lax.all_to_all(packed_rows.reshape(leaf_count, slot_count, cube_len), 'le...  40.4 us
    dot_general x4, matrix products, apply_parent(): jnp.einsum('ktaed,ktfa->kfed', section_y, factor_set[:, 0], preferred_ele...  35.2 us
    unnamed x2, waiting for transfers between devices  28.8 us
    all_to_all x1, blocking collectives, local(): lax.all_to_all(child_blocks, 'oct', split_axis=1, concat_axis=0, tiled=True)  6.85 us
    all_to_all x1, starting transfers between devices, local(): lax.all_to_all(packed_ids.reshape(leaf_count, slot_count), 'leaf', split_...  6.19 us
    all_to_all x1, starting transfers between devices, local(): lax.all_to_all(packed_rows.reshape(leaf_count, slot_count, cube_len), 'le...  6.06 us
  transfers between devices with their start and end apart: 4, of which 3 were waited for; matrix products, arithmetic and copies ran while one was open for 57% of the time, Pallas kernels for 0%

commit v1 on v0

v1 whole, which is shorter than its diff:
```python
import functools

import jax
import jax.numpy as jnp
from jax import lax
from jax.experimental import pallas as pl
from jax.experimental.pallas import tpu as pltpu
from jax.sharding import PartitionSpec as P

BF = jnp.bfloat16
F32 = jnp.float32


def dot(x, y):
    return jnp.dot(x, y, preferred_element_type=F32)


def apply_kernel(
    kind_ref, near_ref, far_ref, ft1_ref, ft2_ref, f0_ref, s1e_ref, s2e_ref, m1_ref, m2_ref,
    fw1_ref, fw2_ref, sa_ref, st_ref, keep_ref, send_ref, cube_ref, sec_ref, *, half,
):
    edge = 2 * half
    low = half // 2
    wide = edge * low
    quarter = wide // 4
    terms = f0_ref.shape[2] // edge

    @pl.when(pl.program_id(0) == 0)
    def _():
        total = None
        for bit in range(2):
            rows = []
            for mid in range(2):
                rows += [near_ref[0, 2 * mid + bit], far_ref[0, 2 * mid + bit]]
            part = dot(jnp.concatenate(rows, axis=0), fw1_ref[bit])
            total = part if total is None else total + part
        total = total.astype(BF)
        lanes = wide // 2
        moved = jnp.concatenate(
            [
                jnp.concatenate(
                    [
                        total[:edge, lanes * i : lanes * (i + 1)],
                        total[edge:, lanes * i : lanes * (i + 1)],
                    ],
                    axis=1,
                )
                for i in range(4)
            ],
            axis=0,
        )
        second = dot(moved, fw2_ref[...]).astype(BF)
        for i in range(4):
            cube_ref[edge * i : edge * (i + 1), :] = dot(
                sa_ref[...], second[edge * i : edge * (i + 1)]
            ).astype(BF)

    cube = cube_ref[...]
    w1e = dot(ft1_ref[0], s1e_ref[...]).astype(BF)
    w2e = dot(ft2_ref[0], s2e_ref[...]).astype(BF)
    g0 = dot(st_ref[...], f0_ref[0]).astype(BF)
    for t in range(terms):
        one = w1e[edge * t : edge * (t + 1)]
        w1 = jnp.concatenate(
            [one * m1_ref[edge * i : edge * (i + 1), :] for i in range(low)], axis=0
        )
        first = dot(cube, w1).astype(BF)
        moved = jnp.concatenate(
            [
                jnp.concatenate(
                    [
                        first[edge * i : edge * (i + 1), quarter * j : quarter * (j + 1)]
                        for i in range(4)
                    ],
                    axis=1,
                )
                for j in range(4)
            ],
            axis=0,
        )
        base = 2 * edge * t
        w2 = jnp.concatenate(
            [
                w2e[base + half * i : base + half * (i + 1)] * m2_ref[half * q : half * (q + 1), :]
                for i in range(4)
                for q in range(low // 2)
            ],
            axis=0,
        )
        second = dot(moved, w2).astype(BF)
        for i in range(4):
            sec_ref[i, edge * t : edge * (t + 1), :] = second[edge * i : edge * (i + 1)]
    for i in range(4):
        out = dot(g0, sec_ref[i]).astype(BF)
        keep_ref[0, :, wide * i : wide * (i + 1)] = out[:half]
        send_ref[0, :, wide * i : wide * (i + 1)] = out[half:]


def apply_parent(parent, kinds, near, far, ft1, ft2, f0, consts, half):
    s1e, s2e, m1, m2, fw1, fw2, sa, st = consts
    disps = kinds.shape[0]
    edge = 2 * half
    wide = edge * half // 2
    terms = f0.shape[2] // edge

    def whole(array):
        return pl.BlockSpec(array.shape, lambda k, kinds: (0,) * array.ndim)

    def of_kind(array):
        return pl.BlockSpec((1,) + array.shape[1:], lambda k, kinds: (kinds[k], 0, 0))

    def of_parent(array):
        return pl.BlockSpec((1,) + array.shape[1:], lambda k, kinds: (parent, 0, 0, 0))

    shape = jax.ShapeDtypeStruct((disps, half, 4 * wide), BF)
    out_spec = pl.BlockSpec((1, half, 4 * wide), lambda k, kinds: (k, 0, 0))
    return pl.pallas_call(
        functools.partial(apply_kernel, half=half),
        grid_spec=pltpu.PrefetchScalarGridSpec(
            num_scalar_prefetch=1,
            grid=(disps,),
            in_specs=[
                of_parent(near),
                of_parent(far),
                of_kind(ft1),
                of_kind(ft2),
                of_kind(f0),
                whole(s1e),
                whole(s2e),
                whole(m1),
                whole(m2),
                whole(fw1),
                whole(fw2),
                whole(sa),
                whole(st),
            ],
            out_specs=[out_spec, out_spec],
            scratch_shapes=[
                pltpu.VMEM((4 * edge, wide), BF),
                pltpu.VMEM((4, terms * edge, wide), BF),
            ],
        ),
        out_shape=[shape, shape],
        compiler_params=pltpu.CompilerParams(vmem_limit_bytes=48 * 1024 * 1024),
    )(kinds, near, far, ft1, ft2, f0, s1e, s2e, m1, m2, fw1, fw2, sa, st)


def sum_kernel(slot_ref, *refs, rows):
    row_refs, (even_ref, odd_ref, total_ref) = refs[:-3], refs[-3:]
    total_ref[...] = jnp.zeros_like(total_ref)
    for i in range(len(row_refs)):
        for j in range(rows):
            slot = slot_ref[i * rows + j]
            total_ref[slot] = total_ref[slot] + row_refs[i][j].astype(F32)
    count = even_ref.shape[0]
    even_ref[...] = total_ref[:count].astype(BF)
    odd_ref[...] = total_ref[count:].astype(BF)


def sum_rows(slots, arrays, slot_count):
    rows = arrays[0].shape[0]
    tail = arrays[0].shape[1:]
    shape = jax.ShapeDtypeStruct((slot_count // 2,) + tail, BF)
    return pl.pallas_call(
        functools.partial(sum_kernel, rows=rows),
        in_specs=[pl.BlockSpec(memory_space=pltpu.SMEM)]
        + [pl.BlockSpec(memory_space=pltpu.VMEM)] * len(arrays),
        out_specs=[pl.BlockSpec(memory_space=pltpu.VMEM)] * 2,
        out_shape=[shape, shape],
        scratch_shapes=[pltpu.VMEM((slot_count,) + tail, F32)],
        compiler_params=pltpu.CompilerParams(vmem_limit_bytes=60 * 1024 * 1024),
    )(slots, *arrays)


def swap(x, axis, mask):
    count = lax.axis_size(axis)
    return lax.ppermute(x, axis, [(i, i ^ mask) for i in range(count)])


def local(children, child_slot, two_scale, factors, disp_kind, target_leaf, target_node):
    oct_count = lax.axis_size("oct")
    leaf_count = lax.axis_size("leaf")
    my_leaf = lax.axis_index("leaf")
    my_oct = lax.axis_index("oct")
    edge = two_scale.shape[0]
    half = edge // 2
    low = half // 2
    wide = edge * low
    held = child_slot.shape[1]
    parents, disps = disp_kind.shape
    paired = oct_count == 2

    blocks = children.reshape(-1, half, half * half)
    if paired:
        theirs = lax.dynamic_slice_in_dim(child_slot, (1 - my_oct) * parents, parents, 0)
        mine = lax.dynamic_slice_in_dim(child_slot, my_oct * parents, parents, 0)
        far = swap(blocks[theirs], "oct", 1)
        near = blocks[mine]
    else:
        arrived = lax.all_to_all(
            blocks[child_slot], "oct", split_axis=0, concat_axis=1, tiled=True
        ).reshape(parents, 2, 4, half, half * half)
        near, far = arrived[:, 0], arrived[:, 1]

    nodes = 2 * oct_count
    goal = target_leaf.reshape(parents, disps) * nodes + target_node
    if paired:
        goals = jnp.stack([goal, swap(goal, "oct", 1)], axis=1)
    else:
        goals = lax.all_gather(goal, "oct").transpose(1, 0, 2)
    leaf_off = jnp.bitwise_xor(goals // nodes, my_leaf)
    slots = ((leaf_off % 2) * (leaf_count // 2) + leaf_off // 2) * nodes + goals % nodes

    kinds = factors.shape[0]
    table = factors.reshape(kinds, 3, -1, edge, edge)
    terms = table.shape[2]
    f0 = table[:, 0].transpose(0, 2, 1, 3).reshape(kinds, edge, terms * edge)
    ft1 = table[:, 1].transpose(0, 1, 3, 2).reshape(kinds, terms * edge, edge)
    ft2 = table[:, 2].transpose(0, 1, 3, 2).reshape(kinds, terms * 4, 1, low, edge)
    ft2 = jnp.broadcast_to(ft2, (kinds, terms * 4, 2, low, edge)).reshape(
        kinds, terms * 2 * edge, edge
    )
    lane = jnp.arange(wide)
    row = jnp.arange(wide)
    s1e = jnp.repeat(two_scale, low, axis=1)
    s2e = jnp.broadcast_to(
        two_scale.reshape(edge, 2, 1, half), (edge, 2, low, half)
    ).reshape(edge, wide)
    m1 = (row[:, None] // edge == lane[None, :] % low).astype(BF)
    dup_rows = jnp.arange(2 * edge)
    m2 = (dup_rows[:, None] // low == (lane[None, :] // half) % low).astype(BF)
    transposed = two_scale.T
    by_bit = jnp.repeat(transposed.reshape(2, half, edge), half, axis=2)
    fw1 = jnp.where(
        (row[:, None] // half == jnp.arange(2 * wide)[None, :] % half)[None],
        jnp.tile(by_bit, (1, half, 1)),
        jnp.zeros((), BF),
    )
    spread = jnp.broadcast_to(
        jnp.tile(transposed, (1, low)).reshape(2, 1, half, wide), (2, low, half, wide)
    ).reshape(wide, wide)
    fw2 = jnp.where(
        (row[:, None] // half) % low == lane[None, :] // edge, spread, jnp.zeros((), BF)
    )
    if paired:
        turned = two_scale.reshape(edge, 2, half)
        turned = jnp.where(my_oct == 0, turned, turned[:, ::-1]).reshape(edge, edge)
    else:
        turned = two_scale
    consts = (s1e, s2e, m1, m2, fw1, fw2, turned, turned.T)

    arrays = []
    for parent in range(parents):
        kept, sent = apply_parent(
            parent, disp_kind[parent], near, far, ft1, ft2, f0, consts, half
        )
        if paired:
            arrays += [kept, swap(sent, "oct", 1)]
        else:
            rows = jnp.stack([kept, sent], axis=1).reshape(disps, 2, half, 2, 2, 2, low * half)
            rows = rows.transpose(1, 3, 5, 0, 2, 4, 6)
            rows = rows.reshape(oct_count, held, disps, half, half * half)
            rows = rows.transpose(0, 2, 1, 3, 4)
            rows = lax.all_to_all(rows, "oct", split_axis=0, concat_axis=0, tiled=True)
            arrays += [rows.reshape(oct_count * disps, held * half, half * half)]

    even, odd = sum_rows(slots.reshape(-1), arrays, leaf_count * nodes)
    total = even.astype(F32) + swap(odd, "leaf", 1).astype(F32)
    total = total.astype(BF).reshape((leaf_count // 2, nodes) + total.shape[1:])
    mask = 2
    while mask < leaf_count:
        pairs = total.reshape((-1, 2) + total.shape[1:])
        total = pairs[:, 0].astype(F32) + swap(pairs[:, 1], "leaf", mask).astype(F32)
        total = total.astype(BF)
        mask *= 2
    total = total.reshape(nodes, -1)
    if paired:
        out = total.reshape(nodes, half, 2, 2, 2, low * half)
        return out.transpose(0, 2, 4, 1, 3, 5).reshape(nodes, held, -1)
    return total.reshape(nodes, held, -1)


def solution(mesh):
    placed = (
        P(("leaf", "oct"), None),
        P("leaf", "oct"),
        P(),
        P(),
        P(("leaf", "oct"), None),
        P(("leaf", "oct"), None, None),
        P(("leaf", "oct"), None),
    )
    return jax.shard_map(
        local, mesh=mesh, in_specs=placed, out_specs=P("leaf", "oct", None), check_vma=False
    )
```

time: 291 us -> 129 us (0.44)
  matrix products: 135 us -> 0 us
  waiting for transfers between devices: 70 us -> 30.5 us
  Pallas kernels: 0 us -> 27.5 us
  between operations: 14.2 us -> 0.35 us
  blocking collectives: 6.85 us -> 0 us
  other arithmetic: 2.43 us -> 9.26 us
  starting transfers between devices: 16.5 us -> 12.9 us
    dot_general x14 -> x0, matrix products: 135 us -> none  [the longest x4 87.5 us: apply_parent(): jnp.einsum('ktabd,kteb->ktaed', section_z, factor_set[:, 1], preferred_el...]
    all_to_all x3 -> x0, waiting for transfers between devices: 41.1 us -> none  [the longest x1 40.4 us: local(): lax.all_to_all(packed_rows.reshape(leaf_count, slot_count, cube_len), 'le...]
    ppermute x0 -> x10, waiting for transfers between devices: none -> 30.5 us  [swap(): return lax.ppermute(x, axis, [(i, i ^ mask) for i in range(count)])]
    unnamed x2 -> x0, waiting for transfers between devices: 28.8 us -> none
    pallas_call x0 -> x5, Pallas kernels: none -> 27.5 us  [the longest x4 24.2 us: apply_parent(): pl.pallas_call(functools.partial(apply_kernel, half=half), grid_spec=pltp...]
    all_to_all x3 -> x0, starting transfers between devices: 16.5 us -> none  [the longest x1 6.19 us: local(): lax.all_to_all(packed_ids.reshape(leaf_count, slot_count), 'leaf', split_...]
    unnamed x16 -> x43, local copies, waits for them, and re-layouts: 2.31 us -> 16.1 us
    ppermute x0 -> x10, starting transfers between devices: none -> 12.9 us  [swap(): return lax.ppermute(x, axis, [(i, i ^ mask) for i in range(count)])]
  transfers between devices with their start and end apart: 4 -> 10, of which waited for: 3 -> 5; matrix products, arithmetic and copies ran while one was open for 57% -> 35% of each run, Pallas kernels for 0% -> 14%
where the time goes in v1:
time: 129 us; the launch traced here: 128 us
  local copies, waits for them, and re-layouts  47.7 us (37%)
  waiting for transfers between devices  30.5 us (24%)
  Pallas kernels  27.5 us (21%)
  starting transfers between devices  12.9 us (10%)
  other arithmetic  9.26 us (7%)
    ppermute x10, waiting for transfers between devices, swap(): return lax.ppermute(x, axis, [(i, i ^ mask) for i in range(count)])  30.5 us
    pallas_call x4, Pallas kernels, apply_parent(): pl.pallas_call(functools.partial(apply_kernel, half=half), grid_spec=pltp...  24.2 us
    unnamed x43, local copies, waits for them, and re-layouts  16.1 us
    ppermute x10, starting transfers between devices, swap(): return lax.ppermute(x, axis, [(i, i ^ mask) for i in range(count)])  12.9 us
    reshape x1, local copies, waits for them, and re-layouts, local(): table = factors.reshape(kinds, 3, -1, edge, edge)  7.27 us
    slice x1, local copies, waits for them, and re-layouts, local(): f0 = table[:, 0].transpose(0, 2, 1, 3).reshape(kinds, edge, terms * edge)  6.31 us
    broadcast_in_dim x1, local copies, waits for them, and re-layouts, local(): jnp.broadcast_to(ft2, (kinds, terms * 4, 2, low, edge))  4.4 us
    reshape x1, local copies, waits for them, and re-layouts, local(): f0 = table[:, 0].transpose(0, 2, 1, 3).reshape(kinds, edge, terms * edge)  3.98 us
  transfers between devices with their start and end apart: 10, of which 5 were waited for; matrix products, arithmetic and copies ran while one was open for 35% of the time, Pallas kernels for 14%

profile of v1, /device:TPU:0, one launch (start us, length us, event | category | flops | bytes accessed | tf_op | source)
XLA Modules:
  0.0 128.2 jit_solution(16307883034967829756)
XLA Ops:
  0.0 0.7 broadcast_multiply_fusion
  0.7 1.3 add.138
  1.9 2.9 %collective-permute-start = (s32[4,4]{1,0:T(4,128)}, s32[4,4]{1,0:T(4,128)}, u32[]{:S(2)}, u32[]{:S(2)}) collective-permute-start(s32[4,4]{1,0:T(4,128)} %add.138), channel_id=1, source_target_pairs={{0,1},{1,0},{2,3},{3,2},{4,5},{5,4},{6,7},{7,6},{8,9},{9,8},{10,11... | collective-permute-start | bytes 200 | tf_op jit(solution)/shard_map/ppermute | solution.py:177
  4.9 1.0 copy.76
  5.9 0.8 compare_select_fusion.1
  6.7 0.1 copy.47
  6.8 0.1 reshape.369
  6.9 1.2 gather_fusion.1
  8.2 1.4 %slice_bitcast_fusion.6 = (s32[4]{0:T(128)}, s32[4]{0:T(128)}, s32[4]{0:T(128)}, s32[4]{0:T(128)}) fusion(s32[4,4]{1,0:T(4,128)} %param.11), kind=kLoop, calls=%fused_computation.65 | loop fusion | bytes 128 | tf_op jit(solution)/shard_map/squeeze | solution.py:255
  9.6 0.1 copy.46
  9.7 0.1 reshape.361
  9.8 7.3 %reshape.344 = bf16[27,3,10,32,32]{4,3,2,1,0:T(8,128)(2,1)} reshape(bf16[27,30720]{1,0:T(8,128)(2,1)} %param.10) | data formatting | bytes 3317760 | tf_op jit(solution)/shard_map/reshape | solution.py:215
  17.0 6.3 %fusion.12 = (bf16[27,1,10,32,32]{4,3,2,1,0:T(8,128)(2,1)}, bf16[27,1,10,32,32]{4,3,2,1,0:T(8,128)(2,1)}, bf16[27,1,10,32,32]{4,3,2,1,0:T(8,128)(2,1)}) fusion(bf16[27,3,10,32,32]{4,3,2,1,0:T(8,128)(2,1)} %reshape.344), kind=kLoop, calls=%fused_computation.69 | loop fusion | bytes 3317760 | tf_op jit(solution)/shard_map/slice | solution.py:217
  23.3 0.1 copy.51
  23.4 0.1 compare_convert_fusion.m1_ref
  23.6 0.7 compare_convert_fusion.1.m2_ref
  24.2 0.8 broadcast_compare_fusion
  25.0 1.2 gather_fusion
  26.3 2.9 %copy.70 = bf16[27,1,10,32,32]{3,4,2,0,1:T(8,128)(2,1)S(1)} copy(bf16[27,1,10,32,32]{4,3,2,1,0:T(8,128)(2,1)} %get-tuple-element.26) | data formatting | bytes 1105920
  29.2 4.2 %copy.71 = bf16[27,1,10,32,32]{3,4,2,0,1:T(8,128)(2,1)} copy(bf16[27,1,10,32,32]{4,3,2,1,0:T(8,128)(2,1)} %get-tuple-element.27) | data formatting | bytes 1105920
  33.4 4.6 %copy.78 = bf16[27,1,10,32,32]{4,2,3,0,1:T(8,128)(2,1)} copy(bf16[27,1,10,32,32]{4,3,2,1,0:T(8,128)(2,1)} %get-tuple-element.25) | data formatting | bytes 1105920
  38.0 4.0 %reshape.347.f0_ref = bf16[27,32,320]{2,1,0:T(8,128)(2,1)S(1)} reshape(bf16[27,32,10,32]{3,2,1,0:T(8,128)(2,1)} %bitcast.98) | data formatting | bytes 1105920 | tf_op jit(solution)/shard_map/reshape | solution.py:217
  42.0 0.1 copy.54.s1e_ref
  42.1 0.7 copy.55.s2e_ref
  42.8 0.2 broadcast_in_dim.66
  43.0 0.9 tile.16
  43.9 0.1 broadcast_in_dim.68
  44.0 0.8 compare_select_fusion.fw2_ref
  44.8 0.7 copy.56.sa_ref
  45.5 1.0 bitcast_select_fusion.fw1_ref
  46.4 0.7 pad_add_fusion
  47.1 0.6 copy.45
  47.7 1.3 stack.14
  49.0 4.4 %broadcast_in_dim.61 = bf16[27,40,2,8,32]{4,3,2,1,0:T(8,128)(2,1)} broadcast(bf16[27,40,8,32]{3,2,1,0:T(8,128)(2,1)} %bitcast.99), dimensions={0,1,3,4} | broadcast | bytes 1658880 | tf_op jit(solution)/shard_map/broadcast_in_dim | solution.py:220
  53.5 6.1 %shard_map.73 = (bf16[4,16,1024]{2,1,0:T(8,128)(2,1)S(1)}, bf16[4,16,1024]{2,1,0:T(8,128)(2,1)S(1)}) custom-call(s32[4]{0:T(128)S(1)} %copy-done.12, bf16[4,4,16,256]{3,2,1,0:T(8,128)(2,1)S(1)} %bitcast.85, bf16[4,4,16,256]{3,2,1,0:T(8,128)(2,1)} %collective-permute-done.1.far_ref, bf16[27,320,32]{2,1,0:T(8,128)(2,1)S(1)} %bitcast.81, ...), custom_call_target="tpu_custom_call" | custom-call | tf_op jit(solution)/shard_map/pallas_call | solution.py:117
  59.5 0.0 copy-start.5
  59.5 0.6 copy-done.5
  60.2 2.0 %collective-permute-start.2 = (bf16[4,16,1024]{2,1,0:T(8,128)(2,1)S(1)}, bf16[4,16,1024]{2,1,0:T(8,128)(2,1)S(1)}, u32[]{:S(2)}, u32[]{:S(2)}) collective-permute-start(bf16[4,16,1024]{2,1,0:T(8,128)(2,1)S(1)} %get-tuple-element.16), channel_id=1, source_target_pairs={{0,1},{1,0},{2,3},{3,2},{4,5},{5,4},{6,7},{7,6},{8,9},{9,8},{10,11... | collective-permute-start | bytes 393224 | tf_op jit(solution)/shard_map/ppermute | solution.py:177
  62.2 6.1 %shard_map.74 = (bf16[4,16,1024]{2,1,0:T(8,128)(2,1)S(1)}, bf16[4,16,1024]{2,1,0:T(8,128)(2,1)S(1)}) custom-call(s32[4]{0:T(128)S(1)} %copy-done.11, bf16[4,4,16,256]{3,2,1,0:T(8,128)(2,1)S(1)} %bitcast.86, bf16[4,4,16,256]{3,2,1,0:T(8,128)(2,1)} %collective-permute-done.1.far_ref, bf16[27,320,32]{2,1,0:T(8,128)(2,1)S(1)} %bitcast.82, ...), custom_call_target="tpu_custom_call" | custom-call | tf_op jit(solution)/shard_map/pallas_call | solution.py:117
  68.3 0.6 copy-done.6
  68.9 0.0 collective-permute-start.3
  68.9 6.1 %shard_map.75 = (bf16[4,16,1024]{2,1,0:T(8,128)(2,1)S(1)}, bf16[4,16,1024]{2,1,0:T(8,128)(2,1)S(1)}) custom-call(s32[4]{0:T(128)S(1)} %copy-done.10, bf16[4,4,16,256]{3,2,1,0:T(8,128)(2,1)S(1)} %bitcast.87, bf16[4,4,16,256]{3,2,1,0:T(8,128)(2,1)} %collective-permute-done.1.far_ref, bf16[27,320,32]{2,1,0:T(8,128)(2,1)S(1)} %bitcast.83, ...), custom_call_target="tpu_custom_call" | custom-call | tf_op jit(solution)/shard_map/pallas_call | solution.py:117
  75.0 0.7 copy-done.7
  75.7 2.0 %collective-permute-start.4 = (bf16[4,16,1024]{2,1,0:T(8,128)(2,1)S(1)}, bf16[4,16,1024]{2,1,0:T(8,128)(2,1)S(1)}, u32[]{:S(2)}, u32[]{:S(2)}) collective-permute-start(bf16[4,16,1024]{2,1,0:T(8,128)(2,1)S(1)} %get-tuple-element.20), channel_id=1, source_target_pairs={{0,1},{1,0},{2,3},{3,2},{4,5},{5,4},{6,7},{7,6},{8,9},{9,8},{10,11... | collective-permute-start | bytes 393224 | tf_op jit(solution)/shard_map/ppermute | solution.py:177
  77.7 6.1 %shard_map.76 = (bf16[4,16,1024]{2,1,0:T(8,128)(2,1)S(1)}, bf16[4,16,1024]{2,1,0:T(8,128)(2,1)S(1)}) custom-call(s32[4]{0:T(128)S(1)} %copy-done.9, bf16[4,4,16,256]{3,2,1,0:T(8,128)(2,1)S(1)} %bitcast.88, bf16[4,4,16,256]{3,2,1,0:T(8,128)(2,1)} %collective-permute-done.1.far_ref, bf16[27,320,32]{2,1,0:T(8,128)(2,1)S(1)} %bitcast.84, ...), custom_call_target="tpu_custom_call" | custom-call | tf_op jit(solution)/shard_map/pallas_call | solution.py:117
  83.8 0.6 copy-done.8
  84.4 0.0 collective-permute-start.5
  84.4 0.5 fusion.9.slot_ref
  85.0 4.4 %collective-permute-done.5.refs_7_ = bf16[4,16,1024]{2,1,0:T(8,128)(2,1)S(1)} collective-permute-done((bf16[4,16,1024]{2,1,0:T(8,128)(2,1)S(1)}, bf16[4,16,1024]{2,1,0:T(8,128)(2,1)S(1)}, u32[]{:S(2)}, u32[]{:S(2)}) %collective-permute-start.5) | collective-permute-done | bytes 131104 | tf_op jit(solution)/shard_map/ppermute | solution.py:177
  89.4 0.6 copy-done.16
  90.0 3.2 %shard_map.77 = (bf16[32,16,1024]{2,1,0:T(8,128)(2,1)}, bf16[32,16,1024]{2,1,0:T(8,128)(2,1)}) custom-call(s32[32]{0:T(128)} %fusion.9.slot_ref, bf16[4,16,1024]{2,1,0:T(8,128)(2,1)} %copy-done.5, bf16[4,16,1024]{2,1,0:T(8,128)(2,1)} %copy-done.13, bf16[4,16,1024]{2,1,0:T(8,128)(2,1)} %copy-done.6, bf16[4,16,1024]{2,1,0:T(8,128)(2,1)} %copy-done.14, ...), custom_call_target="tpu_custom_call" | custom-call | tf_op jit(solution)/shard_map/pallas_call | solution.py:164
  93.2 2.9 %collective-permute-done.6 = bf16[32,16,1024]{2,1,0:T(8,128)(2,1)S(1)} collective-permute-done((bf16[32,16,1024]{2,1,0:T(8,128)(2,1)}, bf16[32,16,1024]{2,1,0:T(8,128)(2,1)S(1)}, u32[]{:S(2)}, u32[]{:S(2)}) %collective-permute-start.6) | collective-permute-done | bytes 1048608 | tf_op jit(solution)/shard_map/ppermute | solution.py:177
  96.1 1.6 %add_convert_fusion = bf16[32,16,1024]{2,1,0:T(8,128)(2,1)S(1)} fusion(bf16[32,16,1024]{2,1,0:T(8,128)(2,1)S(1)} %collective-permute-done.6, bf16[32,16,1024]{2,1,0:T(8,128)(2,1)} %get-tuple-element.23), kind=kLoop, calls=%fused_computation.3 | loop fusion | flops 2097152 | bytes 3145728 | tf_op jit(solution)/shard_map/convert_element_type | solution.py:269
  97.8 1.6 %collective-permute-start.7 = (bf16[4,4,16,1024]{3,2,1,0:T(8,128)(2,1)S(1)}, bf16[4,4,16,1024]{3,2,1,0:T(8,128)(2,1)S(1)}, u32[]{:S(2)}, u32[]{:S(2)}) collective-permute-start(bf16[4,4,16,1024]{3,2,1,0:T(8,128)(2,1)S(1)} %slice_bitcast_fusion), channel_id=1, source_target_pairs={{0,4},{2,6},{4,0},{6,2},{8,12},{10,14},{12,8},{14,10},{16,20},{18,... | collective-permute-start | bytes 1572872 | tf_op jit(solution)/shard_map/ppermute | solution.py:177
  99.4 12.4 %collective-permute-done.7 = bf16[4,4,16,1024]{3,2,1,0:T(8,128)(2,1)S(1)} collective-permute-done((bf16[4,4,16,1024]{3,2,1,0:T(8,128)(2,1)S(1)}, bf16[4,4,16,1024]{3,2,1,0:T(8,128)(2,1)S(1)}, u32[]{:S(2)}, u32[]{:S(2)}) %collective-permute-start.7) | collective-permute-done | bytes 524320 | tf_op jit(solution)/shard_map/ppermute | solution.py:177
  111.8 0.2 fusion
  112.0 1.7 %collective-permute-start.8 = (bf16[2,4,16,1024]{3,2,1,0:T(8,128)(2,1)S(1)}, bf16[2,4,16,1024]{3,2,1,0:T(8,128)(2,1)S(1)}, u32[]{:S(2)}, u32[]{:S(2)}) collective-permute-start(bf16[2,4,16,1024]{3,2,1,0:T(8,128)(2,1)S(1)} %slice_bitcast_fusion.2), channel_id=1, source_target_pairs={{0,8},{2,10},{4,12},{6,14},{8,0},{10,2},{12,4},{14,6},{16,24},{18,... | collective-permute-start | bytes 786440 | tf_op jit(solution)/shard_map/ppermute | solution.py:177
  113.7 5.9 %collective-permute-done.8 = bf16[2,4,16,1024]{3,2,1,0:T(8,128)(2,1)S(1)} collective-permute-done((bf16[2,4,16,1024]{3,2,1,0:T(8,128)(2,1)S(1)}, bf16[2,4,16,1024]{3,2,1,0:T(8,128)(2,1)S(1)}, u32[]{:S(2)}, u32[]{:S(2)}) %collective-permute-start.8) | collective-permute-done | bytes 262176 | tf_op jit(solution)/shard_map/ppermute | solution.py:177
  119.6 0.1 fusion.2
  119.7 2.7 %collective-permute-start.9 = (bf16[1,4,16,1024]{3,2,1,0:T(8,128)(2,1)S(1)}, bf16[1,4,16,1024]{3,2,1,0:T(8,128)(2,1)S(1)}, u32[]{:S(2)}, u32[]{:S(2)}) collective-permute-start(bf16[1,4,16,1024]{3,2,1,0:T(8,128)(2,1)S(1)} %slice_bitcast_fusion.4), channel_id=1, source_target_pairs={{0,16},{2,18},{4,20},{6,22},{8,24},{10,26},{12,28},{14,30},{16,0},... | collective-permute-start | bytes 393224 | tf_op jit(solution)/shard_map/ppermute | solution.py:177
  122.4 4.9 %collective-permute-done.9 = bf16[1,4,16,1024]{3,2,1,0:T(8,128)(2,1)S(1)} collective-permute-done((bf16[1,4,16,1024]{3,2,1,0:T(8,128)(2,1)S(1)}, bf16[1,4,16,1024]{3,2,1,0:T(8,128)(2,1)S(1)}, u32[]{:S(2)}, u32[]{:S(2)}) %collective-permute-start.9) | collective-permute-done | bytes 131104 | tf_op jit(solution)/shard_map/ppermute | solution.py:177
  127.3 0.1 reshape_reshape.7
  127.4 0.1 copy.69
  127.5 0.7 reshape.355
  (54 shorter events, 0.3 us)
Async XLA Ops:
  1.9 44.5 %collective-permute-start = (s32[4,4]{1,0:T(4,128)}, s32[4,4]{1,0:T(4,128)}, u32[]{:S(2)}, u32[]{:S(2)}) collective-permute-start(s32[4,4]{1,0:T(4,128)} %add.138), channel_id=1, source_target_pairs={{0,1},{1,0},{2,3},{3,2},{4,5},{5,4},{6,7},{7,6},{8,9},{9,8},{10,11... | collective-permute-start | bytes 200 | tf_op jit(solution)/shard_map/ppermute | solution.py:177
  8.1 40.9 %collective-permute-start.1 = (bf16[4,4,16,256]{3,2,1,0:T(8,128)(2,1)}, bf16[4,4,16,256]{3,2,1,0:T(8,128)(2,1)}, u32[]{:S(2)}, u32[]{:S(2)}) collective-permute-start(bf16[4,4,16,256]{3,2,1,0:T(8,128)(2,1)} %bitcast.5), channel_id=1, source_target_pairs={{0,1},{1,0},{2,3},{3,2},{4,5},{5,4},{6,7},{7,6},{8,9},{9,8},{10,11... | collective-permute-start | bytes 393224 | tf_op jit(solution)/shard_map/ppermute | solution.py:177
  17.0 6.3 %copy-start.17 = (bf16[32,32]{1,0:T(8,128)(2,1)S(1)}, bf16[32,32]{1,0:T(8,128)(2,1)}, u32[]{:S(2)}) copy-start(bf16[32,32]{1,0:T(8,128)(2,1)} %param.9) | copy-start | bytes 6148
  49.0 4.4 %copy-start = (bf16[16,16,256]{2,1,0:T(8,128)(2,1)S(1)}, bf16[16,16,256]{2,1,0:T(8,128)(2,1)}, u32[]{:S(2)}) copy-start(bf16[16,16,256]{2,1,0:T(8,128)(2,1)} %gather_fusion) | copy-start | bytes 393220
  49.0 4.4 %copy-start.1 = (bf16[256,256]{1,0:T(8,128)(2,1)S(1)}, bf16[256,256]{1,0:T(8,128)(2,1)}, u32[]{:S(2)}) copy-start(bf16[256,256]{1,0:T(8,128)(2,1)} %compare_select_fusion.fw2_ref) | copy-start | bytes 393220
  49.0 4.4 %copy-start.2 = (bf16[64,256]{1,0:T(8,128)(2,1)S(1)}, bf16[64,256]{1,0:T(8,128)(2,1)}, u32[]{:S(2)}) copy-start(bf16[64,256]{1,0:T(8,128)(2,1)} %compare_convert_fusion.1.m2_ref) | copy-start | bytes 98308
  49.0 4.4 %copy-start.3 = (bf16[32,256]{1,0:T(8,128)(2,1)S(1)}, bf16[32,256]{1,0:T(8,128)(2,1)}, u32[]{:S(2)}) copy-start(bf16[32,256]{1,0:T(8,128)(2,1)} %copy.55.s2e_ref) | copy-start | bytes 49156
  49.0 4.4 %copy-start.4 = (bf16[32,32]{1,0:T(8,128)(2,1)S(1)}, bf16[32,32]{1,0:T(8,128)(2,1)}, u32[]{:S(2)}) copy-start(bf16[32,32]{1,0:T(8,128)(2,1)} %copy.56.sa_ref) | copy-start | bytes 6148
  49.0 4.4 %copy-start.12 = (s32[4]{0:T(128)S(1)}, s32[4]{0:T(128)}, u32[]{:S(2)}) copy-start(s32[4]{0:T(128)} %get-tuple-element.30.kind_ref) | copy-start | bytes 52
  53.4 8.8 %copy-start.11 = (s32[4]{0:T(128)S(1)}, s32[4]{0:T(128)}, u32[]{:S(2)}) copy-start(s32[4]{0:T(128)} %get-tuple-element.29.kind_ref) | copy-start | bytes 52
  59.5 0.7 copy-start.5
  60.2 24.8 %collective-permute-start.2 = (bf16[4,16,1024]{2,1,0:T(8,128)(2,1)S(1)}, bf16[4,16,1024]{2,1,0:T(8,128)(2,1)S(1)}, u32[]{:S(2)}, u32[]{:S(2)}) collective-permute-start(bf16[4,16,1024]{2,1,0:T(8,128)(2,1)S(1)} %get-tuple-element.16), channel_id=1, source_target_pairs={{0,1},{1,0},{2,3},{3,2},{4,5},{5,4},{6,7},{7,6},{8,9},{9,8},{10,11... | collective-permute-start | bytes 393224 | tf_op jit(solution)/shard_map/ppermute | solution.py:177
  62.2 6.7 %copy-start.10 = (s32[4]{0:T(128)S(1)}, s32[4]{0:T(128)}, u32[]{:S(2)}) copy-start(s32[4]{0:T(128)} %get-tuple-element.31.kind_ref) | copy-start | bytes 52
  68.3 0.7 copy-start.6
  68.9 16.1 %collective-permute-start.3 = (bf16[4,16,1024]{2,1,0:T(8,128)(2,1)S(1)}, bf16[4,16,1024]{2,1,0:T(8,128)(2,1)S(1)}, u32[]{:S(2)}, u32[]{:S(2)}) collective-permute-start(bf16[4,16,1024]{2,1,0:T(8,128)(2,1)S(1)} %get-tuple-element.18), channel_id=1, source_target_pairs={{0,1},{1,0},{2,3},{3,2},{4,5},{5,4},{6,7},{7,6},{8,9},{9,8},{10,11... | collective-permute-start | bytes 393224 | tf_op jit(solution)/shard_map/ppermute | solution.py:177
  68.9 8.7 %copy-start.9 = (s32[4]{0:T(128)S(1)}, s32[4]{0:T(128)}, u32[]{:S(2)}) copy-start(s32[4]{0:T(128)} %get-tuple-element.28.kind_ref) | copy-start | bytes 52
  75.0 0.7 copy-start.7
  75.7 9.3 %collective-permute-start.4 = (bf16[4,16,1024]{2,1,0:T(8,128)(2,1)S(1)}, bf16[4,16,1024]{2,1,0:T(8,128)(2,1)S(1)}, u32[]{:S(2)}, u32[]{:S(2)}) collective-permute-start(bf16[4,16,1024]{2,1,0:T(8,128)(2,1)S(1)} %get-tuple-element.20), channel_id=1, source_target_pairs={{0,1},{1,0},{2,3},{3,2},{4,5},{5,4},{6,7},{7,6},{8,9},{9,8},{10,11... | collective-permute-start | bytes 393224 | tf_op jit(solution)/shard_map/ppermute | solution.py:177
  77.7 6.7 %copy-start.18 = (s32[32]{0:T(128)S(1)}, s32[32]{0:T(128)}, u32[]{:S(2)}) copy-start(s32[32]{0:T(128)} %stack.14) | copy-start | bytes 388
  83.7 0.7 copy-start.8
  84.4 5.0 %collective-permute-start.5 = (bf16[4,16,1024]{2,1,0:T(8,128)(2,1)S(1)}, bf16[4,16,1024]{2,1,0:T(8,128)(2,1)S(1)}, u32[]{:S(2)}, u32[]{:S(2)}) collective-permute-start(bf16[4,16,1024]{2,1,0:T(8,128)(2,1)S(1)} %get-tuple-element.22), channel_id=1, source_target_pairs={{0,1},{1,0},{2,3},{3,2},{4,5},{5,4},{6,7},{7,6},{8,9},{9,8},{10,11... | collective-permute-start | bytes 393224 | tf_op jit(solution)/shard_map/ppermute | solution.py:177
  85.0 4.4 %copy-start.13 = (bf16[4,16,1024]{2,1,0:T(8,128)(2,1)}, bf16[4,16,1024]{2,1,0:T(8,128)(2,1)S(1)}, u32[]{:S(2)}) copy-start(bf16[4,16,1024]{2,1,0:T(8,128)(2,1)S(1)} %collective-permute-done.2.refs_1_) | copy-start | bytes 393220
  85.0 4.4 %copy-start.14 = (bf16[4,16,1024]{2,1,0:T(8,128)(2,1)}, bf16[4,16,1024]{2,1,0:T(8,128)(2,1)S(1)}, u32[]{:S(2)}) copy-start(bf16[4,16,1024]{2,1,0:T(8,128)(2,1)S(1)} %collective-permute-done.3.refs_3_) | copy-start | bytes 393220
  85.0 4.4 %copy-start.15 = (bf16[4,16,1024]{2,1,0:T(8,128)(2,1)}, bf16[4,16,1024]{2,1,0:T(8,128)(2,1)S(1)}, u32[]{:S(2)}) copy-start(bf16[4,16,1024]{2,1,0:T(8,128)(2,1)S(1)} %collective-permute-done.4.refs_5_) | copy-start | bytes 393220
  89.4 0.7 copy-start.16
  93.2 2.9 %collective-permute-start.6 = (bf16[32,16,1024]{2,1,0:T(8,128)(2,1)}, bf16[32,16,1024]{2,1,0:T(8,128)(2,1)S(1)}, u32[]{:S(2)}, u32[]{:S(2)}) collective-permute-start(bf16[32,16,1024]{2,1,0:T(8,128)(2,1)} %get-tuple-element.24), channel_id=1, source_target_pairs={{0,2},{2,0},{4,6},{6,4},{8,10},{10,8},{12,14},{14,12},{16,18},{18,... | collective-permute-start | bytes 3145736 | tf_op jit(solution)/shard_map/ppermute | solution.py:177
  97.8 14.0 %collective-permute-start.7 = (bf16[4,4,16,1024]{3,2,1,0:T(8,128)(2,1)S(1)}, bf16[4,4,16,1024]{3,2,1,0:T(8,128)(2,1)S(1)}, u32[]{:S(2)}, u32[]{:S(2)}) collective-permute-start(bf16[4,4,16,1024]{3,2,1,0:T(8,128)(2,1)S(1)} %slice_bitcast_fusion), channel_id=1, source_target_pairs={{0,4},{2,6},{4,0},{6,2},{8,12},{10,14},{12,8},{14,10},{16,20},{18,... | collective-permute-start | bytes 1572872 | tf_op jit(solution)/shard_map/ppermute | solution.py:177
  112.0 7.6 %collective-permute-start.8 = (bf16[2,4,16,1024]{3,2,1,0:T(8,128)(2,1)S(1)}, bf16[2,4,16,1024]{3,2,1,0:T(8,128)(2,1)S(1)}, u32[]{:S(2)}, u32[]{:S(2)}) collective-permute-start(bf16[2,4,16,1024]{3,2,1,0:T(8,128)(2,1)S(1)} %slice_bitcast_fusion.2), channel_id=1, source_target_pairs={{0,8},{2,10},{4,12},{6,14},{8,0},{10,2},{12,4},{14,6},{16,24},{18,... | collective-permute-start | bytes 786440 | tf_op jit(solution)/shard_map/ppermute | solution.py:177
  119.7 7.6 %collective-permute-start.9 = (bf16[1,4,16,1024]{3,2,1,0:T(8,128)(2,1)S(1)}, bf16[1,4,16,1024]{3,2,1,0:T(8,128)(2,1)S(1)}, u32[]{:S(2)}, u32[]{:S(2)}) collective-permute-start(bf16[1,4,16,1024]{3,2,1,0:T(8,128)(2,1)S(1)} %slice_bitcast_fusion.4), channel_id=1, source_target_pairs={{0,16},{2,18},{4,20},{6,22},{8,24},{10,26},{12,28},{14,30},{16,0},... | collective-permute-start | bytes 393224 | tf_op jit(solution)/shard_map/ppermute | solution.py:177

commit v2 on v1

--- a/solution.py
+++ b/solution.py
@@ -15,23 +15,150 @@
     return jnp.dot(x, y, preferred_element_type=F32)
 
 
+def one_hot(shape, row_of, lane_of):
+    rows = lax.broadcasted_iota(jnp.int32, shape, 0)
+    lanes = lax.broadcasted_iota(jnp.int32, shape, 1)
+    return (row_of(rows) == lane_of(lanes)).astype(BF)
+
+
+def exact(x, y):
+    return dot(x, y).astype(BF)
+
+
+def weights_kernel(
+    scale_ref, s1e_ref, s2e_ref, m1_ref, m2_ref, fw1_ref, fw2_ref, sa_ref, st_ref, *, half, paired
+):
+    edge = 2 * half
+    low = half // 2
+    wide = edge * low
+    scale = scale_ref[...]
+    turn = lax.axis_index("oct") * half if paired else 0
+
+    def same(x):
+        return x
+
+    def turned(x):
+        return lax.rem(x + turn, edge)
+
+    def chunked(x):
+        return (x % low) * 4 + x // low
+
+    by_chunk = exact(one_hot((edge, edge), chunked, same), scale)
+    s1e_ref[...] = exact(by_chunk, one_hot((edge, wide), same, lambda x: x // low))
+    s2e_ref[...] = exact(
+        by_chunk, one_hot((edge, wide), same, lambda x: x // (wide // 2) * half + x % half)
+    )
+    m1_ref[...] = one_hot((wide, wide), lambda x: x // edge, lambda x: x % low)
+    m2_ref[...] = one_hot((2 * edge, wide), lambda x: x // low, lambda x: x // half % low)
+    sa_ref[...] = exact(scale, one_hot((edge, edge), same, turned))
+    pick = one_hot((edge, edge), turned, same)
+    st_ref[...] = lax.dot_general(
+        pick, by_chunk, (((1,), (1,)), ((), ())), preferred_element_type=F32
+    ).astype(BF)
+
+    def spread(row_of, lane_of, lane_count):
+        rows = lax.dot_general(
+            one_hot((wide, edge), row_of, same),
+            scale,
+            (((1,), (1,)), ((), ())),
+            preferred_element_type=F32,
+        ).astype(BF)
+        return exact(rows, one_hot((edge, lane_count), same, lane_of))
+
+    for bit in range(2):
+        fw1_ref[bit] = spread(
+            lambda x: x % half + bit * half, lambda x: x // half, 2 * wide
+        ) * one_hot((wide, 2 * wide), lambda x: x // half, lambda x: x % half)
+    fw2_ref[...] = spread(
+        lambda x: x // (wide // 2) * half + x % half, lambda x: x % edge, wide
+    ) * one_hot((wide, wide), lambda x: x // half % low, lambda x: x // edge)
+
+
+def make_weights(two_scale, paired):
+    edge = two_scale.shape[0]
+    half = edge // 2
+    wide = edge * half // 2
+    shapes = [
+        (edge, wide), (edge, wide), (wide, wide), (2 * edge, wide),
+        (2, wide, 2 * wide), (wide, wide), (edge, edge), (edge, edge),
+    ]
+    return pl.pallas_call(
+        functools.partial(weights_kernel, half=half, paired=paired),
+        in_specs=[pl.BlockSpec(memory_space=pltpu.VMEM)],
+        out_specs=[pl.BlockSpec(memory_space=pltpu.VMEM)] * len(shapes),
+        out_shape=[jax.ShapeDtypeStruct(shape, BF) for shape in shapes],
+        compiler_params=pltpu.CompilerParams(vmem_limit_bytes=32 * 1024 * 1024),
+    )(two_scale)
+
+
+def pick_kernel(slot_ref, blocks_ref, out_ref, *, parents):
+    first = (1 - lax.axis_index("oct")) * parents
+    for i in range(parents):
+        for j in range(out_ref.shape[1]):
+            out_ref[i, j] = blocks_ref[slot_ref[first + i, j]]
+
+
+def pick_blocks(child_slot, blocks, parents):
+    shape = (parents, child_slot.shape[1]) + blocks.shape[1:]
+    return pl.pallas_call(
+        functools.partial(pick_kernel, parents=parents),
+        in_specs=[
+            pl.BlockSpec(memory_space=pltpu.SMEM),
+            pl.BlockSpec(memory_space=pltpu.VMEM),
+        ],
+        out_specs=pl.BlockSpec(memory_space=pltpu.VMEM),
+        out_shape=jax.ShapeDtypeStruct(shape, BF),
+    )(child_slot, blocks)
+
+
+def by_output(table, edge, terms):
+    low = edge // 4
+    lanes = 4 * edge
+    chunk = lax.broadcasted_iota(jnp.int32, (low, lanes), 1) // edge
+    groups = []
+    for start in range(0, terms, 4):
+        tiles = [
+            table[low * min(t, terms - 1) : low * (min(t, terms - 1) + 1)]
+            for t in range(start, start + 4)
+        ]
+        for step in (1, 2):
+            upper = (chunk // step) % 2 == 1
+            mixed = list(tiles)
+            for i in range(4):
+                if i & step == 0:
+                    mixed[i] = jnp.where(
+                        upper, pltpu.roll(tiles[i + step], edge * step, 1), tiles[i]
+                    )
+                    mixed[i + step] = jnp.where(
+                        upper, tiles[i + step], pltpu.roll(tiles[i], lanes - edge * step, 1)
+                    )
+            tiles = mixed
+        groups.append(jnp.concatenate(tiles, axis=0))
+    return jnp.concatenate(groups, axis=1)[:, : terms * edge]
+
+
 def apply_kernel(
-    kind_ref, near_ref, far_ref, ft1_ref, ft2_ref, f0_ref, s1e_ref, s2e_ref, m1_ref, m2_ref,
-    fw1_ref, fw2_ref, sa_ref, st_ref, keep_ref, send_ref, cube_ref, sec_ref, *, half,
+    kind_ref, slot_ref, blocks_ref, far_ref, table_ref, s1e_ref, s2e_ref, m1_ref, m2_ref,
+    fw1_ref, fw2_ref, sa_ref, st_ref, keep_ref, send_ref, cube_ref, sec_ref,
+    *, half, terms, parent,
 ):
     edge = 2 * half
     low = half // 2
     wide = edge * low
     quarter = wide // 4
-    terms = f0_ref.shape[2] // edge
 
     @pl.when(pl.program_id(0) == 0)
     def _():
+        if slot_ref is None:
+            near = [blocks_ref[0, i] for i in range(4)]
+        else:
+            first = lax.axis_index("oct") * far_ref.shape[0] + parent
+            near = [blocks_ref[slot_ref[first, i]] for i in range(4)]
         total = None
         for bit in range(2):
             rows = []
             for mid in range(2):
-                rows += [near_ref[0, 2 * mid + bit], far_ref[0, 2 * mid + bit]]
+                rows += [near[2 * mid + bit], far_ref[parent, 2 * mid + bit]]
             part = dot(jnp.concatenate(rows, axis=0), fw1_ref[bit])
             total = part if total is None else total + part
         total = total.astype(BF)
@@ -56,9 +183,17 @@
             ).astype(BF)
 
     cube = cube_ref[...]
-    w1e = dot(ft1_ref[0], s1e_ref[...]).astype(BF)
-    w2e = dot(ft2_ref[0], s2e_ref[...]).astype(BF)
-    g0 = dot(st_ref[...], f0_ref[0]).astype(BF)
+    table = table_ref[0].astype(F32)
+    rows = terms * low
+    f0, f1, f2 = [
+        by_output(table[rows * i : rows * (i + 1)], edge, terms) for i in range(3)
+    ]
+    ft1 = f1.T.astype(BF)
+    ft2 = f2.T.reshape(terms * 4, 1, low, edge)
+    ft2 = jnp.broadcast_to(ft2, (terms * 4, 2, low, edge)).reshape(terms * 2 * edge, edge)
+    w1e = dot(ft1, s1e_ref[...]).astype(BF)
+    w2e = dot(ft2.astype(BF), s2e_ref[...]).astype(BF)
+    g0 = dot(st_ref[...], f0.astype(BF)).astype(BF)
     for t in range(terms):
         one = w1e[edge * t : edge * (t + 1)]
         w1 = jnp.concatenate(
@@ -96,44 +231,38 @@
         send_ref[0, :, wide * i : wide * (i + 1)] = out[half:]
 
 
-def apply_parent(parent, kinds, near, far, ft1, ft2, f0, consts, half):
-    s1e, s2e, m1, m2, fw1, fw2, sa, st = consts
-    disps = kinds.shape[0]
+def apply_parent(parent, kinds, child_slot, near, far, table, weights, half):
     edge = 2 * half
     wide = edge * half // 2
-    terms = f0.shape[2] // edge
+    terms = table.shape[1] // (3 * edge // 4)
+    disps = kinds.shape[1]
 
     def whole(array):
-        return pl.BlockSpec(array.shape, lambda k, kinds: (0,) * array.ndim)
+        return pl.BlockSpec(array.shape, lambda k, *scalars: (0,) * array.ndim)
 
     def of_kind(array):
-        return pl.BlockSpec((1,) + array.shape[1:], lambda k, kinds: (kinds[k], 0, 0))
+        return pl.BlockSpec((1,) + array.shape[1:], lambda k, kinds, *rest: (kinds[parent, k], 0, 0))
 
     def of_parent(array):
-        return pl.BlockSpec((1,) + array.shape[1:], lambda k, kinds: (parent, 0, 0, 0))
+        return pl.BlockSpec((1,) + array.shape[1:], lambda k, *scalars: (parent, 0, 0, 0))
 
     shape = jax.ShapeDtypeStruct((disps, half, 4 * wide), BF)
-    out_spec = pl.BlockSpec((1, half, 4 * wide), lambda k, kinds: (k, 0, 0))
+    out_spec = pl.BlockSpec((1, half, 4 * wide), lambda k, *scalars: (k, 0, 0))
+    kernel = functools.partial(apply_kernel, half=half, terms=terms, parent=parent)
+    if child_slot is None:
+        scalars = (kinds,)
+        body = lambda kind_ref, *refs: kernel(kind_ref, None, *refs)
+        near_spec = of_parent(near)
+    else:
+        scalars = (kinds, child_slot)
+        body = kernel
+        near_spec = whole(near)
     return pl.pallas_call(
-        functools.partial(apply_kernel, half=half),
+        body,
         grid_spec=pltpu.PrefetchScalarGridSpec(
-            num_scalar_prefetch=1,
+            num_scalar_prefetch=len(scalars),
             grid=(disps,),
-            in_specs=[
-                of_parent(near),
-                of_parent(far),
-                of_kind(ft1),
-                of_kind(ft2),
-                of_kind(f0),
-                whole(s1e),
-                whole(s2e),
-                whole(m1),
-                whole(m2),
-                whole(fw1),
-                whole(fw2),
-                whole(sa),
-                whole(st),
-            ],
+            in_specs=[near_spec, whole(far), of_kind(table)] + [whole(w) for w in weights],
             out_specs=[out_spec, out_spec],
             scratch_shapes=[
                 pltpu.VMEM((4 * edge, wide), BF),
@@ -142,7 +271,7 @@
         ),
         out_shape=[shape, shape],
         compiler_params=pltpu.CompilerParams(vmem_limit_bytes=48 * 1024 * 1024),
-    )(kinds, near, far, ft1, ft2, f0, s1e, s2e, m1, m2, fw1, fw2, sa, st)
+    )(*scalars, near, far, table, *weights)
 
 
 def sum_kernel(slot_ref, *refs, rows):
@@ -181,26 +310,24 @@
     oct_count = lax.axis_size("oct")
     leaf_count = lax.axis_size("leaf")
     my_leaf = lax.axis_index("leaf")
-    my_oct = lax.axis_index("oct")
     edge = two_scale.shape[0]
     half = edge // 2
     low = half // 2
-    wide = edge * low
     held = child_slot.shape[1]
     parents, disps = disp_kind.shape
     paired = oct_count == 2
 
     blocks = children.reshape(-1, half, half * half)
     if paired:
-        theirs = lax.dynamic_slice_in_dim(child_slot, (1 - my_oct) * parents, parents, 0)
-        mine = lax.dynamic_slice_in_dim(child_slot, my_oct * parents, parents, 0)
-        far = swap(blocks[theirs], "oct", 1)
-        near = blocks[mine]
+        near = blocks
+        far = swap(pick_blocks(child_slot, blocks, parents), "oct", 1)
+        near_slot = child_slot
     else:
         arrived = lax.all_to_all(
             blocks[child_slot], "oct", split_axis=0, concat_axis=1, tiled=True
         ).reshape(parents, 2, 4, half, half * half)
         near, far = arrived[:, 0], arrived[:, 1]
+        near_slot = None
 
     nodes = 2 * oct_count
     goal = target_leaf.reshape(parents, disps) * nodes + target_node
@@ -211,48 +338,13 @@
     leaf_off = jnp.bitwise_xor(goals // nodes, my_leaf)
     slots = ((leaf_off % 2) * (leaf_count // 2) + leaf_off // 2) * nodes + goals % nodes
 
-    kinds = factors.shape[0]
-    table = factors.reshape(kinds, 3, -1, edge, edge)
-    terms = table.shape[2]
-    f0 = table[:, 0].transpose(0, 2, 1, 3).reshape(kinds, edge, terms * edge)
-    ft1 = table[:, 1].transpose(0, 1, 3, 2).reshape(kinds, terms * edge, edge)
-    ft2 = table[:, 2].transpose(0, 1, 3, 2).reshape(kinds, terms * 4, 1, low, edge)
-    ft2 = jnp.broadcast_to(ft2, (kinds, terms * 4, 2, low, edge)).reshape(
-        kinds, terms * 2 * edge, edge
-    )
-    lane = jnp.arange(wide)
-    row = jnp.arange(wide)
-    s1e = jnp.repeat(two_scale, low, axis=1)
-    s2e = jnp.broadcast_to(
-        two_scale.reshape(edge, 2, 1, half), (edge, 2, low, half)
-    ).reshape(edge, wide)
-    m1 = (row[:, None] // edge == lane[None, :] % low).astype(BF)
-    dup_rows = jnp.arange(2 * edge)
-    m2 = (dup_rows[:, None] // low == (lane[None, :] // half) % low).astype(BF)
-    transposed = two_scale.T
-    by_bit = jnp.repeat(transposed.reshape(2, half, edge), half, axis=2)
-    fw1 = jnp.where(
-        (row[:, None] // half == jnp.arange(2 * wide)[None, :] % half)[None],
-        jnp.tile(by_bit, (1, half, 1)),
-        jnp.zeros((), BF),
-    )
-    spread = jnp.broadcast_to(
-        jnp.tile(transposed, (1, low)).reshape(2, 1, half, wide), (2, low, half, wide)
-    ).reshape(wide, wide)
-    fw2 = jnp.where(
-        (row[:, None] // half) % low == lane[None, :] // edge, spread, jnp.zeros((), BF)
-    )
-    if paired:
-        turned = two_scale.reshape(edge, 2, half)
-        turned = jnp.where(my_oct == 0, turned, turned[:, ::-1]).reshape(edge, edge)
-    else:
-        turned = two_scale
-    consts = (s1e, s2e, m1, m2, fw1, fw2, turned, turned.T)
+    table = factors.reshape(factors.shape[0], -1, 4 * edge)
+    weights = make_weights(two_scale, paired)
 
     arrays = []
     for parent in range(parents):
         kept, sent = apply_parent(
-            parent, disp_kind[parent], near, far, ft1, ft2, f0, consts, half
+            parent, disp_kind, near_slot, near, far, table, weights, half
         )
         if paired:
             arrays += [kept, swap(sent, "oct", 1)]

time: 129 us -> 88 us (0.68)
  local copies, waits for them, and re-layouts: 47.7 us -> 7.81 us
  other arithmetic: 9.26 us -> 3.82 us
  Pallas kernels: 27.5 us -> 32.1 us
    reshape x6 -> x1, local copies, waits for them, and re-layouts: 12.7 us -> 0.11 us  [local(): table = factors.reshape(factors.shape[0], -1, 4 * edge)]
    unnamed x43 -> x27, local copies, waits for them, and re-layouts: 16.1 us -> 6.7 us
    slice x1 -> x0, local copies, waits for them, and re-layouts: 6.31 us -> none  [local(): f0 = table[:, 0].transpose(0, 2, 1, 3).reshape(kinds, edge, terms * edge)]
    broadcast_in_dim x6 -> x0, local copies, waits for them, and re-layouts: 4.9 us -> none  [the longest x1 4.4 us: local(): jnp.broadcast_to(ft2, (kinds, terms * 4, 2, low, edge))]
    pallas_call x4 -> x6, Pallas kernels: 24.2 us -> 28.9 us  [the longest x4 26.3 us: apply_parent(): pl.pallas_call(body, grid_spec=pltpu.PrefetchScalarGridSpec(num_scalar_pr...]
    select_n x9 -> x0, other arithmetic: 2.59 us -> none  [the longest x1 0.96 us: local(): jnp.where((row[:, None] // half == jnp.arange(2 * wide)[None, :] % half)[...]
    gather x2 -> x0, local copies, waits for them, and re-layouts: 2.42 us -> none  [the longest x1 1.21 us: local(): near = blocks[mine]]
    another operation x2, local copies, waits for them, and re-layouts: 1.84 us -> 0.09 us  [local(): goals = jnp.stack([goal, swap(goal, 'oct', 1)], axis=1)]
  transfers between devices with their start and end apart: 10 -> 10, of which waited for: 5 -> 6; matrix products, arithmetic and copies ran while one was open for 35% -> 4% of each run, Pallas kernels for 14% -> 24%
where the time goes in v2:
time: 88 us; the launch traced here: 87.6 us
  Pallas kernels  32.1 us (36%)
  waiting for transfers between devices  30.6 us (35%)
  starting transfers between devices  13.1 us (15%)
  local copies, waits for them, and re-layouts  7.81 us (9%)
  other arithmetic  3.82 us (4%)
    ppermute x10, waiting for transfers between devices, swap(): return lax.ppermute(x, axis, [(i, i ^ mask) for i in range(count)])  30.6 us
    pallas_call x4, Pallas kernels, apply_parent(): pl.pallas_call(body, grid_spec=pltpu.PrefetchScalarGridSpec(num_scalar_pr...  26.3 us
    ppermute x10, starting transfers between devices, swap(): return lax.ppermute(x, axis, [(i, i ^ mask) for i in range(count)])  13.1 us
    unnamed x27, local copies, waits for them, and re-layouts  6.7 us
    pallas_call x1, Pallas kernels, sum_rows(): pl.pallas_call(functools.partial(sum_kernel, rows=rows), in_specs=[pl.Blo...  3.2 us
  transfers between devices with their start and end apart: 10, of which 6 were waited for; matrix products, arithmetic and copies ran while one was open for 4% of the time, Pallas kernels for 24%

profile of v2, /device:TPU:0, one launch (start us, length us, event | category | flops | bytes accessed | tf_op | source)
XLA Modules:
  0.0 87.6 jit_solution(13283133671724545848)
XLA Ops:
  0.0 1.3 %copy.25.slot_ref = s32[8,4]{1,0:T(8,128)} copy(s32[8,4]{0,1:T(4,128)} %param.8) | data formatting | bytes 256 | tf_op args[1]
  1.3 1.7 %copy.36 = bf16[4,8,16,256]{3,2,1,0:T(8,128)(2,1)} copy(bf16[4,8,16,256]{3,1,2,0:T(8,128)(2,1)} %bitcast.54) | data formatting | bytes 524288
  3.0 1.6 %shard_map.73 = bf16[4,4,16,256]{3,2,1,0:T(8,128)(2,1)} custom-call(s32[8,4]{1,0:T(8,128)} %copy.25.slot_ref, bf16[32,16,256]{2,1,0:T(8,128)(2,1)} %bitcast.42), custom_call_target="tpu_custom_call" | custom-call | tf_op jit(solution)/shard_map/pallas_call | solution.py:103
  4.7 2.9 %collective-permute-start.1 = (bf16[4,4,16,256]{3,2,1,0:T(8,128)(2,1)}, bf16[4,4,16,256]{3,2,1,0:T(8,128)(2,1)S(1)}, u32[]{:S(2)}, u32[]{:S(2)}) collective-permute-start(bf16[4,4,16,256]{3,2,1,0:T(8,128)(2,1)} %shard_map.73), channel_id=1, source_target_pairs={{0,1},{1,0},{2,3},{3,2},{4,5},{5,4},{6,7},{7,6},{8,9},{9,8},{10,11... | collective-permute-start | bytes 393224 | tf_op jit(solution)/shard_map/ppermute | solution.py:306
  7.6 0.7 broadcast_multiply_fusion
  8.3 0.7 add.39
  9.0 0.0 collective-permute-start
  9.0 1.8 %copy.37 = bf16[4,8,240,128]{3,2,1,0:T(8,128)(2,1)S(1)} copy(bf16[4,8,240,128]{3,1,2,0:T(8,128)(2,1)} %bitcast.52) | data formatting | bytes 3932160
  10.8 0.0 copy-start.7
  10.8 0.0 copy-start
  10.8 0.0 copy-start.1
  10.8 0.0 copy-start.6
  10.9 0.1 slice.30.table_ref
  11.0 0.5 copy-done.7
  11.5 0.9 %shard_map.74 = (bf16[32,256]{1,0:T(8,128)(2,1)S(1)}, bf16[32,256]{1,0:T(8,128)(2,1)S(1)}, bf16[256,256]{1,0:T(8,128)(2,1)S(1)}, bf16[64,256]{1,0:T(8,128)(2,1)S...) custom-call(bf16[32,32]{1,0:T(8,128)(2,1)S(1)} %copy-done.7), custom_call_target="tpu_custom_call" | custom-call | tf_op jit(solution)/shard_map/pallas_call | solution.py:85
  12.4 0.2 collective-permute-done
  12.6 0.1 stack.14
  12.7 0.0 collective-permute-done.1.far_ref
  12.7 0.0 copy-done
  12.7 0.0 copy-done.1
  12.7 0.0 copy-done.6
  12.7 6.6 %shard_map.75 = (bf16[4,16,1024]{2,1,0:T(8,128)(2,1)S(1)}, bf16[4,16,1024]{2,1,0:T(8,128)(2,1)S(1)}) custom-call(s32[4,4]{1,0:T(4,128)S(1)} %copy-done.6, s32[8,4]{1,0:T(8,128)S(1)} %copy-done.1, bf16[32,16,256]{2,1,0:T(8,128)(2,1)S(1)} %bitcast.43, bf16[4,4,16,256]{3,2,1,0:T(8,128)(2,1)S(1)} %collective-permute-done.1.far_ref, ...), custom_call_target="tpu_custom_call" | custom-call | tf_op jit(solution)/shard_map/pallas_call | solution.py:260
  19.3 0.0 copy-start.2
  19.3 1.9 %collective-permute-start.2 = (bf16[4,16,1024]{2,1,0:T(8,128)(2,1)S(1)}, bf16[4,16,1024]{2,1,0:T(8,128)(2,1)S(1)}, u32[]{:S(2)}, u32[]{:S(2)}) collective-permute-start(bf16[4,16,1024]{2,1,0:T(8,128)(2,1)S(1)} %get-tuple-element.32), channel_id=1, source_target_pairs={{0,1},{1,0},{2,3},{3,2},{4,5},{5,4},{6,7},{7,6},{8,9},{9,8},{10,11... | collective-permute-start | bytes 393224 | tf_op jit(solution)/shard_map/ppermute | solution.py:306
  21.2 6.6 %shard_map.76 = (bf16[4,16,1024]{2,1,0:T(8,128)(2,1)S(1)}, bf16[4,16,1024]{2,1,0:T(8,128)(2,1)S(1)}) custom-call(s32[4,4]{1,0:T(4,128)S(1)} %copy-done.6, s32[8,4]{1,0:T(8,128)S(1)} %copy-done.1, bf16[32,16,256]{2,1,0:T(8,128)(2,1)S(1)} %bitcast.44, bf16[4,4,16,256]{3,2,1,0:T(8,128)(2,1)S(1)} %collective-permute-done.1.far_ref, ...), custom_call_target="tpu_custom_call" | custom-call | tf_op jit(solution)/shard_map/pallas_call | solution.py:260
  27.8 0.0 copy-start.3
  27.8 0.2 collective-permute-start.3
  28.1 6.6 %shard_map.77 = (bf16[4,16,1024]{2,1,0:T(8,128)(2,1)S(1)}, bf16[4,16,1024]{2,1,0:T(8,128)(2,1)S(1)}) custom-call(s32[4,4]{1,0:T(4,128)S(1)} %copy-done.6, s32[8,4]{1,0:T(8,128)S(1)} %copy-done.1, bf16[32,16,256]{2,1,0:T(8,128)(2,1)S(1)} %bitcast.45, bf16[4,4,16,256]{3,2,1,0:T(8,128)(2,1)S(1)} %collective-permute-done.1.far_ref, ...), custom_call_target="tpu_custom_call" | custom-call | tf_op jit(solution)/shard_map/pallas_call | solution.py:260
  34.7 0.0 copy-done.2
  34.7 0.0 copy-start.4
  34.7 1.9 %collective-permute-start.4 = (bf16[4,16,1024]{2,1,0:T(8,128)(2,1)S(1)}, bf16[4,16,1024]{2,1,0:T(8,128)(2,1)S(1)}, u32[]{:S(2)}, u32[]{:S(2)}) collective-permute-start(bf16[4,16,1024]{2,1,0:T(8,128)(2,1)S(1)} %get-tuple-element.36), channel_id=1, source_target_pairs={{0,1},{1,0},{2,3},{3,2},{4,5},{5,4},{6,7},{7,6},{8,9},{9,8},{10,11... | collective-permute-start | bytes 393224 | tf_op jit(solution)/shard_map/ppermute | solution.py:306
  36.6 6.6 %shard_map.78 = (bf16[4,16,1024]{2,1,0:T(8,128)(2,1)S(1)}, bf16[4,16,1024]{2,1,0:T(8,128)(2,1)S(1)}) custom-call(s32[4,4]{1,0:T(4,128)S(1)} %copy-done.6, s32[8,4]{1,0:T(8,128)S(1)} %copy-done.1, bf16[32,16,256]{2,1,0:T(8,128)(2,1)S(1)} %bitcast.46, bf16[4,4,16,256]{3,2,1,0:T(8,128)(2,1)S(1)} %collective-permute-done.1.far_ref, ...), custom_call_target="tpu_custom_call" | custom-call | tf_op jit(solution)/shard_map/pallas_call | solution.py:260
  43.2 0.0 copy-done.3
  43.2 0.0 copy-start.5
  43.2 0.6 copy-done.5
  43.9 0.0 copy-done.4
  43.9 0.2 collective-permute-start.5
  44.0 0.5 fusion.4.slot_ref
  44.6 0.0 collective-permute-done.2.refs_1_
  44.6 0.0 copy-start.8
  44.6 0.0 collective-permute-done.3.refs_3_
  44.6 0.0 copy-start.9
  44.6 0.0 collective-permute-done.4.refs_5_
  44.6 0.0 copy-start.10
  44.6 4.2 %collective-permute-done.5.refs_7_ = bf16[4,16,1024]{2,1,0:T(8,128)(2,1)S(1)} collective-permute-done((bf16[4,16,1024]{2,1,0:T(8,128)(2,1)S(1)}, bf16[4,16,1024]{2,1,0:T(8,128)(2,1)S(1)}, u32[]{:S(2)}, u32[]{:S(2)}) %collective-permute-start.5) | collective-permute-done | bytes 131104 | tf_op jit(solution)/shard_map/ppermute | solution.py:306
  48.8 0.0 copy-done.8
  48.8 0.0 copy-done.9
  48.8 0.0 copy-done.10
  48.8 0.6 copy-done.11
  49.5 3.2 %shard_map.79 = (bf16[32,16,1024]{2,1,0:T(8,128)(2,1)}, bf16[32,16,1024]{2,1,0:T(8,128)(2,1)}) custom-call(s32[32]{0:T(128)} %fusion.4.slot_ref, bf16[4,16,1024]{2,1,0:T(8,128)(2,1)} %copy-done.2, bf16[4,16,1024]{2,1,0:T(8,128)(2,1)} %copy-done.8, bf16[4,16,1024]{2,1,0:T(8,128)(2,1)} %copy-done.3, bf16[4,16,1024]{2,1,0:T(8,128)(2,1)} %copy-done.9, ...), custom_call_target="tpu_custom_call" | custom-call | tf_op jit(solution)/shard_map/pallas_call | solution.py:293
  52.7 0.0 collective-permute-start.6
  52.7 2.9 %collective-permute-done.6 = bf16[32,16,1024]{2,1,0:T(8,128)(2,1)S(1)} collective-permute-done((bf16[32,16,1024]{2,1,0:T(8,128)(2,1)}, bf16[32,16,1024]{2,1,0:T(8,128)(2,1)S(1)}, u32[]{:S(2)}, u32[]{:S(2)}) %collective-permute-start.6) | collective-permute-done | bytes 1048608 | tf_op jit(solution)/shard_map/ppermute | solution.py:306
  55.5 1.6 %add_convert_fusion = bf16[32,16,1024]{2,1,0:T(8,128)(2,1)S(1)} fusion(bf16[32,16,1024]{2,1,0:T(8,128)(2,1)S(1)} %collective-permute-done.6, bf16[32,16,1024]{2,1,0:T(8,128)(2,1)} %get-tuple-element.39), kind=kLoop, calls=%fused_computation | loop fusion | flops 2097152 | bytes 3145728 | tf_op jit(solution)/shard_map/convert_element_type | solution.py:361
  57.2 1.6 %collective-permute-start.7 = (bf16[4,4,16,1024]{3,2,1,0:T(8,128)(2,1)S(1)}, bf16[4,4,16,1024]{3,2,1,0:T(8,128)(2,1)S(1)}, u32[]{:S(2)}, u32[]{:S(2)}) collective-permute-start(bf16[4,4,16,1024]{3,2,1,0:T(8,128)(2,1)S(1)} %slice_bitcast_fusion), channel_id=1, source_target_pairs={{0,4},{2,6},{4,0},{6,2},{8,12},{10,14},{12,8},{14,10},{16,20},{18,... | collective-permute-start | bytes 1572872 | tf_op jit(solution)/shard_map/ppermute | solution.py:306
  58.8 12.4 %collective-permute-done.7 = bf16[4,4,16,1024]{3,2,1,0:T(8,128)(2,1)S(1)} collective-permute-done((bf16[4,4,16,1024]{3,2,1,0:T(8,128)(2,1)S(1)}, bf16[4,4,16,1024]{3,2,1,0:T(8,128)(2,1)S(1)}, u32[]{:S(2)}, u32[]{:S(2)}) %collective-permute-start.7) | collective-permute-done | bytes 524320 | tf_op jit(solution)/shard_map/ppermute | solution.py:306
  71.2 0.2 fusion
  71.5 1.6 %collective-permute-start.8 = (bf16[2,4,16,1024]{3,2,1,0:T(8,128)(2,1)S(1)}, bf16[2,4,16,1024]{3,2,1,0:T(8,128)(2,1)S(1)}, u32[]{:S(2)}, u32[]{:S(2)}) collective-permute-start(bf16[2,4,16,1024]{3,2,1,0:T(8,128)(2,1)S(1)} %slice_bitcast_fusion.2), channel_id=1, source_target_pairs={{0,8},{2,10},{4,12},{6,14},{8,0},{10,2},{12,4},{14,6},{16,24},{18,... | collective-permute-start | bytes 786440 | tf_op jit(solution)/shard_map/ppermute | solution.py:306
  73.1 5.9 %collective-permute-done.8 = bf16[2,4,16,1024]{3,2,1,0:T(8,128)(2,1)S(1)} collective-permute-done((bf16[2,4,16,1024]{3,2,1,0:T(8,128)(2,1)S(1)}, bf16[2,4,16,1024]{3,2,1,0:T(8,128)(2,1)S(1)}, u32[]{:S(2)}, u32[]{:S(2)}) %collective-permute-start.8) | collective-permute-done | bytes 262176 | tf_op jit(solution)/shard_map/ppermute | solution.py:306
  79.1 0.1 fusion.2
  79.2 2.7 %collective-permute-start.9 = (bf16[1,4,16,1024]{3,2,1,0:T(8,128)(2,1)S(1)}, bf16[1,4,16,1024]{3,2,1,0:T(8,128)(2,1)S(1)}, u32[]{:S(2)}, u32[]{:S(2)}) collective-permute-start(bf16[1,4,16,1024]{3,2,1,0:T(8,128)(2,1)S(1)} %slice_bitcast_fusion.4), channel_id=1, source_target_pairs={{0,16},{2,18},{4,20},{6,22},{8,24},{10,26},{12,28},{14,30},{16,0},... | collective-permute-start | bytes 393224 | tf_op jit(solution)/shard_map/ppermute | solution.py:306
  81.8 4.9 %collective-permute-done.9 = bf16[1,4,16,1024]{3,2,1,0:T(8,128)(2,1)S(1)} collective-permute-done((bf16[1,4,16,1024]{3,2,1,0:T(8,128)(2,1)S(1)}, bf16[1,4,16,1024]{3,2,1,0:T(8,128)(2,1)S(1)}, u32[]{:S(2)}, u32[]{:S(2)}) %collective-permute-start.9) | collective-permute-done | bytes 131104 | tf_op jit(solution)/shard_map/ppermute | solution.py:306
  86.8 0.1 reshape_reshape.7
  86.8 0.1 copy.32
  86.9 0.7 reshape.42
  (7 shorter events, 0.1 us)
Async XLA Ops:
  4.7 8.0 %collective-permute-start.1 = (bf16[4,4,16,256]{3,2,1,0:T(8,128)(2,1)}, bf16[4,4,16,256]{3,2,1,0:T(8,128)(2,1)S(1)}, u32[]{:S(2)}, u32[]{:S(2)}) collective-permute-start(bf16[4,4,16,256]{3,2,1,0:T(8,128)(2,1)} %shard_map.73), channel_id=1, source_target_pairs={{0,1},{1,0},{2,3},{3,2},{4,5},{5,4},{6,7},{7,6},{8,9},{9,8},{10,11... | collective-permute-start | bytes 393224 | tf_op jit(solution)/shard_map/ppermute | solution.py:306
  9.0 3.6 %collective-permute-start = (s32[4,4]{1,0:T(4,128)S(1)}, s32[4,4]{1,0:T(4,128)S(1)}, u32[]{:S(2)}, u32[]{:S(2)}) collective-permute-start(s32[4,4]{1,0:T(4,128)S(1)} %add.39), channel_id=1, source_target_pairs={{0,1},{1,0},{2,3},{3,2},{4,5},{5,4},{6,7},{7,6},{8,9},{9,8},{10,11... | collective-permute-start | bytes 200 | tf_op jit(solution)/shard_map/ppermute | solution.py:306
  10.8 0.7 copy-start.7
  10.8 1.9 %copy-start = (bf16[4,8,16,256]{3,2,1,0:T(8,128)(2,1)S(1)}, bf16[4,8,16,256]{3,2,1,0:T(8,128)(2,1)}, u32[]{:S(2)}) copy-start(bf16[4,8,16,256]{3,2,1,0:T(8,128)(2,1)} %copy.36) | copy-start | bytes 786436
  10.8 1.9 %copy-start.1 = (s32[8,4]{1,0:T(8,128)S(1)}, s32[8,4]{1,0:T(8,128)}, u32[]{:S(2)}) copy-start(s32[8,4]{1,0:T(8,128)} %copy.25.slot_ref) | copy-start | bytes 388
  10.8 1.9 %copy-start.6 = (s32[4,4]{1,0:T(4,128)S(1)}, s32[4,4]{1,0:T(4,128)}, u32[]{:S(2)}) copy-start(s32[4,4]{1,0:T(4,128)} %kind_ref.7) | copy-start | bytes 196
  19.3 15.4 %copy-start.2 = (bf16[4,16,1024]{2,1,0:T(8,128)(2,1)}, bf16[4,16,1024]{2,1,0:T(8,128)(2,1)S(1)}, u32[]{:S(2)}) copy-start(bf16[4,16,1024]{2,1,0:T(8,128)(2,1)S(1)} %get-tuple-element.31.refs_0_) | copy-start | bytes 393220
  19.3 25.3 %collective-permute-start.2 = (bf16[4,16,1024]{2,1,0:T(8,128)(2,1)S(1)}, bf16[4,16,1024]{2,1,0:T(8,128)(2,1)S(1)}, u32[]{:S(2)}, u32[]{:S(2)}) collective-permute-start(bf16[4,16,1024]{2,1,0:T(8,128)(2,1)S(1)} %get-tuple-element.32), channel_id=1, source_target_pairs={{0,1},{1,0},{2,3},{3,2},{4,5},{5,4},{6,7},{7,6},{8,9},{9,8},{10,11... | collective-permute-start | bytes 393224 | tf_op jit(solution)/shard_map/ppermute | solution.py:306
  27.8 15.4 %copy-start.3 = (bf16[4,16,1024]{2,1,0:T(8,128)(2,1)}, bf16[4,16,1024]{2,1,0:T(8,128)(2,1)S(1)}, u32[]{:S(2)}) copy-start(bf16[4,16,1024]{2,1,0:T(8,128)(2,1)S(1)} %get-tuple-element.33.refs_2_) | copy-start | bytes 393220
  27.8 16.7 %collective-permute-start.3 = (bf16[4,16,1024]{2,1,0:T(8,128)(2,1)S(1)}, bf16[4,16,1024]{2,1,0:T(8,128)(2,1)S(1)}, u32[]{:S(2)}, u32[]{:S(2)}) collective-permute-start(bf16[4,16,1024]{2,1,0:T(8,128)(2,1)S(1)} %get-tuple-element.34), channel_id=1, source_target_pairs={{0,1},{1,0},{2,3},{3,2},{4,5},{5,4},{6,7},{7,6},{8,9},{9,8},{10,11... | collective-permute-start | bytes 393224 | tf_op jit(solution)/shard_map/ppermute | solution.py:306
  34.7 9.2 %copy-start.4 = (bf16[4,16,1024]{2,1,0:T(8,128)(2,1)}, bf16[4,16,1024]{2,1,0:T(8,128)(2,1)S(1)}, u32[]{:S(2)}) copy-start(bf16[4,16,1024]{2,1,0:T(8,128)(2,1)S(1)} %get-tuple-element.35.refs_4_) | copy-start | bytes 393220
  34.7 9.9 %collective-permute-start.4 = (bf16[4,16,1024]{2,1,0:T(8,128)(2,1)S(1)}, bf16[4,16,1024]{2,1,0:T(8,128)(2,1)S(1)}, u32[]{:S(2)}, u32[]{:S(2)}) collective-permute-start(bf16[4,16,1024]{2,1,0:T(8,128)(2,1)S(1)} %get-tuple-element.36), channel_id=1, source_target_pairs={{0,1},{1,0},{2,3},{3,2},{4,5},{5,4},{6,7},{7,6},{8,9},{9,8},{10,11... | collective-permute-start | bytes 393224 | tf_op jit(solution)/shard_map/ppermute | solution.py:306
  43.2 0.6 copy-start.5
  43.9 5.0 %collective-permute-start.5 = (bf16[4,16,1024]{2,1,0:T(8,128)(2,1)S(1)}, bf16[4,16,1024]{2,1,0:T(8,128)(2,1)S(1)}, u32[]{:S(2)}, u32[]{:S(2)}) collective-permute-start(bf16[4,16,1024]{2,1,0:T(8,128)(2,1)S(1)} %get-tuple-element.38), channel_id=1, source_target_pairs={{0,1},{1,0},{2,3},{3,2},{4,5},{5,4},{6,7},{7,6},{8,9},{9,8},{10,11... | collective-permute-start | bytes 393224 | tf_op jit(solution)/shard_map/ppermute | solution.py:306
  44.6 4.3 %copy-start.8 = (bf16[4,16,1024]{2,1,0:T(8,128)(2,1)}, bf16[4,16,1024]{2,1,0:T(8,128)(2,1)S(1)}, u32[]{:S(2)}) copy-start(bf16[4,16,1024]{2,1,0:T(8,128)(2,1)S(1)} %collective-permute-done.2.refs_1_) | copy-start | bytes 393220
  44.6 4.3 %copy-start.9 = (bf16[4,16,1024]{2,1,0:T(8,128)(2,1)}, bf16[4,16,1024]{2,1,0:T(8,128)(2,1)S(1)}, u32[]{:S(2)}) copy-start(bf16[4,16,1024]{2,1,0:T(8,128)(2,1)S(1)} %collective-permute-done.3.refs_3_) | copy-start | bytes 393220
  44.6 4.2 %copy-start.10 = (bf16[4,16,1024]{2,1,0:T(8,128)(2,1)}, bf16[4,16,1024]{2,1,0:T(8,128)(2,1)S(1)}, u32[]{:S(2)}) copy-start(bf16[4,16,1024]{2,1,0:T(8,128)(2,1)S(1)} %collective-permute-done.4.refs_5_) | copy-start | bytes 393220
  48.8 0.6 copy-start.11
  52.7 2.9 %collective-permute-start.6 = (bf16[32,16,1024]{2,1,0:T(8,128)(2,1)}, bf16[32,16,1024]{2,1,0:T(8,128)(2,1)S(1)}, u32[]{:S(2)}, u32[]{:S(2)}) collective-permute-start(bf16[32,16,1024]{2,1,0:T(8,128)(2,1)} %get-tuple-element.40), channel_id=1, source_target_pairs={{0,2},{2,0},{4,6},{6,4},{8,10},{10,8},{12,14},{14,12},{16,18},{18,... | collective-permute-start | bytes 3145736 | tf_op jit(solution)/shard_map/ppermute | solution.py:306
  57.2 14.0 %collective-permute-start.7 = (bf16[4,4,16,1024]{3,2,1,0:T(8,128)(2,1)S(1)}, bf16[4,4,16,1024]{3,2,1,0:T(8,128)(2,1)S(1)}, u32[]{:S(2)}, u32[]{:S(2)}) collective-permute-start(bf16[4,4,16,1024]{3,2,1,0:T(8,128)(2,1)S(1)} %slice_bitcast_fusion), channel_id=1, source_target_pairs={{0,4},{2,6},{4,0},{6,2},{8,12},{10,14},{12,8},{14,10},{16,20},{18,... | collective-permute-start | bytes 1572872 | tf_op jit(solution)/shard_map/ppermute | solution.py:306
  71.5 7.6 %collective-permute-start.8 = (bf16[2,4,16,1024]{3,2,1,0:T(8,128)(2,1)S(1)}, bf16[2,4,16,1024]{3,2,1,0:T(8,128)(2,1)S(1)}, u32[]{:S(2)}, u32[]{:S(2)}) collective-permute-start(bf16[2,4,16,1024]{3,2,1,0:T(8,128)(2,1)S(1)} %slice_bitcast_fusion.2), channel_id=1, source_target_pairs={{0,8},{2,10},{4,12},{6,14},{8,0},{10,2},{12,4},{14,6},{16,24},{18,... | collective-permute-start | bytes 786440 | tf_op jit(solution)/shard_map/ppermute | solution.py:306
  79.2 7.6 %collective-permute-start.9 = (bf16[1,4,16,1024]{3,2,1,0:T(8,128)(2,1)S(1)}, bf16[1,4,16,1024]{3,2,1,0:T(8,128)(2,1)S(1)}, u32[]{:S(2)}, u32[]{:S(2)}) collective-permute-start(bf16[1,4,16,1024]{3,2,1,0:T(8,128)(2,1)S(1)} %slice_bitcast_fusion.4), channel_id=1, source_target_pairs={{0,16},{2,18},{4,20},{6,22},{8,24},{10,26},{12,28},{14,30},{16,0},... | collective-permute-start | bytes 393224 | tf_op jit(solution)/shard_map/ppermute | solution.py:306

commit v3 on v2

--- a/solution.py
+++ b/solution.py
@@ -301,6 +301,46 @@
     )(slots, *arrays)
 
 
+def combine_kernel(*refs, bits, lanes, inputs, last):
+    kept, arrived, outs = refs[:inputs], refs[inputs : 2 * inputs], refs[2 * inputs :]
+    for i, bit in enumerate(bits):
+        source, start = (i, 0) if inputs == len(bits) else (0, lanes * i)
+        for r in range(arrived[source].shape[0]):
+            total = kept[source][r, :, :, start : start + lanes].astype(F32)
+            total = total + arrived[source][r, :, :, start : start + lanes].astype(F32)
+            total = total.astype(BF)
+            if not last:
+                place = (r >> (bit + 1) << bit) | (r & ((1 << bit) - 1))
+                outs[2 * i + (r >> bit & 1)][place] = total
+            elif outs[0].shape[1] == 4:
+                half = lanes // 4
+                for c in range(4):
+                    to = half * (c // 2)
+                    outs[0][:, 2 * i + c % 2, :, to : to + half] = total[
+                        :, :, half * c : half * (c + 1)
+                    ]
+            else:
+                outs[0][:, 0, :, lanes * i : lanes * (i + 1)] = total
+
+
+def combine(kept, arrived, bits, out=None):
+    lanes = arrived[0].shape[-1] * len(arrived) // len(bits)
+    if out is None:
+        shape = (arrived[0].shape[0] // 2,) + arrived[0].shape[1:3] + (lanes,)
+        shapes = [shape] * (2 * len(bits))
+    else:
+        shapes = [out]
+    return pl.pallas_call(
+        functools.partial(
+            combine_kernel, bits=bits, lanes=lanes, inputs=len(kept), last=out is not None
+        ),
+        in_specs=[pl.BlockSpec(memory_space=pltpu.VMEM)] * (2 * len(kept)),
+        out_specs=[pl.BlockSpec(memory_space=pltpu.VMEM)] * len(shapes),
+        out_shape=[jax.ShapeDtypeStruct(shape, BF) for shape in shapes],
+        compiler_params=pltpu.CompilerParams(vmem_limit_bytes=48 * 1024 * 1024),
+    )(*kept, *arrived)
+
+
 def swap(x, axis, mask):
     count = lax.axis_size(axis)
     return lax.ppermute(x, axis, [(i, i ^ mask) for i in range(count)])
@@ -357,19 +397,23 @@
             arrays += [rows.reshape(oct_count * disps, held * half, half * half)]
 
     even, odd = sum_rows(slots.reshape(-1), arrays, leaf_count * nodes)
-    total = even.astype(F32) + swap(odd, "leaf", 1).astype(F32)
-    total = total.astype(BF).reshape((leaf_count // 2, nodes) + total.shape[1:])
-    mask = 2
-    while mask < leaf_count:
-        pairs = total.reshape((-1, 2) + total.shape[1:])
-        total = pairs[:, 0].astype(F32) + swap(pairs[:, 1], "leaf", mask).astype(F32)
-        total = total.astype(BF)
-        mask *= 2
-    total = total.reshape(nodes, -1)
-    if paired:
-        out = total.reshape(nodes, half, 2, 2, 2, low * half)
-        return out.transpose(0, 2, 4, 1, 3, 5).reshape(nodes, held, -1)
-    return total.reshape(nodes, held, -1)
+    shape = (leaf_count // 2, nodes) + even.shape[1:]
+    even = even.reshape(shape)
+    odd = swap(odd, "leaf", 1).reshape(shape)
+    masks = [1 << i for i in range(1, (leaf_count - 1).bit_length())]
+    orders = [masks, masks[1::-1] + masks[2:]]
+    left = [list(masks), list(masks)]
+    kept, arrived = [even], [odd]
+    for step in range(len(masks)):
+        bits = [left[i].index(orders[i][step]) for i in range(2)]
+        parts = combine(kept, arrived, bits)
+        kept = [parts[0], parts[2]]
+        arrived = [swap(parts[2 * i + 1], "leaf", orders[i][step]) for i in range(2)]
+        for i in range(2):
+            left[i].remove(orders[i][step])
+    tail = (nodes, held, half, half * half) if paired else (nodes, 1) + shape[2:]
+    (out,) = combine(kept, arrived, (0, 0), tail)
+    return out.reshape(nodes, held, -1)
 
 
 def solution(mesh):

time: 88 us -> 83 us (0.943)
  waiting for transfers between devices: 30.6 us -> 23.6 us
  starting transfers between devices: 13.1 us -> 15.5 us
  other arithmetic: 3.82 us -> 1.92 us
  local copies, waits for them, and re-layouts: 7.81 us -> 8.88 us
    ppermute x10 -> x13, waiting for transfers between devices: 30.6 us -> 23.6 us  [swap(): return lax.ppermute(x, axis, [(i, i ^ mask) for i in range(count)])]
    ppermute x10 -> x13, starting transfers between devices: 13.1 us -> 15.5 us  [swap(): return lax.ppermute(x, axis, [(i, i ^ mask) for i in range(count)])]
    convert_element_type x3 -> x0, other arithmetic: 1.85 us -> none  [the longest x1 1.62 us: local(): total = total.astype(BF).reshape((leaf_count // 2, nodes) + total.shape[1:])]
    unnamed x27 -> x29, local copies, waits for them, and re-layouts: 6.7 us -> 7.95 us
  transfers between devices with their start and end apart: 10 -> 13, of which waited for: 6 -> 9; matrix products, arithmetic and copies ran while one was open for 4% -> 5% of each run, Pallas kernels for 24% -> 25%
where the time goes in v3:
time: 83 us; the launch traced here: 82.6 us
  Pallas kernels  32.5 us (39%)
  waiting for transfers between devices  23.6 us (28%)
  starting transfers between devices  15.5 us (19%)
  local copies, waits for them, and re-layouts  8.88 us (11%)
  other arithmetic  1.92 us (2%)
    pallas_call x4, Pallas kernels, apply_parent(): pl.pallas_call(body, grid_spec=pltpu.PrefetchScalarGridSpec(num_scalar_pr...  26.3 us
    ppermute x13, waiting for transfers between devices, swap(): return lax.ppermute(x, axis, [(i, i ^ mask) for i in range(count)])  23.6 us
    ppermute x13, starting transfers between devices, swap(): return lax.ppermute(x, axis, [(i, i ^ mask) for i in range(count)])  15.5 us
    unnamed x29, local copies, waits for them, and re-layouts  7.95 us
    pallas_call x1, Pallas kernels, sum_rows(): pl.pallas_call(functools.partial(sum_kernel, rows=rows), in_specs=[pl.Blo...  3.22 us
  transfers between devices with their start and end apart: 13, of which 9 were waited for; matrix products, arithmetic and copies ran while one was open for 5% of the time, Pallas kernels for 25%

profile of v3, /device:TPU:0, one launch (start us, length us, event | category | flops | bytes accessed | tf_op | source)
XLA Modules:
  0.0 82.6 jit_solution(14363960713994311467)
XLA Ops:
  0.0 1.3 %copy.10.slot_ref = s32[8,4]{1,0:T(8,128)} copy(s32[8,4]{0,1:T(4,128)} %param.8) | data formatting | bytes 256 | tf_op args[1]
  1.3 1.7 %copy.14 = bf16[4,8,16,256]{3,2,1,0:T(8,128)(2,1)} copy(bf16[4,8,16,256]{3,1,2,0:T(8,128)(2,1)} %bitcast.21) | data formatting | bytes 524288
  3.0 1.6 %shard_map.73 = bf16[4,4,16,256]{3,2,1,0:T(8,128)(2,1)} custom-call(s32[8,4]{1,0:T(8,128)} %copy.10.slot_ref, bf16[32,16,256]{2,1,0:T(8,128)(2,1)} %bitcast.12), custom_call_target="tpu_custom_call" | custom-call | tf_op jit(solution)/shard_map/pallas_call | solution.py:103
  4.7 2.9 %collective-permute-start.1 = (bf16[4,4,16,256]{3,2,1,0:T(8,128)(2,1)}, bf16[4,4,16,256]{3,2,1,0:T(8,128)(2,1)S(1)}, u32[]{:S(2)}, u32[]{:S(2)}) collective-permute-start(bf16[4,4,16,256]{3,2,1,0:T(8,128)(2,1)} %shard_map.73), channel_id=1, source_target_pairs={{0,1},{1,0},{2,3},{3,2},{4,5},{5,4},{6,7},{7,6},{8,9},{9,8},{10,11... | collective-permute-start | bytes 393224 | tf_op jit(solution)/shard_map/ppermute | solution.py:346
  7.6 0.7 broadcast_multiply_fusion
  8.3 0.7 add.27
  9.0 0.0 collective-permute-start
  9.0 1.8 %copy.15 = bf16[4,8,240,128]{3,2,1,0:T(8,128)(2,1)S(1)} copy(bf16[4,8,240,128]{3,1,2,0:T(8,128)(2,1)} %bitcast.20) | data formatting | bytes 3932160
  10.8 0.0 copy-start.8
  10.8 0.0 copy-start
  10.8 0.0 copy-start.2
  10.8 0.0 copy-start.7
  10.8 0.1 slice.table_ref
  11.0 0.5 copy-done.8
  11.5 0.9 %shard_map.74 = (bf16[32,256]{1,0:T(8,128)(2,1)S(1)}, bf16[32,256]{1,0:T(8,128)(2,1)S(1)}, bf16[256,256]{1,0:T(8,128)(2,1)S(1)}, bf16[64,256]{1,0:T(8,128)(2,1)S...) custom-call(bf16[32,32]{1,0:T(8,128)(2,1)S(1)} %copy-done.8), custom_call_target="tpu_custom_call" | custom-call | tf_op jit(solution)/shard_map/pallas_call | solution.py:85
  12.4 0.2 collective-permute-done
  12.6 0.1 stack.14
  12.7 0.0 collective-permute-done.1.far_ref
  12.7 0.0 copy-done
  12.7 0.0 copy-done.2
  12.7 0.0 copy-done.7
  12.7 6.6 %shard_map.75 = (bf16[4,16,1024]{2,1,0:T(8,128)(2,1)S(1)}, bf16[4,16,1024]{2,1,0:T(8,128)(2,1)S(1)}) custom-call(s32[4,4]{1,0:T(4,128)S(1)} %copy-done.7, s32[8,4]{1,0:T(8,128)S(1)} %copy-done.2, bf16[32,16,256]{2,1,0:T(8,128)(2,1)S(1)} %bitcast.13, bf16[4,4,16,256]{3,2,1,0:T(8,128)(2,1)S(1)} %collective-permute-done.1.far_ref, ...), custom_call_target="tpu_custom_call" | custom-call | tf_op jit(solution)/shard_map/pallas_call | solution.py:260
  19.3 0.0 copy-start.3
  19.3 1.9 %collective-permute-start.2 = (bf16[4,16,1024]{2,1,0:T(8,128)(2,1)S(1)}, bf16[4,16,1024]{2,1,0:T(8,128)(2,1)S(1)}, u32[]{:S(2)}, u32[]{:S(2)}) collective-permute-start(bf16[4,16,1024]{2,1,0:T(8,128)(2,1)S(1)} %get-tuple-element.44), channel_id=1, source_target_pairs={{0,1},{1,0},{2,3},{3,2},{4,5},{5,4},{6,7},{7,6},{8,9},{9,8},{10,11... | collective-permute-start | bytes 393224 | tf_op jit(solution)/shard_map/ppermute | solution.py:346
  21.2 6.6 %shard_map.76 = (bf16[4,16,1024]{2,1,0:T(8,128)(2,1)S(1)}, bf16[4,16,1024]{2,1,0:T(8,128)(2,1)S(1)}) custom-call(s32[4,4]{1,0:T(4,128)S(1)} %copy-done.7, s32[8,4]{1,0:T(8,128)S(1)} %copy-done.2, bf16[32,16,256]{2,1,0:T(8,128)(2,1)S(1)} %bitcast.14, bf16[4,4,16,256]{3,2,1,0:T(8,128)(2,1)S(1)} %collective-permute-done.1.far_ref, ...), custom_call_target="tpu_custom_call" | custom-call | tf_op jit(solution)/shard_map/pallas_call | solution.py:260
  27.8 0.0 copy-start.4
  27.8 0.2 collective-permute-start.3
  28.0 6.6 %shard_map.77 = (bf16[4,16,1024]{2,1,0:T(8,128)(2,1)S(1)}, bf16[4,16,1024]{2,1,0:T(8,128)(2,1)S(1)}) custom-call(s32[4,4]{1,0:T(4,128)S(1)} %copy-done.7, s32[8,4]{1,0:T(8,128)S(1)} %copy-done.2, bf16[32,16,256]{2,1,0:T(8,128)(2,1)S(1)} %bitcast.15, bf16[4,4,16,256]{3,2,1,0:T(8,128)(2,1)S(1)} %collective-permute-done.1.far_ref, ...), custom_call_target="tpu_custom_call" | custom-call | tf_op jit(solution)/shard_map/pallas_call | solution.py:260
  34.6 0.0 copy-done.3
  34.6 0.0 copy-start.5
  34.6 1.9 %collective-permute-start.4 = (bf16[4,16,1024]{2,1,0:T(8,128)(2,1)S(1)}, bf16[4,16,1024]{2,1,0:T(8,128)(2,1)S(1)}, u32[]{:S(2)}, u32[]{:S(2)}) collective-permute-start(bf16[4,16,1024]{2,1,0:T(8,128)(2,1)S(1)} %get-tuple-element.48), channel_id=1, source_target_pairs={{0,1},{1,0},{2,3},{3,2},{4,5},{5,4},{6,7},{7,6},{8,9},{9,8},{10,11... | collective-permute-start | bytes 393224 | tf_op jit(solution)/shard_map/ppermute | solution.py:346
  36.6 6.6 %shard_map.78 = (bf16[4,16,1024]{2,1,0:T(8,128)(2,1)S(1)}, bf16[4,16,1024]{2,1,0:T(8,128)(2,1)S(1)}) custom-call(s32[4,4]{1,0:T(4,128)S(1)} %copy-done.7, s32[8,4]{1,0:T(8,128)S(1)} %copy-done.2, bf16[32,16,256]{2,1,0:T(8,128)(2,1)S(1)} %bitcast.16, bf16[4,4,16,256]{3,2,1,0:T(8,128)(2,1)S(1)} %collective-permute-done.1.far_ref, ...), custom_call_target="tpu_custom_call" | custom-call | tf_op jit(solution)/shard_map/pallas_call | solution.py:260
  43.1 0.0 copy-done.4
  43.1 0.0 copy-start.6
  43.2 0.6 copy-done.6
  43.8 0.0 copy-done.5
  43.8 0.2 collective-permute-start.5
  44.0 0.5 fusion.slot_ref
  44.5 0.0 collective-permute-done.2.refs_1_
  44.5 0.0 collective-permute-done.3.refs_3_
  44.5 0.0 copy-start.10
  44.5 0.0 collective-permute-done.4.refs_5_
  44.6 4.2 %collective-permute-done.5.refs_7_ = bf16[4,16,1024]{2,1,0:T(8,128)(2,1)S(1)} collective-permute-done((bf16[4,16,1024]{2,1,0:T(8,128)(2,1)S(1)}, bf16[4,16,1024]{2,1,0:T(8,128)(2,1)S(1)}, u32[]{:S(2)}, u32[]{:S(2)}) %collective-permute-start.5) | collective-permute-done | bytes 131104 | tf_op jit(solution)/shard_map/ppermute | solution.py:346
  48.8 0.6 copy-done.12
  49.4 3.2 %shard_map.79 = (bf16[32,16,1024]{2,1,0:T(8,128)(2,1)}, bf16[32,16,1024]{2,1,0:T(8,128)(2,1)}) custom-call(s32[32]{0:T(128)} %fusion.slot_ref, bf16[4,16,1024]{2,1,0:T(8,128)(2,1)} %copy-done.3, bf16[4,16,1024]{2,1,0:T(8,128)(2,1)} %copy-done.9, bf16[4,16,1024]{2,1,0:T(8,128)(2,1)} %copy-done.4, bf16[4,16,1024]{2,1,0:T(8,128)(2,1)} %copy-done.10, ...), custom_call_target="tpu_custom_call" | custom-call | tf_op jit(solution)/shard_map/pallas_call | solution.py:293
  52.7 0.0 collective-permute-start.6
  52.7 2.9 %collective-permute-done.6 = bf16[32,16,1024]{2,1,0:T(8,128)(2,1)S(1)} collective-permute-done((bf16[32,16,1024]{2,1,0:T(8,128)(2,1)}, bf16[32,16,1024]{2,1,0:T(8,128)(2,1)S(1)}, u32[]{:S(2)}, u32[]{:S(2)}) %collective-permute-start.6) | collective-permute-done | bytes 1048608 | tf_op jit(solution)/shard_map/ppermute | solution.py:346
  55.5 1.2 %copy-done.1 = bf16[32,16,1024]{2,1,0:T(8,128)(2,1)S(1)} copy-done((bf16[32,16,1024]{2,1,0:T(8,128)(2,1)S(1)}, bf16[32,16,1024]{2,1,0:T(8,128)(2,1)}, u32[]{:S(2)}) %copy-start.1) | copy-done | bytes 1048600
  56.8 0.2 shard_map.80
  57.0 1.6 %collective-permute-start.7 = (bf16[4,4,16,512]{3,2,1,0:T(8,128)(2,1)S(1)}, bf16[4,4,16,512]{3,2,1,0:T(8,128)(2,1)S(1)}, u32[]{:S(2)}, u32[]{:S(2)}) collective-permute-start(bf16[4,4,16,512]{3,2,1,0:T(8,128)(2,1)S(1)} %get-tuple-element.55), channel_id=1, source_target_pairs={{0,4},{2,6},{4,0},{6,2},{8,12},{10,14},{12,8},{14,10},{16,20},{18,... | collective-permute-start | bytes 786440 | tf_op jit(solution)/shard_map/ppermute | solution.py:346
  58.6 1.6 %collective-permute-start.8 = (bf16[4,4,16,512]{3,2,1,0:T(8,128)(2,1)S(1)}, bf16[4,4,16,512]{3,2,1,0:T(8,128)(2,1)S(1)}, u32[]{:S(2)}, u32[]{:S(2)}) collective-permute-start(bf16[4,4,16,512]{3,2,1,0:T(8,128)(2,1)S(1)} %get-tuple-element.56), channel_id=1, source_target_pairs={{0,8},{2,10},{4,12},{6,14},{8,0},{10,2},{12,4},{14,6},{16,24},{18,... | collective-permute-start | bytes 786440 | tf_op jit(solution)/shard_map/ppermute | solution.py:346
  60.2 5.3 %collective-permute-done.7.refs_2_ = bf16[4,4,16,512]{3,2,1,0:T(8,128)(2,1)S(1)} collective-permute-done((bf16[4,4,16,512]{3,2,1,0:T(8,128)(2,1)S(1)}, bf16[4,4,16,512]{3,2,1,0:T(8,128)(2,1)S(1)}, u32[]{:S(2)}, u32[]{:S(2)}) %collective-permute-start.7) | collective-permute-done | bytes 262176 | tf_op jit(solution)/shard_map/ppermute | solution.py:346
  65.4 1.2 %collective-permute-done.8.refs_3_ = bf16[4,4,16,512]{3,2,1,0:T(8,128)(2,1)S(1)} collective-permute-done((bf16[4,4,16,512]{3,2,1,0:T(8,128)(2,1)S(1)}, bf16[4,4,16,512]{3,2,1,0:T(8,128)(2,1)S(1)}, u32[]{:S(2)}, u32[]{:S(2)}) %collective-permute-start.8) | collective-permute-done | bytes 262176 | tf_op jit(solution)/shard_map/ppermute | solution.py:346
  66.7 0.1 shard_map.81
  66.8 1.6 %collective-permute-start.9 = (bf16[2,4,16,512]{3,2,1,0:T(8,128)(2,1)S(1)}, bf16[2,4,16,512]{3,2,1,0:T(8,128)(2,1)S(1)}, u32[]{:S(2)}, u32[]{:S(2)}) collective-permute-start(bf16[2,4,16,512]{3,2,1,0:T(8,128)(2,1)S(1)} %get-tuple-element.59), channel_id=1, source_target_pairs={{0,8},{2,10},{4,12},{6,14},{8,0},{10,2},{12,4},{14,6},{16,24},{18,... | collective-permute-start | bytes 393224 | tf_op jit(solution)/shard_map/ppermute | solution.py:346
  68.4 0.5 collective-permute-start.10
  68.9 2.9 %collective-permute-done.9.refs_2_ = bf16[2,4,16,512]{3,2,1,0:T(8,128)(2,1)S(1)} collective-permute-done((bf16[2,4,16,512]{3,2,1,0:T(8,128)(2,1)S(1)}, bf16[2,4,16,512]{3,2,1,0:T(8,128)(2,1)S(1)}, u32[]{:S(2)}, u32[]{:S(2)}) %collective-permute-start.9) | collective-permute-done | bytes 131104 | tf_op jit(solution)/shard_map/ppermute | solution.py:346
  71.8 1.6 %collective-permute-done.10.refs_3_ = bf16[2,4,16,512]{3,2,1,0:T(8,128)(2,1)S(1)} collective-permute-done((bf16[2,4,16,512]{3,2,1,0:T(8,128)(2,1)S(1)}, bf16[2,4,16,512]{3,2,1,0:T(8,128)(2,1)S(1)}, u32[]{:S(2)}, u32[]{:S(2)}) %collective-permute-start.10) | collective-permute-done | bytes 131104 | tf_op jit(solution)/shard_map/ppermute | solution.py:346
  73.4 0.1 shard_map.82
  73.5 2.6 %collective-permute-start.11 = (bf16[1,4,16,512]{3,2,1,0:T(8,128)(2,1)S(1)}, bf16[1,4,16,512]{3,2,1,0:T(8,128)(2,1)S(1)}, u32[]{:S(2)}, u32[]{:S(2)}) collective-permute-start(bf16[1,4,16,512]{3,2,1,0:T(8,128)(2,1)S(1)} %get-tuple-element.63), channel_id=1, source_target_pairs={{0,16},{2,18},{4,20},{6,22},{8,24},{10,26},{12,28},{14,30},{16,0},... | collective-permute-start | bytes 196616 | tf_op jit(solution)/shard_map/ppermute | solution.py:346
  76.1 0.3 collective-permute-start.12
  76.4 3.1 %collective-permute-done.11.refs_2_ = bf16[1,4,16,512]{3,2,1,0:T(8,128)(2,1)S(1)} collective-permute-done((bf16[1,4,16,512]{3,2,1,0:T(8,128)(2,1)S(1)}, bf16[1,4,16,512]{3,2,1,0:T(8,128)(2,1)S(1)}, u32[]{:S(2)}, u32[]{:S(2)}) %collective-permute-start.11) | collective-permute-done | bytes 65568 | tf_op jit(solution)/shard_map/ppermute | solution.py:346
  79.6 2.3 %collective-permute-done.12.refs_3_ = bf16[1,4,16,512]{3,2,1,0:T(8,128)(2,1)S(1)} collective-permute-done((bf16[1,4,16,512]{3,2,1,0:T(8,128)(2,1)S(1)}, bf16[1,4,16,512]{3,2,1,0:T(8,128)(2,1)S(1)}, u32[]{:S(2)}, u32[]{:S(2)}) %collective-permute-start.12) | collective-permute-done | bytes 65568 | tf_op jit(solution)/shard_map/ppermute | solution.py:346
  81.9 0.7 reshape.24
  (10 shorter events, 0.1 us)
Async XLA Ops:
  4.7 8.0 %collective-permute-start.1 = (bf16[4,4,16,256]{3,2,1,0:T(8,128)(2,1)}, bf16[4,4,16,256]{3,2,1,0:T(8,128)(2,1)S(1)}, u32[]{:S(2)}, u32[]{:S(2)}) collective-permute-start(bf16[4,4,16,256]{3,2,1,0:T(8,128)(2,1)} %shard_map.73), channel_id=1, source_target_pairs={{0,1},{1,0},{2,3},{3,2},{4,5},{5,4},{6,7},{7,6},{8,9},{9,8},{10,11... | collective-permute-start | bytes 393224 | tf_op jit(solution)/shard_map/ppermute | solution.py:346
  9.0 3.6 %collective-permute-start = (s32[4,4]{1,0:T(4,128)S(1)}, s32[4,4]{1,0:T(4,128)S(1)}, u32[]{:S(2)}, u32[]{:S(2)}) collective-permute-start(s32[4,4]{1,0:T(4,128)S(1)} %add.27), channel_id=1, source_target_pairs={{0,1},{1,0},{2,3},{3,2},{4,5},{5,4},{6,7},{7,6},{8,9},{9,8},{10,11... | collective-permute-start | bytes 200 | tf_op jit(solution)/shard_map/ppermute | solution.py:346
  10.8 0.7 copy-start.8
  10.8 1.9 %copy-start = (bf16[4,8,16,256]{3,2,1,0:T(8,128)(2,1)S(1)}, bf16[4,8,16,256]{3,2,1,0:T(8,128)(2,1)}, u32[]{:S(2)}) copy-start(bf16[4,8,16,256]{3,2,1,0:T(8,128)(2,1)} %copy.14) | copy-start | bytes 786436
  10.8 1.9 %copy-start.2 = (s32[8,4]{1,0:T(8,128)S(1)}, s32[8,4]{1,0:T(8,128)}, u32[]{:S(2)}) copy-start(s32[8,4]{1,0:T(8,128)} %copy.10.slot_ref) | copy-start | bytes 388
  10.8 1.9 %copy-start.7 = (s32[4,4]{1,0:T(4,128)S(1)}, s32[4,4]{1,0:T(4,128)}, u32[]{:S(2)}) copy-start(s32[4,4]{1,0:T(4,128)} %kind_ref.7) | copy-start | bytes 196
  19.3 15.3 %copy-start.3 = (bf16[4,16,1024]{2,1,0:T(8,128)(2,1)}, bf16[4,16,1024]{2,1,0:T(8,128)(2,1)S(1)}, u32[]{:S(2)}) copy-start(bf16[4,16,1024]{2,1,0:T(8,128)(2,1)S(1)} %get-tuple-element.43.refs_0_) | copy-start | bytes 393220
  19.3 25.2 %collective-permute-start.2 = (bf16[4,16,1024]{2,1,0:T(8,128)(2,1)S(1)}, bf16[4,16,1024]{2,1,0:T(8,128)(2,1)S(1)}, u32[]{:S(2)}, u32[]{:S(2)}) collective-permute-start(bf16[4,16,1024]{2,1,0:T(8,128)(2,1)S(1)} %get-tuple-element.44), channel_id=1, source_target_pairs={{0,1},{1,0},{2,3},{3,2},{4,5},{5,4},{6,7},{7,6},{8,9},{9,8},{10,11... | collective-permute-start | bytes 393224 | tf_op jit(solution)/shard_map/ppermute | solution.py:346
  27.8 15.3 %copy-start.4 = (bf16[4,16,1024]{2,1,0:T(8,128)(2,1)}, bf16[4,16,1024]{2,1,0:T(8,128)(2,1)S(1)}, u32[]{:S(2)}) copy-start(bf16[4,16,1024]{2,1,0:T(8,128)(2,1)S(1)} %get-tuple-element.45.refs_2_) | copy-start | bytes 393220
  27.8 16.7 %collective-permute-start.3 = (bf16[4,16,1024]{2,1,0:T(8,128)(2,1)S(1)}, bf16[4,16,1024]{2,1,0:T(8,128)(2,1)S(1)}, u32[]{:S(2)}, u32[]{:S(2)}) collective-permute-start(bf16[4,16,1024]{2,1,0:T(8,128)(2,1)S(1)} %get-tuple-element.46), channel_id=1, source_target_pairs={{0,1},{1,0},{2,3},{3,2},{4,5},{5,4},{6,7},{7,6},{8,9},{9,8},{10,11... | collective-permute-start | bytes 393224 | tf_op jit(solution)/shard_map/ppermute | solution.py:346
  34.6 9.2 %copy-start.5 = (bf16[4,16,1024]{2,1,0:T(8,128)(2,1)}, bf16[4,16,1024]{2,1,0:T(8,128)(2,1)S(1)}, u32[]{:S(2)}) copy-start(bf16[4,16,1024]{2,1,0:T(8,128)(2,1)S(1)} %get-tuple-element.47.refs_4_) | copy-start | bytes 393220
  34.6 9.9 %collective-permute-start.4 = (bf16[4,16,1024]{2,1,0:T(8,128)(2,1)S(1)}, bf16[4,16,1024]{2,1,0:T(8,128)(2,1)S(1)}, u32[]{:S(2)}, u32[]{:S(2)}) collective-permute-start(bf16[4,16,1024]{2,1,0:T(8,128)(2,1)S(1)} %get-tuple-element.48), channel_id=1, source_target_pairs={{0,1},{1,0},{2,3},{3,2},{4,5},{5,4},{6,7},{7,6},{8,9},{9,8},{10,11... | collective-permute-start | bytes 393224 | tf_op jit(solution)/shard_map/ppermute | solution.py:346
  43.1 0.7 copy-start.6
  43.8 5.0 %collective-permute-start.5 = (bf16[4,16,1024]{2,1,0:T(8,128)(2,1)S(1)}, bf16[4,16,1024]{2,1,0:T(8,128)(2,1)S(1)}, u32[]{:S(2)}, u32[]{:S(2)}) collective-permute-start(bf16[4,16,1024]{2,1,0:T(8,128)(2,1)S(1)} %get-tuple-element.50), channel_id=1, source_target_pairs={{0,1},{1,0},{2,3},{3,2},{4,5},{5,4},{6,7},{7,6},{8,9},{9,8},{10,11... | collective-permute-start | bytes 393224 | tf_op jit(solution)/shard_map/ppermute | solution.py:346
  44.5 4.3 %copy-start.9 = (bf16[4,16,1024]{2,1,0:T(8,128)(2,1)}, bf16[4,16,1024]{2,1,0:T(8,128)(2,1)S(1)}, u32[]{:S(2)}) copy-start(bf16[4,16,1024]{2,1,0:T(8,128)(2,1)S(1)} %collective-permute-done.2.refs_1_) | copy-start | bytes 393220
  44.5 4.3 %copy-start.10 = (bf16[4,16,1024]{2,1,0:T(8,128)(2,1)}, bf16[4,16,1024]{2,1,0:T(8,128)(2,1)S(1)}, u32[]{:S(2)}) copy-start(bf16[4,16,1024]{2,1,0:T(8,128)(2,1)S(1)} %collective-permute-done.3.refs_3_) | copy-start | bytes 393220
  44.6 4.2 %copy-start.11 = (bf16[4,16,1024]{2,1,0:T(8,128)(2,1)}, bf16[4,16,1024]{2,1,0:T(8,128)(2,1)S(1)}, u32[]{:S(2)}) copy-start(bf16[4,16,1024]{2,1,0:T(8,128)(2,1)S(1)} %collective-permute-done.4.refs_5_) | copy-start | bytes 393220
  48.8 0.7 copy-start.12
  52.7 2.9 %collective-permute-start.6 = (bf16[32,16,1024]{2,1,0:T(8,128)(2,1)}, bf16[32,16,1024]{2,1,0:T(8,128)(2,1)S(1)}, u32[]{:S(2)}, u32[]{:S(2)}) collective-permute-start(bf16[32,16,1024]{2,1,0:T(8,128)(2,1)} %get-tuple-element.52), channel_id=1, source_target_pairs={{0,2},{2,0},{4,6},{6,4},{8,10},{10,8},{12,14},{14,12},{16,18},{18,... | collective-permute-start | bytes 3145736 | tf_op jit(solution)/shard_map/ppermute | solution.py:346
  55.5 1.2 %copy-start.1 = (bf16[32,16,1024]{2,1,0:T(8,128)(2,1)S(1)}, bf16[32,16,1024]{2,1,0:T(8,128)(2,1)}, u32[]{:S(2)}) copy-start(bf16[32,16,1024]{2,1,0:T(8,128)(2,1)} %get-tuple-element.51) | copy-start | bytes 3145732
  57.0 8.4 %collective-permute-start.7 = (bf16[4,4,16,512]{3,2,1,0:T(8,128)(2,1)S(1)}, bf16[4,4,16,512]{3,2,1,0:T(8,128)(2,1)S(1)}, u32[]{:S(2)}, u32[]{:S(2)}) collective-permute-start(bf16[4,4,16,512]{3,2,1,0:T(8,128)(2,1)S(1)} %get-tuple-element.55), channel_id=1, source_target_pairs={{0,4},{2,6},{4,0},{6,2},{8,12},{10,14},{12,8},{14,10},{16,20},{18,... | collective-permute-start | bytes 786440 | tf_op jit(solution)/shard_map/ppermute | solution.py:346
  58.6 8.1 %collective-permute-start.8 = (bf16[4,4,16,512]{3,2,1,0:T(8,128)(2,1)S(1)}, bf16[4,4,16,512]{3,2,1,0:T(8,128)(2,1)S(1)}, u32[]{:S(2)}, u32[]{:S(2)}) collective-permute-start(bf16[4,4,16,512]{3,2,1,0:T(8,128)(2,1)S(1)} %get-tuple-element.56), channel_id=1, source_target_pairs={{0,8},{2,10},{4,12},{6,14},{8,0},{10,2},{12,4},{14,6},{16,24},{18,... | collective-permute-start | bytes 786440 | tf_op jit(solution)/shard_map/ppermute | solution.py:346
  66.8 5.0 %collective-permute-start.9 = (bf16[2,4,16,512]{3,2,1,0:T(8,128)(2,1)S(1)}, bf16[2,4,16,512]{3,2,1,0:T(8,128)(2,1)S(1)}, u32[]{:S(2)}, u32[]{:S(2)}) collective-permute-start(bf16[2,4,16,512]{3,2,1,0:T(8,128)(2,1)S(1)} %get-tuple-element.59), channel_id=1, source_target_pairs={{0,8},{2,10},{4,12},{6,14},{8,0},{10,2},{12,4},{14,6},{16,24},{18,... | collective-permute-start | bytes 393224 | tf_op jit(solution)/shard_map/ppermute | solution.py:346
  68.4 5.0 %collective-permute-start.10 = (bf16[2,4,16,512]{3,2,1,0:T(8,128)(2,1)S(1)}, bf16[2,4,16,512]{3,2,1,0:T(8,128)(2,1)S(1)}, u32[]{:S(2)}, u32[]{:S(2)}) collective-permute-start(bf16[2,4,16,512]{3,2,1,0:T(8,128)(2,1)S(1)} %get-tuple-element.60), channel_id=1, source_target_pairs={{0,4},{2,6},{4,0},{6,2},{8,12},{10,14},{12,8},{14,10},{16,20},{18,... | collective-permute-start | bytes 393224 | tf_op jit(solution)/shard_map/ppermute | solution.py:346
  73.5 6.1 %collective-permute-start.11 = (bf16[1,4,16,512]{3,2,1,0:T(8,128)(2,1)S(1)}, bf16[1,4,16,512]{3,2,1,0:T(8,128)(2,1)S(1)}, u32[]{:S(2)}, u32[]{:S(2)}) collective-permute-start(bf16[1,4,16,512]{3,2,1,0:T(8,128)(2,1)S(1)} %get-tuple-element.63), channel_id=1, source_target_pairs={{0,16},{2,18},{4,20},{6,22},{8,24},{10,26},{12,28},{14,30},{16,0},... | collective-permute-start | bytes 196616 | tf_op jit(solution)/shard_map/ppermute | solution.py:346
  76.1 5.8 %collective-permute-start.12 = (bf16[1,4,16,512]{3,2,1,0:T(8,128)(2,1)S(1)}, bf16[1,4,16,512]{3,2,1,0:T(8,128)(2,1)S(1)}, u32[]{:S(2)}, u32[]{:S(2)}) collective-permute-start(bf16[1,4,16,512]{3,2,1,0:T(8,128)(2,1)S(1)} %get-tuple-element.64), channel_id=1, source_target_pairs={{0,16},{2,18},{4,20},{6,22},{8,24},{10,26},{12,28},{14,30},{16,0},... | collective-permute-start | bytes 196616 | tf_op jit(solution)/shard_map/ppermute | solution.py:346

commit v4 on v3

--- a/solution.py
+++ b/solution.py
@@ -45,11 +45,9 @@
 
     by_chunk = exact(one_hot((edge, edge), chunked, same), scale)
     s1e_ref[...] = exact(by_chunk, one_hot((edge, wide), same, lambda x: x // low))
-    s2e_ref[...] = exact(
-        by_chunk, one_hot((edge, wide), same, lambda x: x // (wide // 2) * half + x % half)
-    )
-    m1_ref[...] = one_hot((wide, wide), lambda x: x // edge, lambda x: x % low)
-    m2_ref[...] = one_hot((2 * edge, wide), lambda x: x // low, lambda x: x // half % low)
+    s2e_ref[...] = exact(by_chunk, one_hot((edge, wide // 2), same, lambda x: x % edge))
+    m1_ref[...] = one_hot((low * half, wide), lambda x: x // half, lambda x: x % low)
+    m2_ref[...] = one_hot((edge, wide // 2), lambda x: x // low, lambda x: x // edge)
     sa_ref[...] = exact(scale, one_hot((edge, edge), same, turned))
     pick = one_hot((edge, edge), turned, same)
     st_ref[...] = lax.dot_general(
@@ -77,9 +75,10 @@
 def make_weights(two_scale, paired):
     edge = two_scale.shape[0]
     half = edge // 2
-    wide = edge * half // 2
+    low = half // 2
+    wide = edge * low
     shapes = [
-        (edge, wide), (edge, wide), (wide, wide), (2 * edge, wide),
+        (edge, wide), (edge, wide // 2), (low * half, wide), (edge, wide // 2),
         (2, wide, 2 * wide), (wide, wide), (edge, edge), (edge, edge),
     ]
     return pl.pallas_call(
@@ -87,7 +86,7 @@
         in_specs=[pl.BlockSpec(memory_space=pltpu.VMEM)],
         out_specs=[pl.BlockSpec(memory_space=pltpu.VMEM)] * len(shapes),
         out_shape=[jax.ShapeDtypeStruct(shape, BF) for shape in shapes],
-        compiler_params=pltpu.CompilerParams(vmem_limit_bytes=32 * 1024 * 1024),
+        compiler_params=pltpu.CompilerParams(vmem_limit_bytes=24 * 1024 * 1024),
     )(two_scale)
 
 
@@ -95,11 +94,11 @@
     first = (1 - lax.axis_index("oct")) * parents
     for i in range(parents):
         for j in range(out_ref.shape[1]):
-            out_ref[i, j] = blocks_ref[slot_ref[first + i, j]]
+            out_ref[i, j] = blocks_ref[slot_ref[j, first + i]]
 
 
 def pick_blocks(child_slot, blocks, parents):
-    shape = (parents, child_slot.shape[1]) + blocks.shape[1:]
+    shape = (parents, child_slot.shape[0]) + blocks.shape[1:]
     return pl.pallas_call(
         functools.partial(pick_kernel, parents=parents),
         in_specs=[
@@ -138,28 +137,50 @@
 
 
 def apply_kernel(
-    kind_ref, slot_ref, blocks_ref, far_ref, table_ref, s1e_ref, s2e_ref, m1_ref, m2_ref,
-    fw1_ref, fw2_ref, sa_ref, st_ref, keep_ref, send_ref, cube_ref, sec_ref,
-    *, half, terms, parent,
+    kind_ref, *refs, half, terms, parent, picked,
 ):
+    if picked:
+        slot_ref, refs = refs[0], refs[1:]
+    (
+        blocks_ref, far_ref, table_ref, s1e_ref, s2e_ref, m1_ref, m2_ref, fw1_ref, fw2_ref,
+        sa_ref, st_ref, keep_ref, send_ref, cube_ref, sec_ref,
+    ) = refs[:15]
+    sets = refs[15:18], refs[18:21]
     edge = 2 * half
     low = half // 2
     wide = edge * low
     quarter = wide // 4
-
-    @pl.when(pl.program_id(0) == 0)
+    rows = terms * low
+    step = pl.program_id(0)
+
+    def expand(axis, kind, into):
+        table = table_ref[kind, rows * axis : rows * (axis + 1), :].astype(F32)
+        spread = by_output(table, edge, terms)
+        if axis == 0:
+            into[0][...] = dot(st_ref[...], spread.astype(BF)).astype(BF)
+        elif axis == 1:
+            into[1][...] = dot(spread.T.astype(BF), s1e_ref[...]).astype(BF)
+        else:
+            once = dot(spread.T.astype(BF), s2e_ref[...])
+            for i in range(terms * 4):
+                tile = once[low * i : low * (i + 1)]
+                into[2][half * i : half * (i + 1), :] = jnp.concatenate(
+                    [tile, tile], axis=0
+                ).astype(BF)
+
+    @pl.when(step == 0)
     def _():
-        if slot_ref is None:
-            near = [blocks_ref[0, i] for i in range(4)]
+        if picked:
+            first = lax.axis_index("oct") * far_ref.shape[0] + parent
+            near = [blocks_ref[slot_ref[i, first]] for i in range(4)]
         else:
-            first = lax.axis_index("oct") * far_ref.shape[0] + parent
-            near = [blocks_ref[slot_ref[first, i]] for i in range(4)]
+            near = [blocks_ref[parent, i] for i in range(4)]
         total = None
         for bit in range(2):
-            rows = []
+            parts = []
             for mid in range(2):
-                rows += [near[2 * mid + bit], far_ref[parent, 2 * mid + bit]]
-            part = dot(jnp.concatenate(rows, axis=0), fw1_ref[bit])
+                parts += [near[2 * mid + bit], far_ref[parent, 2 * mid + bit]]
+            part = dot(jnp.concatenate(parts, axis=0), fw1_ref[bit])
             total = part if total is None else total + part
         total = total.astype(BF)
         lanes = wide // 2
@@ -181,54 +202,61 @@
             cube_ref[edge * i : edge * (i + 1), :] = dot(
                 sa_ref[...], second[edge * i : edge * (i + 1)]
             ).astype(BF)
-
-    cube = cube_ref[...]
-    table = table_ref[0].astype(F32)
-    rows = terms * low
-    f0, f1, f2 = [
-        by_output(table[rows * i : rows * (i + 1)], edge, terms) for i in range(3)
-    ]
-    ft1 = f1.T.astype(BF)
-    ft2 = f2.T.reshape(terms * 4, 1, low, edge)
-    ft2 = jnp.broadcast_to(ft2, (terms * 4, 2, low, edge)).reshape(terms * 2 * edge, edge)
-    w1e = dot(ft1, s1e_ref[...]).astype(BF)
-    w2e = dot(ft2.astype(BF), s2e_ref[...]).astype(BF)
-    g0 = dot(st_ref[...], f0.astype(BF)).astype(BF)
-    for t in range(terms):
-        one = w1e[edge * t : edge * (t + 1)]
-        w1 = jnp.concatenate(
-            [one * m1_ref[edge * i : edge * (i + 1), :] for i in range(low)], axis=0
-        )
-        first = dot(cube, w1).astype(BF)
-        moved = jnp.concatenate(
-            [
-                jnp.concatenate(
-                    [
-                        first[edge * i : edge * (i + 1), quarter * j : quarter * (j + 1)]
-                        for i in range(4)
-                    ],
-                    axis=1,
-                )
-                for j in range(4)
-            ],
-            axis=0,
-        )
-        base = 2 * edge * t
-        w2 = jnp.concatenate(
-            [
-                w2e[base + half * i : base + half * (i + 1)] * m2_ref[half * q : half * (q + 1), :]
-                for i in range(4)
-                for q in range(low // 2)
-            ],
-            axis=0,
-        )
-        second = dot(moved, w2).astype(BF)
+        for axis in range(3):
+            expand(axis, kind_ref[parent, 0], sets[0])
+
+    def entry(now, after):
+        g0_ref, w1e_ref, w2e_ref = now
+        next_kind = kind_ref[parent, jnp.minimum(step + 1, kind_ref.shape[1] - 1)]
+        cube = cube_ref[...]
+        none = jnp.zeros((half, wide // 2), BF)
+        for t in range(terms):
+            one = w1e_ref[edge * t : edge * (t + 1), :]
+            w1 = jnp.concatenate(
+                [
+                    one[half * j : half * (j + 1)] * m1_ref[half * i : half * (i + 1), :]
+                    for i in range(low)
+                    for j in range(2)
+                ],
+                axis=0,
+            )
+            first = dot(cube, w1).astype(BF)
+            moved = jnp.concatenate(
+                [
+                    jnp.concatenate(
+                        [
+                            first[edge * i : edge * (i + 1), quarter * j : quarter * (j + 1)]
+                            for i in range(4)
+                        ],
+                        axis=1,
+                    )
+                    for j in range(4)
+                ],
+                axis=0,
+            )
+            w2 = []
+            for i in range(4):
+                tile = w2e_ref[half * (4 * t + i) : half * (4 * t + i + 1), :]
+                pair = [tile * m2_ref[half * q : half * (q + 1), :] for q in range(2)]
+                w2 += [jnp.concatenate([x, none], axis=1) for x in pair]
+                w2 += [jnp.concatenate([none, x], axis=1) for x in pair]
+            second = dot(moved, jnp.concatenate(w2, axis=0)).astype(BF)
+            for i in range(4):
+                sec_ref[i, edge * t : edge * (t + 1), :] = second[edge * i : edge * (i + 1)]
+            if t % 3 == 0 and t // 3 < 3:
+                expand(t // 3, next_kind, after)
         for i in range(4):
-            sec_ref[i, edge * t : edge * (t + 1), :] = second[edge * i : edge * (i + 1)]
-    for i in range(4):
-        out = dot(g0, sec_ref[i]).astype(BF)
-        keep_ref[0, :, wide * i : wide * (i + 1)] = out[:half]
-        send_ref[0, :, wide * i : wide * (i + 1)] = out[half:]
+            out = dot(g0_ref[...], sec_ref[i]).astype(BF)
+            keep_ref[step, :, wide * i : wide * (i + 1)] = out[:half]
+            send_ref[step, :, wide * i : wide * (i + 1)] = out[half:]
+
+    @pl.when(step % 2 == 0)
+    def _():
+        entry(sets[0], sets[1])
+
+    @pl.when(step % 2 == 1)
+    def _():
+        entry(sets[1], sets[0])
 
 
 def apply_parent(parent, kinds, child_slot, near, far, table, weights, half):
@@ -236,42 +264,30 @@
     wide = edge * half // 2
     terms = table.shape[1] // (3 * edge // 4)
     disps = kinds.shape[1]
-
-    def whole(array):
-        return pl.BlockSpec(array.shape, lambda k, *scalars: (0,) * array.ndim)
-
-    def of_kind(array):
-        return pl.BlockSpec((1,) + array.shape[1:], lambda k, kinds, *rest: (kinds[parent, k], 0, 0))
-
-    def of_parent(array):
-        return pl.BlockSpec((1,) + array.shape[1:], lambda k, *scalars: (parent, 0, 0, 0))
-
     shape = jax.ShapeDtypeStruct((disps, half, 4 * wide), BF)
-    out_spec = pl.BlockSpec((1, half, 4 * wide), lambda k, *scalars: (k, 0, 0))
-    kernel = functools.partial(apply_kernel, half=half, terms=terms, parent=parent)
-    if child_slot is None:
-        scalars = (kinds,)
-        body = lambda kind_ref, *refs: kernel(kind_ref, None, *refs)
-        near_spec = of_parent(near)
-    else:
-        scalars = (kinds, child_slot)
-        body = kernel
-        near_spec = whole(near)
+    scalars = (kinds,) if child_slot is None else (kinds, child_slot)
+    arrays = (near, far, table) + tuple(weights)
+    expanded = [
+        pltpu.VMEM((edge, terms * edge), BF),
+        pltpu.VMEM((terms * edge, wide), BF),
+        pltpu.VMEM((terms * 2 * edge, wide // 2), BF),
+    ]
     return pl.pallas_call(
-        body,
-        grid_spec=pltpu.PrefetchScalarGridSpec(
-            num_scalar_prefetch=len(scalars),
-            grid=(disps,),
-            in_specs=[near_spec, whole(far), of_kind(table)] + [whole(w) for w in weights],
-            out_specs=[out_spec, out_spec],
-            scratch_shapes=[
-                pltpu.VMEM((4 * edge, wide), BF),
-                pltpu.VMEM((4, terms * edge, wide), BF),
-            ],
+        functools.partial(
+            apply_kernel, half=half, terms=terms, parent=parent, picked=child_slot is not None
         ),
+        grid=(disps,),
+        in_specs=[pl.BlockSpec(memory_space=pltpu.SMEM)] * len(scalars)
+        + [pl.BlockSpec(memory_space=pltpu.VMEM)] * len(arrays),
+        out_specs=[pl.BlockSpec(memory_space=pltpu.VMEM)] * 2,
         out_shape=[shape, shape],
-        compiler_params=pltpu.CompilerParams(vmem_limit_bytes=48 * 1024 * 1024),
-    )(*scalars, near, far, table, *weights)
+        scratch_shapes=[
+            pltpu.VMEM((4 * edge, wide), BF),
+            pltpu.VMEM((4, terms * edge, wide), BF),
+        ]
+        + expanded * 2,
+        compiler_params=pltpu.CompilerParams(vmem_limit_bytes=24 * 1024 * 1024),
+    )(*scalars, *arrays)
 
 
 def sum_kernel(slot_ref, *refs, rows):
@@ -297,7 +313,7 @@
         out_specs=[pl.BlockSpec(memory_space=pltpu.VMEM)] * 2,
         out_shape=[shape, shape],
         scratch_shapes=[pltpu.VMEM((slot_count,) + tail, F32)],
-        compiler_params=pltpu.CompilerParams(vmem_limit_bytes=60 * 1024 * 1024),
+        compiler_params=pltpu.CompilerParams(vmem_limit_bytes=24 * 1024 * 1024),
     )(slots, *arrays)
 
 
@@ -313,12 +329,21 @@
                 place = (r >> (bit + 1) << bit) | (r & ((1 << bit) - 1))
                 outs[2 * i + (r >> bit & 1)][place] = total
             elif outs[0].shape[1] == 4:
-                half = lanes // 4
-                for c in range(4):
-                    to = half * (c // 2)
-                    outs[0][:, 2 * i + c % 2, :, to : to + half] = total[
-                        :, :, half * c : half * (c + 1)
-                    ]
+                wide = lanes // 2
+                half = wide // 16
+                order = one_hot(
+                    (wide, wide),
+                    lambda x: x % (2 * half) // half * (wide // 2) + x // (2 * half) * half + x % half,
+                    lambda x: x,
+                )
+                for n in range(total.shape[0]):
+                    for c in range(2):
+                        moved = exact(total[n, :, wide * c : wide * (c + 1)], order)
+                        to = wide // 2 * c
+                        for bit in range(2):
+                            outs[0][n, 2 * i + bit, :, to : to + wide // 2] = moved[
+                                :, wide // 2 * bit : wide // 2 * (bit + 1)
+                            ]
             else:
                 outs[0][:, 0, :, lanes * i : lanes * (i + 1)] = total
 
@@ -337,7 +362,7 @@
         in_specs=[pl.BlockSpec(memory_space=pltpu.VMEM)] * (2 * len(kept)),
         out_specs=[pl.BlockSpec(memory_space=pltpu.VMEM)] * len(shapes),
         out_shape=[jax.ShapeDtypeStruct(shape, BF) for shape in shapes],
-        compiler_params=pltpu.CompilerParams(vmem_limit_bytes=48 * 1024 * 1024),
+        compiler_params=pltpu.CompilerParams(vmem_limit_bytes=24 * 1024 * 1024),
     )(*kept, *arrived)
 
 
@@ -352,7 +377,6 @@
     my_leaf = lax.axis_index("leaf")
     edge = two_scale.shape[0]
     half = edge // 2
-    low = half // 2
     held = child_slot.shape[1]
     parents, disps = disp_kind.shape
     paired = oct_count == 2
@@ -360,8 +384,8 @@
     blocks = children.reshape(-1, half, half * half)
     if paired:
         near = blocks
-        far = swap(pick_blocks(child_slot, blocks, parents), "oct", 1)
-        near_slot = child_slot
+        near_slot = child_slot.T
+        far = swap(pick_blocks(near_slot, blocks, parents), "oct", 1)
     else:
         arrived = lax.all_to_all(
             blocks[child_slot], "oct", split_axis=0, concat_axis=1, tiled=True
@@ -389,7 +413,7 @@
         if paired:
             arrays += [kept, swap(sent, "oct", 1)]
         else:
-            rows = jnp.stack([kept, sent], axis=1).reshape(disps, 2, half, 2, 2, 2, low * half)
+            rows = jnp.stack([kept, sent], axis=1).reshape(disps, 2, half, 2, half, 2, half)
             rows = rows.transpose(1, 3, 5, 0, 2, 4, 6)
             rows = rows.reshape(oct_count, held, disps, half, half * half)
             rows = rows.transpose(0, 2, 1, 3, 4)

time: 83 us -> 83.6 us (level)
  Pallas kernels: 32.5 us -> 37.2 us
  local copies, waits for them, and re-layouts: 8.88 us -> 5.02 us
    pallas_call x4, Pallas kernels: 26.3 us -> 32.6 us  [apply_parent(): pl.pallas_call(functools.partial(apply_kernel, half=half, terms=terms, pa...]
    unnamed x29 -> x10, local copies, waits for them, and re-layouts: 7.95 us -> 4.07 us
    pallas_call x1, Pallas kernels: 3.22 us -> 1.26 us  [sum_rows(): pl.pallas_call(functools.partial(sum_kernel, rows=rows), in_specs=[pl.Blo...]
  transfers between devices with their start and end apart: 13 -> 13, of which waited for: 9 -> 9; matrix products, arithmetic and copies ran while one was open for 5% -> 4% of each run, Pallas kernels for 25% -> 30%
where the time goes in v4:
time: 83.6 us; the launch traced here: 83.4 us
  Pallas kernels  37.2 us (44%)
  waiting for transfers between devices  24 us (29%)
  starting transfers between devices  15.6 us (19%)
  local copies, waits for them, and re-layouts  5.02 us (6%)
  other arithmetic  1.39 us (2%)
    pallas_call x4, Pallas kernels, apply_parent(): pl.pallas_call(functools.partial(apply_kernel, half=half, terms=terms, pa...  32.6 us
    ppermute x13, waiting for transfers between devices, swap(): return lax.ppermute(x, axis, [(i, i ^ mask) for i in range(count)])  24 us
    ppermute x13, starting transfers between devices, swap(): return lax.ppermute(x, axis, [(i, i ^ mask) for i in range(count)])  15.6 us
    unnamed x10, local copies, waits for them, and re-layouts  4.07 us
  transfers between devices with their start and end apart: 13, of which 9 were waited for; matrix products, arithmetic and copies ran while one was open for 4% of the time, Pallas kernels for 30%

profile of v4, /device:TPU:0, one launch (start us, length us, event | category | flops | bytes accessed | tf_op | source)
XLA Modules:
  0.0 83.4 jit_solution(7611086769451054595)
XLA Ops:
  0.0 1.7 %copy.9 = bf16[4,8,16,256]{3,2,1,0:T(8,128)(2,1)} copy(bf16[4,8,16,256]{3,1,2,0:T(8,128)(2,1)} %bitcast.27) | data formatting | bytes 524288
  1.7 1.6 %shard_map.73 = bf16[4,4,16,256]{3,2,1,0:T(8,128)(2,1)} custom-call(s32[4,8]{1,0:T(4,128)} %bitcast.20, bf16[32,16,256]{2,1,0:T(8,128)(2,1)} %bitcast.13), custom_call_target="tpu_custom_call" | custom-call | tf_op jit(solution)/shard_map/pallas_call | solution.py:102
  3.3 2.9 %collective-permute-start.1 = (bf16[4,4,16,256]{3,2,1,0:T(8,128)(2,1)}, bf16[4,4,16,256]{3,2,1,0:T(8,128)(2,1)S(1)}, u32[]{:S(2)}, u32[]{:S(2)}) collective-permute-start(bf16[4,4,16,256]{3,2,1,0:T(8,128)(2,1)} %shard_map.73), channel_id=1, source_target_pairs={{0,1},{1,0},{2,3},{3,2},{4,5},{5,4},{6,7},{7,6},{8,9},{9,8},{10,11... | collective-permute-start | bytes 393224 | tf_op jit(solution)/shard_map/ppermute | solution.py:371
  6.3 0.7 broadcast_multiply_fusion
  7.0 0.7 add.27
  7.7 0.0 collective-permute-start
  7.7 1.8 %copy.10 = bf16[4,8,240,128]{3,2,1,0:T(8,128)(2,1)S(1)} copy(bf16[4,8,240,128]{3,1,2,0:T(8,128)(2,1)} %bitcast.26) | data formatting | bytes 3932160
  9.5 0.0 copy-start.3
  9.5 0.0 copy-start
  9.5 0.0 copy-start.1
  9.5 0.0 copy-start.2
  9.5 0.1 slice.refs_3_
  9.6 0.5 copy-done.3
  10.2 0.9 %shard_map.74 = (bf16[32,256]{1,0:T(8,128)(2,1)S(1)}, bf16[32,128]{1,0:T(8,128)(2,1)S(1)}, bf16[128,256]{1,0:T(8,128)(2,1)S(1)}, bf16[32,128]{1,0:T(8,128)(2,1)S...) custom-call(bf16[32,32]{1,0:T(8,128)(2,1)S(1)} %copy-done.3), custom_call_target="tpu_custom_call" | custom-call | tf_op jit(solution)/shard_map/pallas_call | solution.py:84
  11.0 0.2 collective-permute-done
  11.3 0.1 stack.14
  11.3 0.0 collective-permute-done.1.refs_2_
  11.3 0.0 copy-done
  11.4 0.0 copy-done.1
  11.4 0.0 copy-done.2
  11.4 8.2 %shard_map.75 = (bf16[4,16,1024]{2,1,0:T(8,128)(2,1)S(1)}, bf16[4,16,1024]{2,1,0:T(8,128)(2,1)S(1)}) custom-call(s32[4,4]{1,0:T(4,128)S(1)} %copy-done.2, s32[4,8]{1,0:T(4,128)S(1)} %bitcast.21, bf16[32,16,256]{2,1,0:T(8,128)(2,1)S(1)} %bitcast.14, bf16[4,4,16,256]{3,2,1,0:T(8,128)(2,1)S(1)} %collective-permute-done.1.refs_2_, ...), custom_call_target="tpu_custom_call" | custom-call | tf_op jit(solution)/shard_map/pallas_call | solution.py:275
  19.5 1.9 %collective-permute-start.2 = (bf16[4,16,1024]{2,1,0:T(8,128)(2,1)S(1)}, bf16[4,16,1024]{2,1,0:T(8,128)(2,1)S(1)}, u32[]{:S(2)}, u32[]{:S(2)}) collective-permute-start(bf16[4,16,1024]{2,1,0:T(8,128)(2,1)S(1)} %get-tuple-element.44), channel_id=1, source_target_pairs={{0,1},{1,0},{2,3},{3,2},{4,5},{5,4},{6,7},{7,6},{8,9},{9,8},{10,11... | collective-permute-start | bytes 393224 | tf_op jit(solution)/shard_map/ppermute | solution.py:371
  21.4 8.1 %shard_map.76 = (bf16[4,16,1024]{2,1,0:T(8,128)(2,1)S(1)}, bf16[4,16,1024]{2,1,0:T(8,128)(2,1)S(1)}) custom-call(s32[4,4]{1,0:T(4,128)S(1)} %copy-done.2, s32[4,8]{1,0:T(4,128)S(1)} %bitcast.22, bf16[32,16,256]{2,1,0:T(8,128)(2,1)S(1)} %bitcast.15, bf16[4,4,16,256]{3,2,1,0:T(8,128)(2,1)S(1)} %collective-permute-done.1.refs_2_, ...), custom_call_target="tpu_custom_call" | custom-call | tf_op jit(solution)/shard_map/pallas_call | solution.py:275
  29.6 0.2 collective-permute-start.3
  29.8 8.1 %shard_map.77 = (bf16[4,16,1024]{2,1,0:T(8,128)(2,1)S(1)}, bf16[4,16,1024]{2,1,0:T(8,128)(2,1)S(1)}) custom-call(s32[4,4]{1,0:T(4,128)S(1)} %copy-done.2, s32[4,8]{1,0:T(4,128)S(1)} %bitcast.23, bf16[32,16,256]{2,1,0:T(8,128)(2,1)S(1)} %bitcast.16, bf16[4,4,16,256]{3,2,1,0:T(8,128)(2,1)S(1)} %collective-permute-done.1.refs_2_, ...), custom_call_target="tpu_custom_call" | custom-call | tf_op jit(solution)/shard_map/pallas_call | solution.py:275
  38.0 1.9 %collective-permute-start.4 = (bf16[4,16,1024]{2,1,0:T(8,128)(2,1)S(1)}, bf16[4,16,1024]{2,1,0:T(8,128)(2,1)S(1)}, u32[]{:S(2)}, u32[]{:S(2)}) collective-permute-start(bf16[4,16,1024]{2,1,0:T(8,128)(2,1)S(1)} %get-tuple-element.48), channel_id=1, source_target_pairs={{0,1},{1,0},{2,3},{3,2},{4,5},{5,4},{6,7},{7,6},{8,9},{9,8},{10,11... | collective-permute-start | bytes 393224 | tf_op jit(solution)/shard_map/ppermute | solution.py:371
  39.9 8.1 %shard_map.78 = (bf16[4,16,1024]{2,1,0:T(8,128)(2,1)S(1)}, bf16[4,16,1024]{2,1,0:T(8,128)(2,1)S(1)}) custom-call(s32[4,4]{1,0:T(4,128)S(1)} %copy-done.2, s32[4,8]{1,0:T(4,128)S(1)} %bitcast.24, bf16[32,16,256]{2,1,0:T(8,128)(2,1)S(1)} %bitcast.17, bf16[4,4,16,256]{3,2,1,0:T(8,128)(2,1)S(1)} %collective-permute-done.1.refs_2_, ...), custom_call_target="tpu_custom_call" | custom-call | tf_op jit(solution)/shard_map/pallas_call | solution.py:275
  48.0 0.2 collective-permute-start.5
  48.3 0.0 collective-permute-done.2.refs_1_
  48.3 0.0 collective-permute-done.3.refs_3_
  48.3 0.0 collective-permute-done.4.refs_5_
  48.3 4.7 %collective-permute-done.5.refs_7_ = bf16[4,16,1024]{2,1,0:T(8,128)(2,1)S(1)} collective-permute-done((bf16[4,16,1024]{2,1,0:T(8,128)(2,1)S(1)}, bf16[4,16,1024]{2,1,0:T(8,128)(2,1)S(1)}, u32[]{:S(2)}, u32[]{:S(2)}) %collective-permute-start.5) | collective-permute-done | bytes 131104 | tf_op jit(solution)/shard_map/ppermute | solution.py:371
  53.1 1.3 %shard_map.79 = (bf16[32,16,1024]{2,1,0:T(8,128)(2,1)S(1)}, bf16[32,16,1024]{2,1,0:T(8,128)(2,1)S(1)}) custom-call(s32[32]{0:T(128)S(1)} %fusion.slot_ref, bf16[4,16,1024]{2,1,0:T(8,128)(2,1)S(1)} %get-tuple-element.43.refs_0_, bf16[4,16,1024]{2,1,0:T(8,128)(2,1)S(1)} %collective-permute-done.2.refs_1_, bf16[4,16,1024]{2,1,0:T(8,128)(2,1)S(1)} %get-tuple-element.45.refs_2_, ...), custom_call_target="tpu_custom_call" | custom-call | tf_op jit(solution)/shard_map/pallas_call | solution.py:309
  54.3 0.1 collective-permute-start.6
  54.4 2.6 %collective-permute-done.6 = bf16[32,16,1024]{2,1,0:T(8,128)(2,1)S(1)} collective-permute-done((bf16[32,16,1024]{2,1,0:T(8,128)(2,1)S(1)}, bf16[32,16,1024]{2,1,0:T(8,128)(2,1)S(1)}, u32[]{:S(2)}, u32[]{:S(2)}) %collective-permute-start.6) | collective-permute-done | bytes 1048608 | tf_op jit(solution)/shard_map/ppermute | solution.py:371
  57.1 0.3 shard_map.80
  57.3 1.6 %collective-permute-start.7 = (bf16[4,4,16,512]{3,2,1,0:T(8,128)(2,1)S(1)}, bf16[4,4,16,512]{3,2,1,0:T(8,128)(2,1)S(1)}, u32[]{:S(2)}, u32[]{:S(2)}) collective-permute-start(bf16[4,4,16,512]{3,2,1,0:T(8,128)(2,1)S(1)} %get-tuple-element.55), channel_id=1, source_target_pairs={{0,4},{2,6},{4,0},{6,2},{8,12},{10,14},{12,8},{14,10},{16,20},{18,... | collective-permute-start | bytes 786440 | tf_op jit(solution)/shard_map/ppermute | solution.py:371
  58.9 1.6 %collective-permute-start.8 = (bf16[4,4,16,512]{3,2,1,0:T(8,128)(2,1)S(1)}, bf16[4,4,16,512]{3,2,1,0:T(8,128)(2,1)S(1)}, u32[]{:S(2)}, u32[]{:S(2)}) collective-permute-start(bf16[4,4,16,512]{3,2,1,0:T(8,128)(2,1)S(1)} %get-tuple-element.56), channel_id=1, source_target_pairs={{0,8},{2,10},{4,12},{6,14},{8,0},{10,2},{12,4},{14,6},{16,24},{18,... | collective-permute-start | bytes 786440 | tf_op jit(solution)/shard_map/ppermute | solution.py:371
  60.5 5.3 %collective-permute-done.7.refs_2_ = bf16[4,4,16,512]{3,2,1,0:T(8,128)(2,1)S(1)} collective-permute-done((bf16[4,4,16,512]{3,2,1,0:T(8,128)(2,1)S(1)}, bf16[4,4,16,512]{3,2,1,0:T(8,128)(2,1)S(1)}, u32[]{:S(2)}, u32[]{:S(2)}) %collective-permute-start.7) | collective-permute-done | bytes 262176 | tf_op jit(solution)/shard_map/ppermute | solution.py:371
  65.8 1.2 %collective-permute-done.8.refs_3_ = bf16[4,4,16,512]{3,2,1,0:T(8,128)(2,1)S(1)} collective-permute-done((bf16[4,4,16,512]{3,2,1,0:T(8,128)(2,1)S(1)}, bf16[4,4,16,512]{3,2,1,0:T(8,128)(2,1)S(1)}, u32[]{:S(2)}, u32[]{:S(2)}) %collective-permute-start.8) | collective-permute-done | bytes 262176 | tf_op jit(solution)/shard_map/ppermute | solution.py:371
  67.0 0.1 shard_map.81
  67.1 1.6 %collective-permute-start.9 = (bf16[2,4,16,512]{3,2,1,0:T(8,128)(2,1)S(1)}, bf16[2,4,16,512]{3,2,1,0:T(8,128)(2,1)S(1)}, u32[]{:S(2)}, u32[]{:S(2)}) collective-permute-start(bf16[2,4,16,512]{3,2,1,0:T(8,128)(2,1)S(1)} %get-tuple-element.59), channel_id=1, source_target_pairs={{0,8},{2,10},{4,12},{6,14},{8,0},{10,2},{12,4},{14,6},{16,24},{18,... | collective-permute-start | bytes 393224 | tf_op jit(solution)/shard_map/ppermute | solution.py:371
  68.8 0.5 collective-permute-start.10
  69.3 2.9 %collective-permute-done.9.refs_2_ = bf16[2,4,16,512]{3,2,1,0:T(8,128)(2,1)S(1)} collective-permute-done((bf16[2,4,16,512]{3,2,1,0:T(8,128)(2,1)S(1)}, bf16[2,4,16,512]{3,2,1,0:T(8,128)(2,1)S(1)}, u32[]{:S(2)}, u32[]{:S(2)}) %collective-permute-start.9) | collective-permute-done | bytes 131104 | tf_op jit(solution)/shard_map/ppermute | solution.py:371
  72.2 1.6 %collective-permute-done.10.refs_3_ = bf16[2,4,16,512]{3,2,1,0:T(8,128)(2,1)S(1)} collective-permute-done((bf16[2,4,16,512]{3,2,1,0:T(8,128)(2,1)S(1)}, bf16[2,4,16,512]{3,2,1,0:T(8,128)(2,1)S(1)}, u32[]{:S(2)}, u32[]{:S(2)}) %collective-permute-start.10) | collective-permute-done | bytes 131104 | tf_op jit(solution)/shard_map/ppermute | solution.py:371
  73.7 0.1 shard_map.82
  73.8 2.7 %collective-permute-start.11 = (bf16[1,4,16,512]{3,2,1,0:T(8,128)(2,1)S(1)}, bf16[1,4,16,512]{3,2,1,0:T(8,128)(2,1)S(1)}, u32[]{:S(2)}, u32[]{:S(2)}) collective-permute-start(bf16[1,4,16,512]{3,2,1,0:T(8,128)(2,1)S(1)} %get-tuple-element.63), channel_id=1, source_target_pairs={{0,16},{2,18},{4,20},{6,22},{8,24},{10,26},{12,28},{14,30},{16,0},... | collective-permute-start | bytes 196616 | tf_op jit(solution)/shard_map/ppermute | solution.py:371
  76.5 0.3 collective-permute-start.12
  76.8 3.1 %collective-permute-done.11.refs_2_ = bf16[1,4,16,512]{3,2,1,0:T(8,128)(2,1)S(1)} collective-permute-done((bf16[1,4,16,512]{3,2,1,0:T(8,128)(2,1)S(1)}, bf16[1,4,16,512]{3,2,1,0:T(8,128)(2,1)S(1)}, u32[]{:S(2)}, u32[]{:S(2)}) %collective-permute-start.11) | collective-permute-done | bytes 65568 | tf_op jit(solution)/shard_map/ppermute | solution.py:371
  79.9 2.3 %collective-permute-done.12.refs_3_ = bf16[1,4,16,512]{3,2,1,0:T(8,128)(2,1)S(1)} collective-permute-done((bf16[1,4,16,512]{3,2,1,0:T(8,128)(2,1)S(1)}, bf16[1,4,16,512]{3,2,1,0:T(8,128)(2,1)S(1)}, u32[]{:S(2)}, u32[]{:S(2)}) %collective-permute-start.12) | collective-permute-done | bytes 65568 | tf_op jit(solution)/shard_map/ppermute | solution.py:371
  82.2 0.4 shard_map.83
  82.6 0.7 reshape.24
  (3 shorter events, 0.0 us)
Async XLA Ops:
  3.3 8.0 %collective-permute-start.1 = (bf16[4,4,16,256]{3,2,1,0:T(8,128)(2,1)}, bf16[4,4,16,256]{3,2,1,0:T(8,128)(2,1)S(1)}, u32[]{:S(2)}, u32[]{:S(2)}) collective-permute-start(bf16[4,4,16,256]{3,2,1,0:T(8,128)(2,1)} %shard_map.73), channel_id=1, source_target_pairs={{0,1},{1,0},{2,3},{3,2},{4,5},{5,4},{6,7},{7,6},{8,9},{9,8},{10,11... | collective-permute-start | bytes 393224 | tf_op jit(solution)/shard_map/ppermute | solution.py:371
  7.7 3.6 %collective-permute-start = (s32[4,4]{1,0:T(4,128)S(1)}, s32[4,4]{1,0:T(4,128)S(1)}, u32[]{:S(2)}, u32[]{:S(2)}) collective-permute-start(s32[4,4]{1,0:T(4,128)S(1)} %add.27), channel_id=1, source_target_pairs={{0,1},{1,0},{2,3},{3,2},{4,5},{5,4},{6,7},{7,6},{8,9},{9,8},{10,11... | collective-permute-start | bytes 200 | tf_op jit(solution)/shard_map/ppermute | solution.py:371
  9.5 0.7 copy-start.3
  9.5 1.9 %copy-start = (bf16[4,8,16,256]{3,2,1,0:T(8,128)(2,1)S(1)}, bf16[4,8,16,256]{3,2,1,0:T(8,128)(2,1)}, u32[]{:S(2)}) copy-start(bf16[4,8,16,256]{3,2,1,0:T(8,128)(2,1)} %copy.9) | copy-start | bytes 786436
  9.5 1.9 %copy-start.1 = (s32[8,4]{0,1:T(4,128)S(1)}, s32[8,4]{0,1:T(4,128)}, u32[]{:S(2)}) copy-start(s32[8,4]{0,1:T(4,128)} %param.8) | copy-start | bytes 388
  9.5 1.9 %copy-start.2 = (s32[4,4]{1,0:T(4,128)S(1)}, s32[4,4]{1,0:T(4,128)}, u32[]{:S(2)}) copy-start(s32[4,4]{1,0:T(4,128)} %kind_ref.7) | copy-start | bytes 196
  19.5 28.8 %collective-permute-start.2 = (bf16[4,16,1024]{2,1,0:T(8,128)(2,1)S(1)}, bf16[4,16,1024]{2,1,0:T(8,128)(2,1)S(1)}, u32[]{:S(2)}, u32[]{:S(2)}) collective-permute-start(bf16[4,16,1024]{2,1,0:T(8,128)(2,1)S(1)} %get-tuple-element.44), channel_id=1, source_target_pairs={{0,1},{1,0},{2,3},{3,2},{4,5},{5,4},{6,7},{7,6},{8,9},{9,8},{10,11... | collective-permute-start | bytes 393224 | tf_op jit(solution)/shard_map/ppermute | solution.py:371
  29.6 18.7 %collective-permute-start.3 = (bf16[4,16,1024]{2,1,0:T(8,128)(2,1)S(1)}, bf16[4,16,1024]{2,1,0:T(8,128)(2,1)S(1)}, u32[]{:S(2)}, u32[]{:S(2)}) collective-permute-start(bf16[4,16,1024]{2,1,0:T(8,128)(2,1)S(1)} %get-tuple-element.46), channel_id=1, source_target_pairs={{0,1},{1,0},{2,3},{3,2},{4,5},{5,4},{6,7},{7,6},{8,9},{9,8},{10,11... | collective-permute-start | bytes 393224 | tf_op jit(solution)/shard_map/ppermute | solution.py:371
  38.0 10.3 %collective-permute-start.4 = (bf16[4,16,1024]{2,1,0:T(8,128)(2,1)S(1)}, bf16[4,16,1024]{2,1,0:T(8,128)(2,1)S(1)}, u32[]{:S(2)}, u32[]{:S(2)}) collective-permute-start(bf16[4,16,1024]{2,1,0:T(8,128)(2,1)S(1)} %get-tuple-element.48), channel_id=1, source_target_pairs={{0,1},{1,0},{2,3},{3,2},{4,5},{5,4},{6,7},{7,6},{8,9},{9,8},{10,11... | collective-permute-start | bytes 393224 | tf_op jit(solution)/shard_map/ppermute | solution.py:371
  48.0 5.0 %collective-permute-start.5 = (bf16[4,16,1024]{2,1,0:T(8,128)(2,1)S(1)}, bf16[4,16,1024]{2,1,0:T(8,128)(2,1)S(1)}, u32[]{:S(2)}, u32[]{:S(2)}) collective-permute-start(bf16[4,16,1024]{2,1,0:T(8,128)(2,1)S(1)} %get-tuple-element.50), channel_id=1, source_target_pairs={{0,1},{1,0},{2,3},{3,2},{4,5},{5,4},{6,7},{7,6},{8,9},{9,8},{10,11... | collective-permute-start | bytes 393224 | tf_op jit(solution)/shard_map/ppermute | solution.py:371
  54.3 2.7 %collective-permute-start.6 = (bf16[32,16,1024]{2,1,0:T(8,128)(2,1)S(1)}, bf16[32,16,1024]{2,1,0:T(8,128)(2,1)S(1)}, u32[]{:S(2)}, u32[]{:S(2)}) collective-permute-start(bf16[32,16,1024]{2,1,0:T(8,128)(2,1)S(1)} %get-tuple-element.52), channel_id=1, source_target_pairs={{0,2},{2,0},{4,6},{6,4},{8,10},{10,8},{12,14},{14,12},{16,18},{18,... | collective-permute-start | bytes 3145736 | tf_op jit(solution)/shard_map/ppermute | solution.py:371
  57.3 8.4 %collective-permute-start.7 = (bf16[4,4,16,512]{3,2,1,0:T(8,128)(2,1)S(1)}, bf16[4,4,16,512]{3,2,1,0:T(8,128)(2,1)S(1)}, u32[]{:S(2)}, u32[]{:S(2)}) collective-permute-start(bf16[4,4,16,512]{3,2,1,0:T(8,128)(2,1)S(1)} %get-tuple-element.55), channel_id=1, source_target_pairs={{0,4},{2,6},{4,0},{6,2},{8,12},{10,14},{12,8},{14,10},{16,20},{18,... | collective-permute-start | bytes 786440 | tf_op jit(solution)/shard_map/ppermute | solution.py:371
  58.9 8.1 %collective-permute-start.8 = (bf16[4,4,16,512]{3,2,1,0:T(8,128)(2,1)S(1)}, bf16[4,4,16,512]{3,2,1,0:T(8,128)(2,1)S(1)}, u32[]{:S(2)}, u32[]{:S(2)}) collective-permute-start(bf16[4,4,16,512]{3,2,1,0:T(8,128)(2,1)S(1)} %get-tuple-element.56), channel_id=1, source_target_pairs={{0,8},{2,10},{4,12},{6,14},{8,0},{10,2},{12,4},{14,6},{16,24},{18,... | collective-permute-start | bytes 786440 | tf_op jit(solution)/shard_map/ppermute | solution.py:371
  67.1 5.0 %collective-permute-start.9 = (bf16[2,4,16,512]{3,2,1,0:T(8,128)(2,1)S(1)}, bf16[2,4,16,512]{3,2,1,0:T(8,128)(2,1)S(1)}, u32[]{:S(2)}, u32[]{:S(2)}) collective-permute-start(bf16[2,4,16,512]{3,2,1,0:T(8,128)(2,1)S(1)} %get-tuple-element.59), channel_id=1, source_target_pairs={{0,8},{2,10},{4,12},{6,14},{8,0},{10,2},{12,4},{14,6},{16,24},{18,... | collective-permute-start | bytes 393224 | tf_op jit(solution)/shard_map/ppermute | solution.py:371
  68.8 5.0 %collective-permute-start.10 = (bf16[2,4,16,512]{3,2,1,0:T(8,128)(2,1)S(1)}, bf16[2,4,16,512]{3,2,1,0:T(8,128)(2,1)S(1)}, u32[]{:S(2)}, u32[]{:S(2)}) collective-permute-start(bf16[2,4,16,512]{3,2,1,0:T(8,128)(2,1)S(1)} %get-tuple-element.60), channel_id=1, source_target_pairs={{0,4},{2,6},{4,0},{6,2},{8,12},{10,14},{12,8},{14,10},{16,20},{18,... | collective-permute-start | bytes 393224 | tf_op jit(solution)/shard_map/ppermute | solution.py:371
  73.8 6.1 %collective-permute-start.11 = (bf16[1,4,16,512]{3,2,1,0:T(8,128)(2,1)S(1)}, bf16[1,4,16,512]{3,2,1,0:T(8,128)(2,1)S(1)}, u32[]{:S(2)}, u32[]{:S(2)}) collective-permute-start(bf16[1,4,16,512]{3,2,1,0:T(8,128)(2,1)S(1)} %get-tuple-element.63), channel_id=1, source_target_pairs={{0,16},{2,18},{4,20},{6,22},{8,24},{10,26},{12,28},{14,30},{16,0},... | collective-permute-start | bytes 196616 | tf_op jit(solution)/shard_map/ppermute | solution.py:371
  76.5 5.7 %collective-permute-start.12 = (bf16[1,4,16,512]{3,2,1,0:T(8,128)(2,1)S(1)}, bf16[1,4,16,512]{3,2,1,0:T(8,128)(2,1)S(1)}, u32[]{:S(2)}, u32[]{:S(2)}) collective-permute-start(bf16[1,4,16,512]{3,2,1,0:T(8,128)(2,1)S(1)} %get-tuple-element.64), channel_id=1, source_target_pairs={{0,16},{2,18},{4,20},{6,22},{8,24},{10,26},{12,28},{14,30},{16,0},... | collective-permute-start | bytes 196616 | tf_op jit(solution)/shard_map/ppermute | solution.py:371

commit v5 on v4

--- a/solution.py
+++ b/solution.py
@@ -145,7 +145,7 @@
         blocks_ref, far_ref, table_ref, s1e_ref, s2e_ref, m1_ref, m2_ref, fw1_ref, fw2_ref,
         sa_ref, st_ref, keep_ref, send_ref, cube_ref, sec_ref,
     ) = refs[:15]
-    sets = refs[15:18], refs[18:21]
+    expanded = refs[15:]
     edge = 2 * half
     low = half // 2
     wide = edge * low
@@ -153,18 +153,27 @@
     rows = terms * low
     step = pl.program_id(0)
 
-    def expand(axis, kind, into):
-        table = table_ref[kind, rows * axis : rows * (axis + 1), :].astype(F32)
-        spread = by_output(table, edge, terms)
-        if axis == 0:
-            into[0][...] = dot(st_ref[...], spread.astype(BF)).astype(BF)
-        elif axis == 1:
-            into[1][...] = dot(spread.T.astype(BF), s1e_ref[...]).astype(BF)
-        else:
-            once = dot(spread.T.astype(BF), s2e_ref[...])
+    def expand(kinds):
+        g0_ref, w1e_ref, w2e_ref = expanded
+        spread = [
+            [
+                by_output(
+                    table_ref[kind, rows * axis : rows * (axis + 1), :].astype(F32), edge, terms
+                ).astype(BF)
+                for kind in kinds
+            ]
+            for axis in range(3)
+        ]
+        turned = [[x.T for x in spread[axis]] for axis in (1, 2)]
+        for k in range(len(kinds)):
+            g0_ref[k] = dot(st_ref[...], spread[0][k]).astype(BF)
+        for k in range(len(kinds)):
+            w1e_ref[k] = dot(turned[0][k], s1e_ref[...]).astype(BF)
+        for k in range(len(kinds)):
+            once = dot(turned[1][k], s2e_ref[...])
             for i in range(terms * 4):
                 tile = once[low * i : low * (i + 1)]
-                into[2][half * i : half * (i + 1), :] = jnp.concatenate(
+                w2e_ref[k, half * i : half * (i + 1), :] = jnp.concatenate(
                     [tile, tile], axis=0
                 ).astype(BF)
 
@@ -202,61 +211,48 @@
             cube_ref[edge * i : edge * (i + 1), :] = dot(
                 sa_ref[...], second[edge * i : edge * (i + 1)]
             ).astype(BF)
-        for axis in range(3):
-            expand(axis, kind_ref[parent, 0], sets[0])
-
-    def entry(now, after):
-        g0_ref, w1e_ref, w2e_ref = now
-        next_kind = kind_ref[parent, jnp.minimum(step + 1, kind_ref.shape[1] - 1)]
-        cube = cube_ref[...]
-        none = jnp.zeros((half, wide // 2), BF)
-        for t in range(terms):
-            one = w1e_ref[edge * t : edge * (t + 1), :]
-            w1 = jnp.concatenate(
-                [
-                    one[half * j : half * (j + 1)] * m1_ref[half * i : half * (i + 1), :]
-                    for i in range(low)
-                    for j in range(2)
-                ],
-                axis=0,
-            )
-            first = dot(cube, w1).astype(BF)
-            moved = jnp.concatenate(
-                [
-                    jnp.concatenate(
-                        [
-                            first[edge * i : edge * (i + 1), quarter * j : quarter * (j + 1)]
-                            for i in range(4)
-                        ],
-                        axis=1,
-                    )
-                    for j in range(4)
-                ],
-                axis=0,
-            )
-            w2 = []
-            for i in range(4):
-                tile = w2e_ref[half * (4 * t + i) : half * (4 * t + i + 1), :]
-                pair = [tile * m2_ref[half * q : half * (q + 1), :] for q in range(2)]
-                w2 += [jnp.concatenate([x, none], axis=1) for x in pair]
-                w2 += [jnp.concatenate([none, x], axis=1) for x in pair]
-            second = dot(moved, jnp.concatenate(w2, axis=0)).astype(BF)
-            for i in range(4):
-                sec_ref[i, edge * t : edge * (t + 1), :] = second[edge * i : edge * (i + 1)]
-            if t % 3 == 0 and t // 3 < 3:
-                expand(t // 3, next_kind, after)
+        expand([kind_ref[parent, k] for k in range(kind_ref.shape[1])])
+
+    g0_ref, w1e_ref, w2e_ref = expanded
+    cube = cube_ref[...]
+    none = jnp.zeros((half, wide // 2), BF)
+    for t in range(terms):
+        one = w1e_ref[step, edge * t : edge * (t + 1), :]
+        w1 = jnp.concatenate(
+            [
+                one[half * j : half * (j + 1)] * m1_ref[half * i : half * (i + 1), :]
+                for i in range(low)
+                for j in range(2)
+            ],
+            axis=0,
+        )
+        first = dot(cube, w1).astype(BF)
+        moved = jnp.concatenate(
+            [
+                jnp.concatenate(
+                    [
+                        first[edge * i : edge * (i + 1), quarter * j : quarter * (j + 1)]
+                        for i in range(4)
+                    ],
+                    axis=1,
+                )
+                for j in range(4)
+            ],
+            axis=0,
+        )
+        w2 = []
         for i in range(4):
-            out = dot(g0_ref[...], sec_ref[i]).astype(BF)
-            keep_ref[step, :, wide * i : wide * (i + 1)] = out[:half]
-            send_ref[step, :, wide * i : wide * (i + 1)] = out[half:]
-
-    @pl.when(step % 2 == 0)
-    def _():
-        entry(sets[0], sets[1])
-
-    @pl.when(step % 2 == 1)
-    def _():
-        entry(sets[1], sets[0])
+            tile = w2e_ref[step, half * (4 * t + i) : half * (4 * t + i + 1), :]
+            pair = [tile * m2_ref[half * q : half * (q + 1), :] for q in range(2)]
+            w2 += [jnp.concatenate([x, none], axis=1) for x in pair]
+            w2 += [jnp.concatenate([none, x], axis=1) for x in pair]
+        second = dot(moved, jnp.concatenate(w2, axis=0)).astype(BF)
+        for i in range(4):
+            sec_ref[i, edge * t : edge * (t + 1), :] = second[edge * i : edge * (i + 1)]
+    for i in range(4):
+        out = dot(g0_ref[step], sec_ref[i]).astype(BF)
+        keep_ref[step, :, wide * i : wide * (i + 1)] = out[:half]
+        send_ref[step, :, wide * i : wide * (i + 1)] = out[half:]
 
 
 def apply_parent(parent, kinds, child_slot, near, far, table, weights, half):
@@ -268,9 +264,9 @@
     scalars = (kinds,) if child_slot is None else (kinds, child_slot)
     arrays = (near, far, table) + tuple(weights)
     expanded = [
-        pltpu.VMEM((edge, terms * edge), BF),
-        pltpu.VMEM((terms * edge, wide), BF),
-        pltpu.VMEM((terms * 2 * edge, wide // 2), BF),
+        pltpu.VMEM((disps, edge, terms * edge), BF),
+        pltpu.VMEM((disps, terms * edge, wide), BF),
+        pltpu.VMEM((disps, terms * 2 * edge, wide // 2), BF),
     ]
     return pl.pallas_call(
         functools.partial(
@@ -285,7 +281,7 @@
             pltpu.VMEM((4 * edge, wide), BF),
             pltpu.VMEM((4, terms * edge, wide), BF),
         ]
-        + expanded * 2,
+        + expanded,
         compiler_params=pltpu.CompilerParams(vmem_limit_bytes=24 * 1024 * 1024),
     )(*scalars, *arrays)
 

time: 83.6 us -> 71.2 us (0.85)
  Pallas kernels: 37.2 us -> 24.7 us
    pallas_call x4, Pallas kernels: 32.6 us -> 20.1 us  [apply_parent(): pl.pallas_call(functools.partial(apply_kernel, half=half, terms=terms, pa...]
  transfers between devices with their start and end apart: 13 -> 13, of which waited for: 9 -> 9; matrix products, arithmetic and copies ran while one was open for 4% -> 5% of each run, Pallas kernels for 30% -> 22%
where the time goes in v5:
time: 71.2 us; the launch traced here: 70.9 us
  Pallas kernels  24.7 us (35%)
  waiting for transfers between devices  23.9 us (34%)
  starting transfers between devices  15.6 us (22%)
  local copies, waits for them, and re-layouts  5.02 us (7%)
  other arithmetic  1.39 us (2%)
    ppermute x13, waiting for transfers between devices, swap(): return lax.ppermute(x, axis, [(i, i ^ mask) for i in range(count)])  23.9 us
    pallas_call x4, Pallas kernels, apply_parent(): pl.pallas_call(functools.partial(apply_kernel, half=half, terms=terms, pa...  20.1 us
    ppermute x13, starting transfers between devices, swap(): return lax.ppermute(x, axis, [(i, i ^ mask) for i in range(count)])  15.6 us
    unnamed x10, local copies, waits for them, and re-layouts  4.07 us
    pallas_call x1, Pallas kernels, pick_blocks(): pl.pallas_call(functools.partial(pick_kernel, parents=parents), in_specs=...  1.65 us
  transfers between devices with their start and end apart: 13, of which 9 were waited for; matrix products, arithmetic and copies ran while one was open for 5% of the time, Pallas kernels for 22%

profile of v5, /device:TPU:0, one launch (start us, length us, event | category | flops | bytes accessed | tf_op | source)
XLA Modules:
  0.0 70.9 jit_solution(9509744966093424820)
XLA Ops:
  0.0 1.7 %copy.9 = bf16[4,8,16,256]{3,2,1,0:T(8,128)(2,1)} copy(bf16[4,8,16,256]{3,1,2,0:T(8,128)(2,1)} %bitcast.27) | data formatting | bytes 524288
  1.7 1.6 %shard_map.73 = bf16[4,4,16,256]{3,2,1,0:T(8,128)(2,1)} custom-call(s32[4,8]{1,0:T(4,128)} %bitcast.20, bf16[32,16,256]{2,1,0:T(8,128)(2,1)} %bitcast.13), custom_call_target="tpu_custom_call" | custom-call | tf_op jit(solution)/shard_map/pallas_call | solution.py:102
  3.3 2.9 %collective-permute-start.1 = (bf16[4,4,16,256]{3,2,1,0:T(8,128)(2,1)}, bf16[4,4,16,256]{3,2,1,0:T(8,128)(2,1)S(1)}, u32[]{:S(2)}, u32[]{:S(2)}) collective-permute-start(bf16[4,4,16,256]{3,2,1,0:T(8,128)(2,1)} %shard_map.73), channel_id=1, source_target_pairs={{0,1},{1,0},{2,3},{3,2},{4,5},{5,4},{6,7},{7,6},{8,9},{9,8},{10,11... | collective-permute-start | bytes 393224 | tf_op jit(solution)/shard_map/ppermute | solution.py:367
  6.3 0.7 broadcast_multiply_fusion
  7.0 0.7 add.27
  7.7 0.0 collective-permute-start
  7.7 1.8 %copy.10 = bf16[4,8,240,128]{3,2,1,0:T(8,128)(2,1)S(1)} copy(bf16[4,8,240,128]{3,1,2,0:T(8,128)(2,1)} %bitcast.26) | data formatting | bytes 3932160
  9.5 0.0 copy-start.3
  9.5 0.0 copy-start
  9.5 0.0 copy-start.1
  9.5 0.0 copy-start.2
  9.5 0.1 slice.refs_3_
  9.6 0.5 copy-done.3
  10.2 0.9 %shard_map.74 = (bf16[32,256]{1,0:T(8,128)(2,1)S(1)}, bf16[32,128]{1,0:T(8,128)(2,1)S(1)}, bf16[128,256]{1,0:T(8,128)(2,1)S(1)}, bf16[32,128]{1,0:T(8,128)(2,1)S...) custom-call(bf16[32,32]{1,0:T(8,128)(2,1)S(1)} %copy-done.3), custom_call_target="tpu_custom_call" | custom-call | tf_op jit(solution)/shard_map/pallas_call | solution.py:84
  11.0 0.2 collective-permute-done
  11.3 0.1 stack.14
  11.3 0.0 collective-permute-done.1.refs_2_
  11.3 0.0 copy-done
  11.4 0.0 copy-done.1
  11.4 0.0 copy-done.2
  11.4 5.1 %shard_map.75 = (bf16[4,16,1024]{2,1,0:T(8,128)(2,1)S(1)}, bf16[4,16,1024]{2,1,0:T(8,128)(2,1)S(1)}) custom-call(s32[4,4]{1,0:T(4,128)S(1)} %copy-done.2, s32[4,8]{1,0:T(4,128)S(1)} %bitcast.21, bf16[32,16,256]{2,1,0:T(8,128)(2,1)S(1)} %bitcast.14, bf16[4,4,16,256]{3,2,1,0:T(8,128)(2,1)S(1)} %collective-permute-done.1.refs_2_, ...), custom_call_target="tpu_custom_call" | custom-call | tf_op jit(solution)/shard_map/pallas_call | solution.py:271
  16.4 1.9 %collective-permute-start.2 = (bf16[4,16,1024]{2,1,0:T(8,128)(2,1)S(1)}, bf16[4,16,1024]{2,1,0:T(8,128)(2,1)S(1)}, u32[]{:S(2)}, u32[]{:S(2)}) collective-permute-start(bf16[4,16,1024]{2,1,0:T(8,128)(2,1)S(1)} %get-tuple-element.44), channel_id=1, source_target_pairs={{0,1},{1,0},{2,3},{3,2},{4,5},{5,4},{6,7},{7,6},{8,9},{9,8},{10,11... | collective-permute-start | bytes 393224 | tf_op jit(solution)/shard_map/ppermute | solution.py:367
  18.3 5.0 %shard_map.76 = (bf16[4,16,1024]{2,1,0:T(8,128)(2,1)S(1)}, bf16[4,16,1024]{2,1,0:T(8,128)(2,1)S(1)}) custom-call(s32[4,4]{1,0:T(4,128)S(1)} %copy-done.2, s32[4,8]{1,0:T(4,128)S(1)} %bitcast.22, bf16[32,16,256]{2,1,0:T(8,128)(2,1)S(1)} %bitcast.15, bf16[4,4,16,256]{3,2,1,0:T(8,128)(2,1)S(1)} %collective-permute-done.1.refs_2_, ...), custom_call_target="tpu_custom_call" | custom-call | tf_op jit(solution)/shard_map/pallas_call | solution.py:271
  23.4 0.2 collective-permute-start.3
  23.6 5.0 %shard_map.77 = (bf16[4,16,1024]{2,1,0:T(8,128)(2,1)S(1)}, bf16[4,16,1024]{2,1,0:T(8,128)(2,1)S(1)}) custom-call(s32[4,4]{1,0:T(4,128)S(1)} %copy-done.2, s32[4,8]{1,0:T(4,128)S(1)} %bitcast.23, bf16[32,16,256]{2,1,0:T(8,128)(2,1)S(1)} %bitcast.16, bf16[4,4,16,256]{3,2,1,0:T(8,128)(2,1)S(1)} %collective-permute-done.1.refs_2_, ...), custom_call_target="tpu_custom_call" | custom-call | tf_op jit(solution)/shard_map/pallas_call | solution.py:271
  28.6 1.9 %collective-permute-start.4 = (bf16[4,16,1024]{2,1,0:T(8,128)(2,1)S(1)}, bf16[4,16,1024]{2,1,0:T(8,128)(2,1)S(1)}, u32[]{:S(2)}, u32[]{:S(2)}) collective-permute-start(bf16[4,16,1024]{2,1,0:T(8,128)(2,1)S(1)} %get-tuple-element.48), channel_id=1, source_target_pairs={{0,1},{1,0},{2,3},{3,2},{4,5},{5,4},{6,7},{7,6},{8,9},{9,8},{10,11... | collective-permute-start | bytes 393224 | tf_op jit(solution)/shard_map/ppermute | solution.py:367
  30.6 5.0 %shard_map.78 = (bf16[4,16,1024]{2,1,0:T(8,128)(2,1)S(1)}, bf16[4,16,1024]{2,1,0:T(8,128)(2,1)S(1)}) custom-call(s32[4,4]{1,0:T(4,128)S(1)} %copy-done.2, s32[4,8]{1,0:T(4,128)S(1)} %bitcast.24, bf16[32,16,256]{2,1,0:T(8,128)(2,1)S(1)} %bitcast.17, bf16[4,4,16,256]{3,2,1,0:T(8,128)(2,1)S(1)} %collective-permute-done.1.refs_2_, ...), custom_call_target="tpu_custom_call" | custom-call | tf_op jit(solution)/shard_map/pallas_call | solution.py:271
  35.6 0.2 collective-permute-start.5
  35.9 0.0 collective-permute-done.2.refs_1_
  35.9 0.0 collective-permute-done.3.refs_3_
  35.9 0.0 collective-permute-done.4.refs_5_
  35.9 4.7 %collective-permute-done.5.refs_7_ = bf16[4,16,1024]{2,1,0:T(8,128)(2,1)S(1)} collective-permute-done((bf16[4,16,1024]{2,1,0:T(8,128)(2,1)S(1)}, bf16[4,16,1024]{2,1,0:T(8,128)(2,1)S(1)}, u32[]{:S(2)}, u32[]{:S(2)}) %collective-permute-start.5) | collective-permute-done | bytes 131104 | tf_op jit(solution)/shard_map/ppermute | solution.py:367
  40.6 1.3 %shard_map.79 = (bf16[32,16,1024]{2,1,0:T(8,128)(2,1)S(1)}, bf16[32,16,1024]{2,1,0:T(8,128)(2,1)S(1)}) custom-call(s32[32]{0:T(128)S(1)} %fusion.slot_ref, bf16[4,16,1024]{2,1,0:T(8,128)(2,1)S(1)} %get-tuple-element.43.refs_0_, bf16[4,16,1024]{2,1,0:T(8,128)(2,1)S(1)} %collective-permute-done.2.refs_1_, bf16[4,16,1024]{2,1,0:T(8,128)(2,1)S(1)} %get-tuple-element.45.refs_2_, ...), custom_call_target="tpu_custom_call" | custom-call | tf_op jit(solution)/shard_map/pallas_call | solution.py:305
  41.9 0.1 collective-permute-start.6
  42.0 2.6 %collective-permute-done.6 = bf16[32,16,1024]{2,1,0:T(8,128)(2,1)S(1)} collective-permute-done((bf16[32,16,1024]{2,1,0:T(8,128)(2,1)S(1)}, bf16[32,16,1024]{2,1,0:T(8,128)(2,1)S(1)}, u32[]{:S(2)}, u32[]{:S(2)}) %collective-permute-start.6) | collective-permute-done | bytes 1048608 | tf_op jit(solution)/shard_map/ppermute | solution.py:367
  44.6 0.3 shard_map.80
  44.9 1.6 %collective-permute-start.7 = (bf16[4,4,16,512]{3,2,1,0:T(8,128)(2,1)S(1)}, bf16[4,4,16,512]{3,2,1,0:T(8,128)(2,1)S(1)}, u32[]{:S(2)}, u32[]{:S(2)}) collective-permute-start(bf16[4,4,16,512]{3,2,1,0:T(8,128)(2,1)S(1)} %get-tuple-element.55), channel_id=1, source_target_pairs={{0,4},{2,6},{4,0},{6,2},{8,12},{10,14},{12,8},{14,10},{16,20},{18,... | collective-permute-start | bytes 786440 | tf_op jit(solution)/shard_map/ppermute | solution.py:367
  46.5 1.6 %collective-permute-start.8 = (bf16[4,4,16,512]{3,2,1,0:T(8,128)(2,1)S(1)}, bf16[4,4,16,512]{3,2,1,0:T(8,128)(2,1)S(1)}, u32[]{:S(2)}, u32[]{:S(2)}) collective-permute-start(bf16[4,4,16,512]{3,2,1,0:T(8,128)(2,1)S(1)} %get-tuple-element.56), channel_id=1, source_target_pairs={{0,8},{2,10},{4,12},{6,14},{8,0},{10,2},{12,4},{14,6},{16,24},{18,... | collective-permute-start | bytes 786440 | tf_op jit(solution)/shard_map/ppermute | solution.py:367
  48.0 5.2 %collective-permute-done.7.refs_2_ = bf16[4,4,16,512]{3,2,1,0:T(8,128)(2,1)S(1)} collective-permute-done((bf16[4,4,16,512]{3,2,1,0:T(8,128)(2,1)S(1)}, bf16[4,4,16,512]{3,2,1,0:T(8,128)(2,1)S(1)}, u32[]{:S(2)}, u32[]{:S(2)}) %collective-permute-start.7) | collective-permute-done | bytes 262176 | tf_op jit(solution)/shard_map/ppermute | solution.py:367
  53.3 1.2 %collective-permute-done.8.refs_3_ = bf16[4,4,16,512]{3,2,1,0:T(8,128)(2,1)S(1)} collective-permute-done((bf16[4,4,16,512]{3,2,1,0:T(8,128)(2,1)S(1)}, bf16[4,4,16,512]{3,2,1,0:T(8,128)(2,1)S(1)}, u32[]{:S(2)}, u32[]{:S(2)}) %collective-permute-start.8) | collective-permute-done | bytes 262176 | tf_op jit(solution)/shard_map/ppermute | solution.py:367
  54.5 0.1 shard_map.81
  54.7 1.6 %collective-permute-start.9 = (bf16[2,4,16,512]{3,2,1,0:T(8,128)(2,1)S(1)}, bf16[2,4,16,512]{3,2,1,0:T(8,128)(2,1)S(1)}, u32[]{:S(2)}, u32[]{:S(2)}) collective-permute-start(bf16[2,4,16,512]{3,2,1,0:T(8,128)(2,1)S(1)} %get-tuple-element.59), channel_id=1, source_target_pairs={{0,8},{2,10},{4,12},{6,14},{8,0},{10,2},{12,4},{14,6},{16,24},{18,... | collective-permute-start | bytes 393224 | tf_op jit(solution)/shard_map/ppermute | solution.py:367
  56.3 0.5 collective-permute-start.10
  56.8 2.9 %collective-permute-done.9.refs_2_ = bf16[2,4,16,512]{3,2,1,0:T(8,128)(2,1)S(1)} collective-permute-done((bf16[2,4,16,512]{3,2,1,0:T(8,128)(2,1)S(1)}, bf16[2,4,16,512]{3,2,1,0:T(8,128)(2,1)S(1)}, u32[]{:S(2)}, u32[]{:S(2)}) %collective-permute-start.9) | collective-permute-done | bytes 131104 | tf_op jit(solution)/shard_map/ppermute | solution.py:367
  59.7 1.6 %collective-permute-done.10.refs_3_ = bf16[2,4,16,512]{3,2,1,0:T(8,128)(2,1)S(1)} collective-permute-done((bf16[2,4,16,512]{3,2,1,0:T(8,128)(2,1)S(1)}, bf16[2,4,16,512]{3,2,1,0:T(8,128)(2,1)S(1)}, u32[]{:S(2)}, u32[]{:S(2)}) %collective-permute-start.10) | collective-permute-done | bytes 131104 | tf_op jit(solution)/shard_map/ppermute | solution.py:367
  61.3 0.1 shard_map.82
  61.3 2.7 %collective-permute-start.11 = (bf16[1,4,16,512]{3,2,1,0:T(8,128)(2,1)S(1)}, bf16[1,4,16,512]{3,2,1,0:T(8,128)(2,1)S(1)}, u32[]{:S(2)}, u32[]{:S(2)}) collective-permute-start(bf16[1,4,16,512]{3,2,1,0:T(8,128)(2,1)S(1)} %get-tuple-element.63), channel_id=1, source_target_pairs={{0,16},{2,18},{4,20},{6,22},{8,24},{10,26},{12,28},{14,30},{16,0},... | collective-permute-start | bytes 196616 | tf_op jit(solution)/shard_map/ppermute | solution.py:367
  64.0 0.3 collective-permute-start.12
  64.3 3.1 %collective-permute-done.11.refs_2_ = bf16[1,4,16,512]{3,2,1,0:T(8,128)(2,1)S(1)} collective-permute-done((bf16[1,4,16,512]{3,2,1,0:T(8,128)(2,1)S(1)}, bf16[1,4,16,512]{3,2,1,0:T(8,128)(2,1)S(1)}, u32[]{:S(2)}, u32[]{:S(2)}) %collective-permute-start.11) | collective-permute-done | bytes 65568 | tf_op jit(solution)/shard_map/ppermute | solution.py:367
  67.5 2.3 %collective-permute-done.12.refs_3_ = bf16[1,4,16,512]{3,2,1,0:T(8,128)(2,1)S(1)} collective-permute-done((bf16[1,4,16,512]{3,2,1,0:T(8,128)(2,1)S(1)}, bf16[1,4,16,512]{3,2,1,0:T(8,128)(2,1)S(1)}, u32[]{:S(2)}, u32[]{:S(2)}) %collective-permute-start.12) | collective-permute-done | bytes 65568 | tf_op jit(solution)/shard_map/ppermute | solution.py:367
  69.7 0.4 shard_map.83
  70.2 0.7 %reshape.24 = bf16[4,4,4096]{2,1,0:T(4,128)(2,1)} reshape(bf16[4,4,16,256]{3,2,1,0:T(8,128)(2,1)S(1)} %shard_map.83) | data formatting | bytes 262144 | tf_op jit(solution)/shard_map/reshape | solution.py:436
  (3 shorter events, 0.0 us)
Async XLA Ops:
  3.3 8.0 %collective-permute-start.1 = (bf16[4,4,16,256]{3,2,1,0:T(8,128)(2,1)}, bf16[4,4,16,256]{3,2,1,0:T(8,128)(2,1)S(1)}, u32[]{:S(2)}, u32[]{:S(2)}) collective-permute-start(bf16[4,4,16,256]{3,2,1,0:T(8,128)(2,1)} %shard_map.73), channel_id=1, source_target_pairs={{0,1},{1,0},{2,3},{3,2},{4,5},{5,4},{6,7},{7,6},{8,9},{9,8},{10,11... | collective-permute-start | bytes 393224 | tf_op jit(solution)/shard_map/ppermute | solution.py:367
  7.7 3.6 %collective-permute-start = (s32[4,4]{1,0:T(4,128)S(1)}, s32[4,4]{1,0:T(4,128)S(1)}, u32[]{:S(2)}, u32[]{:S(2)}) collective-permute-start(s32[4,4]{1,0:T(4,128)S(1)} %add.27), channel_id=1, source_target_pairs={{0,1},{1,0},{2,3},{3,2},{4,5},{5,4},{6,7},{7,6},{8,9},{9,8},{10,11... | collective-permute-start | bytes 200 | tf_op jit(solution)/shard_map/ppermute | solution.py:367
  9.5 0.7 copy-start.3
  9.5 1.9 %copy-start = (bf16[4,8,16,256]{3,2,1,0:T(8,128)(2,1)S(1)}, bf16[4,8,16,256]{3,2,1,0:T(8,128)(2,1)}, u32[]{:S(2)}) copy-start(bf16[4,8,16,256]{3,2,1,0:T(8,128)(2,1)} %copy.9) | copy-start | bytes 786436
  9.5 1.9 %copy-start.1 = (s32[8,4]{0,1:T(4,128)S(1)}, s32[8,4]{0,1:T(4,128)}, u32[]{:S(2)}) copy-start(s32[8,4]{0,1:T(4,128)} %param.8) | copy-start | bytes 388
  9.5 1.9 %copy-start.2 = (s32[4,4]{1,0:T(4,128)S(1)}, s32[4,4]{1,0:T(4,128)}, u32[]{:S(2)}) copy-start(s32[4,4]{1,0:T(4,128)} %kind_ref.7) | copy-start | bytes 196
  16.4 19.4 %collective-permute-start.2 = (bf16[4,16,1024]{2,1,0:T(8,128)(2,1)S(1)}, bf16[4,16,1024]{2,1,0:T(8,128)(2,1)S(1)}, u32[]{:S(2)}, u32[]{:S(2)}) collective-permute-start(bf16[4,16,1024]{2,1,0:T(8,128)(2,1)S(1)} %get-tuple-element.44), channel_id=1, source_target_pairs={{0,1},{1,0},{2,3},{3,2},{4,5},{5,4},{6,7},{7,6},{8,9},{9,8},{10,11... | collective-permute-start | bytes 393224 | tf_op jit(solution)/shard_map/ppermute | solution.py:367
  23.4 12.5 %collective-permute-start.3 = (bf16[4,16,1024]{2,1,0:T(8,128)(2,1)S(1)}, bf16[4,16,1024]{2,1,0:T(8,128)(2,1)S(1)}, u32[]{:S(2)}, u32[]{:S(2)}) collective-permute-start(bf16[4,16,1024]{2,1,0:T(8,128)(2,1)S(1)} %get-tuple-element.46), channel_id=1, source_target_pairs={{0,1},{1,0},{2,3},{3,2},{4,5},{5,4},{6,7},{7,6},{8,9},{9,8},{10,11... | collective-permute-start | bytes 393224 | tf_op jit(solution)/shard_map/ppermute | solution.py:367
  28.6 7.2 %collective-permute-start.4 = (bf16[4,16,1024]{2,1,0:T(8,128)(2,1)S(1)}, bf16[4,16,1024]{2,1,0:T(8,128)(2,1)S(1)}, u32[]{:S(2)}, u32[]{:S(2)}) collective-permute-start(bf16[4,16,1024]{2,1,0:T(8,128)(2,1)S(1)} %get-tuple-element.48), channel_id=1, source_target_pairs={{0,1},{1,0},{2,3},{3,2},{4,5},{5,4},{6,7},{7,6},{8,9},{9,8},{10,11... | collective-permute-start | bytes 393224 | tf_op jit(solution)/shard_map/ppermute | solution.py:367
  35.6 5.0 %collective-permute-start.5 = (bf16[4,16,1024]{2,1,0:T(8,128)(2,1)S(1)}, bf16[4,16,1024]{2,1,0:T(8,128)(2,1)S(1)}, u32[]{:S(2)}, u32[]{:S(2)}) collective-permute-start(bf16[4,16,1024]{2,1,0:T(8,128)(2,1)S(1)} %get-tuple-element.50), channel_id=1, source_target_pairs={{0,1},{1,0},{2,3},{3,2},{4,5},{5,4},{6,7},{7,6},{8,9},{9,8},{10,11... | collective-permute-start | bytes 393224 | tf_op jit(solution)/shard_map/ppermute | solution.py:367
  41.9 2.7 %collective-permute-start.6 = (bf16[32,16,1024]{2,1,0:T(8,128)(2,1)S(1)}, bf16[32,16,1024]{2,1,0:T(8,128)(2,1)S(1)}, u32[]{:S(2)}, u32[]{:S(2)}) collective-permute-start(bf16[32,16,1024]{2,1,0:T(8,128)(2,1)S(1)} %get-tuple-element.52), channel_id=1, source_target_pairs={{0,2},{2,0},{4,6},{6,4},{8,10},{10,8},{12,14},{14,12},{16,18},{18,... | collective-permute-start | bytes 3145736 | tf_op jit(solution)/shard_map/ppermute | solution.py:367
  44.9 8.4 %collective-permute-start.7 = (bf16[4,4,16,512]{3,2,1,0:T(8,128)(2,1)S(1)}, bf16[4,4,16,512]{3,2,1,0:T(8,128)(2,1)S(1)}, u32[]{:S(2)}, u32[]{:S(2)}) collective-permute-start(bf16[4,4,16,512]{3,2,1,0:T(8,128)(2,1)S(1)} %get-tuple-element.55), channel_id=1, source_target_pairs={{0,4},{2,6},{4,0},{6,2},{8,12},{10,14},{12,8},{14,10},{16,20},{18,... | collective-permute-start | bytes 786440 | tf_op jit(solution)/shard_map/ppermute | solution.py:367
  46.5 8.1 %collective-permute-start.8 = (bf16[4,4,16,512]{3,2,1,0:T(8,128)(2,1)S(1)}, bf16[4,4,16,512]{3,2,1,0:T(8,128)(2,1)S(1)}, u32[]{:S(2)}, u32[]{:S(2)}) collective-permute-start(bf16[4,4,16,512]{3,2,1,0:T(8,128)(2,1)S(1)} %get-tuple-element.56), channel_id=1, source_target_pairs={{0,8},{2,10},{4,12},{6,14},{8,0},{10,2},{12,4},{14,6},{16,24},{18,... | collective-permute-start | bytes 786440 | tf_op jit(solution)/shard_map/ppermute | solution.py:367
  54.7 5.0 %collective-permute-start.9 = (bf16[2,4,16,512]{3,2,1,0:T(8,128)(2,1)S(1)}, bf16[2,4,16,512]{3,2,1,0:T(8,128)(2,1)S(1)}, u32[]{:S(2)}, u32[]{:S(2)}) collective-permute-start(bf16[2,4,16,512]{3,2,1,0:T(8,128)(2,1)S(1)} %get-tuple-element.59), channel_id=1, source_target_pairs={{0,8},{2,10},{4,12},{6,14},{8,0},{10,2},{12,4},{14,6},{16,24},{18,... | collective-permute-start | bytes 393224 | tf_op jit(solution)/shard_map/ppermute | solution.py:367
  56.3 5.0 %collective-permute-start.10 = (bf16[2,4,16,512]{3,2,1,0:T(8,128)(2,1)S(1)}, bf16[2,4,16,512]{3,2,1,0:T(8,128)(2,1)S(1)}, u32[]{:S(2)}, u32[]{:S(2)}) collective-permute-start(bf16[2,4,16,512]{3,2,1,0:T(8,128)(2,1)S(1)} %get-tuple-element.60), channel_id=1, source_target_pairs={{0,4},{2,6},{4,0},{6,2},{8,12},{10,14},{12,8},{14,10},{16,20},{18,... | collective-permute-start | bytes 393224 | tf_op jit(solution)/shard_map/ppermute | solution.py:367
  61.3 6.1 %collective-permute-start.11 = (bf16[1,4,16,512]{3,2,1,0:T(8,128)(2,1)S(1)}, bf16[1,4,16,512]{3,2,1,0:T(8,128)(2,1)S(1)}, u32[]{:S(2)}, u32[]{:S(2)}) collective-permute-start(bf16[1,4,16,512]{3,2,1,0:T(8,128)(2,1)S(1)} %get-tuple-element.63), channel_id=1, source_target_pairs={{0,16},{2,18},{4,20},{6,22},{8,24},{10,26},{12,28},{14,30},{16,0},... | collective-permute-start | bytes 196616 | tf_op jit(solution)/shard_map/ppermute | solution.py:367
  64.0 5.7 %collective-permute-start.12 = (bf16[1,4,16,512]{3,2,1,0:T(8,128)(2,1)S(1)}, bf16[1,4,16,512]{3,2,1,0:T(8,128)(2,1)S(1)}, u32[]{:S(2)}, u32[]{:S(2)}) collective-permute-start(bf16[1,4,16,512]{3,2,1,0:T(8,128)(2,1)S(1)} %get-tuple-element.64), channel_id=1, source_target_pairs={{0,16},{2,18},{4,20},{6,22},{8,24},{10,26},{12,28},{14,30},{16,0},... | collective-permute-start | bytes 196616 | tf_op jit(solution)/shard_map/ppermute | solution.py:367

commit v6 on v5

--- a/solution.py
+++ b/solution.py
@@ -137,7 +137,7 @@
 
 
 def apply_kernel(
-    kind_ref, *refs, half, terms, parent, picked,
+    kind_ref, *refs, half, terms, first_parent, picked,
 ):
     if picked:
         slot_ref, refs = refs[0], refs[1:]
@@ -151,7 +151,9 @@
     wide = edge * low
     quarter = wide // 4
     rows = terms * low
-    step = pl.program_id(0)
+    step = pl.program_id(1)
+    parent = first_parent + pl.program_id(0)
+    item = pl.program_id(0) * pl.num_programs(1) + step
 
     def expand(kinds):
         g0_ref, w1e_ref, w2e_ref = expanded
@@ -251,16 +253,16 @@
             sec_ref[i, edge * t : edge * (t + 1), :] = second[edge * i : edge * (i + 1)]
     for i in range(4):
         out = dot(g0_ref[step], sec_ref[i]).astype(BF)
-        keep_ref[step, :, wide * i : wide * (i + 1)] = out[:half]
-        send_ref[step, :, wide * i : wide * (i + 1)] = out[half:]
-
-
-def apply_parent(parent, kinds, child_slot, near, far, table, weights, half):
+        keep_ref[item, :, wide * i : wide * (i + 1)] = out[:half]
+        send_ref[item, :, wide * i : wide * (i + 1)] = out[half:]
+
+
+def apply_parents(first_parent, count, kinds, child_slot, near, far, table, weights, half):
     edge = 2 * half
     wide = edge * half // 2
     terms = table.shape[1] // (3 * edge // 4)
     disps = kinds.shape[1]
-    shape = jax.ShapeDtypeStruct((disps, half, 4 * wide), BF)
+    shape = jax.ShapeDtypeStruct((count * disps, half, 4 * wide), BF)
     scalars = (kinds,) if child_slot is None else (kinds, child_slot)
     arrays = (near, far, table) + tuple(weights)
     expanded = [
@@ -270,9 +272,13 @@
     ]
     return pl.pallas_call(
         functools.partial(
-            apply_kernel, half=half, terms=terms, parent=parent, picked=child_slot is not None
+            apply_kernel,
+            half=half,
+            terms=terms,
+            first_parent=first_parent,
+            picked=child_slot is not None,
         ),
-        grid=(disps,),
+        grid=(count, disps),
         in_specs=[pl.BlockSpec(memory_space=pltpu.SMEM)] * len(scalars)
         + [pl.BlockSpec(memory_space=pltpu.VMEM)] * len(arrays),
         out_specs=[pl.BlockSpec(memory_space=pltpu.VMEM)] * 2,
@@ -286,78 +292,115 @@
     )(*scalars, *arrays)
 
 
-def sum_kernel(slot_ref, *refs, rows):
+def target(goal_ref, item, nodes):
+    goal = goal_ref[item]
+    offset = jnp.bitwise_xor(goal // nodes, lax.axis_index("leaf"))
+    return offset % 2, offset // 2 * nodes + goal % nodes
+
+
+def sum_kernel(goal_ref, *refs, sources, nodes):
     row_refs, (even_ref, odd_ref, total_ref) = refs[:-3], refs[-3:]
     total_ref[...] = jnp.zeros_like(total_ref)
-    for i in range(len(row_refs)):
-        for j in range(rows):
-            slot = slot_ref[i * rows + j]
-            total_ref[slot] = total_ref[slot] + row_refs[i][j].astype(F32)
     count = even_ref.shape[0]
+    for row_ref, items in zip(row_refs, sources):
+        for i, item in enumerate(items):
+            parity, slot = target(goal_ref, item, nodes)
+            slot = parity * count + slot
+            total_ref[slot] = total_ref[slot] + row_ref[i].astype(F32)
     even_ref[...] = total_ref[:count].astype(BF)
     odd_ref[...] = total_ref[count:].astype(BF)
 
 
-def sum_rows(slots, arrays, slot_count):
-    rows = arrays[0].shape[0]
+def sum_rows(goals, arrays, sources, nodes, leaf_count):
     tail = arrays[0].shape[1:]
+    slot_count = leaf_count * nodes
     shape = jax.ShapeDtypeStruct((slot_count // 2,) + tail, BF)
     return pl.pallas_call(
-        functools.partial(sum_kernel, rows=rows),
+        functools.partial(sum_kernel, sources=sources, nodes=nodes),
         in_specs=[pl.BlockSpec(memory_space=pltpu.SMEM)]
         + [pl.BlockSpec(memory_space=pltpu.VMEM)] * len(arrays),
         out_specs=[pl.BlockSpec(memory_space=pltpu.VMEM)] * 2,
         out_shape=[shape, shape],
         scratch_shapes=[pltpu.VMEM((slot_count,) + tail, F32)],
         compiler_params=pltpu.CompilerParams(vmem_limit_bytes=24 * 1024 * 1024),
-    )(slots, *arrays)
-
-
-def combine_kernel(*refs, bits, lanes, inputs, last):
-    kept, arrived, outs = refs[:inputs], refs[inputs : 2 * inputs], refs[2 * inputs :]
+    )(goals, *arrays)
+
+
+def place(offset, bit):
+    return (offset >> (bit + 1) << bit) | (offset & ((1 << bit) - 1))
+
+
+def first_kernel(even_ref, odd_ref, *outs, bits):
+    lanes = outs[0].shape[-1]
     for i, bit in enumerate(bits):
-        source, start = (i, 0) if inputs == len(bits) else (0, lanes * i)
-        for r in range(arrived[source].shape[0]):
-            total = kept[source][r, :, :, start : start + lanes].astype(F32)
-            total = total + arrived[source][r, :, :, start : start + lanes].astype(F32)
-            total = total.astype(BF)
-            if not last:
-                place = (r >> (bit + 1) << bit) | (r & ((1 << bit) - 1))
-                outs[2 * i + (r >> bit & 1)][place] = total
-            elif outs[0].shape[1] == 4:
-                wide = lanes // 2
-                half = wide // 16
-                order = one_hot(
-                    (wide, wide),
-                    lambda x: x % (2 * half) // half * (wide // 2) + x // (2 * half) * half + x % half,
-                    lambda x: x,
-                )
-                for n in range(total.shape[0]):
-                    for c in range(2):
-                        moved = exact(total[n, :, wide * c : wide * (c + 1)], order)
-                        to = wide // 2 * c
-                        for bit in range(2):
-                            outs[0][n, 2 * i + bit, :, to : to + wide // 2] = moved[
-                                :, wide // 2 * bit : wide // 2 * (bit + 1)
-                            ]
-            else:
-                outs[0][:, 0, :, lanes * i : lanes * (i + 1)] = total
-
-
-def combine(kept, arrived, bits, out=None):
-    lanes = arrived[0].shape[-1] * len(arrived) // len(bits)
-    if out is None:
-        shape = (arrived[0].shape[0] // 2,) + arrived[0].shape[1:3] + (lanes,)
-        shapes = [shape] * (2 * len(bits))
-    else:
-        shapes = [out]
-    return pl.pallas_call(
-        functools.partial(
-            combine_kernel, bits=bits, lanes=lanes, inputs=len(kept), last=out is not None
-        ),
-        in_specs=[pl.BlockSpec(memory_space=pltpu.VMEM)] * (2 * len(kept)),
-        out_specs=[pl.BlockSpec(memory_space=pltpu.VMEM)] * len(shapes),
-        out_shape=[jax.ShapeDtypeStruct(shape, BF) for shape in shapes],
+        for r in range(even_ref.shape[0]):
+            here = (slice(None), slice(None), slice(lanes * i, lanes * (i + 1)))
+            total = even_ref[(r,) + here].astype(F32) + odd_ref[(r,) + here].astype(F32)
+            outs[2 * i + (r >> bit & 1)][place(r, bit)] = total.astype(BF)
+
+
+def first_combine(even, odd, bits):
+    offsets, nodes, rows, lanes = even.shape
+    shape = jax.ShapeDtypeStruct((offsets // 2, nodes, rows, lanes // 2), BF)
+    return pl.pallas_call(
+        functools.partial(first_kernel, bits=bits),
+        in_specs=[pl.BlockSpec(memory_space=pltpu.VMEM)] * 2,
+        out_specs=[pl.BlockSpec(memory_space=pltpu.VMEM)] * 4,
+        out_shape=[shape] * 4,
+        compiler_params=pltpu.CompilerParams(vmem_limit_bytes=24 * 1024 * 1024),
+    )(even, odd)
+
+
+def combine_kernel(kept_ref, arrived_ref, keep_ref, send_ref, *, bit):
+    for r in range(kept_ref.shape[0]):
+        total = (kept_ref[r].astype(F32) + arrived_ref[r].astype(F32)).astype(BF)
+        out_ref = send_ref if r >> bit & 1 else keep_ref
+        out_ref[place(r, bit)] = total
+
+
+def combine(kept, arrived, bit):
+    shape = jax.ShapeDtypeStruct((kept.shape[0] // 2,) + kept.shape[1:], BF)
+    return pl.pallas_call(
+        functools.partial(combine_kernel, bit=bit),
+        in_specs=[pl.BlockSpec(memory_space=pltpu.VMEM)] * 2,
+        out_specs=[pl.BlockSpec(memory_space=pltpu.VMEM)] * 2,
+        out_shape=[shape, shape],
+        compiler_params=pltpu.CompilerParams(vmem_limit_bytes=24 * 1024 * 1024),
+    )(kept, arrived)
+
+
+def last_kernel(kept0_ref, kept1_ref, arrived0_ref, arrived1_ref, out_ref):
+    for i, (kept_ref, arrived_ref) in enumerate(
+        ((kept0_ref, arrived0_ref), (kept1_ref, arrived1_ref))
+    ):
+        lanes = kept_ref.shape[-1]
+        total = (kept_ref[0].astype(F32) + arrived_ref[0].astype(F32)).astype(BF)
+        if out_ref.shape[1] != 4:
+            out_ref[:, 0, :, lanes * i : lanes * (i + 1)] = total
+            continue
+        wide = lanes // 2
+        half = wide // 16
+        order = one_hot(
+            (wide, wide),
+            lambda x: x % (2 * half) // half * (wide // 2) + x // (2 * half) * half + x % half,
+            lambda x: x,
+        )
+        for n in range(total.shape[0]):
+            for c in range(2):
+                moved = exact(total[n, :, wide * c : wide * (c + 1)], order)
+                to = wide // 2 * c
+                for bit in range(2):
+                    out_ref[n, 2 * i + bit, :, to : to + wide // 2] = moved[
+                        :, wide // 2 * bit : wide // 2 * (bit + 1)
+                    ]
+
+
+def last_combine(kept, arrived, shape):
+    return pl.pallas_call(
+        last_kernel,
+        in_specs=[pl.BlockSpec(memory_space=pltpu.VMEM)] * 4,
+        out_specs=pl.BlockSpec(memory_space=pltpu.VMEM),
+        out_shape=jax.ShapeDtypeStruct(shape, BF),
         compiler_params=pltpu.CompilerParams(vmem_limit_bytes=24 * 1024 * 1024),
     )(*kept, *arrived)
 
@@ -370,7 +413,6 @@
 def local(children, child_slot, two_scale, factors, disp_kind, target_leaf, target_node):
     oct_count = lax.axis_size("oct")
     leaf_count = lax.axis_size("leaf")
-    my_leaf = lax.axis_index("leaf")
     edge = two_scale.shape[0]
     half = edge // 2
     held = child_slot.shape[1]
@@ -389,51 +431,62 @@
         near, far = arrived[:, 0], arrived[:, 1]
         near_slot = None
 
-    nodes = 2 * oct_count
-    goal = target_leaf.reshape(parents, disps) * nodes + target_node
-    if paired:
-        goals = jnp.stack([goal, swap(goal, "oct", 1)], axis=1)
-    else:
-        goals = lax.all_gather(goal, "oct").transpose(1, 0, 2)
-    leaf_off = jnp.bitwise_xor(goals // nodes, my_leaf)
-    slots = ((leaf_off % 2) * (leaf_count // 2) + leaf_off // 2) * nodes + goals % nodes
-
     table = factors.reshape(factors.shape[0], -1, 4 * edge)
     weights = make_weights(two_scale, paired)
 
-    arrays = []
-    for parent in range(parents):
-        kept, sent = apply_parent(
-            parent, disp_kind, near_slot, near, far, table, weights, half
+    arrays, sources = [], []
+    done, counts = 0, [max(1, parents - 2)] + [1] * min(2, parents - 1)
+    for count in counts:
+        kept, sent = apply_parents(
+            done, count, disp_kind, near_slot, near, far, table, weights, half
         )
+        if done == 0:
+            target_leaf, target_node, kept = lax.optimization_barrier(
+                (target_leaf, target_node, kept)
+            )
+            nodes = 2 * oct_count
+            goal = (target_leaf.reshape(parents, disps) * nodes + target_node).reshape(-1)
+            if paired:
+                goals = jnp.concatenate([goal, swap(goal, "oct", 1)])
+            else:
+                goals = lax.all_gather(goal, "oct", tiled=True)
+        items = [done * disps + i for i in range(count * disps)]
         if paired:
             arrays += [kept, swap(sent, "oct", 1)]
+            sources += [items, [goal.size + item for item in items]]
         else:
-            rows = jnp.stack([kept, sent], axis=1).reshape(disps, 2, half, 2, half, 2, half)
+            rows = jnp.stack([kept, sent], axis=1).reshape(-1, 2, half, 2, half, 2, half)
             rows = rows.transpose(1, 3, 5, 0, 2, 4, 6)
-            rows = rows.reshape(oct_count, held, disps, half, half * half)
+            rows = rows.reshape(oct_count, held, -1, half, half * half)
             rows = rows.transpose(0, 2, 1, 3, 4)
             rows = lax.all_to_all(rows, "oct", split_axis=0, concat_axis=0, tiled=True)
-            arrays += [rows.reshape(oct_count * disps, held * half, half * half)]
-
-    even, odd = sum_rows(slots.reshape(-1), arrays, leaf_count * nodes)
+            arrays += [rows.reshape(-1, held * half, half * half)]
+            sources += [[goal.size * o + item for o in range(oct_count) for item in items]]
+        done += count
+
+    even, odd = sum_rows(goals, arrays, sources, nodes, leaf_count)
     shape = (leaf_count // 2, nodes) + even.shape[1:]
     even = even.reshape(shape)
     odd = swap(odd, "leaf", 1).reshape(shape)
     masks = [1 << i for i in range(1, (leaf_count - 1).bit_length())]
-    orders = [masks, masks[1::-1] + masks[2:]]
-    left = [list(masks), list(masks)]
-    kept, arrived = [even], [odd]
-    for step in range(len(masks)):
-        bits = [left[i].index(orders[i][step]) for i in range(2)]
-        parts = combine(kept, arrived, bits)
-        kept = [parts[0], parts[2]]
-        arrived = [swap(parts[2 * i + 1], "leaf", orders[i][step]) for i in range(2)]
-        for i in range(2):
-            left[i].remove(orders[i][step])
-    tail = (nodes, held, half, half * half) if paired else (nodes, 1) + shape[2:]
-    (out,) = combine(kept, arrived, (0, 0), tail)
-    return out.reshape(nodes, held, -1)
+    orders = [masks[1::-1] + masks[2:], masks]
+    parts = first_combine(even, odd, [masks.index(order[0]) for order in orders])
+    kept, arrived = [], []
+    for i in range(2):
+        left = list(masks)
+        left.remove(orders[i][0])
+        keep, come = parts[2 * i], swap(parts[2 * i + 1], "leaf", orders[i][0])
+        for mask in orders[i][1:]:
+            keep, send = combine(keep, come, left.index(mask))
+            left.remove(mask)
+            come = swap(send, "leaf", mask)
+        kept.append(keep)
+        arrived.append(come)
+    if paired:
+        shape = (nodes, held, half, half * half)
+    else:
+        shape = (nodes, 1) + shape[2:]
+    return last_combine(kept, arrived, shape).reshape(nodes, held, -1)
 
 
 def solution(mesh):

time: 71.2 us -> 64.6 us (0.907)
  waiting for transfers between devices: 23.9 us -> 16.1 us
  starting transfers between devices: 15.6 us -> 18.6 us
  other arithmetic: 1.39 us -> 0.08 us
    ppermute x13 -> x12, waiting for transfers between devices: 23.9 us -> 16.1 us  [swap(): return lax.ppermute(x, axis, [(i, i ^ mask) for i in range(count)])]
    ppermute x13 -> x12, starting transfers between devices: 15.6 us -> 18.6 us  [swap(): return lax.ppermute(x, axis, [(i, i ^ mask) for i in range(count)])]
    pallas_call x9 -> x10, Pallas kernels: 22.2 us -> 21.8 us  [the longest x3 19.6 us: apply_parents(): pl.pallas_call(functools.partial(apply_kernel, half=half, terms=terms, fi...]
    unnamed x10 -> x14, local copies, waits for them, and re-layouts: 4.07 us -> 4.07 us
  transfers between devices with their start and end apart: 13 -> 12, of which waited for: 9 -> 7; matrix products, arithmetic and copies ran while one was open for 5% -> 3% of each run, Pallas kernels for 22% -> 17%
where the time goes in v6:
time: 64.6 us; the launch traced here: 64.4 us
  Pallas kernels  24.3 us (38%)
  starting transfers between devices  18.6 us (29%)
  waiting for transfers between devices  16.1 us (25%)
  local copies, waits for them, and re-layouts  5.01 us (8%)
    pallas_call x3, Pallas kernels, apply_parents(): pl.pallas_call(functools.partial(apply_kernel, half=half, terms=terms, fi...  19.6 us
    ppermute x12, starting transfers between devices, swap(): return lax.ppermute(x, axis, [(i, i ^ mask) for i in range(count)])  18.6 us
    ppermute x12, waiting for transfers between devices, swap(): return lax.ppermute(x, axis, [(i, i ^ mask) for i in range(count)])  16.1 us
    unnamed x14, local copies, waits for them, and re-layouts  4.07 us
    pallas_call x1, Pallas kernels, pick_blocks(): pl.pallas_call(functools.partial(pick_kernel, parents=parents), in_specs=...  1.65 us
    pallas_call x1, Pallas kernels, sum_rows(): pl.pallas_call(functools.partial(sum_kernel, sources=sources, nodes=nodes...  1.38 us
  transfers between devices with their start and end apart: 12, of which 7 were waited for; matrix products, arithmetic and copies ran while one was open for 3% of the time, Pallas kernels for 17%

profile of v6, /device:TPU:0, one launch (start us, length us, event | category | flops | bytes accessed | tf_op | source)
XLA Modules:
  0.0 64.4 jit_solution(6148724965309203585)
XLA Ops:
  0.0 1.7 %copy.8 = bf16[4,8,16,256]{3,2,1,0:T(8,128)(2,1)} copy(bf16[4,8,16,256]{3,1,2,0:T(8,128)(2,1)} %bitcast.23) | data formatting | bytes 524288
  1.7 1.6 %shard_map.73 = bf16[4,4,16,256]{3,2,1,0:T(8,128)(2,1)} custom-call(s32[4,8]{1,0:T(4,128)} %bitcast.17, bf16[32,16,256]{2,1,0:T(8,128)(2,1)} %bitcast.11), custom_call_target="tpu_custom_call" | custom-call | tf_op jit(solution)/shard_map/pallas_call | solution.py:102
  3.3 2.9 %collective-permute-start = (bf16[4,4,16,256]{3,2,1,0:T(8,128)(2,1)}, bf16[4,4,16,256]{3,2,1,0:T(8,128)(2,1)S(1)}, u32[]{:S(2)}, u32[]{:S(2)}) collective-permute-start(bf16[4,4,16,256]{3,2,1,0:T(8,128)(2,1)} %shard_map.73), channel_id=1, source_target_pairs={{0,1},{1,0},{2,3},{3,2},{4,5},{5,4},{6,7},{7,6},{8,9},{9,8},{10,11... | collective-permute-start | bytes 393224 | tf_op jit(solution)/shard_map/ppermute | solution.py:410
  6.3 1.8 %copy.9 = bf16[4,8,240,128]{3,2,1,0:T(8,128)(2,1)S(1)} copy(bf16[4,8,240,128]{3,1,2,0:T(8,128)(2,1)} %bitcast.22) | data formatting | bytes 3932160
  8.1 0.0 copy-start.3
  8.1 0.0 copy-start
  8.1 0.0 copy-start.1
  8.1 0.0 copy-start.2
  8.1 0.1 slice.refs_3_
  8.3 0.5 copy-done.3
  8.8 0.9 %shard_map.74 = (bf16[32,256]{1,0:T(8,128)(2,1)S(1)}, bf16[32,128]{1,0:T(8,128)(2,1)S(1)}, bf16[128,256]{1,0:T(8,128)(2,1)S(1)}, bf16[32,128]{1,0:T(8,128)(2,1)S...) custom-call(bf16[32,32]{1,0:T(8,128)(2,1)S(1)} %copy-done.3), custom_call_target="tpu_custom_call" | custom-call | tf_op jit(solution)/shard_map/pallas_call | solution.py:84
  9.7 0.3 collective-permute-done.refs_2_
  10.0 0.0 copy-done
  10.0 0.0 copy-done.1
  10.0 0.0 copy-done.2
  10.0 9.6 %shard_map.75 = (bf16[8,16,1024]{2,1,0:T(8,128)(2,1)S(1)}, bf16[8,16,1024]{2,1,0:T(8,128)(2,1)S(1)}) custom-call(s32[4,4]{1,0:T(4,128)S(1)} %copy-done.2, s32[4,8]{1,0:T(4,128)S(1)} %bitcast.18, bf16[32,16,256]{2,1,0:T(8,128)(2,1)S(1)} %bitcast.12, bf16[4,4,16,256]{3,2,1,0:T(8,128)(2,1)S(1)} %collective-permute-done.refs_2_, ...), custom_call_target="tpu_custom_call" | custom-call | tf_op jit(solution)/shard_map/pallas_call | solution.py:273
  19.6 1.8 %collective-permute-start.2 = (bf16[8,16,1024]{2,1,0:T(8,128)(2,1)S(1)}, bf16[8,16,1024]{2,1,0:T(8,128)(2,1)S(1)}, u32[]{:S(2)}, u32[]{:S(2)}) collective-permute-start(bf16[8,16,1024]{2,1,0:T(8,128)(2,1)S(1)} %get-tuple-element.48), channel_id=1, source_target_pairs={{0,1},{1,0},{2,3},{3,2},{4,5},{5,4},{6,7},{7,6},{8,9},{9,8},{10,11... | collective-permute-start | bytes 786440 | tf_op jit(solution)/shard_map/ppermute | solution.py:410
  21.4 5.0 %shard_map.76 = (bf16[4,16,1024]{2,1,0:T(8,128)(2,1)S(1)}, bf16[4,16,1024]{2,1,0:T(8,128)(2,1)S(1)}) custom-call(s32[4,4]{1,0:T(4,128)S(1)} %copy-done.2, s32[4,8]{1,0:T(4,128)S(1)} %bitcast.19, bf16[32,16,256]{2,1,0:T(8,128)(2,1)S(1)} %bitcast.13, bf16[4,4,16,256]{3,2,1,0:T(8,128)(2,1)S(1)} %collective-permute-done.refs_2_, ...), custom_call_target="tpu_custom_call" | custom-call | tf_op jit(solution)/shard_map/pallas_call | solution.py:273
  26.4 0.0 copy-start.5
  26.4 0.0 copy-start.4
  26.4 0.3 collective-permute-start.3
  26.8 5.0 %shard_map.77 = (bf16[4,16,1024]{2,1,0:T(8,128)(2,1)S(1)}, bf16[4,16,1024]{2,1,0:T(8,128)(2,1)S(1)}) custom-call(s32[4,4]{1,0:T(4,128)S(1)} %copy-done.2, s32[4,8]{1,0:T(4,128)S(1)} %bitcast.20, bf16[32,16,256]{2,1,0:T(8,128)(2,1)S(1)} %bitcast.14, bf16[4,4,16,256]{3,2,1,0:T(8,128)(2,1)S(1)} %collective-permute-done.refs_2_, ...), custom_call_target="tpu_custom_call" | custom-call | tf_op jit(solution)/shard_map/pallas_call | solution.py:273
  31.8 1.8 %collective-permute-start.4 = (bf16[4,16,1024]{2,1,0:T(8,128)(2,1)S(1)}, bf16[4,16,1024]{2,1,0:T(8,128)(2,1)S(1)}, u32[]{:S(2)}, u32[]{:S(2)}) collective-permute-start(bf16[4,16,1024]{2,1,0:T(8,128)(2,1)S(1)} %get-tuple-element.52), channel_id=1, source_target_pairs={{0,1},{1,0},{2,3},{3,2},{4,5},{5,4},{6,7},{7,6},{8,9},{9,8},{10,11... | collective-permute-start | bytes 393224 | tf_op jit(solution)/shard_map/ppermute | solution.py:410
  33.6 0.0 copy-done.5
  33.6 0.0 copy-done.4
  33.6 0.1 reshape.23
  33.7 0.3 collective-permute-start.1
  34.0 3.3 %collective-permute-done.1 = s32[16]{0:T(128)S(1)} collective-permute-done((s32[16]{0:T(128)S(1)}, s32[16]{0:T(128)S(1)}, u32[]{:S(2)}, u32[]{:S(2)}) %collective-permute-start.1) | collective-permute-done | bytes 96 | tf_op jit(solution)/shard_map/ppermute | solution.py:410
  37.3 0.1 pad_add_fusion.goal_ref
  37.3 0.0 collective-permute-done.3.refs_3_
  37.4 0.0 collective-permute-done.4.refs_5_
  37.4 0.0 collective-permute-done.2.refs_1_
  37.4 1.4 %shard_map.78 = (bf16[32,16,1024]{2,1,0:T(8,128)(2,1)S(1)}, bf16[32,16,1024]{2,1,0:T(8,128)(2,1)S(1)}) custom-call(s32[32]{0:T(128)S(1)} %pad_add_fusion.goal_ref, bf16[8,16,1024]{2,1,0:T(8,128)(2,1)S(1)} %get-tuple-element.47.refs_0_, bf16[8,16,1024]{2,1,0:T(8,128)(2,1)S(1)} %collective-permute-done.2.refs_1_, ...), custom_call_target="tpu_custom_call" | custom-call | tf_op jit(solution)/shard_map/pallas_call | solution.py:318
  38.7 0.1 collective-permute-start.5
  38.8 2.6 %collective-permute-done.5 = bf16[32,16,1024]{2,1,0:T(8,128)(2,1)S(1)} collective-permute-done((bf16[32,16,1024]{2,1,0:T(8,128)(2,1)S(1)}, bf16[32,16,1024]{2,1,0:T(8,128)(2,1)S(1)}, u32[]{:S(2)}, u32[]{:S(2)}) %collective-permute-start.5) | collective-permute-done | bytes 1048608 | tf_op jit(solution)/shard_map/ppermute | solution.py:410
  41.5 0.2 shard_map.79
  41.7 1.7 %collective-permute-start.6 = (bf16[4,4,16,512]{3,2,1,0:T(8,128)(2,1)S(1)}, bf16[4,4,16,512]{3,2,1,0:T(8,128)(2,1)S(1)}, u32[]{:S(2)}, u32[]{:S(2)}) collective-permute-start(bf16[4,4,16,512]{3,2,1,0:T(8,128)(2,1)S(1)} %get-tuple-element.56), channel_id=1, source_target_pairs={{0,8},{2,10},{4,12},{6,14},{8,0},{10,2},{12,4},{14,6},{16,24},{18,... | collective-permute-start | bytes 786440 | tf_op jit(solution)/shard_map/ppermute | solution.py:410
  43.4 1.5 %collective-permute-start.8 = (bf16[4,4,16,512]{3,2,1,0:T(8,128)(2,1)S(1)}, bf16[4,4,16,512]{3,2,1,0:T(8,128)(2,1)S(1)}, u32[]{:S(2)}, u32[]{:S(2)}) collective-permute-start(bf16[4,4,16,512]{3,2,1,0:T(8,128)(2,1)S(1)} %get-tuple-element.61), channel_id=1, source_target_pairs={{0,4},{2,6},{4,0},{6,2},{8,12},{10,14},{12,8},{14,10},{16,20},{18,... | collective-permute-start | bytes 786440 | tf_op jit(solution)/shard_map/ppermute | solution.py:410
  44.9 5.2 %collective-permute-done.6.arrived_ref = bf16[4,4,16,512]{3,2,1,0:T(8,128)(2,1)S(1)} collective-permute-done((bf16[4,4,16,512]{3,2,1,0:T(8,128)(2,1)S(1)}, bf16[4,4,16,512]{3,2,1,0:T(8,128)(2,1)S(1)}, u32[]{:S(2)}, u32[]{:S(2)}) %collective-permute-start.6) | collective-permute-done | bytes 262176 | tf_op jit(solution)/shard_map/ppermute | solution.py:410
  50.1 0.1 shard_map.80
  50.2 1.6 %collective-permute-start.7 = (bf16[2,4,16,512]{3,2,1,0:T(8,128)(2,1)S(1)}, bf16[2,4,16,512]{3,2,1,0:T(8,128)(2,1)S(1)}, u32[]{:S(2)}, u32[]{:S(2)}) collective-permute-start(bf16[2,4,16,512]{3,2,1,0:T(8,128)(2,1)S(1)} %get-tuple-element.58), channel_id=1, source_target_pairs={{0,4},{2,6},{4,0},{6,2},{8,12},{10,14},{12,8},{14,10},{16,20},{18,... | collective-permute-start | bytes 393224 | tf_op jit(solution)/shard_map/ppermute | solution.py:410
  51.8 0.0 collective-permute-done.8.arrived_ref
  51.8 0.1 shard_map.82
  51.9 1.6 %collective-permute-start.9 = (bf16[2,4,16,512]{3,2,1,0:T(8,128)(2,1)S(1)}, bf16[2,4,16,512]{3,2,1,0:T(8,128)(2,1)S(1)}, u32[]{:S(2)}, u32[]{:S(2)}) collective-permute-start(bf16[2,4,16,512]{3,2,1,0:T(8,128)(2,1)S(1)} %get-tuple-element.63), channel_id=1, source_target_pairs={{0,8},{2,10},{4,12},{6,14},{8,0},{10,2},{12,4},{14,6},{16,24},{18,... | collective-permute-start | bytes 393224 | tf_op jit(solution)/shard_map/ppermute | solution.py:410
  53.5 1.7 %collective-permute-done.7.arrived_ref = bf16[2,4,16,512]{3,2,1,0:T(8,128)(2,1)S(1)} collective-permute-done((bf16[2,4,16,512]{3,2,1,0:T(8,128)(2,1)S(1)}, bf16[2,4,16,512]{3,2,1,0:T(8,128)(2,1)S(1)}, u32[]{:S(2)}, u32[]{:S(2)}) %collective-permute-start.7) | collective-permute-done | bytes 131104 | tf_op jit(solution)/shard_map/ppermute | solution.py:410
  55.3 2.7 %collective-permute-start.10 = (bf16[1,4,16,512]{3,2,1,0:T(8,128)(2,1)S(1)}, bf16[1,4,16,512]{3,2,1,0:T(8,128)(2,1)S(1)}, u32[]{:S(2)}, u32[]{:S(2)}) collective-permute-start(bf16[1,4,16,512]{3,2,1,0:T(8,128)(2,1)S(1)} %get-tuple-element.65), channel_id=1, source_target_pairs={{0,16},{2,18},{4,20},{6,22},{8,24},{10,26},{12,28},{14,30},{16,0},... | collective-permute-start | bytes 196616 | tf_op jit(solution)/shard_map/ppermute | solution.py:410
  57.9 0.0 collective-permute-done.9.arrived_ref
  58.0 2.3 %collective-permute-start.11 = (bf16[1,4,16,512]{3,2,1,0:T(8,128)(2,1)S(1)}, bf16[1,4,16,512]{3,2,1,0:T(8,128)(2,1)S(1)}, u32[]{:S(2)}, u32[]{:S(2)}) collective-permute-start(bf16[1,4,16,512]{3,2,1,0:T(8,128)(2,1)S(1)} %get-tuple-element.66), channel_id=1, source_target_pairs={{0,16},{2,18},{4,20},{6,22},{8,24},{10,26},{12,28},{14,30},{16,0},... | collective-permute-start | bytes 196616 | tf_op jit(solution)/shard_map/ppermute | solution.py:410
  60.3 1.9 %collective-permute-done.10.arrived0_ref = bf16[1,4,16,512]{3,2,1,0:T(8,128)(2,1)S(1)} collective-permute-done((bf16[1,4,16,512]{3,2,1,0:T(8,128)(2,1)S(1)}, bf16[1,4,16,512]{3,2,1,0:T(8,128)(2,1)S(1)}, u32[]{:S(2)}, u32[]{:S(2)}) %collective-permute-start.10) | collective-permute-done | bytes 65568 | tf_op jit(solution)/shard_map/ppermute | solution.py:410
  62.2 1.0 %collective-permute-done.11.arrived1_ref = bf16[1,4,16,512]{3,2,1,0:T(8,128)(2,1)S(1)} collective-permute-done((bf16[1,4,16,512]{3,2,1,0:T(8,128)(2,1)S(1)}, bf16[1,4,16,512]{3,2,1,0:T(8,128)(2,1)S(1)}, u32[]{:S(2)}, u32[]{:S(2)}) %collective-permute-start.11) | collective-permute-done | bytes 65568 | tf_op jit(solution)/shard_map/ppermute | solution.py:410
  63.2 0.4 shard_map.84
  63.6 0.7 %reshape.26 = bf16[4,4,4096]{2,1,0:T(4,128)(2,1)} reshape(bf16[4,4,16,256]{3,2,1,0:T(8,128)(2,1)S(1)} %shard_map.84) | data formatting | bytes 262144 | tf_op jit(solution)/shard_map/reshape | solution.py:489
  (4 shorter events, 0.1 us)
Async XLA Ops:
  3.3 6.6 %collective-permute-start = (bf16[4,4,16,256]{3,2,1,0:T(8,128)(2,1)}, bf16[4,4,16,256]{3,2,1,0:T(8,128)(2,1)S(1)}, u32[]{:S(2)}, u32[]{:S(2)}) collective-permute-start(bf16[4,4,16,256]{3,2,1,0:T(8,128)(2,1)} %shard_map.73), channel_id=1, source_target_pairs={{0,1},{1,0},{2,3},{3,2},{4,5},{5,4},{6,7},{7,6},{8,9},{9,8},{10,11... | collective-permute-start | bytes 393224 | tf_op jit(solution)/shard_map/ppermute | solution.py:410
  8.1 0.7 %copy-start.3 = (bf16[32,32]{1,0:T(8,128)(2,1)S(1)}, bf16[32,32]{1,0:T(8,128)(2,1)}, u32[]{:S(2)}) copy-start(bf16[32,32]{1,0:T(8,128)(2,1)} %scale_ref.1) | copy-start | bytes 6148
  8.1 1.9 %copy-start = (bf16[4,8,16,256]{3,2,1,0:T(8,128)(2,1)S(1)}, bf16[4,8,16,256]{3,2,1,0:T(8,128)(2,1)}, u32[]{:S(2)}) copy-start(bf16[4,8,16,256]{3,2,1,0:T(8,128)(2,1)} %copy.8) | copy-start | bytes 786436
  8.1 1.9 %copy-start.1 = (s32[8,4]{0,1:T(4,128)S(1)}, s32[8,4]{0,1:T(4,128)}, u32[]{:S(2)}) copy-start(s32[8,4]{0,1:T(4,128)} %param.8) | copy-start | bytes 388
  8.1 1.9 %copy-start.2 = (s32[4,4]{1,0:T(4,128)S(1)}, s32[4,4]{1,0:T(4,128)}, u32[]{:S(2)}) copy-start(s32[4,4]{1,0:T(4,128)} %kind_ref.5) | copy-start | bytes 196
  19.6 17.8 %collective-permute-start.2 = (bf16[8,16,1024]{2,1,0:T(8,128)(2,1)S(1)}, bf16[8,16,1024]{2,1,0:T(8,128)(2,1)S(1)}, u32[]{:S(2)}, u32[]{:S(2)}) collective-permute-start(bf16[8,16,1024]{2,1,0:T(8,128)(2,1)S(1)} %get-tuple-element.48), channel_id=1, source_target_pairs={{0,1},{1,0},{2,3},{3,2},{4,5},{5,4},{6,7},{7,6},{8,9},{9,8},{10,11... | collective-permute-start | bytes 786440 | tf_op jit(solution)/shard_map/ppermute | solution.py:410
  26.4 7.2 %copy-start.5 = (s32[4,4,1]{1,2,0:T(1,128)S(1)}, s32[4,4,1]{1,2,0:T(1,128)}, u32[]{:S(2)}) copy-start(s32[4,4,1]{1,2,0:T(1,128)} %param.12) | copy-start | bytes 196
  26.4 7.2 %copy-start.4 = (s32[4,4]{1,0:T(4,128)S(1)}, s32[4,4]{1,0:T(4,128)}, u32[]{:S(2)}) copy-start(s32[4,4]{1,0:T(4,128)} %param.13) | copy-start | bytes 196
  26.4 10.9 %collective-permute-start.3 = (bf16[4,16,1024]{2,1,0:T(8,128)(2,1)S(1)}, bf16[4,16,1024]{2,1,0:T(8,128)(2,1)S(1)}, u32[]{:S(2)}, u32[]{:S(2)}) collective-permute-start(bf16[4,16,1024]{2,1,0:T(8,128)(2,1)S(1)} %get-tuple-element.50), channel_id=1, source_target_pairs={{0,1},{1,0},{2,3},{3,2},{4,5},{5,4},{6,7},{7,6},{8,9},{9,8},{10,11... | collective-permute-start | bytes 393224 | tf_op jit(solution)/shard_map/ppermute | solution.py:410
  31.8 5.5 %collective-permute-start.4 = (bf16[4,16,1024]{2,1,0:T(8,128)(2,1)S(1)}, bf16[4,16,1024]{2,1,0:T(8,128)(2,1)S(1)}, u32[]{:S(2)}, u32[]{:S(2)}) collective-permute-start(bf16[4,16,1024]{2,1,0:T(8,128)(2,1)S(1)} %get-tuple-element.52), channel_id=1, source_target_pairs={{0,1},{1,0},{2,3},{3,2},{4,5},{5,4},{6,7},{7,6},{8,9},{9,8},{10,11... | collective-permute-start | bytes 393224 | tf_op jit(solution)/shard_map/ppermute | solution.py:410
  33.7 3.5 %collective-permute-start.1 = (s32[16]{0:T(128)S(1)}, s32[16]{0:T(128)S(1)}, u32[]{:S(2)}, u32[]{:S(2)}) collective-permute-start(s32[16]{0:T(128)S(1)} %reshape.23), channel_id=1, source_target_pairs={{0,1},{1,0},{2,3},{3,2},{4,5},{5,4},{6,7},{7,6},{8,9},{9,8},{10,11... | collective-permute-start | bytes 200 | tf_op jit(solution)/shard_map/ppermute | solution.py:410
  38.7 2.7 %collective-permute-start.5 = (bf16[32,16,1024]{2,1,0:T(8,128)(2,1)S(1)}, bf16[32,16,1024]{2,1,0:T(8,128)(2,1)S(1)}, u32[]{:S(2)}, u32[]{:S(2)}) collective-permute-start(bf16[32,16,1024]{2,1,0:T(8,128)(2,1)S(1)} %get-tuple-element.54), channel_id=1, source_target_pairs={{0,2},{2,0},{4,6},{6,4},{8,10},{10,8},{12,14},{14,12},{16,18},{18,... | collective-permute-start | bytes 3145736 | tf_op jit(solution)/shard_map/ppermute | solution.py:410
  41.7 8.4 %collective-permute-start.6 = (bf16[4,4,16,512]{3,2,1,0:T(8,128)(2,1)S(1)}, bf16[4,4,16,512]{3,2,1,0:T(8,128)(2,1)S(1)}, u32[]{:S(2)}, u32[]{:S(2)}) collective-permute-start(bf16[4,4,16,512]{3,2,1,0:T(8,128)(2,1)S(1)} %get-tuple-element.56), channel_id=1, source_target_pairs={{0,8},{2,10},{4,12},{6,14},{8,0},{10,2},{12,4},{14,6},{16,24},{18,... | collective-permute-start | bytes 786440 | tf_op jit(solution)/shard_map/ppermute | solution.py:410
  43.4 8.4 %collective-permute-start.8 = (bf16[4,4,16,512]{3,2,1,0:T(8,128)(2,1)S(1)}, bf16[4,4,16,512]{3,2,1,0:T(8,128)(2,1)S(1)}, u32[]{:S(2)}, u32[]{:S(2)}) collective-permute-start(bf16[4,4,16,512]{3,2,1,0:T(8,128)(2,1)S(1)} %get-tuple-element.61), channel_id=1, source_target_pairs={{0,4},{2,6},{4,0},{6,2},{8,12},{10,14},{12,8},{14,10},{16,20},{18,... | collective-permute-start | bytes 786440 | tf_op jit(solution)/shard_map/ppermute | solution.py:410
  50.2 5.0 %collective-permute-start.7 = (bf16[2,4,16,512]{3,2,1,0:T(8,128)(2,1)S(1)}, bf16[2,4,16,512]{3,2,1,0:T(8,128)(2,1)S(1)}, u32[]{:S(2)}, u32[]{:S(2)}) collective-permute-start(bf16[2,4,16,512]{3,2,1,0:T(8,128)(2,1)S(1)} %get-tuple-element.58), channel_id=1, source_target_pairs={{0,4},{2,6},{4,0},{6,2},{8,12},{10,14},{12,8},{14,10},{16,20},{18,... | collective-permute-start | bytes 393224 | tf_op jit(solution)/shard_map/ppermute | solution.py:410
  51.9 6.1 %collective-permute-start.9 = (bf16[2,4,16,512]{3,2,1,0:T(8,128)(2,1)S(1)}, bf16[2,4,16,512]{3,2,1,0:T(8,128)(2,1)S(1)}, u32[]{:S(2)}, u32[]{:S(2)}) collective-permute-start(bf16[2,4,16,512]{3,2,1,0:T(8,128)(2,1)S(1)} %get-tuple-element.63), channel_id=1, source_target_pairs={{0,8},{2,10},{4,12},{6,14},{8,0},{10,2},{12,4},{14,6},{16,24},{18,... | collective-permute-start | bytes 393224 | tf_op jit(solution)/shard_map/ppermute | solution.py:410
  55.3 7.0 %collective-permute-start.10 = (bf16[1,4,16,512]{3,2,1,0:T(8,128)(2,1)S(1)}, bf16[1,4,16,512]{3,2,1,0:T(8,128)(2,1)S(1)}, u32[]{:S(2)}, u32[]{:S(2)}) collective-permute-start(bf16[1,4,16,512]{3,2,1,0:T(8,128)(2,1)S(1)} %get-tuple-element.65), channel_id=1, source_target_pairs={{0,16},{2,18},{4,20},{6,22},{8,24},{10,26},{12,28},{14,30},{16,0},... | collective-permute-start | bytes 196616 | tf_op jit(solution)/shard_map/ppermute | solution.py:410
  58.0 5.2 %collective-permute-start.11 = (bf16[1,4,16,512]{3,2,1,0:T(8,128)(2,1)S(1)}, bf16[1,4,16,512]{3,2,1,0:T(8,128)(2,1)S(1)}, u32[]{:S(2)}, u32[]{:S(2)}) collective-permute-start(bf16[1,4,16,512]{3,2,1,0:T(8,128)(2,1)S(1)} %get-tuple-element.66), channel_id=1, source_target_pairs={{0,16},{2,18},{4,20},{6,22},{8,24},{10,26},{12,28},{14,30},{16,0},... | collective-permute-start | bytes 196616 | tf_op jit(solution)/shard_map/ppermute | solution.py:410

commit v7 on v6

--- a/solution.py
+++ b/solution.py
@@ -1,4 +1,5 @@
 import functools
+import math
 
 import jax
 import jax.numpy as jnp
@@ -90,24 +91,39 @@
     )(two_scale)
 
 
-def pick_kernel(slot_ref, blocks_ref, out_ref, *, parents):
-    first = (1 - lax.axis_index("oct")) * parents
-    for i in range(parents):
-        for j in range(out_ref.shape[1]):
-            out_ref[i, j] = blocks_ref[slot_ref[j, first + i]]
-
-
-def pick_blocks(child_slot, blocks, parents):
-    shape = (parents, child_slot.shape[0]) + blocks.shape[1:]
-    return pl.pallas_call(
-        functools.partial(pick_kernel, parents=parents),
+def pick_kernel(slot_ref, children_ref, near_ref, send_ref, wide_ref):
+    blocks, size = children_ref.shape
+    groups = size // 128
+    for v in range(groups):
+        wide_ref[blocks * v : blocks * (v + 1), :] = children_ref[
+            :, 128 * v : 128 * (v + 1)
+        ].astype(F32)
+    parents, held, rows, lanes = near_ref.shape
+    across = lanes // 128
+    mine = lax.axis_index("oct")
+    for out_ref, owner in ((send_ref, 1 - mine), (near_ref, mine)):
+        for i in range(parents):
+            for j in range(held):
+                slot = slot_ref[j, owner * parents + i]
+                for h in range(across):
+                    out_ref[i, j, :, 128 * h : 128 * (h + 1)] = wide_ref[
+                        pl.ds(blocks * h + slot, rows, stride=blocks * across), :
+                    ].astype(BF)
+
+
+def pick_blocks(child_slot, children, parents, half):
+    shape = jax.ShapeDtypeStruct((parents, child_slot.shape[0], half, half * half), BF)
+    return pl.pallas_call(
+        pick_kernel,
         in_specs=[
             pl.BlockSpec(memory_space=pltpu.SMEM),
             pl.BlockSpec(memory_space=pltpu.VMEM),
         ],
-        out_specs=pl.BlockSpec(memory_space=pltpu.VMEM),
-        out_shape=jax.ShapeDtypeStruct(shape, BF),
-    )(child_slot, blocks)
+        out_specs=[pl.BlockSpec(memory_space=pltpu.VMEM)] * 2,
+        out_shape=[shape, shape],
+        scratch_shapes=[pltpu.VMEM((children.size // 128, 128), F32)],
+        compiler_params=pltpu.CompilerParams(vmem_limit_bytes=16 * 1024 * 1024),
+    )(child_slot, children)
 
 
 def by_output(table, edge, terms):
@@ -137,26 +153,23 @@
 
 
 def apply_kernel(
-    kind_ref, *refs, half, terms, first_parent, picked,
+    kind_ref, *refs, half, terms, first_parent,
 ):
-    if picked:
-        slot_ref, refs = refs[0], refs[1:]
     (
-        blocks_ref, far_ref, table_ref, s1e_ref, s2e_ref, m1_ref, m2_ref, fw1_ref, fw2_ref,
+        near_ref, far_ref, table_ref, s1e_ref, s2e_ref, m1_ref, m2_ref, fw1_ref, fw2_ref,
         sa_ref, st_ref, keep_ref, send_ref, cube_ref, sec_ref,
     ) = refs[:15]
-    expanded = refs[15:]
+    g0_ref, w1e_ref, w2e_ref = refs[15:]
     edge = 2 * half
     low = half // 2
     wide = edge * low
     quarter = wide // 4
     rows = terms * low
-    step = pl.program_id(1)
     parent = first_parent + pl.program_id(0)
-    item = pl.program_id(0) * pl.num_programs(1) + step
-
-    def expand(kinds):
-        g0_ref, w1e_ref, w2e_ref = expanded
+    disps = kind_ref.shape[1]
+
+    def expand(entries):
+        kinds = [kind_ref[parent, k] for k in entries]
         spread = [
             [
                 by_output(
@@ -167,30 +180,24 @@
             for axis in range(3)
         ]
         turned = [[x.T for x in spread[axis]] for axis in (1, 2)]
-        for k in range(len(kinds)):
-            g0_ref[k] = dot(st_ref[...], spread[0][k]).astype(BF)
-        for k in range(len(kinds)):
-            w1e_ref[k] = dot(turned[0][k], s1e_ref[...]).astype(BF)
-        for k in range(len(kinds)):
-            once = dot(turned[1][k], s2e_ref[...])
+        for k, x in zip(entries, spread[0]):
+            g0_ref[k] = dot(st_ref[...], x).astype(BF)
+        for k, x in zip(entries, turned[0]):
+            w1e_ref[k] = dot(x, s1e_ref[...]).astype(BF)
+        for k, x in zip(entries, turned[1]):
+            once = dot(x, s2e_ref[...])
             for i in range(terms * 4):
                 tile = once[low * i : low * (i + 1)]
                 w2e_ref[k, half * i : half * (i + 1), :] = jnp.concatenate(
                     [tile, tile], axis=0
                 ).astype(BF)
 
-    @pl.when(step == 0)
-    def _():
-        if picked:
-            first = lax.axis_index("oct") * far_ref.shape[0] + parent
-            near = [blocks_ref[slot_ref[i, first]] for i in range(4)]
-        else:
-            near = [blocks_ref[parent, i] for i in range(4)]
+    def filtered():
         total = None
         for bit in range(2):
             parts = []
             for mid in range(2):
-                parts += [near[2 * mid + bit], far_ref[parent, 2 * mid + bit]]
+                parts += [near_ref[parent, 2 * mid + bit], far_ref[parent, 2 * mid + bit]]
             part = dot(jnp.concatenate(parts, axis=0), fw1_ref[bit])
             total = part if total is None else total + part
         total = total.astype(BF)
@@ -209,61 +216,72 @@
             axis=0,
         )
         second = dot(moved, fw2_ref[...]).astype(BF)
-        for i in range(4):
-            cube_ref[edge * i : edge * (i + 1), :] = dot(
-                sa_ref[...], second[edge * i : edge * (i + 1)]
-            ).astype(BF)
-        expand([kind_ref[parent, k] for k in range(kind_ref.shape[1])])
-
-    g0_ref, w1e_ref, w2e_ref = expanded
-    cube = cube_ref[...]
-    none = jnp.zeros((half, wide // 2), BF)
-    for t in range(terms):
-        one = w1e_ref[step, edge * t : edge * (t + 1), :]
-        w1 = jnp.concatenate(
+        return jnp.concatenate(
             [
-                one[half * j : half * (j + 1)] * m1_ref[half * i : half * (i + 1), :]
-                for i in range(low)
-                for j in range(2)
+                dot(sa_ref[...], second[edge * i : edge * (i + 1)]).astype(BF)
+                for i in range(4)
             ],
             axis=0,
         )
-        first = dot(cube, w1).astype(BF)
-        moved = jnp.concatenate(
-            [
-                jnp.concatenate(
-                    [
-                        first[edge * i : edge * (i + 1), quarter * j : quarter * (j + 1)]
-                        for i in range(4)
-                    ],
-                    axis=1,
-                )
-                for j in range(4)
-            ],
-            axis=0,
-        )
-        w2 = []
+
+    def products(k):
+        cube = cube_ref[...]
+        none = jnp.zeros((half, wide // 2), BF)
+        for t in range(terms):
+            one = w1e_ref[k, edge * t : edge * (t + 1), :]
+            w1 = jnp.concatenate(
+                [
+                    one[half * j : half * (j + 1)] * m1_ref[half * i : half * (i + 1), :]
+                    for i in range(low)
+                    for j in range(2)
+                ],
+                axis=0,
+            )
+            first = dot(cube, w1).astype(BF)
+            moved = jnp.concatenate(
+                [
+                    jnp.concatenate(
+                        [
+                            first[edge * i : edge * (i + 1), quarter * j : quarter * (j + 1)]
+                            for i in range(4)
+                        ],
+                        axis=1,
+                    )
+                    for j in range(4)
+                ],
+                axis=0,
+            )
+            w2 = []
+            for i in range(4):
+                tile = w2e_ref[k, half * (4 * t + i) : half * (4 * t + i + 1), :]
+                pair = [tile * m2_ref[half * q : half * (q + 1), :] for q in range(2)]
+                w2 += [jnp.concatenate([x, none], axis=1) for x in pair]
+                w2 += [jnp.concatenate([none, x], axis=1) for x in pair]
+            second = dot(moved, jnp.concatenate(w2, axis=0)).astype(BF)
+            for i in range(4):
+                sec_ref[k, i, edge * t : edge * (t + 1), :] = second[edge * i : edge * (i + 1)]
+
+    def finish(k):
+        item = pl.program_id(0) * disps + k
         for i in range(4):
-            tile = w2e_ref[step, half * (4 * t + i) : half * (4 * t + i + 1), :]
-            pair = [tile * m2_ref[half * q : half * (q + 1), :] for q in range(2)]
-            w2 += [jnp.concatenate([x, none], axis=1) for x in pair]
-            w2 += [jnp.concatenate([none, x], axis=1) for x in pair]
-        second = dot(moved, jnp.concatenate(w2, axis=0)).astype(BF)
-        for i in range(4):
-            sec_ref[i, edge * t : edge * (t + 1), :] = second[edge * i : edge * (i + 1)]
-    for i in range(4):
-        out = dot(g0_ref[step], sec_ref[i]).astype(BF)
-        keep_ref[item, :, wide * i : wide * (i + 1)] = out[:half]
-        send_ref[item, :, wide * i : wide * (i + 1)] = out[half:]
-
-
-def apply_parents(first_parent, count, kinds, child_slot, near, far, table, weights, half):
+            out = dot(g0_ref[k], sec_ref[k, i]).astype(BF)
+            keep_ref[item, :, wide * i : wide * (i + 1)] = out[:half]
+            send_ref[item, :, wide * i : wide * (i + 1)] = out[half:]
+
+    cube_ref[...] = filtered()
+    expand(range(disps))
+    for k in range(disps):
+        products(k)
+    for k in range(disps):
+        finish(k)
+
+
+def apply_parents(first_parent, count, kinds, near, far, table, weights, half):
     edge = 2 * half
     wide = edge * half // 2
     terms = table.shape[1] // (3 * edge // 4)
     disps = kinds.shape[1]
     shape = jax.ShapeDtypeStruct((count * disps, half, 4 * wide), BF)
-    scalars = (kinds,) if child_slot is None else (kinds, child_slot)
     arrays = (near, far, table) + tuple(weights)
     expanded = [
         pltpu.VMEM((disps, edge, terms * edge), BF),
@@ -276,20 +294,19 @@
             half=half,
             terms=terms,
             first_parent=first_parent,
-            picked=child_slot is not None,
         ),
-        grid=(count, disps),
-        in_specs=[pl.BlockSpec(memory_space=pltpu.SMEM)] * len(scalars)
+        grid=(count,),
+        in_specs=[pl.BlockSpec(memory_space=pltpu.SMEM)]
         + [pl.BlockSpec(memory_space=pltpu.VMEM)] * len(arrays),
         out_specs=[pl.BlockSpec(memory_space=pltpu.VMEM)] * 2,
         out_shape=[shape, shape],
         scratch_shapes=[
             pltpu.VMEM((4 * edge, wide), BF),
-            pltpu.VMEM((4, terms * edge, wide), BF),
+            pltpu.VMEM((disps, 4, terms * edge, wide), BF),
         ]
         + expanded,
         compiler_params=pltpu.CompilerParams(vmem_limit_bytes=24 * 1024 * 1024),
-    )(*scalars, *arrays)
+    )(kinds, *arrays)
 
 
 def target(goal_ref, item, nodes):
@@ -369,30 +386,45 @@
     )(kept, arrived)
 
 
-def last_kernel(kept0_ref, kept1_ref, arrived0_ref, arrived1_ref, out_ref):
+def last_kernel(kept0_ref, kept1_ref, arrived0_ref, arrived1_ref, out_ref, wide_ref):
+    nodes, octants, size = out_ref.shape
+    groups = size // 128
+    rows, lanes = kept0_ref.shape[2:]
+
+    def store(total, n, first, step):
+        wide_ref[pl.ds(n * octants * groups + first, rows, stride=step), :] = total[
+            rows * n : rows * (n + 1)
+        ]
+
     for i, (kept_ref, arrived_ref) in enumerate(
         ((kept0_ref, arrived0_ref), (kept1_ref, arrived1_ref))
     ):
-        lanes = kept_ref.shape[-1]
-        total = (kept_ref[0].astype(F32) + arrived_ref[0].astype(F32)).astype(BF)
-        if out_ref.shape[1] != 4:
-            out_ref[:, 0, :, lanes * i : lanes * (i + 1)] = total
-            continue
-        wide = lanes // 2
-        half = wide // 16
-        order = one_hot(
-            (wide, wide),
-            lambda x: x % (2 * half) // half * (wide // 2) + x // (2 * half) * half + x % half,
-            lambda x: x,
-        )
-        for n in range(total.shape[0]):
+        total = kept_ref[0].astype(F32) + arrived_ref[0].astype(F32)
+        total = total.reshape(nodes * rows, lanes)
+        if octants == 4:
+            wide = lanes // 2
+            half = wide // 16
+            order = one_hot(
+                (wide, wide),
+                lambda x: x % (2 * half) // half * (wide // 2) + x // (2 * half) * half + x % half,
+                lambda x: x,
+            )
             for c in range(2):
-                moved = exact(total[n, :, wide * c : wide * (c + 1)], order)
-                to = wide // 2 * c
+                moved = dot(total[:, wide * c : wide * (c + 1)].astype(BF), order)
                 for bit in range(2):
-                    out_ref[n, 2 * i + bit, :, to : to + wide // 2] = moved[
-                        :, wide // 2 * bit : wide // 2 * (bit + 1)
-                    ]
+                    part = moved[:, wide // 2 * bit : wide // 2 * (bit + 1)]
+                    for n in range(nodes):
+                        store(part, n, (2 * i + bit) * groups + c, 2)
+        else:
+            for h in range(lanes // 128):
+                part = total[:, 128 * h : 128 * (h + 1)]
+                for n in range(nodes):
+                    store(part, n, i * (lanes // 128) + h, lanes // 64)
+    for n in range(nodes):
+        for v in range(groups):
+            out_ref[n, :, 128 * v : 128 * (v + 1)] = wide_ref[
+                pl.ds(n * octants * groups + v, octants, stride=groups), :
+            ].astype(BF)
 
 
 def last_combine(kept, arrived, shape):
@@ -401,6 +433,7 @@
         in_specs=[pl.BlockSpec(memory_space=pltpu.VMEM)] * 4,
         out_specs=pl.BlockSpec(memory_space=pltpu.VMEM),
         out_shape=jax.ShapeDtypeStruct(shape, BF),
+        scratch_shapes=[pltpu.VMEM((math.prod(shape) // 128, 128), F32)],
         compiler_params=pltpu.CompilerParams(vmem_limit_bytes=24 * 1024 * 1024),
     )(*kept, *arrived)
 
@@ -419,17 +452,15 @@
     parents, disps = disp_kind.shape
     paired = oct_count == 2
 
-    blocks = children.reshape(-1, half, half * half)
     if paired:
-        near = blocks
-        near_slot = child_slot.T
-        far = swap(pick_blocks(near_slot, blocks, parents), "oct", 1)
+        near, sent = pick_blocks(child_slot.T, children, parents, half)
+        far = swap(sent, "oct", 1)
     else:
+        blocks = children.reshape(-1, half, half * half)
         arrived = lax.all_to_all(
             blocks[child_slot], "oct", split_axis=0, concat_axis=1, tiled=True
         ).reshape(parents, 2, 4, half, half * half)
         near, far = arrived[:, 0], arrived[:, 1]
-        near_slot = None
 
     table = factors.reshape(factors.shape[0], -1, 4 * edge)
     weights = make_weights(two_scale, paired)
@@ -438,7 +469,7 @@
     done, counts = 0, [max(1, parents - 2)] + [1] * min(2, parents - 1)
     for count in counts:
         kept, sent = apply_parents(
-            done, count, disp_kind, near_slot, near, far, table, weights, half
+            done, count, disp_kind, near, far, table, weights, half
         )
         if done == 0:
             target_leaf, target_node, kept = lax.optimization_barrier(
@@ -482,11 +513,7 @@
             come = swap(send, "leaf", mask)
         kept.append(keep)
         arrived.append(come)
-    if paired:
-        shape = (nodes, held, half, half * half)
-    else:
-        shape = (nodes, 1) + shape[2:]
-    return last_combine(kept, arrived, shape).reshape(nodes, held, -1)
+    return last_combine(kept, arrived, (nodes, held, half * half * half))
 
 
 def solution(mesh):

time: 64.6 us -> 57.5 us (0.89)
  Pallas kernels: 24.3 us -> 18.2 us
  local copies, waits for them, and re-layouts: 5.01 us -> 4.22 us
    pallas_call x3, Pallas kernels: 19.6 us -> 13.3 us  [apply_parents(): pl.pallas_call(functools.partial(apply_kernel, half=half, terms=terms, fi...]
    reshape x1 -> x0, local copies, waits for them, and re-layouts: 0.75 us -> none  [local(): return last_combine(kept, arrived, shape).reshape(nodes, held, -1)]
    unnamed x14 -> x13, local copies, waits for them, and re-layouts: 4.07 us -> 4.03 us
  transfers between devices with their start and end apart: 12 -> 12, of which waited for: 7 -> 7; matrix products, arithmetic and copies ran while one was open for 3% -> 4% of each run, Pallas kernels for 17% -> 14%
where the time goes in v7:
time: 57.5 us; the launch traced here: 57.2 us
  starting transfers between devices  18.7 us (33%)
  Pallas kernels  18.2 us (32%)
  waiting for transfers between devices  15.9 us (28%)
  local copies, waits for them, and re-layouts  4.22 us (7%)
    ppermute x12, starting transfers between devices, swap(): return lax.ppermute(x, axis, [(i, i ^ mask) for i in range(count)])  18.7 us
    ppermute x12, waiting for transfers between devices, swap(): return lax.ppermute(x, axis, [(i, i ^ mask) for i in range(count)])  15.9 us
    pallas_call x3, Pallas kernels, apply_parents(): pl.pallas_call(functools.partial(apply_kernel, half=half, terms=terms, fi...  13.3 us
    unnamed x13, local copies, waits for them, and re-layouts  4.03 us
    pallas_call x1, Pallas kernels, sum_rows(): pl.pallas_call(functools.partial(sum_kernel, sources=sources, nodes=nodes...  1.38 us
  transfers between devices with their start and end apart: 12, of which 7 were waited for; matrix products, arithmetic and copies ran while one was open for 4% of the time, Pallas kernels for 14%

profile of v7, /device:TPU:0, one launch (start us, length us, event | category | flops | bytes accessed | tf_op | source)
XLA Modules:
  0.0 57.2 jit_solution(17340996206289291395)
XLA Ops:
  0.0 0.0 copy-start
  0.0 0.9 %copy-done = bf16[32,4096]{1,0:T(8,128)(2,1)S(1)} copy-done((bf16[32,4096]{1,0:T(8,128)(2,1)S(1)}, bf16[32,4096]{1,0:T(8,128)(2,1)}, u32[]{:S(2)}) %copy-start) | copy-done | bytes 262168
  1.0 0.0 copy-start.3
  1.0 0.7 %copy-done.3 = s32[8,4]{0,1:T(4,128)S(1)} copy-done((s32[8,4]{0,1:T(4,128)S(1)}, s32[8,4]{0,1:T(4,128)}, u32[]{:S(2)}) %copy-start.3) | copy-done | bytes 152
  1.6 1.1 %shard_map.73 = (bf16[4,4,16,256]{3,2,1,0:T(8,128)(2,1)S(1)}, bf16[4,4,16,256]{3,2,1,0:T(8,128)(2,1)S(1)}) custom-call(s32[4,8]{1,0:T(4,128)S(1)} %bitcast.9, bf16[32,4096]{1,0:T(8,128)(2,1)S(1)} %copy-done), custom_call_target="tpu_custom_call" | custom-call | tf_op jit(solution)/shard_map/pallas_call | solution.py:116
  2.8 3.0 %collective-permute-start = (bf16[4,4,16,256]{3,2,1,0:T(8,128)(2,1)S(1)}, bf16[4,4,16,256]{3,2,1,0:T(8,128)(2,1)S(1)}, u32[]{:S(2)}, u32[]{:S(2)}) collective-permute-start(bf16[4,4,16,256]{3,2,1,0:T(8,128)(2,1)S(1)} %get-tuple-element.39), channel_id=1, source_target_pairs={{0,1},{1,0},{2,3},{3,2},{4,5},{5,4},{6,7},{7,6},{8,9},{9,8},{10,11... | collective-permute-start | bytes 393224 | tf_op jit(solution)/shard_map/ppermute | solution.py:443
  5.8 1.8 %copy.8 = bf16[4,8,240,128]{3,2,1,0:T(8,128)(2,1)S(1)} copy(bf16[4,8,240,128]{3,1,2,0:T(8,128)(2,1)} %bitcast.11) | data formatting | bytes 3932160
  7.6 0.0 copy-start.2
  7.6 0.0 copy-start.1
  7.6 0.1 slice.refs_2_
  7.7 0.6 copy-done.2
  8.3 0.9 %shard_map.74 = (bf16[32,256]{1,0:T(8,128)(2,1)S(1)}, bf16[32,128]{1,0:T(8,128)(2,1)S(1)}, bf16[128,256]{1,0:T(8,128)(2,1)S(1)}, bf16[32,128]{1,0:T(8,128)(2,1)S...) custom-call(bf16[32,32]{1,0:T(8,128)(2,1)S(1)} %copy-done.2), custom_call_target="tpu_custom_call" | custom-call | tf_op jit(solution)/shard_map/pallas_call | solution.py:85
  9.2 0.1 collective-permute-done.refs_1_
  9.3 0.0 copy-done.1
  9.3 6.4 %shard_map.75 = (bf16[8,16,1024]{2,1,0:T(8,128)(2,1)S(1)}, bf16[8,16,1024]{2,1,0:T(8,128)(2,1)S(1)}) custom-call(s32[4,4]{1,0:T(4,128)S(1)} %copy-done.1, bf16[4,4,16,256]{3,2,1,0:T(8,128)(2,1)S(1)} %get-tuple-element.38.refs_0_, bf16[4,4,16,256]{3,2,1,0:T(8,128)(2,1)S(1)} %collective-permute-done.refs_1_, bf16[27,240,128]{2,1,0:T(8,128)(2,1)S(1)} %slice.refs_2_, ...), custom_call_target="tpu_custom_call" | custom-call | tf_op jit(solution)/shard_map/pallas_call | solution.py:291
  15.7 1.8 %collective-permute-start.2 = (bf16[8,16,1024]{2,1,0:T(8,128)(2,1)S(1)}, bf16[8,16,1024]{2,1,0:T(8,128)(2,1)S(1)}, u32[]{:S(2)}, u32[]{:S(2)}) collective-permute-start(bf16[8,16,1024]{2,1,0:T(8,128)(2,1)S(1)} %get-tuple-element.52), channel_id=1, source_target_pairs={{0,1},{1,0},{2,3},{3,2},{4,5},{5,4},{6,7},{7,6},{8,9},{9,8},{10,11... | collective-permute-start | bytes 786440 | tf_op jit(solution)/shard_map/ppermute | solution.py:443
  17.5 3.5 %shard_map.76 = (bf16[4,16,1024]{2,1,0:T(8,128)(2,1)S(1)}, bf16[4,16,1024]{2,1,0:T(8,128)(2,1)S(1)}) custom-call(s32[4,4]{1,0:T(4,128)S(1)} %copy-done.1, bf16[4,4,16,256]{3,2,1,0:T(8,128)(2,1)S(1)} %get-tuple-element.38.refs_0_, bf16[4,4,16,256]{3,2,1,0:T(8,128)(2,1)S(1)} %collective-permute-done.refs_1_, bf16[27,240,128]{2,1,0:T(8,128)(2,1)S(1)} %slice.refs_2_, ...), custom_call_target="tpu_custom_call" | custom-call | tf_op jit(solution)/shard_map/pallas_call | solution.py:291
  20.9 0.0 copy-start.5
  20.9 0.0 copy-start.4
  21.0 0.4 collective-permute-start.3
  21.3 3.5 %shard_map.77 = (bf16[4,16,1024]{2,1,0:T(8,128)(2,1)S(1)}, bf16[4,16,1024]{2,1,0:T(8,128)(2,1)S(1)}) custom-call(s32[4,4]{1,0:T(4,128)S(1)} %copy-done.1, bf16[4,4,16,256]{3,2,1,0:T(8,128)(2,1)S(1)} %get-tuple-element.38.refs_0_, bf16[4,4,16,256]{3,2,1,0:T(8,128)(2,1)S(1)} %collective-permute-done.refs_1_, bf16[27,240,128]{2,1,0:T(8,128)(2,1)S(1)} %slice.refs_2_, ...), custom_call_target="tpu_custom_call" | custom-call | tf_op jit(solution)/shard_map/pallas_call | solution.py:291
  24.8 1.8 %collective-permute-start.4 = (bf16[4,16,1024]{2,1,0:T(8,128)(2,1)S(1)}, bf16[4,16,1024]{2,1,0:T(8,128)(2,1)S(1)}, u32[]{:S(2)}, u32[]{:S(2)}) collective-permute-start(bf16[4,16,1024]{2,1,0:T(8,128)(2,1)S(1)} %get-tuple-element.56), channel_id=1, source_target_pairs={{0,1},{1,0},{2,3},{3,2},{4,5},{5,4},{6,7},{7,6},{8,9},{9,8},{10,11... | collective-permute-start | bytes 393224 | tf_op jit(solution)/shard_map/ppermute | solution.py:443
  26.6 0.0 copy-done.5
  26.6 0.0 copy-done.4
  26.6 0.1 reshape.16
  26.7 0.3 collective-permute-start.1
  27.0 3.2 %collective-permute-done.1 = s32[16]{0:T(128)S(1)} collective-permute-done((s32[16]{0:T(128)S(1)}, s32[16]{0:T(128)S(1)}, u32[]{:S(2)}, u32[]{:S(2)}) %collective-permute-start.1) | collective-permute-done | bytes 96 | tf_op jit(solution)/shard_map/ppermute | solution.py:443
  30.2 0.1 pad_add_fusion.goal_ref
  30.3 0.0 collective-permute-done.3.refs_3_
  30.3 0.0 collective-permute-done.4.refs_5_
  30.3 0.0 collective-permute-done.2.refs_1_
  30.3 1.4 %shard_map.78 = (bf16[32,16,1024]{2,1,0:T(8,128)(2,1)S(1)}, bf16[32,16,1024]{2,1,0:T(8,128)(2,1)S(1)}) custom-call(s32[32]{0:T(128)S(1)} %pad_add_fusion.goal_ref, bf16[8,16,1024]{2,1,0:T(8,128)(2,1)S(1)} %get-tuple-element.51.refs_0_, bf16[8,16,1024]{2,1,0:T(8,128)(2,1)S(1)} %collective-permute-done.2.refs_1_, ...), custom_call_target="tpu_custom_call" | custom-call | tf_op jit(solution)/shard_map/pallas_call | solution.py:335
  31.7 0.1 collective-permute-start.5
  31.8 2.6 %collective-permute-done.5 = bf16[32,16,1024]{2,1,0:T(8,128)(2,1)S(1)} collective-permute-done((bf16[32,16,1024]{2,1,0:T(8,128)(2,1)S(1)}, bf16[32,16,1024]{2,1,0:T(8,128)(2,1)S(1)}, u32[]{:S(2)}, u32[]{:S(2)}) %collective-permute-start.5) | collective-permute-done | bytes 1048608 | tf_op jit(solution)/shard_map/ppermute | solution.py:443
  34.4 0.3 shard_map.79
  34.7 1.7 %collective-permute-start.6 = (bf16[4,4,16,512]{3,2,1,0:T(8,128)(2,1)S(1)}, bf16[4,4,16,512]{3,2,1,0:T(8,128)(2,1)S(1)}, u32[]{:S(2)}, u32[]{:S(2)}) collective-permute-start(bf16[4,4,16,512]{3,2,1,0:T(8,128)(2,1)S(1)} %get-tuple-element.60), channel_id=1, source_target_pairs={{0,8},{2,10},{4,12},{6,14},{8,0},{10,2},{12,4},{14,6},{16,24},{18,... | collective-permute-start | bytes 786440 | tf_op jit(solution)/shard_map/ppermute | solution.py:443
  36.3 1.5 %collective-permute-start.8 = (bf16[4,4,16,512]{3,2,1,0:T(8,128)(2,1)S(1)}, bf16[4,4,16,512]{3,2,1,0:T(8,128)(2,1)S(1)}, u32[]{:S(2)}, u32[]{:S(2)}) collective-permute-start(bf16[4,4,16,512]{3,2,1,0:T(8,128)(2,1)S(1)} %get-tuple-element.65), channel_id=1, source_target_pairs={{0,4},{2,6},{4,0},{6,2},{8,12},{10,14},{12,8},{14,10},{16,20},{18,... | collective-permute-start | bytes 786440 | tf_op jit(solution)/shard_map/ppermute | solution.py:443
  37.9 5.2 %collective-permute-done.6.arrived_ref = bf16[4,4,16,512]{3,2,1,0:T(8,128)(2,1)S(1)} collective-permute-done((bf16[4,4,16,512]{3,2,1,0:T(8,128)(2,1)S(1)}, bf16[4,4,16,512]{3,2,1,0:T(8,128)(2,1)S(1)}, u32[]{:S(2)}, u32[]{:S(2)}) %collective-permute-start.6) | collective-permute-done | bytes 262176 | tf_op jit(solution)/shard_map/ppermute | solution.py:443
  43.1 0.1 shard_map.80
  43.2 1.6 %collective-permute-start.7 = (bf16[2,4,16,512]{3,2,1,0:T(8,128)(2,1)S(1)}, bf16[2,4,16,512]{3,2,1,0:T(8,128)(2,1)S(1)}, u32[]{:S(2)}, u32[]{:S(2)}) collective-permute-start(bf16[2,4,16,512]{3,2,1,0:T(8,128)(2,1)S(1)} %get-tuple-element.62), channel_id=1, source_target_pairs={{0,4},{2,6},{4,0},{6,2},{8,12},{10,14},{12,8},{14,10},{16,20},{18,... | collective-permute-start | bytes 393224 | tf_op jit(solution)/shard_map/ppermute | solution.py:443
  44.8 0.0 collective-permute-done.8.arrived_ref
  44.8 0.1 shard_map.82
  44.8 1.6 %collective-permute-start.9 = (bf16[2,4,16,512]{3,2,1,0:T(8,128)(2,1)S(1)}, bf16[2,4,16,512]{3,2,1,0:T(8,128)(2,1)S(1)}, u32[]{:S(2)}, u32[]{:S(2)}) collective-permute-start(bf16[2,4,16,512]{3,2,1,0:T(8,128)(2,1)S(1)} %get-tuple-element.67), channel_id=1, source_target_pairs={{0,8},{2,10},{4,12},{6,14},{8,0},{10,2},{12,4},{14,6},{16,24},{18,... | collective-permute-start | bytes 393224 | tf_op jit(solution)/shard_map/ppermute | solution.py:443
  46.5 1.7 %collective-permute-done.7.arrived_ref = bf16[2,4,16,512]{3,2,1,0:T(8,128)(2,1)S(1)} collective-permute-done((bf16[2,4,16,512]{3,2,1,0:T(8,128)(2,1)S(1)}, bf16[2,4,16,512]{3,2,1,0:T(8,128)(2,1)S(1)}, u32[]{:S(2)}, u32[]{:S(2)}) %collective-permute-start.7) | collective-permute-done | bytes 131104 | tf_op jit(solution)/shard_map/ppermute | solution.py:443
  48.2 2.7 %collective-permute-start.10 = (bf16[1,4,16,512]{3,2,1,0:T(8,128)(2,1)S(1)}, bf16[1,4,16,512]{3,2,1,0:T(8,128)(2,1)S(1)}, u32[]{:S(2)}, u32[]{:S(2)}) collective-permute-start(bf16[1,4,16,512]{3,2,1,0:T(8,128)(2,1)S(1)} %get-tuple-element.69), channel_id=1, source_target_pairs={{0,16},{2,18},{4,20},{6,22},{8,24},{10,26},{12,28},{14,30},{16,0},... | collective-permute-start | bytes 196616 | tf_op jit(solution)/shard_map/ppermute | solution.py:443
  50.9 0.0 collective-permute-done.9.arrived_ref
  50.9 2.3 %collective-permute-start.11 = (bf16[1,4,16,512]{3,2,1,0:T(8,128)(2,1)S(1)}, bf16[1,4,16,512]{3,2,1,0:T(8,128)(2,1)S(1)}, u32[]{:S(2)}, u32[]{:S(2)}) collective-permute-start(bf16[1,4,16,512]{3,2,1,0:T(8,128)(2,1)S(1)} %get-tuple-element.70), channel_id=1, source_target_pairs={{0,16},{2,18},{4,20},{6,22},{8,24},{10,26},{12,28},{14,30},{16,0},... | collective-permute-start | bytes 196616 | tf_op jit(solution)/shard_map/ppermute | solution.py:443
  53.3 1.9 %collective-permute-done.10.arrived0_ref = bf16[1,4,16,512]{3,2,1,0:T(8,128)(2,1)S(1)} collective-permute-done((bf16[1,4,16,512]{3,2,1,0:T(8,128)(2,1)S(1)}, bf16[1,4,16,512]{3,2,1,0:T(8,128)(2,1)S(1)}, u32[]{:S(2)}, u32[]{:S(2)}) %collective-permute-start.10) | collective-permute-done | bytes 65568 | tf_op jit(solution)/shard_map/ppermute | solution.py:443
  55.2 1.0 %collective-permute-done.11.arrived1_ref = bf16[1,4,16,512]{3,2,1,0:T(8,128)(2,1)S(1)} collective-permute-done((bf16[1,4,16,512]{3,2,1,0:T(8,128)(2,1)S(1)}, bf16[1,4,16,512]{3,2,1,0:T(8,128)(2,1)S(1)}, u32[]{:S(2)}, u32[]{:S(2)}) %collective-permute-start.11) | collective-permute-done | bytes 65568 | tf_op jit(solution)/shard_map/ppermute | solution.py:443
  56.2 1.1 %shard_map.84 = bf16[4,4,4096]{2,1,0:T(4,128)(2,1)} custom-call(bf16[1,4,16,512]{3,2,1,0:T(8,128)(2,1)S(1)} %get-tuple-element.63.kept0_ref, bf16[1,4,16,512]{3,2,1,0:T(8,128)(2,1)S(1)} %get-tuple-element.68.kept1_ref, bf16[1,4,16,512]{3,2,1,0:T(8,128)(2,1)S(1)} %collective-permute-done.10.arrived0_ref, ...), custom_call_target="tpu_custom_call" | custom-call | tf_op jit(solution)/shard_map/pallas_call | solution.py:431
  (4 shorter events, 0.1 us)
Async XLA Ops:
  0.0 0.9 %copy-start = (bf16[32,4096]{1,0:T(8,128)(2,1)S(1)}, bf16[32,4096]{1,0:T(8,128)(2,1)}, u32[]{:S(2)}) copy-start(bf16[32,4096]{1,0:T(8,128)(2,1)} %children_ref.1) | copy-start | bytes 786436
  1.0 0.7 %copy-start.3 = (s32[8,4]{0,1:T(4,128)S(1)}, s32[8,4]{0,1:T(4,128)}, u32[]{:S(2)}) copy-start(s32[8,4]{0,1:T(4,128)} %param.8) | copy-start | bytes 388
  2.8 6.5 %collective-permute-start = (bf16[4,4,16,256]{3,2,1,0:T(8,128)(2,1)S(1)}, bf16[4,4,16,256]{3,2,1,0:T(8,128)(2,1)S(1)}, u32[]{:S(2)}, u32[]{:S(2)}) collective-permute-start(bf16[4,4,16,256]{3,2,1,0:T(8,128)(2,1)S(1)} %get-tuple-element.39), channel_id=1, source_target_pairs={{0,1},{1,0},{2,3},{3,2},{4,5},{5,4},{6,7},{7,6},{8,9},{9,8},{10,11... | collective-permute-start | bytes 393224 | tf_op jit(solution)/shard_map/ppermute | solution.py:443
  7.6 0.7 %copy-start.2 = (bf16[32,32]{1,0:T(8,128)(2,1)S(1)}, bf16[32,32]{1,0:T(8,128)(2,1)}, u32[]{:S(2)}) copy-start(bf16[32,32]{1,0:T(8,128)(2,1)} %scale_ref.1) | copy-start | bytes 6148
  7.6 1.7 %copy-start.1 = (s32[4,4]{1,0:T(4,128)S(1)}, s32[4,4]{1,0:T(4,128)}, u32[]{:S(2)}) copy-start(s32[4,4]{1,0:T(4,128)} %kind_ref.5) | copy-start | bytes 196
  15.7 14.6 %collective-permute-start.2 = (bf16[8,16,1024]{2,1,0:T(8,128)(2,1)S(1)}, bf16[8,16,1024]{2,1,0:T(8,128)(2,1)S(1)}, u32[]{:S(2)}, u32[]{:S(2)}) collective-permute-start(bf16[8,16,1024]{2,1,0:T(8,128)(2,1)S(1)} %get-tuple-element.52), channel_id=1, source_target_pairs={{0,1},{1,0},{2,3},{3,2},{4,5},{5,4},{6,7},{7,6},{8,9},{9,8},{10,11... | collective-permute-start | bytes 786440 | tf_op jit(solution)/shard_map/ppermute | solution.py:443
  20.9 5.6 %copy-start.5 = (s32[4,4,1]{1,2,0:T(1,128)S(1)}, s32[4,4,1]{1,2,0:T(1,128)}, u32[]{:S(2)}) copy-start(s32[4,4,1]{1,2,0:T(1,128)} %param.12) | copy-start | bytes 196
  20.9 5.6 %copy-start.4 = (s32[4,4]{1,0:T(4,128)S(1)}, s32[4,4]{1,0:T(4,128)}, u32[]{:S(2)}) copy-start(s32[4,4]{1,0:T(4,128)} %param.13) | copy-start | bytes 196
  21.0 9.3 %collective-permute-start.3 = (bf16[4,16,1024]{2,1,0:T(8,128)(2,1)S(1)}, bf16[4,16,1024]{2,1,0:T(8,128)(2,1)S(1)}, u32[]{:S(2)}, u32[]{:S(2)}) collective-permute-start(bf16[4,16,1024]{2,1,0:T(8,128)(2,1)S(1)} %get-tuple-element.54), channel_id=1, source_target_pairs={{0,1},{1,0},{2,3},{3,2},{4,5},{5,4},{6,7},{7,6},{8,9},{9,8},{10,11... | collective-permute-start | bytes 393224 | tf_op jit(solution)/shard_map/ppermute | solution.py:443
  24.8 5.5 %collective-permute-start.4 = (bf16[4,16,1024]{2,1,0:T(8,128)(2,1)S(1)}, bf16[4,16,1024]{2,1,0:T(8,128)(2,1)S(1)}, u32[]{:S(2)}, u32[]{:S(2)}) collective-permute-start(bf16[4,16,1024]{2,1,0:T(8,128)(2,1)S(1)} %get-tuple-element.56), channel_id=1, source_target_pairs={{0,1},{1,0},{2,3},{3,2},{4,5},{5,4},{6,7},{7,6},{8,9},{9,8},{10,11... | collective-permute-start | bytes 393224 | tf_op jit(solution)/shard_map/ppermute | solution.py:443
  26.7 3.5 %collective-permute-start.1 = (s32[16]{0:T(128)S(1)}, s32[16]{0:T(128)S(1)}, u32[]{:S(2)}, u32[]{:S(2)}) collective-permute-start(s32[16]{0:T(128)S(1)} %reshape.16), channel_id=1, source_target_pairs={{0,1},{1,0},{2,3},{3,2},{4,5},{5,4},{6,7},{7,6},{8,9},{9,8},{10,11... | collective-permute-start | bytes 200 | tf_op jit(solution)/shard_map/ppermute | solution.py:443
  31.7 2.7 %collective-permute-start.5 = (bf16[32,16,1024]{2,1,0:T(8,128)(2,1)S(1)}, bf16[32,16,1024]{2,1,0:T(8,128)(2,1)S(1)}, u32[]{:S(2)}, u32[]{:S(2)}) collective-permute-start(bf16[32,16,1024]{2,1,0:T(8,128)(2,1)S(1)} %get-tuple-element.58), channel_id=1, source_target_pairs={{0,2},{2,0},{4,6},{6,4},{8,10},{10,8},{12,14},{14,12},{16,18},{18,... | collective-permute-start | bytes 3145736 | tf_op jit(solution)/shard_map/ppermute | solution.py:443
  34.7 8.4 %collective-permute-start.6 = (bf16[4,4,16,512]{3,2,1,0:T(8,128)(2,1)S(1)}, bf16[4,4,16,512]{3,2,1,0:T(8,128)(2,1)S(1)}, u32[]{:S(2)}, u32[]{:S(2)}) collective-permute-start(bf16[4,4,16,512]{3,2,1,0:T(8,128)(2,1)S(1)} %get-tuple-element.60), channel_id=1, source_target_pairs={{0,8},{2,10},{4,12},{6,14},{8,0},{10,2},{12,4},{14,6},{16,24},{18,... | collective-permute-start | bytes 786440 | tf_op jit(solution)/shard_map/ppermute | solution.py:443
  36.3 8.4 %collective-permute-start.8 = (bf16[4,4,16,512]{3,2,1,0:T(8,128)(2,1)S(1)}, bf16[4,4,16,512]{3,2,1,0:T(8,128)(2,1)S(1)}, u32[]{:S(2)}, u32[]{:S(2)}) collective-permute-start(bf16[4,4,16,512]{3,2,1,0:T(8,128)(2,1)S(1)} %get-tuple-element.65), channel_id=1, source_target_pairs={{0,4},{2,6},{4,0},{6,2},{8,12},{10,14},{12,8},{14,10},{16,20},{18,... | collective-permute-start | bytes 786440 | tf_op jit(solution)/shard_map/ppermute | solution.py:443
  43.2 5.0 %collective-permute-start.7 = (bf16[2,4,16,512]{3,2,1,0:T(8,128)(2,1)S(1)}, bf16[2,4,16,512]{3,2,1,0:T(8,128)(2,1)S(1)}, u32[]{:S(2)}, u32[]{:S(2)}) collective-permute-start(bf16[2,4,16,512]{3,2,1,0:T(8,128)(2,1)S(1)} %get-tuple-element.62), channel_id=1, source_target_pairs={{0,4},{2,6},{4,0},{6,2},{8,12},{10,14},{12,8},{14,10},{16,20},{18,... | collective-permute-start | bytes 393224 | tf_op jit(solution)/shard_map/ppermute | solution.py:443
  44.8 6.1 %collective-permute-start.9 = (bf16[2,4,16,512]{3,2,1,0:T(8,128)(2,1)S(1)}, bf16[2,4,16,512]{3,2,1,0:T(8,128)(2,1)S(1)}, u32[]{:S(2)}, u32[]{:S(2)}) collective-permute-start(bf16[2,4,16,512]{3,2,1,0:T(8,128)(2,1)S(1)} %get-tuple-element.67), channel_id=1, source_target_pairs={{0,8},{2,10},{4,12},{6,14},{8,0},{10,2},{12,4},{14,6},{16,24},{18,... | collective-permute-start | bytes 393224 | tf_op jit(solution)/shard_map/ppermute | solution.py:443
  48.2 7.0 %collective-permute-start.10 = (bf16[1,4,16,512]{3,2,1,0:T(8,128)(2,1)S(1)}, bf16[1,4,16,512]{3,2,1,0:T(8,128)(2,1)S(1)}, u32[]{:S(2)}, u32[]{:S(2)}) collective-permute-start(bf16[1,4,16,512]{3,2,1,0:T(8,128)(2,1)S(1)} %get-tuple-element.69), channel_id=1, source_target_pairs={{0,16},{2,18},{4,20},{6,22},{8,24},{10,26},{12,28},{14,30},{16,0},... | collective-permute-start | bytes 196616 | tf_op jit(solution)/shard_map/ppermute | solution.py:443
  50.9 5.2 %collective-permute-start.11 = (bf16[1,4,16,512]{3,2,1,0:T(8,128)(2,1)S(1)}, bf16[1,4,16,512]{3,2,1,0:T(8,128)(2,1)S(1)}, u32[]{:S(2)}, u32[]{:S(2)}) collective-permute-start(bf16[1,4,16,512]{3,2,1,0:T(8,128)(2,1)S(1)} %get-tuple-element.70), channel_id=1, source_target_pairs={{0,16},{2,18},{4,20},{6,22},{8,24},{10,26},{12,28},{14,30},{16,0},... | collective-permute-start | bytes 196616 | tf_op jit(solution)/shard_map/ppermute | solution.py:443

commit v8 on v7

--- a/solution.py
+++ b/solution.py
@@ -121,8 +121,8 @@
         ],
         out_specs=[pl.BlockSpec(memory_space=pltpu.VMEM)] * 2,
         out_shape=[shape, shape],
-        scratch_shapes=[pltpu.VMEM((children.size // 128, 128), F32)],
-        compiler_params=pltpu.CompilerParams(vmem_limit_bytes=16 * 1024 * 1024),
+        scratch_shapes=[pltpu.VMEM((children.size // 128 + 2 * children.shape[0], 128), F32)],
+        compiler_params=pltpu.CompilerParams(vmem_limit_bytes=60 * 1024 * 1024),
     )(child_slot, children)
 
 
@@ -165,11 +165,11 @@
     wide = edge * low
     quarter = wide // 4
     rows = terms * low
-    parent = first_parent + pl.program_id(0)
     disps = kind_ref.shape[1]
+    count = keep_ref.shape[0] // disps
 
     def expand(entries):
-        kinds = [kind_ref[parent, k] for k in entries]
+        kinds = [kind_ref[first_parent + k // disps, k % disps] for k in entries]
         spread = [
             [
                 by_output(
@@ -192,7 +192,7 @@
                     [tile, tile], axis=0
                 ).astype(BF)
 
-    def filtered():
+    def filtered(parent):
         total = None
         for bit in range(2):
             parts = []
@@ -225,7 +225,7 @@
         )
 
     def products(k):
-        cube = cube_ref[...]
+        cube = cube_ref[k // disps]
         none = jnp.zeros((half, wide // 2), BF)
         for t in range(terms):
             one = w1e_ref[k, edge * t : edge * (t + 1), :]
@@ -262,17 +262,17 @@
                 sec_ref[k, i, edge * t : edge * (t + 1), :] = second[edge * i : edge * (i + 1)]
 
     def finish(k):
-        item = pl.program_id(0) * disps + k
         for i in range(4):
             out = dot(g0_ref[k], sec_ref[k, i]).astype(BF)
-            keep_ref[item, :, wide * i : wide * (i + 1)] = out[:half]
-            send_ref[item, :, wide * i : wide * (i + 1)] = out[half:]
-
-    cube_ref[...] = filtered()
-    expand(range(disps))
-    for k in range(disps):
+            keep_ref[k, :, wide * i : wide * (i + 1)] = out[:half]
+            send_ref[k, :, wide * i : wide * (i + 1)] = out[half:]
+
+    for i in range(count):
+        cube_ref[i] = filtered(first_parent + i)
+    expand(range(count * disps))
+    for k in range(count * disps):
         products(k)
-    for k in range(disps):
+    for k in range(count * disps):
         finish(k)
 
 
@@ -284,9 +284,9 @@
     shape = jax.ShapeDtypeStruct((count * disps, half, 4 * wide), BF)
     arrays = (near, far, table) + tuple(weights)
     expanded = [
-        pltpu.VMEM((disps, edge, terms * edge), BF),
-        pltpu.VMEM((disps, terms * edge, wide), BF),
-        pltpu.VMEM((disps, terms * 2 * edge, wide // 2), BF),
+        pltpu.VMEM((count * disps, edge, terms * edge), BF),
+        pltpu.VMEM((count * disps, terms * edge, wide), BF),
+        pltpu.VMEM((count * disps, terms * 2 * edge, wide // 2), BF),
     ]
     return pl.pallas_call(
         functools.partial(
@@ -295,14 +295,13 @@
             terms=terms,
             first_parent=first_parent,
         ),
-        grid=(count,),
         in_specs=[pl.BlockSpec(memory_space=pltpu.SMEM)]
         + [pl.BlockSpec(memory_space=pltpu.VMEM)] * len(arrays),
         out_specs=[pl.BlockSpec(memory_space=pltpu.VMEM)] * 2,
         out_shape=[shape, shape],
         scratch_shapes=[
-            pltpu.VMEM((4 * edge, wide), BF),
-            pltpu.VMEM((disps, 4, terms * edge, wide), BF),
+            pltpu.VMEM((count, 4 * edge, wide), BF),
+            pltpu.VMEM((count * disps, 4, terms * edge, wide), BF),
         ]
         + expanded,
         compiler_params=pltpu.CompilerParams(vmem_limit_bytes=24 * 1024 * 1024),
@@ -311,34 +310,43 @@
 
 def target(goal_ref, item, nodes):
     goal = goal_ref[item]
-    offset = jnp.bitwise_xor(goal // nodes, lax.axis_index("leaf"))
-    return offset % 2, offset // 2 * nodes + goal % nodes
+    offset = jnp.bitwise_xor(lax.div(goal, nodes), lax.axis_index("leaf"))
+    return offset & 1, (offset >> 1) * nodes + lax.rem(goal, nodes)
+
+
+LANE_PARTS = 2
 
 
 def sum_kernel(goal_ref, *refs, sources, nodes):
-    row_refs, (even_ref, odd_ref, total_ref) = refs[:-3], refs[-3:]
-    total_ref[...] = jnp.zeros_like(total_ref)
-    count = even_ref.shape[0]
+    count = len(refs) - 2 - LANE_PARTS
+    row_refs, even_ref, odd_ref, totals = refs[:count], refs[count], refs[count + 1], refs[-LANE_PARTS:]
+    slots = even_ref.shape[0]
+    lanes = totals[0].shape[-1]
+    for total_ref in totals:
+        total_ref[...] = jnp.zeros_like(total_ref)
     for row_ref, items in zip(row_refs, sources):
         for i, item in enumerate(items):
             parity, slot = target(goal_ref, item, nodes)
-            slot = parity * count + slot
-            total_ref[slot] = total_ref[slot] + row_ref[i].astype(F32)
-    even_ref[...] = total_ref[:count].astype(BF)
-    odd_ref[...] = total_ref[count:].astype(BF)
+            slot = parity * slots + slot
+            for j, total_ref in enumerate(totals):
+                part = row_ref[i, :, lanes * j : lanes * (j + 1)].astype(F32)
+                total_ref[slot] = (total_ref[slot].astype(F32) + part).astype(BF)
+    for j, total_ref in enumerate(totals):
+        even_ref[:, :, lanes * j : lanes * (j + 1)] = total_ref[:slots].astype(BF)
+        odd_ref[:, :, lanes * j : lanes * (j + 1)] = total_ref[slots:].astype(BF)
 
 
 def sum_rows(goals, arrays, sources, nodes, leaf_count):
-    tail = arrays[0].shape[1:]
-    slot_count = leaf_count * nodes
-    shape = jax.ShapeDtypeStruct((slot_count // 2,) + tail, BF)
+    rows, lanes = arrays[0].shape[1:]
+    slots = leaf_count // 2 * nodes
+    shape = jax.ShapeDtypeStruct((slots, rows, lanes), BF)
     return pl.pallas_call(
         functools.partial(sum_kernel, sources=sources, nodes=nodes),
         in_specs=[pl.BlockSpec(memory_space=pltpu.SMEM)]
         + [pl.BlockSpec(memory_space=pltpu.VMEM)] * len(arrays),
         out_specs=[pl.BlockSpec(memory_space=pltpu.VMEM)] * 2,
         out_shape=[shape, shape],
-        scratch_shapes=[pltpu.VMEM((slot_count,) + tail, F32)],
+        scratch_shapes=[pltpu.VMEM((2 * slots, rows, lanes // LANE_PARTS), BF)] * LANE_PARTS,
         compiler_params=pltpu.CompilerParams(vmem_limit_bytes=24 * 1024 * 1024),
     )(goals, *arrays)
 

time: 57.5 us -> 56.4 us (0.981)
  local copies, waits for them, and re-layouts: 4.22 us -> 2.59 us
    unnamed x13 -> x11, local copies, waits for them, and re-layouts: 4.03 us -> 2.39 us
    pallas_call x1, Pallas kernels: 1.14 us -> 2.23 us  [pick_blocks(): pl.pallas_call(pick_kernel, in_specs=[pl.BlockSpec(memory_space=pltpu.SME...]
where the time goes in v8:
time: 56.4 us; the launch traced here: 56.2 us
  Pallas kernels  18.7 us (33%)
  starting transfers between devices  18.6 us (33%)
  waiting for transfers between devices  16.1 us (29%)
  local copies, waits for them, and re-layouts  2.59 us (5%)
    ppermute x12, starting transfers between devices, swap(): return lax.ppermute(x, axis, [(i, i ^ mask) for i in range(count)])  18.6 us
    ppermute x12, waiting for transfers between devices, swap(): return lax.ppermute(x, axis, [(i, i ^ mask) for i in range(count)])  16.1 us
    pallas_call x3, Pallas kernels, apply_parents(): pl.pallas_call(functools.partial(apply_kernel, half=half, terms=terms, fi...  13 us
    unnamed x11, local copies, waits for them, and re-layouts  2.39 us
    pallas_call x1, Pallas kernels, pick_blocks(): pl.pallas_call(pick_kernel, in_specs=[pl.BlockSpec(memory_space=pltpu.SME...  2.23 us
  transfers between devices with their start and end apart: 12, of which 7 were waited for; matrix products, arithmetic and copies ran while one was open for 4% of the time, Pallas kernels for 14%

profile of v8, /device:TPU:0, one launch (start us, length us, event | category | flops | bytes accessed | tf_op | source)
XLA Modules:
  0.0 56.2 jit_solution(15607020290288777076)
XLA Ops:
  0.0 2.2 %shard_map.73 = (bf16[4,4,16,256]{3,2,1,0:T(8,128)(2,1)}, bf16[4,4,16,256]{3,2,1,0:T(8,128)(2,1)}) custom-call(s32[4,8]{1,0:T(4,128)} %bitcast.12, bf16[32,4096]{1,0:T(8,128)(2,1)} %children_ref.1), custom_call_target="tpu_custom_call" | custom-call | tf_op jit(solution)/shard_map/pallas_call | solution.py:116
  2.2 2.9 %collective-permute-start = (bf16[4,4,16,256]{3,2,1,0:T(8,128)(2,1)}, bf16[4,4,16,256]{3,2,1,0:T(8,128)(2,1)S(1)}, u32[]{:S(2)}, u32[]{:S(2)}) collective-permute-start(bf16[4,4,16,256]{3,2,1,0:T(8,128)(2,1)} %get-tuple-element.39), channel_id=1, source_target_pairs={{0,1},{1,0},{2,3},{3,2},{4,5},{5,4},{6,7},{7,6},{8,9},{9,8},{10,11... | collective-permute-start | bytes 393224 | tf_op jit(solution)/shard_map/ppermute | solution.py:451
  5.2 1.8 %copy.8 = bf16[4,8,240,128]{3,2,1,0:T(8,128)(2,1)S(1)} copy(bf16[4,8,240,128]{3,1,2,0:T(8,128)(2,1)} %bitcast.10) | data formatting | bytes 3932160
  7.0 0.0 copy-start.2
  7.0 0.0 copy-start
  7.0 0.0 copy-start.1
  7.0 0.1 slice.refs_2_
  7.1 0.5 copy-done.2
  7.7 0.9 %shard_map.74 = (bf16[32,256]{1,0:T(8,128)(2,1)S(1)}, bf16[32,128]{1,0:T(8,128)(2,1)S(1)}, bf16[128,256]{1,0:T(8,128)(2,1)S(1)}, bf16[32,128]{1,0:T(8,128)(2,1)S...) custom-call(bf16[32,32]{1,0:T(8,128)(2,1)S(1)} %copy-done.2), custom_call_target="tpu_custom_call" | custom-call | tf_op jit(solution)/shard_map/pallas_call | solution.py:85
  8.6 0.3 collective-permute-done.refs_1_
  8.9 0.0 copy-done
  8.9 0.0 copy-done.1
  8.9 6.1 %shard_map.75 = (bf16[8,16,1024]{2,1,0:T(8,128)(2,1)S(1)}, bf16[8,16,1024]{2,1,0:T(8,128)(2,1)S(1)}) custom-call(s32[4,4]{1,0:T(4,128)S(1)} %copy-done.1, bf16[4,4,16,256]{3,2,1,0:T(8,128)(2,1)S(1)} %copy-done, bf16[4,4,16,256]{3,2,1,0:T(8,128)(2,1)S(1)} %collective-permute-done.refs_1_, bf16[27,240,128]{2,1,0:T(8,128)(2,1)S(1)} %slice.refs_2_, ...), custom_call_target="tpu_custom_call" | custom-call | tf_op jit(solution)/shard_map/pallas_call | solution.py:291
  15.0 1.8 %collective-permute-start.2 = (bf16[8,16,1024]{2,1,0:T(8,128)(2,1)S(1)}, bf16[8,16,1024]{2,1,0:T(8,128)(2,1)S(1)}, u32[]{:S(2)}, u32[]{:S(2)}) collective-permute-start(bf16[8,16,1024]{2,1,0:T(8,128)(2,1)S(1)} %get-tuple-element.52), channel_id=1, source_target_pairs={{0,1},{1,0},{2,3},{3,2},{4,5},{5,4},{6,7},{7,6},{8,9},{9,8},{10,11... | collective-permute-start | bytes 786440 | tf_op jit(solution)/shard_map/ppermute | solution.py:451
  16.7 3.5 %shard_map.76 = (bf16[4,16,1024]{2,1,0:T(8,128)(2,1)S(1)}, bf16[4,16,1024]{2,1,0:T(8,128)(2,1)S(1)}) custom-call(s32[4,4]{1,0:T(4,128)S(1)} %copy-done.1, bf16[4,4,16,256]{3,2,1,0:T(8,128)(2,1)S(1)} %copy-done, bf16[4,4,16,256]{3,2,1,0:T(8,128)(2,1)S(1)} %collective-permute-done.refs_1_, bf16[27,240,128]{2,1,0:T(8,128)(2,1)S(1)} %slice.refs_2_, ...), custom_call_target="tpu_custom_call" | custom-call | tf_op jit(solution)/shard_map/pallas_call | solution.py:291
  20.2 0.0 copy-start.4
  20.2 0.0 copy-start.3
  20.2 0.3 collective-permute-start.3
  20.6 3.5 %shard_map.77 = (bf16[4,16,1024]{2,1,0:T(8,128)(2,1)S(1)}, bf16[4,16,1024]{2,1,0:T(8,128)(2,1)S(1)}) custom-call(s32[4,4]{1,0:T(4,128)S(1)} %copy-done.1, bf16[4,4,16,256]{3,2,1,0:T(8,128)(2,1)S(1)} %copy-done, bf16[4,4,16,256]{3,2,1,0:T(8,128)(2,1)S(1)} %collective-permute-done.refs_1_, bf16[27,240,128]{2,1,0:T(8,128)(2,1)S(1)} %slice.refs_2_, ...), custom_call_target="tpu_custom_call" | custom-call | tf_op jit(solution)/shard_map/pallas_call | solution.py:291
  24.0 1.8 %collective-permute-start.4 = (bf16[4,16,1024]{2,1,0:T(8,128)(2,1)S(1)}, bf16[4,16,1024]{2,1,0:T(8,128)(2,1)S(1)}, u32[]{:S(2)}, u32[]{:S(2)}) collective-permute-start(bf16[4,16,1024]{2,1,0:T(8,128)(2,1)S(1)} %get-tuple-element.56), channel_id=1, source_target_pairs={{0,1},{1,0},{2,3},{3,2},{4,5},{5,4},{6,7},{7,6},{8,9},{9,8},{10,11... | collective-permute-start | bytes 393224 | tf_op jit(solution)/shard_map/ppermute | solution.py:451
  25.8 0.0 copy-done.4
  25.8 0.0 copy-done.3
  25.9 0.1 reshape.16
  25.9 0.3 collective-permute-start.1
  26.2 3.3 %collective-permute-done.1 = s32[16]{0:T(128)S(1)} collective-permute-done((s32[16]{0:T(128)S(1)}, s32[16]{0:T(128)S(1)}, u32[]{:S(2)}, u32[]{:S(2)}) %collective-permute-start.1) | collective-permute-done | bytes 96 | tf_op jit(solution)/shard_map/ppermute | solution.py:451
  29.5 0.1 pad_add_fusion.goal_ref
  29.6 0.0 collective-permute-done.3.refs_3_
  29.6 0.0 collective-permute-done.4.refs_5_
  29.6 0.0 collective-permute-done.2.refs_1_
  29.6 1.1 %shard_map.78 = (bf16[32,16,1024]{2,1,0:T(8,128)(2,1)S(1)}, bf16[32,16,1024]{2,1,0:T(8,128)(2,1)S(1)}) custom-call(s32[32]{0:T(128)S(1)} %pad_add_fusion.goal_ref, bf16[8,16,1024]{2,1,0:T(8,128)(2,1)S(1)} %get-tuple-element.51.refs_0_, bf16[8,16,1024]{2,1,0:T(8,128)(2,1)S(1)} %collective-permute-done.2.refs_1_, ...), custom_call_target="tpu_custom_call" | custom-call | tf_op jit(solution)/shard_map/pallas_call | solution.py:343
  30.7 0.1 collective-permute-start.5
  30.8 2.6 %collective-permute-done.5 = bf16[32,16,1024]{2,1,0:T(8,128)(2,1)S(1)} collective-permute-done((bf16[32,16,1024]{2,1,0:T(8,128)(2,1)S(1)}, bf16[32,16,1024]{2,1,0:T(8,128)(2,1)S(1)}, u32[]{:S(2)}, u32[]{:S(2)}) %collective-permute-start.5) | collective-permute-done | bytes 1048608 | tf_op jit(solution)/shard_map/ppermute | solution.py:451
  33.4 0.3 shard_map.79
  33.7 1.6 %collective-permute-start.6 = (bf16[4,4,16,512]{3,2,1,0:T(8,128)(2,1)S(1)}, bf16[4,4,16,512]{3,2,1,0:T(8,128)(2,1)S(1)}, u32[]{:S(2)}, u32[]{:S(2)}) collective-permute-start(bf16[4,4,16,512]{3,2,1,0:T(8,128)(2,1)S(1)} %get-tuple-element.60), channel_id=1, source_target_pairs={{0,8},{2,10},{4,12},{6,14},{8,0},{10,2},{12,4},{14,6},{16,24},{18,... | collective-permute-start | bytes 786440 | tf_op jit(solution)/shard_map/ppermute | solution.py:451
  35.3 1.5 %collective-permute-start.8 = (bf16[4,4,16,512]{3,2,1,0:T(8,128)(2,1)S(1)}, bf16[4,4,16,512]{3,2,1,0:T(8,128)(2,1)S(1)}, u32[]{:S(2)}, u32[]{:S(2)}) collective-permute-start(bf16[4,4,16,512]{3,2,1,0:T(8,128)(2,1)S(1)} %get-tuple-element.65), channel_id=1, source_target_pairs={{0,4},{2,6},{4,0},{6,2},{8,12},{10,14},{12,8},{14,10},{16,20},{18,... | collective-permute-start | bytes 786440 | tf_op jit(solution)/shard_map/ppermute | solution.py:451
  36.8 5.3 %collective-permute-done.6.arrived_ref = bf16[4,4,16,512]{3,2,1,0:T(8,128)(2,1)S(1)} collective-permute-done((bf16[4,4,16,512]{3,2,1,0:T(8,128)(2,1)S(1)}, bf16[4,4,16,512]{3,2,1,0:T(8,128)(2,1)S(1)}, u32[]{:S(2)}, u32[]{:S(2)}) %collective-permute-start.6) | collective-permute-done | bytes 262176 | tf_op jit(solution)/shard_map/ppermute | solution.py:451
  42.1 0.1 shard_map.80
  42.1 1.6 %collective-permute-start.7 = (bf16[2,4,16,512]{3,2,1,0:T(8,128)(2,1)S(1)}, bf16[2,4,16,512]{3,2,1,0:T(8,128)(2,1)S(1)}, u32[]{:S(2)}, u32[]{:S(2)}) collective-permute-start(bf16[2,4,16,512]{3,2,1,0:T(8,128)(2,1)S(1)} %get-tuple-element.62), channel_id=1, source_target_pairs={{0,4},{2,6},{4,0},{6,2},{8,12},{10,14},{12,8},{14,10},{16,20},{18,... | collective-permute-start | bytes 393224 | tf_op jit(solution)/shard_map/ppermute | solution.py:451
  43.7 0.0 collective-permute-done.8.arrived_ref
  43.7 0.1 shard_map.82
  43.8 1.6 %collective-permute-start.9 = (bf16[2,4,16,512]{3,2,1,0:T(8,128)(2,1)S(1)}, bf16[2,4,16,512]{3,2,1,0:T(8,128)(2,1)S(1)}, u32[]{:S(2)}, u32[]{:S(2)}) collective-permute-start(bf16[2,4,16,512]{3,2,1,0:T(8,128)(2,1)S(1)} %get-tuple-element.67), channel_id=1, source_target_pairs={{0,8},{2,10},{4,12},{6,14},{8,0},{10,2},{12,4},{14,6},{16,24},{18,... | collective-permute-start | bytes 393224 | tf_op jit(solution)/shard_map/ppermute | solution.py:451
  45.4 1.7 %collective-permute-done.7.arrived_ref = bf16[2,4,16,512]{3,2,1,0:T(8,128)(2,1)S(1)} collective-permute-done((bf16[2,4,16,512]{3,2,1,0:T(8,128)(2,1)S(1)}, bf16[2,4,16,512]{3,2,1,0:T(8,128)(2,1)S(1)}, u32[]{:S(2)}, u32[]{:S(2)}) %collective-permute-start.7) | collective-permute-done | bytes 131104 | tf_op jit(solution)/shard_map/ppermute | solution.py:451
  47.2 2.7 %collective-permute-start.10 = (bf16[1,4,16,512]{3,2,1,0:T(8,128)(2,1)S(1)}, bf16[1,4,16,512]{3,2,1,0:T(8,128)(2,1)S(1)}, u32[]{:S(2)}, u32[]{:S(2)}) collective-permute-start(bf16[1,4,16,512]{3,2,1,0:T(8,128)(2,1)S(1)} %get-tuple-element.69), channel_id=1, source_target_pairs={{0,16},{2,18},{4,20},{6,22},{8,24},{10,26},{12,28},{14,30},{16,0},... | collective-permute-start | bytes 196616 | tf_op jit(solution)/shard_map/ppermute | solution.py:451
  49.9 0.0 collective-permute-done.9.arrived_ref
  49.9 2.3 %collective-permute-start.11 = (bf16[1,4,16,512]{3,2,1,0:T(8,128)(2,1)S(1)}, bf16[1,4,16,512]{3,2,1,0:T(8,128)(2,1)S(1)}, u32[]{:S(2)}, u32[]{:S(2)}) collective-permute-start(bf16[1,4,16,512]{3,2,1,0:T(8,128)(2,1)S(1)} %get-tuple-element.70), channel_id=1, source_target_pairs={{0,16},{2,18},{4,20},{6,22},{8,24},{10,26},{12,28},{14,30},{16,0},... | collective-permute-start | bytes 196616 | tf_op jit(solution)/shard_map/ppermute | solution.py:451
  52.2 1.9 %collective-permute-done.10.arrived0_ref = bf16[1,4,16,512]{3,2,1,0:T(8,128)(2,1)S(1)} collective-permute-done((bf16[1,4,16,512]{3,2,1,0:T(8,128)(2,1)S(1)}, bf16[1,4,16,512]{3,2,1,0:T(8,128)(2,1)S(1)}, u32[]{:S(2)}, u32[]{:S(2)}) %collective-permute-start.10) | collective-permute-done | bytes 65568 | tf_op jit(solution)/shard_map/ppermute | solution.py:451
  54.2 1.0 %collective-permute-done.11.arrived1_ref = bf16[1,4,16,512]{3,2,1,0:T(8,128)(2,1)S(1)} collective-permute-done((bf16[1,4,16,512]{3,2,1,0:T(8,128)(2,1)S(1)}, bf16[1,4,16,512]{3,2,1,0:T(8,128)(2,1)S(1)}, u32[]{:S(2)}, u32[]{:S(2)}) %collective-permute-start.11) | collective-permute-done | bytes 65568 | tf_op jit(solution)/shard_map/ppermute | solution.py:451
  55.1 1.1 %shard_map.84 = bf16[4,4,4096]{2,1,0:T(4,128)(2,1)} custom-call(bf16[1,4,16,512]{3,2,1,0:T(8,128)(2,1)S(1)} %get-tuple-element.63.kept0_ref, bf16[1,4,16,512]{3,2,1,0:T(8,128)(2,1)S(1)} %get-tuple-element.68.kept1_ref, bf16[1,4,16,512]{3,2,1,0:T(8,128)(2,1)S(1)} %collective-permute-done.10.arrived0_ref, ...), custom_call_target="tpu_custom_call" | custom-call | tf_op jit(solution)/shard_map/pallas_call | solution.py:439
  (4 shorter events, 0.1 us)
Async XLA Ops:
  2.2 6.6 %collective-permute-start = (bf16[4,4,16,256]{3,2,1,0:T(8,128)(2,1)}, bf16[4,4,16,256]{3,2,1,0:T(8,128)(2,1)S(1)}, u32[]{:S(2)}, u32[]{:S(2)}) collective-permute-start(bf16[4,4,16,256]{3,2,1,0:T(8,128)(2,1)} %get-tuple-element.39), channel_id=1, source_target_pairs={{0,1},{1,0},{2,3},{3,2},{4,5},{5,4},{6,7},{7,6},{8,9},{9,8},{10,11... | collective-permute-start | bytes 393224 | tf_op jit(solution)/shard_map/ppermute | solution.py:451
  7.0 0.7 %copy-start.2 = (bf16[32,32]{1,0:T(8,128)(2,1)S(1)}, bf16[32,32]{1,0:T(8,128)(2,1)}, u32[]{:S(2)}) copy-start(bf16[32,32]{1,0:T(8,128)(2,1)} %scale_ref.1) | copy-start | bytes 6148
  7.0 1.9 %copy-start = (bf16[4,4,16,256]{3,2,1,0:T(8,128)(2,1)S(1)}, bf16[4,4,16,256]{3,2,1,0:T(8,128)(2,1)}, u32[]{:S(2)}) copy-start(bf16[4,4,16,256]{3,2,1,0:T(8,128)(2,1)} %get-tuple-element.38.refs_0_) | copy-start | bytes 393220
  7.0 1.9 %copy-start.1 = (s32[4,4]{1,0:T(4,128)S(1)}, s32[4,4]{1,0:T(4,128)}, u32[]{:S(2)}) copy-start(s32[4,4]{1,0:T(4,128)} %kind_ref.5) | copy-start | bytes 196
  15.0 14.6 %collective-permute-start.2 = (bf16[8,16,1024]{2,1,0:T(8,128)(2,1)S(1)}, bf16[8,16,1024]{2,1,0:T(8,128)(2,1)S(1)}, u32[]{:S(2)}, u32[]{:S(2)}) collective-permute-start(bf16[8,16,1024]{2,1,0:T(8,128)(2,1)S(1)} %get-tuple-element.52), channel_id=1, source_target_pairs={{0,1},{1,0},{2,3},{3,2},{4,5},{5,4},{6,7},{7,6},{8,9},{9,8},{10,11... | collective-permute-start | bytes 786440 | tf_op jit(solution)/shard_map/ppermute | solution.py:451
  20.2 5.6 %copy-start.4 = (s32[4,4,1]{1,2,0:T(1,128)S(1)}, s32[4,4,1]{1,2,0:T(1,128)}, u32[]{:S(2)}) copy-start(s32[4,4,1]{1,2,0:T(1,128)} %param.12) | copy-start | bytes 196
  20.2 5.6 %copy-start.3 = (s32[4,4]{1,0:T(4,128)S(1)}, s32[4,4]{1,0:T(4,128)}, u32[]{:S(2)}) copy-start(s32[4,4]{1,0:T(4,128)} %param.13) | copy-start | bytes 196
  20.2 9.3 %collective-permute-start.3 = (bf16[4,16,1024]{2,1,0:T(8,128)(2,1)S(1)}, bf16[4,16,1024]{2,1,0:T(8,128)(2,1)S(1)}, u32[]{:S(2)}, u32[]{:S(2)}) collective-permute-start(bf16[4,16,1024]{2,1,0:T(8,128)(2,1)S(1)} %get-tuple-element.54), channel_id=1, source_target_pairs={{0,1},{1,0},{2,3},{3,2},{4,5},{5,4},{6,7},{7,6},{8,9},{9,8},{10,11... | collective-permute-start | bytes 393224 | tf_op jit(solution)/shard_map/ppermute | solution.py:451
  24.0 5.5 %collective-permute-start.4 = (bf16[4,16,1024]{2,1,0:T(8,128)(2,1)S(1)}, bf16[4,16,1024]{2,1,0:T(8,128)(2,1)S(1)}, u32[]{:S(2)}, u32[]{:S(2)}) collective-permute-start(bf16[4,16,1024]{2,1,0:T(8,128)(2,1)S(1)} %get-tuple-element.56), channel_id=1, source_target_pairs={{0,1},{1,0},{2,3},{3,2},{4,5},{5,4},{6,7},{7,6},{8,9},{9,8},{10,11... | collective-permute-start | bytes 393224 | tf_op jit(solution)/shard_map/ppermute | solution.py:451
  25.9 3.5 %collective-permute-start.1 = (s32[16]{0:T(128)S(1)}, s32[16]{0:T(128)S(1)}, u32[]{:S(2)}, u32[]{:S(2)}) collective-permute-start(s32[16]{0:T(128)S(1)} %reshape.16), channel_id=1, source_target_pairs={{0,1},{1,0},{2,3},{3,2},{4,5},{5,4},{6,7},{7,6},{8,9},{9,8},{10,11... | collective-permute-start | bytes 200 | tf_op jit(solution)/shard_map/ppermute | solution.py:451
  30.7 2.7 %collective-permute-start.5 = (bf16[32,16,1024]{2,1,0:T(8,128)(2,1)S(1)}, bf16[32,16,1024]{2,1,0:T(8,128)(2,1)S(1)}, u32[]{:S(2)}, u32[]{:S(2)}) collective-permute-start(bf16[32,16,1024]{2,1,0:T(8,128)(2,1)S(1)} %get-tuple-element.58), channel_id=1, source_target_pairs={{0,2},{2,0},{4,6},{6,4},{8,10},{10,8},{12,14},{14,12},{16,18},{18,... | collective-permute-start | bytes 3145736 | tf_op jit(solution)/shard_map/ppermute | solution.py:451
  33.7 8.4 %collective-permute-start.6 = (bf16[4,4,16,512]{3,2,1,0:T(8,128)(2,1)S(1)}, bf16[4,4,16,512]{3,2,1,0:T(8,128)(2,1)S(1)}, u32[]{:S(2)}, u32[]{:S(2)}) collective-permute-start(bf16[4,4,16,512]{3,2,1,0:T(8,128)(2,1)S(1)} %get-tuple-element.60), channel_id=1, source_target_pairs={{0,8},{2,10},{4,12},{6,14},{8,0},{10,2},{12,4},{14,6},{16,24},{18,... | collective-permute-start | bytes 786440 | tf_op jit(solution)/shard_map/ppermute | solution.py:451
  35.3 8.4 %collective-permute-start.8 = (bf16[4,4,16,512]{3,2,1,0:T(8,128)(2,1)S(1)}, bf16[4,4,16,512]{3,2,1,0:T(8,128)(2,1)S(1)}, u32[]{:S(2)}, u32[]{:S(2)}) collective-permute-start(bf16[4,4,16,512]{3,2,1,0:T(8,128)(2,1)S(1)} %get-tuple-element.65), channel_id=1, source_target_pairs={{0,4},{2,6},{4,0},{6,2},{8,12},{10,14},{12,8},{14,10},{16,20},{18,... | collective-permute-start | bytes 786440 | tf_op jit(solution)/shard_map/ppermute | solution.py:451
  42.1 5.0 %collective-permute-start.7 = (bf16[2,4,16,512]{3,2,1,0:T(8,128)(2,1)S(1)}, bf16[2,4,16,512]{3,2,1,0:T(8,128)(2,1)S(1)}, u32[]{:S(2)}, u32[]{:S(2)}) collective-permute-start(bf16[2,4,16,512]{3,2,1,0:T(8,128)(2,1)S(1)} %get-tuple-element.62), channel_id=1, source_target_pairs={{0,4},{2,6},{4,0},{6,2},{8,12},{10,14},{12,8},{14,10},{16,20},{18,... | collective-permute-start | bytes 393224 | tf_op jit(solution)/shard_map/ppermute | solution.py:451
  43.8 6.1 %collective-permute-start.9 = (bf16[2,4,16,512]{3,2,1,0:T(8,128)(2,1)S(1)}, bf16[2,4,16,512]{3,2,1,0:T(8,128)(2,1)S(1)}, u32[]{:S(2)}, u32[]{:S(2)}) collective-permute-start(bf16[2,4,16,512]{3,2,1,0:T(8,128)(2,1)S(1)} %get-tuple-element.67), channel_id=1, source_target_pairs={{0,8},{2,10},{4,12},{6,14},{8,0},{10,2},{12,4},{14,6},{16,24},{18,... | collective-permute-start | bytes 393224 | tf_op jit(solution)/shard_map/ppermute | solution.py:451
  47.2 6.9 %collective-permute-start.10 = (bf16[1,4,16,512]{3,2,1,0:T(8,128)(2,1)S(1)}, bf16[1,4,16,512]{3,2,1,0:T(8,128)(2,1)S(1)}, u32[]{:S(2)}, u32[]{:S(2)}) collective-permute-start(bf16[1,4,16,512]{3,2,1,0:T(8,128)(2,1)S(1)} %get-tuple-element.69), channel_id=1, source_target_pairs={{0,16},{2,18},{4,20},{6,22},{8,24},{10,26},{12,28},{14,30},{16,0},... | collective-permute-start | bytes 196616 | tf_op jit(solution)/shard_map/ppermute | solution.py:451
  49.9 5.2 %collective-permute-start.11 = (bf16[1,4,16,512]{3,2,1,0:T(8,128)(2,1)S(1)}, bf16[1,4,16,512]{3,2,1,0:T(8,128)(2,1)S(1)}, u32[]{:S(2)}, u32[]{:S(2)}) collective-permute-start(bf16[1,4,16,512]{3,2,1,0:T(8,128)(2,1)S(1)} %get-tuple-element.70), channel_id=1, source_target_pairs={{0,16},{2,18},{4,20},{6,22},{8,24},{10,26},{12,28},{14,30},{16,0},... | collective-permute-start | bytes 196616 | tf_op jit(solution)/shard_map/ppermute | solution.py:451

commit v9 on v8

--- a/solution.py
+++ b/solution.py
@@ -314,66 +314,37 @@
     return offset & 1, (offset >> 1) * nodes + lax.rem(goal, nodes)
 
 
-LANE_PARTS = 2
-
-
-def sum_kernel(goal_ref, *refs, sources, nodes):
-    count = len(refs) - 2 - LANE_PARTS
-    row_refs, even_ref, odd_ref, totals = refs[:count], refs[count], refs[count + 1], refs[-LANE_PARTS:]
-    slots = even_ref.shape[0]
-    lanes = totals[0].shape[-1]
-    for total_ref in totals:
-        total_ref[...] = jnp.zeros_like(total_ref)
+def sum_kernel(goal_ref, *refs, sources, nodes, start):
+    row_refs, (even_ref, odd_ref, total_ref) = refs[:-3], refs[-3:]
+    slots, _, lanes = even_ref.shape
+    total_ref[...] = jnp.zeros_like(total_ref)
     for row_ref, items in zip(row_refs, sources):
         for i, item in enumerate(items):
             parity, slot = target(goal_ref, item, nodes)
             slot = parity * slots + slot
-            for j, total_ref in enumerate(totals):
-                part = row_ref[i, :, lanes * j : lanes * (j + 1)].astype(F32)
-                total_ref[slot] = (total_ref[slot].astype(F32) + part).astype(BF)
-    for j, total_ref in enumerate(totals):
-        even_ref[:, :, lanes * j : lanes * (j + 1)] = total_ref[:slots].astype(BF)
-        odd_ref[:, :, lanes * j : lanes * (j + 1)] = total_ref[slots:].astype(BF)
-
-
-def sum_rows(goals, arrays, sources, nodes, leaf_count):
-    rows, lanes = arrays[0].shape[1:]
+            part = row_ref[i, :, start : start + lanes].astype(F32)
+            total_ref[slot] = (total_ref[slot].astype(F32) + part).astype(BF)
+    even_ref[...] = total_ref[:slots]
+    odd_ref[...] = total_ref[slots:]
+
+
+def sum_rows(goals, arrays, sources, nodes, leaf_count, start, lanes):
+    rows = arrays[0].shape[1]
     slots = leaf_count // 2 * nodes
     shape = jax.ShapeDtypeStruct((slots, rows, lanes), BF)
     return pl.pallas_call(
-        functools.partial(sum_kernel, sources=sources, nodes=nodes),
+        functools.partial(sum_kernel, sources=sources, nodes=nodes, start=start),
         in_specs=[pl.BlockSpec(memory_space=pltpu.SMEM)]
         + [pl.BlockSpec(memory_space=pltpu.VMEM)] * len(arrays),
         out_specs=[pl.BlockSpec(memory_space=pltpu.VMEM)] * 2,
         out_shape=[shape, shape],
-        scratch_shapes=[pltpu.VMEM((2 * slots, rows, lanes // LANE_PARTS), BF)] * LANE_PARTS,
+        scratch_shapes=[pltpu.VMEM((2 * slots, rows, lanes), BF)],
         compiler_params=pltpu.CompilerParams(vmem_limit_bytes=24 * 1024 * 1024),
     )(goals, *arrays)
 
 
 def place(offset, bit):
     return (offset >> (bit + 1) << bit) | (offset & ((1 << bit) - 1))
-
-
-def first_kernel(even_ref, odd_ref, *outs, bits):
-    lanes = outs[0].shape[-1]
-    for i, bit in enumerate(bits):
-        for r in range(even_ref.shape[0]):
-            here = (slice(None), slice(None), slice(lanes * i, lanes * (i + 1)))
-            total = even_ref[(r,) + here].astype(F32) + odd_ref[(r,) + here].astype(F32)
-            outs[2 * i + (r >> bit & 1)][place(r, bit)] = total.astype(BF)
-
-
-def first_combine(even, odd, bits):
-    offsets, nodes, rows, lanes = even.shape
-    shape = jax.ShapeDtypeStruct((offsets // 2, nodes, rows, lanes // 2), BF)
-    return pl.pallas_call(
-        functools.partial(first_kernel, bits=bits),
-        in_specs=[pl.BlockSpec(memory_space=pltpu.VMEM)] * 2,
-        out_specs=[pl.BlockSpec(memory_space=pltpu.VMEM)] * 4,
-        out_shape=[shape] * 4,
-        compiler_params=pltpu.CompilerParams(vmem_limit_bytes=24 * 1024 * 1024),
-    )(even, odd)
 
 
 def combine_kernel(kept_ref, arrived_ref, keep_ref, send_ref, *, bit):
@@ -503,19 +474,15 @@
             sources += [[goal.size * o + item for o in range(oct_count) for item in items]]
         done += count
 
-    even, odd = sum_rows(goals, arrays, sources, nodes, leaf_count)
-    shape = (leaf_count // 2, nodes) + even.shape[1:]
-    even = even.reshape(shape)
-    odd = swap(odd, "leaf", 1).reshape(shape)
+    lanes = arrays[0].shape[-1] // 2
     masks = [1 << i for i in range(1, (leaf_count - 1).bit_length())]
-    orders = [masks[1::-1] + masks[2:], masks]
-    parts = first_combine(even, odd, [masks.index(order[0]) for order in orders])
     kept, arrived = [], []
-    for i in range(2):
+    for i, order in enumerate((masks[1::-1] + masks[2:], masks)):
+        keep, send = sum_rows(goals, arrays, sources, nodes, leaf_count, lanes * i, lanes)
+        shape = (leaf_count // 2, nodes, -1, lanes)
+        keep, come = keep.reshape(shape), swap(send, "leaf", 1).reshape(shape)
         left = list(masks)
-        left.remove(orders[i][0])
-        keep, come = parts[2 * i], swap(parts[2 * i + 1], "leaf", orders[i][0])
-        for mask in orders[i][1:]:
+        for mask in order:
             keep, send = combine(keep, come, left.index(mask))
             left.remove(mask)
             come = swap(send, "leaf", mask)

time: 56.4 us -> 55.5 us (0.984)
  waiting for transfers between devices: 16.1 us -> 13.7 us
  Pallas kernels: 18.7 us -> 19.6 us
  starting transfers between devices: 18.6 us -> 19.2 us
    ppermute x12 -> x13, waiting for transfers between devices: 16.1 us -> 13.7 us  [swap(): return lax.ppermute(x, axis, [(i, i ^ mask) for i in range(count)])]
    pallas_call x1 -> x2, Pallas kernels: 1.09 us -> 1.84 us  [sum_rows(): pl.pallas_call(functools.partial(sum_kernel, sources=sources, nodes=nodes...]
    ppermute x12 -> x13, starting transfers between devices: 18.6 us -> 19.2 us  [swap(): return lax.ppermute(x, axis, [(i, i ^ mask) for i in range(count)])]
  transfers between devices with their start and end apart: 12 -> 13, of which waited for: 7 -> 7; matrix products, arithmetic and copies ran while one was open for 4% -> 4% of each run, Pallas kernels for 14% -> 17%
where the time goes in v9:
time: 55.5 us; the launch traced here: 55.3 us
  Pallas kernels  19.6 us (35%)
  starting transfers between devices  19.2 us (35%)
  waiting for transfers between devices  13.7 us (25%)
  local copies, waits for them, and re-layouts  2.59 us (5%)
    ppermute x13, starting transfers between devices, swap(): return lax.ppermute(x, axis, [(i, i ^ mask) for i in range(count)])  19.2 us
    ppermute x13, waiting for transfers between devices, swap(): return lax.ppermute(x, axis, [(i, i ^ mask) for i in range(count)])  13.7 us
    pallas_call x3, Pallas kernels, apply_parents(): pl.pallas_call(functools.partial(apply_kernel, half=half, terms=terms, fi...  13.2 us
    unnamed x11, local copies, waits for them, and re-layouts  2.39 us
    pallas_call x1, Pallas kernels, pick_blocks(): pl.pallas_call(pick_kernel, in_specs=[pl.BlockSpec(memory_space=pltpu.SME...  2.23 us
    pallas_call x2, Pallas kernels, sum_rows(): pl.pallas_call(functools.partial(sum_kernel, sources=sources, nodes=nodes...  1.84 us
  transfers between devices with their start and end apart: 13, of which 7 were waited for; matrix products, arithmetic and copies ran while one was open for 4% of the time, Pallas kernels for 17%

profile of v9, /device:TPU:0, one launch (start us, length us, event | category | flops | bytes accessed | tf_op | source)
XLA Modules:
  0.0 55.3 jit_solution(7457618870139083224)
XLA Ops:
  0.0 2.2 %shard_map.73 = (bf16[4,4,16,256]{3,2,1,0:T(8,128)(2,1)}, bf16[4,4,16,256]{3,2,1,0:T(8,128)(2,1)}) custom-call(s32[4,8]{1,0:T(4,128)} %bitcast.16, bf16[32,4096]{1,0:T(8,128)(2,1)} %children_ref.1), custom_call_target="tpu_custom_call" | custom-call | tf_op jit(solution)/shard_map/pallas_call | solution.py:116
  2.2 2.9 %collective-permute-start = (bf16[4,4,16,256]{3,2,1,0:T(8,128)(2,1)}, bf16[4,4,16,256]{3,2,1,0:T(8,128)(2,1)S(1)}, u32[]{:S(2)}, u32[]{:S(2)}) collective-permute-start(bf16[4,4,16,256]{3,2,1,0:T(8,128)(2,1)} %get-tuple-element.41), channel_id=1, source_target_pairs={{0,1},{1,0},{2,3},{3,2},{4,5},{5,4},{6,7},{7,6},{8,9},{9,8},{10,11... | collective-permute-start | bytes 393224 | tf_op jit(solution)/shard_map/ppermute | solution.py:422
  5.2 1.8 %copy.8 = bf16[4,8,240,128]{3,2,1,0:T(8,128)(2,1)S(1)} copy(bf16[4,8,240,128]{3,1,2,0:T(8,128)(2,1)} %bitcast.14) | data formatting | bytes 3932160
  7.0 0.0 copy-start.2
  7.0 0.0 copy-start
  7.0 0.0 copy-start.1
  7.0 0.1 slice.refs_2_
  7.1 0.5 copy-done.2
  7.7 0.9 %shard_map.74 = (bf16[32,256]{1,0:T(8,128)(2,1)S(1)}, bf16[32,128]{1,0:T(8,128)(2,1)S(1)}, bf16[128,256]{1,0:T(8,128)(2,1)S(1)}, bf16[32,128]{1,0:T(8,128)(2,1)S...) custom-call(bf16[32,32]{1,0:T(8,128)(2,1)S(1)} %copy-done.2), custom_call_target="tpu_custom_call" | custom-call | tf_op jit(solution)/shard_map/pallas_call | solution.py:85
  8.6 0.3 collective-permute-done.refs_1_
  8.9 0.0 copy-done
  8.9 0.0 copy-done.1
  8.9 6.1 %shard_map.75 = (bf16[8,16,1024]{2,1,0:T(8,128)(2,1)S(1)}, bf16[8,16,1024]{2,1,0:T(8,128)(2,1)S(1)}) custom-call(s32[4,4]{1,0:T(4,128)S(1)} %copy-done.1, bf16[4,4,16,256]{3,2,1,0:T(8,128)(2,1)S(1)} %copy-done, bf16[4,4,16,256]{3,2,1,0:T(8,128)(2,1)S(1)} %collective-permute-done.refs_1_, bf16[27,240,128]{2,1,0:T(8,128)(2,1)S(1)} %slice.refs_2_, ...), custom_call_target="tpu_custom_call" | custom-call | tf_op jit(solution)/shard_map/pallas_call | solution.py:291
  15.0 1.8 %collective-permute-start.2 = (bf16[8,16,1024]{2,1,0:T(8,128)(2,1)S(1)}, bf16[8,16,1024]{2,1,0:T(8,128)(2,1)S(1)}, u32[]{:S(2)}, u32[]{:S(2)}) collective-permute-start(bf16[8,16,1024]{2,1,0:T(8,128)(2,1)S(1)} %get-tuple-element.54), channel_id=1, source_target_pairs={{0,1},{1,0},{2,3},{3,2},{4,5},{5,4},{6,7},{7,6},{8,9},{9,8},{10,11... | collective-permute-start | bytes 786440 | tf_op jit(solution)/shard_map/ppermute | solution.py:422
  16.7 3.5 %shard_map.76 = (bf16[4,16,1024]{2,1,0:T(8,128)(2,1)S(1)}, bf16[4,16,1024]{2,1,0:T(8,128)(2,1)S(1)}) custom-call(s32[4,4]{1,0:T(4,128)S(1)} %copy-done.1, bf16[4,4,16,256]{3,2,1,0:T(8,128)(2,1)S(1)} %copy-done, bf16[4,4,16,256]{3,2,1,0:T(8,128)(2,1)S(1)} %collective-permute-done.refs_1_, bf16[27,240,128]{2,1,0:T(8,128)(2,1)S(1)} %slice.refs_2_, ...), custom_call_target="tpu_custom_call" | custom-call | tf_op jit(solution)/shard_map/pallas_call | solution.py:291
  20.2 0.0 copy-start.4
  20.2 0.0 copy-start.3
  20.2 0.3 collective-permute-start.3
  20.6 3.6 %shard_map.77 = (bf16[4,16,1024]{2,1,0:T(8,128)(2,1)S(1)}, bf16[4,16,1024]{2,1,0:T(8,128)(2,1)S(1)}) custom-call(s32[4,4]{1,0:T(4,128)S(1)} %copy-done.1, bf16[4,4,16,256]{3,2,1,0:T(8,128)(2,1)S(1)} %copy-done, bf16[4,4,16,256]{3,2,1,0:T(8,128)(2,1)S(1)} %collective-permute-done.refs_1_, bf16[27,240,128]{2,1,0:T(8,128)(2,1)S(1)} %slice.refs_2_, ...), custom_call_target="tpu_custom_call" | custom-call | tf_op jit(solution)/shard_map/pallas_call | solution.py:291
  24.2 1.8 %collective-permute-start.4 = (bf16[4,16,1024]{2,1,0:T(8,128)(2,1)S(1)}, bf16[4,16,1024]{2,1,0:T(8,128)(2,1)S(1)}, u32[]{:S(2)}, u32[]{:S(2)}) collective-permute-start(bf16[4,16,1024]{2,1,0:T(8,128)(2,1)S(1)} %get-tuple-element.58), channel_id=1, source_target_pairs={{0,1},{1,0},{2,3},{3,2},{4,5},{5,4},{6,7},{7,6},{8,9},{9,8},{10,11... | collective-permute-start | bytes 393224 | tf_op jit(solution)/shard_map/ppermute | solution.py:422
  26.0 0.0 copy-done.4
  26.0 0.0 copy-done.3
  26.0 0.1 reshape.22
  26.1 0.3 collective-permute-start.1
  26.4 3.3 %collective-permute-done.1 = s32[16]{0:T(128)S(1)} collective-permute-done((s32[16]{0:T(128)S(1)}, s32[16]{0:T(128)S(1)}, u32[]{:S(2)}, u32[]{:S(2)}) %collective-permute-start.1) | collective-permute-done | bytes 96 | tf_op jit(solution)/shard_map/ppermute | solution.py:422
  29.7 0.1 pad_add_fusion.goal_ref
  29.7 0.0 collective-permute-done.3.refs_3_
  29.7 0.0 collective-permute-done.4.refs_5_
  29.7 0.0 collective-permute-done.2.refs_1_
  29.7 0.9 %shard_map.78 = (bf16[32,16,512]{2,1,0:T(8,128)(2,1)S(1)}, bf16[32,16,512]{2,1,0:T(8,128)(2,1)S(1)}) custom-call(s32[32]{0:T(128)S(1)} %pad_add_fusion.goal_ref, bf16[8,16,1024]{2,1,0:T(8,128)(2,1)S(1)} %get-tuple-element.53.refs_0_, bf16[8,16,1024]{2,1,0:T(8,128)(2,1)S(1)} %collective-permute-done.2.refs_1_, ...), custom_call_target="tpu_custom_call" | custom-call | tf_op jit(solution)/shard_map/pallas_call | solution.py:335
  30.7 0.1 collective-permute-start.5
  30.7 0.9 %shard_map.82 = (bf16[32,16,512]{2,1,0:T(8,128)(2,1)S(1)}, bf16[32,16,512]{2,1,0:T(8,128)(2,1)S(1)}) custom-call(s32[32]{0:T(128)S(1)} %pad_add_fusion.goal_ref, bf16[8,16,1024]{2,1,0:T(8,128)(2,1)S(1)} %get-tuple-element.53.refs_0_, bf16[8,16,1024]{2,1,0:T(8,128)(2,1)S(1)} %collective-permute-done.2.refs_1_, ...), custom_call_target="tpu_custom_call" | custom-call | tf_op jit(solution)/shard_map/pallas_call | solution.py:335
  31.7 0.6 %collective-permute-start.8 = (bf16[32,16,512]{2,1,0:T(8,128)(2,1)S(1)}, bf16[32,16,512]{2,1,0:T(8,128)(2,1)S(1)}, u32[]{:S(2)}, u32[]{:S(2)}) collective-permute-start(bf16[32,16,512]{2,1,0:T(8,128)(2,1)S(1)} %get-tuple-element.67), channel_id=1, source_target_pairs={{0,2},{2,0},{4,6},{6,4},{8,10},{10,8},{12,14},{14,12},{16,18},{18,... | collective-permute-start | bytes 1572872 | tf_op jit(solution)/shard_map/ppermute | solution.py:422
  32.2 0.4 collective-permute-done.5
  32.6 0.1 shard_map.79
  32.8 1.6 %collective-permute-start.6 = (bf16[4,4,16,512]{3,2,1,0:T(8,128)(2,1)S(1)}, bf16[4,4,16,512]{3,2,1,0:T(8,128)(2,1)S(1)}, u32[]{:S(2)}, u32[]{:S(2)}) collective-permute-start(bf16[4,4,16,512]{3,2,1,0:T(8,128)(2,1)S(1)} %get-tuple-element.62), channel_id=1, source_target_pairs={{0,8},{2,10},{4,12},{6,14},{8,0},{10,2},{12,4},{14,6},{16,24},{18,... | collective-permute-start | bytes 786440 | tf_op jit(solution)/shard_map/ppermute | solution.py:422
  34.4 0.0 collective-permute-done.8
  34.4 0.1 shard_map.83
  34.5 1.6 %collective-permute-start.9 = (bf16[4,4,16,512]{3,2,1,0:T(8,128)(2,1)S(1)}, bf16[4,4,16,512]{3,2,1,0:T(8,128)(2,1)S(1)}, u32[]{:S(2)}, u32[]{:S(2)}) collective-permute-start(bf16[4,4,16,512]{3,2,1,0:T(8,128)(2,1)S(1)} %get-tuple-element.69), channel_id=1, source_target_pairs={{0,4},{2,6},{4,0},{6,2},{8,12},{10,14},{12,8},{14,10},{16,20},{18,... | collective-permute-start | bytes 786440 | tf_op jit(solution)/shard_map/ppermute | solution.py:422
  36.1 5.1 %collective-permute-done.6.arrived_ref = bf16[4,4,16,512]{3,2,1,0:T(8,128)(2,1)S(1)} collective-permute-done((bf16[4,4,16,512]{3,2,1,0:T(8,128)(2,1)S(1)}, bf16[4,4,16,512]{3,2,1,0:T(8,128)(2,1)S(1)}, u32[]{:S(2)}, u32[]{:S(2)}) %collective-permute-start.6) | collective-permute-done | bytes 262176 | tf_op jit(solution)/shard_map/ppermute | solution.py:422
  41.2 0.1 shard_map.80
  41.2 1.6 %collective-permute-start.7 = (bf16[2,4,16,512]{3,2,1,0:T(8,128)(2,1)S(1)}, bf16[2,4,16,512]{3,2,1,0:T(8,128)(2,1)S(1)}, u32[]{:S(2)}, u32[]{:S(2)}) collective-permute-start(bf16[2,4,16,512]{3,2,1,0:T(8,128)(2,1)S(1)} %get-tuple-element.64), channel_id=1, source_target_pairs={{0,4},{2,6},{4,0},{6,2},{8,12},{10,14},{12,8},{14,10},{16,20},{18,... | collective-permute-start | bytes 393224 | tf_op jit(solution)/shard_map/ppermute | solution.py:422
  42.8 0.0 collective-permute-done.9.arrived_ref
  42.8 0.1 shard_map.84
  42.9 1.6 %collective-permute-start.10 = (bf16[2,4,16,512]{3,2,1,0:T(8,128)(2,1)S(1)}, bf16[2,4,16,512]{3,2,1,0:T(8,128)(2,1)S(1)}, u32[]{:S(2)}, u32[]{:S(2)}) collective-permute-start(bf16[2,4,16,512]{3,2,1,0:T(8,128)(2,1)S(1)} %get-tuple-element.71), channel_id=1, source_target_pairs={{0,8},{2,10},{4,12},{6,14},{8,0},{10,2},{12,4},{14,6},{16,24},{18,... | collective-permute-start | bytes 393224 | tf_op jit(solution)/shard_map/ppermute | solution.py:422
  44.5 1.7 %collective-permute-done.7.arrived_ref = bf16[2,4,16,512]{3,2,1,0:T(8,128)(2,1)S(1)} collective-permute-done((bf16[2,4,16,512]{3,2,1,0:T(8,128)(2,1)S(1)}, bf16[2,4,16,512]{3,2,1,0:T(8,128)(2,1)S(1)}, u32[]{:S(2)}, u32[]{:S(2)}) %collective-permute-start.7) | collective-permute-done | bytes 131104 | tf_op jit(solution)/shard_map/ppermute | solution.py:422
  46.3 2.7 %collective-permute-start.11 = (bf16[1,4,16,512]{3,2,1,0:T(8,128)(2,1)S(1)}, bf16[1,4,16,512]{3,2,1,0:T(8,128)(2,1)S(1)}, u32[]{:S(2)}, u32[]{:S(2)}) collective-permute-start(bf16[1,4,16,512]{3,2,1,0:T(8,128)(2,1)S(1)} %get-tuple-element.73), channel_id=1, source_target_pairs={{0,16},{2,18},{4,20},{6,22},{8,24},{10,26},{12,28},{14,30},{16,0},... | collective-permute-start | bytes 196616 | tf_op jit(solution)/shard_map/ppermute | solution.py:422
  49.0 0.0 collective-permute-done.10.arrived_ref
  49.0 2.3 %collective-permute-start.12 = (bf16[1,4,16,512]{3,2,1,0:T(8,128)(2,1)S(1)}, bf16[1,4,16,512]{3,2,1,0:T(8,128)(2,1)S(1)}, u32[]{:S(2)}, u32[]{:S(2)}) collective-permute-start(bf16[1,4,16,512]{3,2,1,0:T(8,128)(2,1)S(1)} %get-tuple-element.74), channel_id=1, source_target_pairs={{0,16},{2,18},{4,20},{6,22},{8,24},{10,26},{12,28},{14,30},{16,0},... | collective-permute-start | bytes 196616 | tf_op jit(solution)/shard_map/ppermute | solution.py:422
  51.3 1.9 %collective-permute-done.11.arrived0_ref = bf16[1,4,16,512]{3,2,1,0:T(8,128)(2,1)S(1)} collective-permute-done((bf16[1,4,16,512]{3,2,1,0:T(8,128)(2,1)S(1)}, bf16[1,4,16,512]{3,2,1,0:T(8,128)(2,1)S(1)}, u32[]{:S(2)}, u32[]{:S(2)}) %collective-permute-start.11) | collective-permute-done | bytes 65568 | tf_op jit(solution)/shard_map/ppermute | solution.py:422
  53.3 1.0 %collective-permute-done.12.arrived1_ref = bf16[1,4,16,512]{3,2,1,0:T(8,128)(2,1)S(1)} collective-permute-done((bf16[1,4,16,512]{3,2,1,0:T(8,128)(2,1)S(1)}, bf16[1,4,16,512]{3,2,1,0:T(8,128)(2,1)S(1)}, u32[]{:S(2)}, u32[]{:S(2)}) %collective-permute-start.12) | collective-permute-done | bytes 65568 | tf_op jit(solution)/shard_map/ppermute | solution.py:422
  54.2 1.1 %shard_map.86 = bf16[4,4,4096]{2,1,0:T(4,128)(2,1)} custom-call(bf16[1,4,16,512]{3,2,1,0:T(8,128)(2,1)S(1)} %get-tuple-element.65.kept0_ref, bf16[1,4,16,512]{3,2,1,0:T(8,128)(2,1)S(1)} %get-tuple-element.72.kept1_ref, bf16[1,4,16,512]{3,2,1,0:T(8,128)(2,1)S(1)} %collective-permute-done.11.arrived0_ref, ...), custom_call_target="tpu_custom_call" | custom-call | tf_op jit(solution)/shard_map/pallas_call | solution.py:410
  (4 shorter events, 0.1 us)
Async XLA Ops:
  2.2 6.6 %collective-permute-start = (bf16[4,4,16,256]{3,2,1,0:T(8,128)(2,1)}, bf16[4,4,16,256]{3,2,1,0:T(8,128)(2,1)S(1)}, u32[]{:S(2)}, u32[]{:S(2)}) collective-permute-start(bf16[4,4,16,256]{3,2,1,0:T(8,128)(2,1)} %get-tuple-element.41), channel_id=1, source_target_pairs={{0,1},{1,0},{2,3},{3,2},{4,5},{5,4},{6,7},{7,6},{8,9},{9,8},{10,11... | collective-permute-start | bytes 393224 | tf_op jit(solution)/shard_map/ppermute | solution.py:422
  7.0 0.7 %copy-start.2 = (bf16[32,32]{1,0:T(8,128)(2,1)S(1)}, bf16[32,32]{1,0:T(8,128)(2,1)}, u32[]{:S(2)}) copy-start(bf16[32,32]{1,0:T(8,128)(2,1)} %scale_ref.1) | copy-start | bytes 6148
  7.0 1.9 %copy-start = (bf16[4,4,16,256]{3,2,1,0:T(8,128)(2,1)S(1)}, bf16[4,4,16,256]{3,2,1,0:T(8,128)(2,1)}, u32[]{:S(2)}) copy-start(bf16[4,4,16,256]{3,2,1,0:T(8,128)(2,1)} %get-tuple-element.40.refs_0_) | copy-start | bytes 393220
  7.0 1.9 %copy-start.1 = (s32[4,4]{1,0:T(4,128)S(1)}, s32[4,4]{1,0:T(4,128)}, u32[]{:S(2)}) copy-start(s32[4,4]{1,0:T(4,128)} %kind_ref.5) | copy-start | bytes 196
  15.0 14.8 %collective-permute-start.2 = (bf16[8,16,1024]{2,1,0:T(8,128)(2,1)S(1)}, bf16[8,16,1024]{2,1,0:T(8,128)(2,1)S(1)}, u32[]{:S(2)}, u32[]{:S(2)}) collective-permute-start(bf16[8,16,1024]{2,1,0:T(8,128)(2,1)S(1)} %get-tuple-element.54), channel_id=1, source_target_pairs={{0,1},{1,0},{2,3},{3,2},{4,5},{5,4},{6,7},{7,6},{8,9},{9,8},{10,11... | collective-permute-start | bytes 786440 | tf_op jit(solution)/shard_map/ppermute | solution.py:422
  20.2 5.8 %copy-start.4 = (s32[4,4,1]{1,2,0:T(1,128)S(1)}, s32[4,4,1]{1,2,0:T(1,128)}, u32[]{:S(2)}) copy-start(s32[4,4,1]{1,2,0:T(1,128)} %param.12) | copy-start | bytes 196
  20.2 5.8 %copy-start.3 = (s32[4,4]{1,0:T(4,128)S(1)}, s32[4,4]{1,0:T(4,128)}, u32[]{:S(2)}) copy-start(s32[4,4]{1,0:T(4,128)} %param.13) | copy-start | bytes 196
  20.2 9.5 %collective-permute-start.3 = (bf16[4,16,1024]{2,1,0:T(8,128)(2,1)S(1)}, bf16[4,16,1024]{2,1,0:T(8,128)(2,1)S(1)}, u32[]{:S(2)}, u32[]{:S(2)}) collective-permute-start(bf16[4,16,1024]{2,1,0:T(8,128)(2,1)S(1)} %get-tuple-element.56), channel_id=1, source_target_pairs={{0,1},{1,0},{2,3},{3,2},{4,5},{5,4},{6,7},{7,6},{8,9},{9,8},{10,11... | collective-permute-start | bytes 393224 | tf_op jit(solution)/shard_map/ppermute | solution.py:422
  24.2 5.5 %collective-permute-start.4 = (bf16[4,16,1024]{2,1,0:T(8,128)(2,1)S(1)}, bf16[4,16,1024]{2,1,0:T(8,128)(2,1)S(1)}, u32[]{:S(2)}, u32[]{:S(2)}) collective-permute-start(bf16[4,16,1024]{2,1,0:T(8,128)(2,1)S(1)} %get-tuple-element.58), channel_id=1, source_target_pairs={{0,1},{1,0},{2,3},{3,2},{4,5},{5,4},{6,7},{7,6},{8,9},{9,8},{10,11... | collective-permute-start | bytes 393224 | tf_op jit(solution)/shard_map/ppermute | solution.py:422
  26.1 3.5 %collective-permute-start.1 = (s32[16]{0:T(128)S(1)}, s32[16]{0:T(128)S(1)}, u32[]{:S(2)}, u32[]{:S(2)}) collective-permute-start(s32[16]{0:T(128)S(1)} %reshape.22), channel_id=1, source_target_pairs={{0,1},{1,0},{2,3},{3,2},{4,5},{5,4},{6,7},{7,6},{8,9},{9,8},{10,11... | collective-permute-start | bytes 200 | tf_op jit(solution)/shard_map/ppermute | solution.py:422
  30.7 2.0 %collective-permute-start.5 = (bf16[32,16,512]{2,1,0:T(8,128)(2,1)S(1)}, bf16[32,16,512]{2,1,0:T(8,128)(2,1)S(1)}, u32[]{:S(2)}, u32[]{:S(2)}) collective-permute-start(bf16[32,16,512]{2,1,0:T(8,128)(2,1)S(1)} %get-tuple-element.60), channel_id=1, source_target_pairs={{0,2},{2,0},{4,6},{6,4},{8,10},{10,8},{12,14},{14,12},{16,18},{18,... | collective-permute-start | bytes 1572872 | tf_op jit(solution)/shard_map/ppermute | solution.py:422
  31.7 2.7 %collective-permute-start.8 = (bf16[32,16,512]{2,1,0:T(8,128)(2,1)S(1)}, bf16[32,16,512]{2,1,0:T(8,128)(2,1)S(1)}, u32[]{:S(2)}, u32[]{:S(2)}) collective-permute-start(bf16[32,16,512]{2,1,0:T(8,128)(2,1)S(1)} %get-tuple-element.67), channel_id=1, source_target_pairs={{0,2},{2,0},{4,6},{6,4},{8,10},{10,8},{12,14},{14,12},{16,18},{18,... | collective-permute-start | bytes 1572872 | tf_op jit(solution)/shard_map/ppermute | solution.py:422
  32.8 8.4 %collective-permute-start.6 = (bf16[4,4,16,512]{3,2,1,0:T(8,128)(2,1)S(1)}, bf16[4,4,16,512]{3,2,1,0:T(8,128)(2,1)S(1)}, u32[]{:S(2)}, u32[]{:S(2)}) collective-permute-start(bf16[4,4,16,512]{3,2,1,0:T(8,128)(2,1)S(1)} %get-tuple-element.62), channel_id=1, source_target_pairs={{0,8},{2,10},{4,12},{6,14},{8,0},{10,2},{12,4},{14,6},{16,24},{18,... | collective-permute-start | bytes 786440 | tf_op jit(solution)/shard_map/ppermute | solution.py:422
  34.5 8.3 %collective-permute-start.9 = (bf16[4,4,16,512]{3,2,1,0:T(8,128)(2,1)S(1)}, bf16[4,4,16,512]{3,2,1,0:T(8,128)(2,1)S(1)}, u32[]{:S(2)}, u32[]{:S(2)}) collective-permute-start(bf16[4,4,16,512]{3,2,1,0:T(8,128)(2,1)S(1)} %get-tuple-element.69), channel_id=1, source_target_pairs={{0,4},{2,6},{4,0},{6,2},{8,12},{10,14},{12,8},{14,10},{16,20},{18,... | collective-permute-start | bytes 786440 | tf_op jit(solution)/shard_map/ppermute | solution.py:422
  41.2 5.0 %collective-permute-start.7 = (bf16[2,4,16,512]{3,2,1,0:T(8,128)(2,1)S(1)}, bf16[2,4,16,512]{3,2,1,0:T(8,128)(2,1)S(1)}, u32[]{:S(2)}, u32[]{:S(2)}) collective-permute-start(bf16[2,4,16,512]{3,2,1,0:T(8,128)(2,1)S(1)} %get-tuple-element.64), channel_id=1, source_target_pairs={{0,4},{2,6},{4,0},{6,2},{8,12},{10,14},{12,8},{14,10},{16,20},{18,... | collective-permute-start | bytes 393224 | tf_op jit(solution)/shard_map/ppermute | solution.py:422
  42.9 6.1 %collective-permute-start.10 = (bf16[2,4,16,512]{3,2,1,0:T(8,128)(2,1)S(1)}, bf16[2,4,16,512]{3,2,1,0:T(8,128)(2,1)S(1)}, u32[]{:S(2)}, u32[]{:S(2)}) collective-permute-start(bf16[2,4,16,512]{3,2,1,0:T(8,128)(2,1)S(1)} %get-tuple-element.71), channel_id=1, source_target_pairs={{0,8},{2,10},{4,12},{6,14},{8,0},{10,2},{12,4},{14,6},{16,24},{18,... | collective-permute-start | bytes 393224 | tf_op jit(solution)/shard_map/ppermute | solution.py:422
  46.3 6.9 %collective-permute-start.11 = (bf16[1,4,16,512]{3,2,1,0:T(8,128)(2,1)S(1)}, bf16[1,4,16,512]{3,2,1,0:T(8,128)(2,1)S(1)}, u32[]{:S(2)}, u32[]{:S(2)}) collective-permute-start(bf16[1,4,16,512]{3,2,1,0:T(8,128)(2,1)S(1)} %get-tuple-element.73), channel_id=1, source_target_pairs={{0,16},{2,18},{4,20},{6,22},{8,24},{10,26},{12,28},{14,30},{16,0},... | collective-permute-start | bytes 196616 | tf_op jit(solution)/shard_map/ppermute | solution.py:422
  49.0 5.2 %collective-permute-start.12 = (bf16[1,4,16,512]{3,2,1,0:T(8,128)(2,1)S(1)}, bf16[1,4,16,512]{3,2,1,0:T(8,128)(2,1)S(1)}, u32[]{:S(2)}, u32[]{:S(2)}) collective-permute-start(bf16[1,4,16,512]{3,2,1,0:T(8,128)(2,1)S(1)} %get-tuple-element.74), channel_id=1, source_target_pairs={{0,16},{2,18},{4,20},{6,22},{8,24},{10,26},{12,28},{14,30},{16,0},... | collective-permute-start | bytes 196616 | tf_op jit(solution)/shard_map/ppermute | solution.py:422

commit v10 on v9

--- a/solution.py
+++ b/solution.py
@@ -91,24 +91,26 @@
     )(two_scale)
 
 
-def pick_kernel(slot_ref, children_ref, near_ref, send_ref, wide_ref):
-    blocks, size = children_ref.shape
-    groups = size // 128
-    for v in range(groups):
-        wide_ref[blocks * v : blocks * (v + 1), :] = children_ref[
-            :, 128 * v : 128 * (v + 1)
-        ].astype(F32)
+def pick_kernel(slot_ref, children_ref, near_ref, send_ref):
+    blocks, _ = children_ref.shape
     parents, held, rows, lanes = near_ref.shape
-    across = lanes // 128
+    stacked = jnp.concatenate(
+        [children_ref[:, lanes * p : lanes * (p + 1)] for p in range(rows)], axis=0
+    )
+    row = lax.broadcasted_iota(jnp.int32, (rows, rows * blocks), 0)
+    place = lax.broadcasted_iota(jnp.int32, (rows, rows * blocks), 1) - row * blocks
     mine = lax.axis_index("oct")
     for out_ref, owner in ((send_ref, 1 - mine), (near_ref, mine)):
+        wanted = [
+            (place == slot_ref[j, owner * parents + i]).astype(F32).astype(BF)
+            for i in range(parents)
+            for j in range(held)
+        ]
+        picked = exact(jnp.concatenate(wanted, axis=0), stacked)
         for i in range(parents):
             for j in range(held):
-                slot = slot_ref[j, owner * parents + i]
-                for h in range(across):
-                    out_ref[i, j, :, 128 * h : 128 * (h + 1)] = wide_ref[
-                        pl.ds(blocks * h + slot, rows, stride=blocks * across), :
-                    ].astype(BF)
+                first = rows * (held * i + j)
+                out_ref[i, j] = picked[first : first + rows]
 
 
 def pick_blocks(child_slot, children, parents, half):
@@ -121,7 +123,6 @@
         ],
         out_specs=[pl.BlockSpec(memory_space=pltpu.VMEM)] * 2,
         out_shape=[shape, shape],
-        scratch_shapes=[pltpu.VMEM((children.size // 128 + 2 * children.shape[0], 128), F32)],
         compiler_params=pltpu.CompilerParams(vmem_limit_bytes=60 * 1024 * 1024),
     )(child_slot, children)
 

time: 55.5 us -> 55.1 us (level)
  no operation moved by 1% of the time
where the time goes in v10:
time: 55.1 us; the launch traced here: 54.9 us
  starting transfers between devices  19.2 us (35%)
  Pallas kernels  19.1 us (35%)
  waiting for transfers between devices  13.7 us (25%)
  local copies, waits for them, and re-layouts  2.59 us (5%)
    ppermute x13, starting transfers between devices, swap(): return lax.ppermute(x, axis, [(i, i ^ mask) for i in range(count)])  19.2 us
    ppermute x13, waiting for transfers between devices, swap(): return lax.ppermute(x, axis, [(i, i ^ mask) for i in range(count)])  13.7 us
    pallas_call x3, Pallas kernels, apply_parents(): pl.pallas_call(functools.partial(apply_kernel, half=half, terms=terms, fi...  13 us
    unnamed x11, local copies, waits for them, and re-layouts  2.39 us
    pallas_call x1, Pallas kernels, pick_blocks(): pl.pallas_call(pick_kernel, in_specs=[pl.BlockSpec(memory_space=pltpu.SME...  1.96 us
    pallas_call x2, Pallas kernels, sum_rows(): pl.pallas_call(functools.partial(sum_kernel, sources=sources, nodes=nodes...  1.84 us
  transfers between devices with their start and end apart: 13, of which 7 were waited for; matrix products, arithmetic and copies ran while one was open for 4% of the time, Pallas kernels for 17%

profile of v10, /device:TPU:0, one launch (start us, length us, event | category | flops | bytes accessed | tf_op | source)
XLA Modules:
  0.0 54.9 jit_solution(13992665990554301532)
XLA Ops:
  0.0 2.0 %shard_map.73 = (bf16[4,4,16,256]{3,2,1,0:T(8,128)(2,1)}, bf16[4,4,16,256]{3,2,1,0:T(8,128)(2,1)}) custom-call(s32[4,8]{1,0:T(4,128)} %bitcast.16, bf16[32,4096]{1,0:T(8,128)(2,1)} %children_ref.1), custom_call_target="tpu_custom_call" | custom-call | tf_op jit(solution)/shard_map/pallas_call | solution.py:118
  2.0 2.9 %collective-permute-start = (bf16[4,4,16,256]{3,2,1,0:T(8,128)(2,1)}, bf16[4,4,16,256]{3,2,1,0:T(8,128)(2,1)S(1)}, u32[]{:S(2)}, u32[]{:S(2)}) collective-permute-start(bf16[4,4,16,256]{3,2,1,0:T(8,128)(2,1)} %get-tuple-element.41), channel_id=1, source_target_pairs={{0,1},{1,0},{2,3},{3,2},{4,5},{5,4},{6,7},{7,6},{8,9},{9,8},{10,11... | collective-permute-start | bytes 393224 | tf_op jit(solution)/shard_map/ppermute | solution.py:423
  4.9 1.8 %copy.8 = bf16[4,8,240,128]{3,2,1,0:T(8,128)(2,1)S(1)} copy(bf16[4,8,240,128]{3,1,2,0:T(8,128)(2,1)} %bitcast.14) | data formatting | bytes 3932160
  6.7 0.0 copy-start.2
  6.7 0.0 copy-start
  6.7 0.0 copy-start.1
  6.8 0.1 slice.refs_2_
  6.9 0.5 copy-done.2
  7.4 0.9 %shard_map.74 = (bf16[32,256]{1,0:T(8,128)(2,1)S(1)}, bf16[32,128]{1,0:T(8,128)(2,1)S(1)}, bf16[128,256]{1,0:T(8,128)(2,1)S(1)}, bf16[32,128]{1,0:T(8,128)(2,1)S...) custom-call(bf16[32,32]{1,0:T(8,128)(2,1)S(1)} %copy-done.2), custom_call_target="tpu_custom_call" | custom-call | tf_op jit(solution)/shard_map/pallas_call | solution.py:85
  8.3 0.3 collective-permute-done.refs_1_
  8.6 0.0 copy-done
  8.6 0.0 copy-done.1
  8.6 6.1 %shard_map.75 = (bf16[8,16,1024]{2,1,0:T(8,128)(2,1)S(1)}, bf16[8,16,1024]{2,1,0:T(8,128)(2,1)S(1)}) custom-call(s32[4,4]{1,0:T(4,128)S(1)} %copy-done.1, bf16[4,4,16,256]{3,2,1,0:T(8,128)(2,1)S(1)} %copy-done, bf16[4,4,16,256]{3,2,1,0:T(8,128)(2,1)S(1)} %collective-permute-done.refs_1_, bf16[27,240,128]{2,1,0:T(8,128)(2,1)S(1)} %slice.refs_2_, ...), custom_call_target="tpu_custom_call" | custom-call | tf_op jit(solution)/shard_map/pallas_call | solution.py:292
  14.7 1.8 %collective-permute-start.2 = (bf16[8,16,1024]{2,1,0:T(8,128)(2,1)S(1)}, bf16[8,16,1024]{2,1,0:T(8,128)(2,1)S(1)}, u32[]{:S(2)}, u32[]{:S(2)}) collective-permute-start(bf16[8,16,1024]{2,1,0:T(8,128)(2,1)S(1)} %get-tuple-element.54), channel_id=1, source_target_pairs={{0,1},{1,0},{2,3},{3,2},{4,5},{5,4},{6,7},{7,6},{8,9},{9,8},{10,11... | collective-permute-start | bytes 786440 | tf_op jit(solution)/shard_map/ppermute | solution.py:423
  16.5 3.5 %shard_map.76 = (bf16[4,16,1024]{2,1,0:T(8,128)(2,1)S(1)}, bf16[4,16,1024]{2,1,0:T(8,128)(2,1)S(1)}) custom-call(s32[4,4]{1,0:T(4,128)S(1)} %copy-done.1, bf16[4,4,16,256]{3,2,1,0:T(8,128)(2,1)S(1)} %copy-done, bf16[4,4,16,256]{3,2,1,0:T(8,128)(2,1)S(1)} %collective-permute-done.refs_1_, bf16[27,240,128]{2,1,0:T(8,128)(2,1)S(1)} %slice.refs_2_, ...), custom_call_target="tpu_custom_call" | custom-call | tf_op jit(solution)/shard_map/pallas_call | solution.py:292
  19.9 0.0 copy-start.4
  19.9 0.0 copy-start.3
  20.0 0.3 collective-permute-start.3
  20.3 3.5 %shard_map.77 = (bf16[4,16,1024]{2,1,0:T(8,128)(2,1)S(1)}, bf16[4,16,1024]{2,1,0:T(8,128)(2,1)S(1)}) custom-call(s32[4,4]{1,0:T(4,128)S(1)} %copy-done.1, bf16[4,4,16,256]{3,2,1,0:T(8,128)(2,1)S(1)} %copy-done, bf16[4,4,16,256]{3,2,1,0:T(8,128)(2,1)S(1)} %collective-permute-done.refs_1_, bf16[27,240,128]{2,1,0:T(8,128)(2,1)S(1)} %slice.refs_2_, ...), custom_call_target="tpu_custom_call" | custom-call | tf_op jit(solution)/shard_map/pallas_call | solution.py:292
  23.8 1.8 %collective-permute-start.4 = (bf16[4,16,1024]{2,1,0:T(8,128)(2,1)S(1)}, bf16[4,16,1024]{2,1,0:T(8,128)(2,1)S(1)}, u32[]{:S(2)}, u32[]{:S(2)}) collective-permute-start(bf16[4,16,1024]{2,1,0:T(8,128)(2,1)S(1)} %get-tuple-element.58), channel_id=1, source_target_pairs={{0,1},{1,0},{2,3},{3,2},{4,5},{5,4},{6,7},{7,6},{8,9},{9,8},{10,11... | collective-permute-start | bytes 393224 | tf_op jit(solution)/shard_map/ppermute | solution.py:423
  25.6 0.0 copy-done.4
  25.6 0.0 copy-done.3
  25.6 0.1 reshape.22
  25.7 0.3 collective-permute-start.1
  26.0 3.3 %collective-permute-done.1 = s32[16]{0:T(128)S(1)} collective-permute-done((s32[16]{0:T(128)S(1)}, s32[16]{0:T(128)S(1)}, u32[]{:S(2)}, u32[]{:S(2)}) %collective-permute-start.1) | collective-permute-done | bytes 96 | tf_op jit(solution)/shard_map/ppermute | solution.py:423
  29.2 0.1 pad_add_fusion.goal_ref
  29.3 0.0 collective-permute-done.3.refs_3_
  29.3 0.0 collective-permute-done.4.refs_5_
  29.3 0.0 collective-permute-done.2.refs_1_
  29.3 0.9 %shard_map.78 = (bf16[32,16,512]{2,1,0:T(8,128)(2,1)S(1)}, bf16[32,16,512]{2,1,0:T(8,128)(2,1)S(1)}) custom-call(s32[32]{0:T(128)S(1)} %pad_add_fusion.goal_ref, bf16[8,16,1024]{2,1,0:T(8,128)(2,1)S(1)} %get-tuple-element.53.refs_0_, bf16[8,16,1024]{2,1,0:T(8,128)(2,1)S(1)} %collective-permute-done.2.refs_1_, ...), custom_call_target="tpu_custom_call" | custom-call | tf_op jit(solution)/shard_map/pallas_call | solution.py:336
  30.2 0.1 collective-permute-start.5
  30.3 0.9 %shard_map.82 = (bf16[32,16,512]{2,1,0:T(8,128)(2,1)S(1)}, bf16[32,16,512]{2,1,0:T(8,128)(2,1)S(1)}) custom-call(s32[32]{0:T(128)S(1)} %pad_add_fusion.goal_ref, bf16[8,16,1024]{2,1,0:T(8,128)(2,1)S(1)} %get-tuple-element.53.refs_0_, bf16[8,16,1024]{2,1,0:T(8,128)(2,1)S(1)} %collective-permute-done.2.refs_1_, ...), custom_call_target="tpu_custom_call" | custom-call | tf_op jit(solution)/shard_map/pallas_call | solution.py:336
  31.2 0.6 %collective-permute-start.8 = (bf16[32,16,512]{2,1,0:T(8,128)(2,1)S(1)}, bf16[32,16,512]{2,1,0:T(8,128)(2,1)S(1)}, u32[]{:S(2)}, u32[]{:S(2)}) collective-permute-start(bf16[32,16,512]{2,1,0:T(8,128)(2,1)S(1)} %get-tuple-element.67), channel_id=1, source_target_pairs={{0,2},{2,0},{4,6},{6,4},{8,10},{10,8},{12,14},{14,12},{16,18},{18,... | collective-permute-start | bytes 1572872 | tf_op jit(solution)/shard_map/ppermute | solution.py:423
  31.8 0.4 collective-permute-done.5
  32.2 0.1 shard_map.79
  32.3 1.6 %collective-permute-start.6 = (bf16[4,4,16,512]{3,2,1,0:T(8,128)(2,1)S(1)}, bf16[4,4,16,512]{3,2,1,0:T(8,128)(2,1)S(1)}, u32[]{:S(2)}, u32[]{:S(2)}) collective-permute-start(bf16[4,4,16,512]{3,2,1,0:T(8,128)(2,1)S(1)} %get-tuple-element.62), channel_id=1, source_target_pairs={{0,8},{2,10},{4,12},{6,14},{8,0},{10,2},{12,4},{14,6},{16,24},{18,... | collective-permute-start | bytes 786440 | tf_op jit(solution)/shard_map/ppermute | solution.py:423
  34.0 0.0 collective-permute-done.8
  34.0 0.1 shard_map.83
  34.1 1.6 %collective-permute-start.9 = (bf16[4,4,16,512]{3,2,1,0:T(8,128)(2,1)S(1)}, bf16[4,4,16,512]{3,2,1,0:T(8,128)(2,1)S(1)}, u32[]{:S(2)}, u32[]{:S(2)}) collective-permute-start(bf16[4,4,16,512]{3,2,1,0:T(8,128)(2,1)S(1)} %get-tuple-element.69), channel_id=1, source_target_pairs={{0,4},{2,6},{4,0},{6,2},{8,12},{10,14},{12,8},{14,10},{16,20},{18,... | collective-permute-start | bytes 786440 | tf_op jit(solution)/shard_map/ppermute | solution.py:423
  35.7 5.1 %collective-permute-done.6.arrived_ref = bf16[4,4,16,512]{3,2,1,0:T(8,128)(2,1)S(1)} collective-permute-done((bf16[4,4,16,512]{3,2,1,0:T(8,128)(2,1)S(1)}, bf16[4,4,16,512]{3,2,1,0:T(8,128)(2,1)S(1)}, u32[]{:S(2)}, u32[]{:S(2)}) %collective-permute-start.6) | collective-permute-done | bytes 262176 | tf_op jit(solution)/shard_map/ppermute | solution.py:423
  40.7 0.1 shard_map.80
  40.8 1.6 %collective-permute-start.7 = (bf16[2,4,16,512]{3,2,1,0:T(8,128)(2,1)S(1)}, bf16[2,4,16,512]{3,2,1,0:T(8,128)(2,1)S(1)}, u32[]{:S(2)}, u32[]{:S(2)}) collective-permute-start(bf16[2,4,16,512]{3,2,1,0:T(8,128)(2,1)S(1)} %get-tuple-element.64), channel_id=1, source_target_pairs={{0,4},{2,6},{4,0},{6,2},{8,12},{10,14},{12,8},{14,10},{16,20},{18,... | collective-permute-start | bytes 393224 | tf_op jit(solution)/shard_map/ppermute | solution.py:423
  42.4 0.0 collective-permute-done.9.arrived_ref
  42.4 0.1 shard_map.84
  42.5 1.6 %collective-permute-start.10 = (bf16[2,4,16,512]{3,2,1,0:T(8,128)(2,1)S(1)}, bf16[2,4,16,512]{3,2,1,0:T(8,128)(2,1)S(1)}, u32[]{:S(2)}, u32[]{:S(2)}) collective-permute-start(bf16[2,4,16,512]{3,2,1,0:T(8,128)(2,1)S(1)} %get-tuple-element.71), channel_id=1, source_target_pairs={{0,8},{2,10},{4,12},{6,14},{8,0},{10,2},{12,4},{14,6},{16,24},{18,... | collective-permute-start | bytes 393224 | tf_op jit(solution)/shard_map/ppermute | solution.py:423
  44.1 1.7 %collective-permute-done.7.arrived_ref = bf16[2,4,16,512]{3,2,1,0:T(8,128)(2,1)S(1)} collective-permute-done((bf16[2,4,16,512]{3,2,1,0:T(8,128)(2,1)S(1)}, bf16[2,4,16,512]{3,2,1,0:T(8,128)(2,1)S(1)}, u32[]{:S(2)}, u32[]{:S(2)}) %collective-permute-start.7) | collective-permute-done | bytes 131104 | tf_op jit(solution)/shard_map/ppermute | solution.py:423
  45.9 2.7 %collective-permute-start.11 = (bf16[1,4,16,512]{3,2,1,0:T(8,128)(2,1)S(1)}, bf16[1,4,16,512]{3,2,1,0:T(8,128)(2,1)S(1)}, u32[]{:S(2)}, u32[]{:S(2)}) collective-permute-start(bf16[1,4,16,512]{3,2,1,0:T(8,128)(2,1)S(1)} %get-tuple-element.73), channel_id=1, source_target_pairs={{0,16},{2,18},{4,20},{6,22},{8,24},{10,26},{12,28},{14,30},{16,0},... | collective-permute-start | bytes 196616 | tf_op jit(solution)/shard_map/ppermute | solution.py:423
  48.5 0.0 collective-permute-done.10.arrived_ref
  48.6 2.3 %collective-permute-start.12 = (bf16[1,4,16,512]{3,2,1,0:T(8,128)(2,1)S(1)}, bf16[1,4,16,512]{3,2,1,0:T(8,128)(2,1)S(1)}, u32[]{:S(2)}, u32[]{:S(2)}) collective-permute-start(bf16[1,4,16,512]{3,2,1,0:T(8,128)(2,1)S(1)} %get-tuple-element.74), channel_id=1, source_target_pairs={{0,16},{2,18},{4,20},{6,22},{8,24},{10,26},{12,28},{14,30},{16,0},... | collective-permute-start | bytes 196616 | tf_op jit(solution)/shard_map/ppermute | solution.py:423
  50.9 1.9 %collective-permute-done.11.arrived0_ref = bf16[1,4,16,512]{3,2,1,0:T(8,128)(2,1)S(1)} collective-permute-done((bf16[1,4,16,512]{3,2,1,0:T(8,128)(2,1)S(1)}, bf16[1,4,16,512]{3,2,1,0:T(8,128)(2,1)S(1)}, u32[]{:S(2)}, u32[]{:S(2)}) %collective-permute-start.11) | collective-permute-done | bytes 65568 | tf_op jit(solution)/shard_map/ppermute | solution.py:423
  52.8 1.0 %collective-permute-done.12.arrived1_ref = bf16[1,4,16,512]{3,2,1,0:T(8,128)(2,1)S(1)} collective-permute-done((bf16[1,4,16,512]{3,2,1,0:T(8,128)(2,1)S(1)}, bf16[1,4,16,512]{3,2,1,0:T(8,128)(2,1)S(1)}, u32[]{:S(2)}, u32[]{:S(2)}) %collective-permute-start.12) | collective-permute-done | bytes 65568 | tf_op jit(solution)/shard_map/ppermute | solution.py:423
  53.8 1.1 %shard_map.86 = bf16[4,4,4096]{2,1,0:T(4,128)(2,1)} custom-call(bf16[1,4,16,512]{3,2,1,0:T(8,128)(2,1)S(1)} %get-tuple-element.65.kept0_ref, bf16[1,4,16,512]{3,2,1,0:T(8,128)(2,1)S(1)} %get-tuple-element.72.kept1_ref, bf16[1,4,16,512]{3,2,1,0:T(8,128)(2,1)S(1)} %collective-permute-done.11.arrived0_ref, ...), custom_call_target="tpu_custom_call" | custom-call | tf_op jit(solution)/shard_map/pallas_call | solution.py:411
  (4 shorter events, 0.1 us)
Async XLA Ops:
  2.0 6.6 %collective-permute-start = (bf16[4,4,16,256]{3,2,1,0:T(8,128)(2,1)}, bf16[4,4,16,256]{3,2,1,0:T(8,128)(2,1)S(1)}, u32[]{:S(2)}, u32[]{:S(2)}) collective-permute-start(bf16[4,4,16,256]{3,2,1,0:T(8,128)(2,1)} %get-tuple-element.41), channel_id=1, source_target_pairs={{0,1},{1,0},{2,3},{3,2},{4,5},{5,4},{6,7},{7,6},{8,9},{9,8},{10,11... | collective-permute-start | bytes 393224 | tf_op jit(solution)/shard_map/ppermute | solution.py:423
  6.7 0.7 %copy-start.2 = (bf16[32,32]{1,0:T(8,128)(2,1)S(1)}, bf16[32,32]{1,0:T(8,128)(2,1)}, u32[]{:S(2)}) copy-start(bf16[32,32]{1,0:T(8,128)(2,1)} %scale_ref.1) | copy-start | bytes 6148
  6.7 1.9 %copy-start = (bf16[4,4,16,256]{3,2,1,0:T(8,128)(2,1)S(1)}, bf16[4,4,16,256]{3,2,1,0:T(8,128)(2,1)}, u32[]{:S(2)}) copy-start(bf16[4,4,16,256]{3,2,1,0:T(8,128)(2,1)} %get-tuple-element.40.refs_0_) | copy-start | bytes 393220
  6.7 1.9 %copy-start.1 = (s32[4,4]{1,0:T(4,128)S(1)}, s32[4,4]{1,0:T(4,128)}, u32[]{:S(2)}) copy-start(s32[4,4]{1,0:T(4,128)} %kind_ref.5) | copy-start | bytes 196
  14.7 14.6 %collective-permute-start.2 = (bf16[8,16,1024]{2,1,0:T(8,128)(2,1)S(1)}, bf16[8,16,1024]{2,1,0:T(8,128)(2,1)S(1)}, u32[]{:S(2)}, u32[]{:S(2)}) collective-permute-start(bf16[8,16,1024]{2,1,0:T(8,128)(2,1)S(1)} %get-tuple-element.54), channel_id=1, source_target_pairs={{0,1},{1,0},{2,3},{3,2},{4,5},{5,4},{6,7},{7,6},{8,9},{9,8},{10,11... | collective-permute-start | bytes 786440 | tf_op jit(solution)/shard_map/ppermute | solution.py:423
  19.9 5.6 %copy-start.4 = (s32[4,4,1]{1,2,0:T(1,128)S(1)}, s32[4,4,1]{1,2,0:T(1,128)}, u32[]{:S(2)}) copy-start(s32[4,4,1]{1,2,0:T(1,128)} %param.12) | copy-start | bytes 196
  19.9 5.6 %copy-start.3 = (s32[4,4]{1,0:T(4,128)S(1)}, s32[4,4]{1,0:T(4,128)}, u32[]{:S(2)}) copy-start(s32[4,4]{1,0:T(4,128)} %param.13) | copy-start | bytes 196
  20.0 9.3 %collective-permute-start.3 = (bf16[4,16,1024]{2,1,0:T(8,128)(2,1)S(1)}, bf16[4,16,1024]{2,1,0:T(8,128)(2,1)S(1)}, u32[]{:S(2)}, u32[]{:S(2)}) collective-permute-start(bf16[4,16,1024]{2,1,0:T(8,128)(2,1)S(1)} %get-tuple-element.56), channel_id=1, source_target_pairs={{0,1},{1,0},{2,3},{3,2},{4,5},{5,4},{6,7},{7,6},{8,9},{9,8},{10,11... | collective-permute-start | bytes 393224 | tf_op jit(solution)/shard_map/ppermute | solution.py:423
  23.8 5.5 %collective-permute-start.4 = (bf16[4,16,1024]{2,1,0:T(8,128)(2,1)S(1)}, bf16[4,16,1024]{2,1,0:T(8,128)(2,1)S(1)}, u32[]{:S(2)}, u32[]{:S(2)}) collective-permute-start(bf16[4,16,1024]{2,1,0:T(8,128)(2,1)S(1)} %get-tuple-element.58), channel_id=1, source_target_pairs={{0,1},{1,0},{2,3},{3,2},{4,5},{5,4},{6,7},{7,6},{8,9},{9,8},{10,11... | collective-permute-start | bytes 393224 | tf_op jit(solution)/shard_map/ppermute | solution.py:423
  25.7 3.5 %collective-permute-start.1 = (s32[16]{0:T(128)S(1)}, s32[16]{0:T(128)S(1)}, u32[]{:S(2)}, u32[]{:S(2)}) collective-permute-start(s32[16]{0:T(128)S(1)} %reshape.22), channel_id=1, source_target_pairs={{0,1},{1,0},{2,3},{3,2},{4,5},{5,4},{6,7},{7,6},{8,9},{9,8},{10,11... | collective-permute-start | bytes 200 | tf_op jit(solution)/shard_map/ppermute | solution.py:423
  30.2 2.0 %collective-permute-start.5 = (bf16[32,16,512]{2,1,0:T(8,128)(2,1)S(1)}, bf16[32,16,512]{2,1,0:T(8,128)(2,1)S(1)}, u32[]{:S(2)}, u32[]{:S(2)}) collective-permute-start(bf16[32,16,512]{2,1,0:T(8,128)(2,1)S(1)} %get-tuple-element.60), channel_id=1, source_target_pairs={{0,2},{2,0},{4,6},{6,4},{8,10},{10,8},{12,14},{14,12},{16,18},{18,... | collective-permute-start | bytes 1572872 | tf_op jit(solution)/shard_map/ppermute | solution.py:423
  31.2 2.7 %collective-permute-start.8 = (bf16[32,16,512]{2,1,0:T(8,128)(2,1)S(1)}, bf16[32,16,512]{2,1,0:T(8,128)(2,1)S(1)}, u32[]{:S(2)}, u32[]{:S(2)}) collective-permute-start(bf16[32,16,512]{2,1,0:T(8,128)(2,1)S(1)} %get-tuple-element.67), channel_id=1, source_target_pairs={{0,2},{2,0},{4,6},{6,4},{8,10},{10,8},{12,14},{14,12},{16,18},{18,... | collective-permute-start | bytes 1572872 | tf_op jit(solution)/shard_map/ppermute | solution.py:423
  32.3 8.4 %collective-permute-start.6 = (bf16[4,4,16,512]{3,2,1,0:T(8,128)(2,1)S(1)}, bf16[4,4,16,512]{3,2,1,0:T(8,128)(2,1)S(1)}, u32[]{:S(2)}, u32[]{:S(2)}) collective-permute-start(bf16[4,4,16,512]{3,2,1,0:T(8,128)(2,1)S(1)} %get-tuple-element.62), channel_id=1, source_target_pairs={{0,8},{2,10},{4,12},{6,14},{8,0},{10,2},{12,4},{14,6},{16,24},{18,... | collective-permute-start | bytes 786440 | tf_op jit(solution)/shard_map/ppermute | solution.py:423
  34.1 8.3 %collective-permute-start.9 = (bf16[4,4,16,512]{3,2,1,0:T(8,128)(2,1)S(1)}, bf16[4,4,16,512]{3,2,1,0:T(8,128)(2,1)S(1)}, u32[]{:S(2)}, u32[]{:S(2)}) collective-permute-start(bf16[4,4,16,512]{3,2,1,0:T(8,128)(2,1)S(1)} %get-tuple-element.69), channel_id=1, source_target_pairs={{0,4},{2,6},{4,0},{6,2},{8,12},{10,14},{12,8},{14,10},{16,20},{18,... | collective-permute-start | bytes 786440 | tf_op jit(solution)/shard_map/ppermute | solution.py:423
  40.8 5.0 %collective-permute-start.7 = (bf16[2,4,16,512]{3,2,1,0:T(8,128)(2,1)S(1)}, bf16[2,4,16,512]{3,2,1,0:T(8,128)(2,1)S(1)}, u32[]{:S(2)}, u32[]{:S(2)}) collective-permute-start(bf16[2,4,16,512]{3,2,1,0:T(8,128)(2,1)S(1)} %get-tuple-element.64), channel_id=1, source_target_pairs={{0,4},{2,6},{4,0},{6,2},{8,12},{10,14},{12,8},{14,10},{16,20},{18,... | collective-permute-start | bytes 393224 | tf_op jit(solution)/shard_map/ppermute | solution.py:423
  42.5 6.1 %collective-permute-start.10 = (bf16[2,4,16,512]{3,2,1,0:T(8,128)(2,1)S(1)}, bf16[2,4,16,512]{3,2,1,0:T(8,128)(2,1)S(1)}, u32[]{:S(2)}, u32[]{:S(2)}) collective-permute-start(bf16[2,4,16,512]{3,2,1,0:T(8,128)(2,1)S(1)} %get-tuple-element.71), channel_id=1, source_target_pairs={{0,8},{2,10},{4,12},{6,14},{8,0},{10,2},{12,4},{14,6},{16,24},{18,... | collective-permute-start | bytes 393224 | tf_op jit(solution)/shard_map/ppermute | solution.py:423
  45.9 6.9 %collective-permute-start.11 = (bf16[1,4,16,512]{3,2,1,0:T(8,128)(2,1)S(1)}, bf16[1,4,16,512]{3,2,1,0:T(8,128)(2,1)S(1)}, u32[]{:S(2)}, u32[]{:S(2)}) collective-permute-start(bf16[1,4,16,512]{3,2,1,0:T(8,128)(2,1)S(1)} %get-tuple-element.73), channel_id=1, source_target_pairs={{0,16},{2,18},{4,20},{6,22},{8,24},{10,26},{12,28},{14,30},{16,0},... | collective-permute-start | bytes 196616 | tf_op jit(solution)/shard_map/ppermute | solution.py:423
  48.6 5.2 %collective-permute-start.12 = (bf16[1,4,16,512]{3,2,1,0:T(8,128)(2,1)S(1)}, bf16[1,4,16,512]{3,2,1,0:T(8,128)(2,1)S(1)}, u32[]{:S(2)}, u32[]{:S(2)}) collective-permute-start(bf16[1,4,16,512]{3,2,1,0:T(8,128)(2,1)S(1)} %get-tuple-element.74), channel_id=1, source_target_pairs={{0,16},{2,18},{4,20},{6,22},{8,24},{10,26},{12,28},{14,30},{16,0},... | collective-permute-start | bytes 196616 | tf_op jit(solution)/shard_map/ppermute | solution.py:423

commit v11 on v10

--- a/solution.py
+++ b/solution.py
@@ -366,7 +366,9 @@
     )(kept, arrived)
 
 
-def last_kernel(kept0_ref, kept1_ref, arrived0_ref, arrived1_ref, out_ref, wide_ref):
+def last_kernel(
+    kept0_ref, kept1_ref, arrived0_ref, arrived1_ref, result_ref, out_ref, wide_ref, sem
+):
     nodes, octants, size = out_ref.shape
     groups = size // 128
     rows, lanes = kept0_ref.shape[2:]
@@ -400,20 +402,29 @@
                 part = total[:, 128 * h : 128 * (h + 1)]
                 for n in range(nodes):
                     store(part, n, i * (lanes // 128) + h, lanes // 64)
+    copies = []
     for n in range(nodes):
         for v in range(groups):
             out_ref[n, :, 128 * v : 128 * (v + 1)] = wide_ref[
                 pl.ds(n * octants * groups + v, octants, stride=groups), :
             ].astype(BF)
+        copies.append(pltpu.make_async_copy(out_ref.at[n], result_ref.at[n], sem.at[n]))
+        copies[-1].start()
+    for copy in copies:
+        copy.wait()
 
 
 def last_combine(kept, arrived, shape):
     return pl.pallas_call(
         last_kernel,
         in_specs=[pl.BlockSpec(memory_space=pltpu.VMEM)] * 4,
-        out_specs=pl.BlockSpec(memory_space=pltpu.VMEM),
+        out_specs=pl.BlockSpec(memory_space=pl.ANY),
         out_shape=jax.ShapeDtypeStruct(shape, BF),
-        scratch_shapes=[pltpu.VMEM((math.prod(shape) // 128, 128), F32)],
+        scratch_shapes=[
+            pltpu.VMEM(shape, BF),
+            pltpu.VMEM((math.prod(shape) // 128, 128), F32),
+            pltpu.SemaphoreType.DMA(shape[:1]),
+        ],
         compiler_params=pltpu.CompilerParams(vmem_limit_bytes=24 * 1024 * 1024),
     )(*kept, *arrived)
 

time: 55.1 us -> 55.1 us (level)
  no operation moved by 1% of the time
where the time goes in v11:
time: 55.1 us; the launch traced here: 54.8 us
  starting transfers between devices  19.2 us (35%)
  Pallas kernels  19.1 us (35%)
  waiting for transfers between devices  13.7 us (25%)
  local copies, waits for them, and re-layouts  2.59 us (5%)
    ppermute x13, starting transfers between devices, swap(): return lax.ppermute(x, axis, [(i, i ^ mask) for i in range(count)])  19.2 us
    ppermute x13, waiting for transfers between devices, swap(): return lax.ppermute(x, axis, [(i, i ^ mask) for i in range(count)])  13.7 us
    pallas_call x3, Pallas kernels, apply_parents(): pl.pallas_call(functools.partial(apply_kernel, half=half, terms=terms, fi...  13 us
    unnamed x11, local copies, waits for them, and re-layouts  2.39 us
    pallas_call x1, Pallas kernels, pick_blocks(): pl.pallas_call(pick_kernel, in_specs=[pl.BlockSpec(memory_space=pltpu.SME...  1.96 us
    pallas_call x2, Pallas kernels, sum_rows(): pl.pallas_call(functools.partial(sum_kernel, sources=sources, nodes=nodes...  1.84 us
  transfers between devices with their start and end apart: 13, of which 7 were waited for; matrix products, arithmetic and copies ran while one was open for 4% of the time, Pallas kernels for 17%

profile of v11, /device:TPU:0, one launch (start us, length us, event | category | flops | bytes accessed | tf_op | source)
XLA Modules:
  0.0 54.8 jit_solution(13393405388560771927)
XLA Ops:
  0.0 2.0 %shard_map.73 = (bf16[4,4,16,256]{3,2,1,0:T(8,128)(2,1)}, bf16[4,4,16,256]{3,2,1,0:T(8,128)(2,1)}) custom-call(s32[4,8]{1,0:T(4,128)} %bitcast.16, bf16[32,4096]{1,0:T(8,128)(2,1)} %children_ref.1), custom_call_target="tpu_custom_call" | custom-call | tf_op jit(solution)/shard_map/pallas_call | solution.py:118
  2.0 2.9 %collective-permute-start = (bf16[4,4,16,256]{3,2,1,0:T(8,128)(2,1)}, bf16[4,4,16,256]{3,2,1,0:T(8,128)(2,1)S(1)}, u32[]{:S(2)}, u32[]{:S(2)}) collective-permute-start(bf16[4,4,16,256]{3,2,1,0:T(8,128)(2,1)} %get-tuple-element.41), channel_id=1, source_target_pairs={{0,1},{1,0},{2,3},{3,2},{4,5},{5,4},{6,7},{7,6},{8,9},{9,8},{10,11... | collective-permute-start | bytes 393224 | tf_op jit(solution)/shard_map/ppermute | solution.py:434
  4.9 1.8 %copy.8 = bf16[4,8,240,128]{3,2,1,0:T(8,128)(2,1)S(1)} copy(bf16[4,8,240,128]{3,1,2,0:T(8,128)(2,1)} %bitcast.14) | data formatting | bytes 3932160
  6.7 0.0 copy-start.2
  6.7 0.0 copy-start
  6.7 0.0 copy-start.1
  6.8 0.1 slice.refs_2_
  6.9 0.5 copy-done.2
  7.4 0.9 %shard_map.74 = (bf16[32,256]{1,0:T(8,128)(2,1)S(1)}, bf16[32,128]{1,0:T(8,128)(2,1)S(1)}, bf16[128,256]{1,0:T(8,128)(2,1)S(1)}, bf16[32,128]{1,0:T(8,128)(2,1)S...) custom-call(bf16[32,32]{1,0:T(8,128)(2,1)S(1)} %copy-done.2), custom_call_target="tpu_custom_call" | custom-call | tf_op jit(solution)/shard_map/pallas_call | solution.py:85
  8.3 0.3 collective-permute-done.refs_1_
  8.6 0.0 copy-done
  8.6 0.0 copy-done.1
  8.6 6.1 %shard_map.75 = (bf16[8,16,1024]{2,1,0:T(8,128)(2,1)S(1)}, bf16[8,16,1024]{2,1,0:T(8,128)(2,1)S(1)}) custom-call(s32[4,4]{1,0:T(4,128)S(1)} %copy-done.1, bf16[4,4,16,256]{3,2,1,0:T(8,128)(2,1)S(1)} %copy-done, bf16[4,4,16,256]{3,2,1,0:T(8,128)(2,1)S(1)} %collective-permute-done.refs_1_, bf16[27,240,128]{2,1,0:T(8,128)(2,1)S(1)} %slice.refs_2_, ...), custom_call_target="tpu_custom_call" | custom-call | tf_op jit(solution)/shard_map/pallas_call | solution.py:292
  14.7 1.8 %collective-permute-start.2 = (bf16[8,16,1024]{2,1,0:T(8,128)(2,1)S(1)}, bf16[8,16,1024]{2,1,0:T(8,128)(2,1)S(1)}, u32[]{:S(2)}, u32[]{:S(2)}) collective-permute-start(bf16[8,16,1024]{2,1,0:T(8,128)(2,1)S(1)} %get-tuple-element.54), channel_id=1, source_target_pairs={{0,1},{1,0},{2,3},{3,2},{4,5},{5,4},{6,7},{7,6},{8,9},{9,8},{10,11... | collective-permute-start | bytes 786440 | tf_op jit(solution)/shard_map/ppermute | solution.py:434
  16.5 3.5 %shard_map.76 = (bf16[4,16,1024]{2,1,0:T(8,128)(2,1)S(1)}, bf16[4,16,1024]{2,1,0:T(8,128)(2,1)S(1)}) custom-call(s32[4,4]{1,0:T(4,128)S(1)} %copy-done.1, bf16[4,4,16,256]{3,2,1,0:T(8,128)(2,1)S(1)} %copy-done, bf16[4,4,16,256]{3,2,1,0:T(8,128)(2,1)S(1)} %collective-permute-done.refs_1_, bf16[27,240,128]{2,1,0:T(8,128)(2,1)S(1)} %slice.refs_2_, ...), custom_call_target="tpu_custom_call" | custom-call | tf_op jit(solution)/shard_map/pallas_call | solution.py:292
  19.9 0.0 copy-start.4
  19.9 0.0 copy-start.3
  20.0 0.4 collective-permute-start.3
  20.3 3.5 %shard_map.77 = (bf16[4,16,1024]{2,1,0:T(8,128)(2,1)S(1)}, bf16[4,16,1024]{2,1,0:T(8,128)(2,1)S(1)}) custom-call(s32[4,4]{1,0:T(4,128)S(1)} %copy-done.1, bf16[4,4,16,256]{3,2,1,0:T(8,128)(2,1)S(1)} %copy-done, bf16[4,4,16,256]{3,2,1,0:T(8,128)(2,1)S(1)} %collective-permute-done.refs_1_, bf16[27,240,128]{2,1,0:T(8,128)(2,1)S(1)} %slice.refs_2_, ...), custom_call_target="tpu_custom_call" | custom-call | tf_op jit(solution)/shard_map/pallas_call | solution.py:292
  23.8 1.8 %collective-permute-start.4 = (bf16[4,16,1024]{2,1,0:T(8,128)(2,1)S(1)}, bf16[4,16,1024]{2,1,0:T(8,128)(2,1)S(1)}, u32[]{:S(2)}, u32[]{:S(2)}) collective-permute-start(bf16[4,16,1024]{2,1,0:T(8,128)(2,1)S(1)} %get-tuple-element.58), channel_id=1, source_target_pairs={{0,1},{1,0},{2,3},{3,2},{4,5},{5,4},{6,7},{7,6},{8,9},{9,8},{10,11... | collective-permute-start | bytes 393224 | tf_op jit(solution)/shard_map/ppermute | solution.py:434
  25.6 0.0 copy-done.4
  25.6 0.0 copy-done.3
  25.6 0.1 reshape.22
  25.7 0.3 collective-permute-start.1
  26.0 3.3 %collective-permute-done.1 = s32[16]{0:T(128)S(1)} collective-permute-done((s32[16]{0:T(128)S(1)}, s32[16]{0:T(128)S(1)}, u32[]{:S(2)}, u32[]{:S(2)}) %collective-permute-start.1) | collective-permute-done | bytes 96 | tf_op jit(solution)/shard_map/ppermute | solution.py:434
  29.2 0.1 pad_add_fusion.goal_ref
  29.3 0.0 collective-permute-done.3.refs_3_
  29.3 0.0 collective-permute-done.4.refs_5_
  29.3 0.0 collective-permute-done.2.refs_1_
  29.3 0.9 %shard_map.78 = (bf16[32,16,512]{2,1,0:T(8,128)(2,1)S(1)}, bf16[32,16,512]{2,1,0:T(8,128)(2,1)S(1)}) custom-call(s32[32]{0:T(128)S(1)} %pad_add_fusion.goal_ref, bf16[8,16,1024]{2,1,0:T(8,128)(2,1)S(1)} %get-tuple-element.53.refs_0_, bf16[8,16,1024]{2,1,0:T(8,128)(2,1)S(1)} %collective-permute-done.2.refs_1_, ...), custom_call_target="tpu_custom_call" | custom-call | tf_op jit(solution)/shard_map/pallas_call | solution.py:336
  30.2 0.1 collective-permute-start.5
  30.3 0.9 %shard_map.82 = (bf16[32,16,512]{2,1,0:T(8,128)(2,1)S(1)}, bf16[32,16,512]{2,1,0:T(8,128)(2,1)S(1)}) custom-call(s32[32]{0:T(128)S(1)} %pad_add_fusion.goal_ref, bf16[8,16,1024]{2,1,0:T(8,128)(2,1)S(1)} %get-tuple-element.53.refs_0_, bf16[8,16,1024]{2,1,0:T(8,128)(2,1)S(1)} %collective-permute-done.2.refs_1_, ...), custom_call_target="tpu_custom_call" | custom-call | tf_op jit(solution)/shard_map/pallas_call | solution.py:336
  31.2 0.6 %collective-permute-start.8 = (bf16[32,16,512]{2,1,0:T(8,128)(2,1)S(1)}, bf16[32,16,512]{2,1,0:T(8,128)(2,1)S(1)}, u32[]{:S(2)}, u32[]{:S(2)}) collective-permute-start(bf16[32,16,512]{2,1,0:T(8,128)(2,1)S(1)} %get-tuple-element.67), channel_id=1, source_target_pairs={{0,2},{2,0},{4,6},{6,4},{8,10},{10,8},{12,14},{14,12},{16,18},{18,... | collective-permute-start | bytes 1572872 | tf_op jit(solution)/shard_map/ppermute | solution.py:434
  31.8 0.4 collective-permute-done.5
  32.2 0.1 shard_map.79
  32.3 1.6 %collective-permute-start.6 = (bf16[4,4,16,512]{3,2,1,0:T(8,128)(2,1)S(1)}, bf16[4,4,16,512]{3,2,1,0:T(8,128)(2,1)S(1)}, u32[]{:S(2)}, u32[]{:S(2)}) collective-permute-start(bf16[4,4,16,512]{3,2,1,0:T(8,128)(2,1)S(1)} %get-tuple-element.62), channel_id=1, source_target_pairs={{0,8},{2,10},{4,12},{6,14},{8,0},{10,2},{12,4},{14,6},{16,24},{18,... | collective-permute-start | bytes 786440 | tf_op jit(solution)/shard_map/ppermute | solution.py:434
  34.0 0.0 collective-permute-done.8
  34.0 0.1 shard_map.83
  34.1 1.6 %collective-permute-start.9 = (bf16[4,4,16,512]{3,2,1,0:T(8,128)(2,1)S(1)}, bf16[4,4,16,512]{3,2,1,0:T(8,128)(2,1)S(1)}, u32[]{:S(2)}, u32[]{:S(2)}) collective-permute-start(bf16[4,4,16,512]{3,2,1,0:T(8,128)(2,1)S(1)} %get-tuple-element.69), channel_id=1, source_target_pairs={{0,4},{2,6},{4,0},{6,2},{8,12},{10,14},{12,8},{14,10},{16,20},{18,... | collective-permute-start | bytes 786440 | tf_op jit(solution)/shard_map/ppermute | solution.py:434
  35.7 5.1 %collective-permute-done.6.arrived_ref = bf16[4,4,16,512]{3,2,1,0:T(8,128)(2,1)S(1)} collective-permute-done((bf16[4,4,16,512]{3,2,1,0:T(8,128)(2,1)S(1)}, bf16[4,4,16,512]{3,2,1,0:T(8,128)(2,1)S(1)}, u32[]{:S(2)}, u32[]{:S(2)}) %collective-permute-start.6) | collective-permute-done | bytes 262176 | tf_op jit(solution)/shard_map/ppermute | solution.py:434
  40.7 0.1 shard_map.80
  40.8 1.6 %collective-permute-start.7 = (bf16[2,4,16,512]{3,2,1,0:T(8,128)(2,1)S(1)}, bf16[2,4,16,512]{3,2,1,0:T(8,128)(2,1)S(1)}, u32[]{:S(2)}, u32[]{:S(2)}) collective-permute-start(bf16[2,4,16,512]{3,2,1,0:T(8,128)(2,1)S(1)} %get-tuple-element.64), channel_id=1, source_target_pairs={{0,4},{2,6},{4,0},{6,2},{8,12},{10,14},{12,8},{14,10},{16,20},{18,... | collective-permute-start | bytes 393224 | tf_op jit(solution)/shard_map/ppermute | solution.py:434
  42.4 0.0 collective-permute-done.9.arrived_ref
  42.4 0.1 shard_map.84
  42.5 1.6 %collective-permute-start.10 = (bf16[2,4,16,512]{3,2,1,0:T(8,128)(2,1)S(1)}, bf16[2,4,16,512]{3,2,1,0:T(8,128)(2,1)S(1)}, u32[]{:S(2)}, u32[]{:S(2)}) collective-permute-start(bf16[2,4,16,512]{3,2,1,0:T(8,128)(2,1)S(1)} %get-tuple-element.71), channel_id=1, source_target_pairs={{0,8},{2,10},{4,12},{6,14},{8,0},{10,2},{12,4},{14,6},{16,24},{18,... | collective-permute-start | bytes 393224 | tf_op jit(solution)/shard_map/ppermute | solution.py:434
  44.1 1.7 %collective-permute-done.7.arrived_ref = bf16[2,4,16,512]{3,2,1,0:T(8,128)(2,1)S(1)} collective-permute-done((bf16[2,4,16,512]{3,2,1,0:T(8,128)(2,1)S(1)}, bf16[2,4,16,512]{3,2,1,0:T(8,128)(2,1)S(1)}, u32[]{:S(2)}, u32[]{:S(2)}) %collective-permute-start.7) | collective-permute-done | bytes 131104 | tf_op jit(solution)/shard_map/ppermute | solution.py:434
  45.9 2.7 %collective-permute-start.11 = (bf16[1,4,16,512]{3,2,1,0:T(8,128)(2,1)S(1)}, bf16[1,4,16,512]{3,2,1,0:T(8,128)(2,1)S(1)}, u32[]{:S(2)}, u32[]{:S(2)}) collective-permute-start(bf16[1,4,16,512]{3,2,1,0:T(8,128)(2,1)S(1)} %get-tuple-element.73), channel_id=1, source_target_pairs={{0,16},{2,18},{4,20},{6,22},{8,24},{10,26},{12,28},{14,30},{16,0},... | collective-permute-start | bytes 196616 | tf_op jit(solution)/shard_map/ppermute | solution.py:434
  48.5 0.0 collective-permute-done.10.arrived_ref
  48.6 2.3 %collective-permute-start.12 = (bf16[1,4,16,512]{3,2,1,0:T(8,128)(2,1)S(1)}, bf16[1,4,16,512]{3,2,1,0:T(8,128)(2,1)S(1)}, u32[]{:S(2)}, u32[]{:S(2)}) collective-permute-start(bf16[1,4,16,512]{3,2,1,0:T(8,128)(2,1)S(1)} %get-tuple-element.74), channel_id=1, source_target_pairs={{0,16},{2,18},{4,20},{6,22},{8,24},{10,26},{12,28},{14,30},{16,0},... | collective-permute-start | bytes 196616 | tf_op jit(solution)/shard_map/ppermute | solution.py:434
  50.9 1.9 %collective-permute-done.11.arrived0_ref = bf16[1,4,16,512]{3,2,1,0:T(8,128)(2,1)S(1)} collective-permute-done((bf16[1,4,16,512]{3,2,1,0:T(8,128)(2,1)S(1)}, bf16[1,4,16,512]{3,2,1,0:T(8,128)(2,1)S(1)}, u32[]{:S(2)}, u32[]{:S(2)}) %collective-permute-start.11) | collective-permute-done | bytes 65568 | tf_op jit(solution)/shard_map/ppermute | solution.py:434
  52.8 1.0 %collective-permute-done.12.arrived1_ref = bf16[1,4,16,512]{3,2,1,0:T(8,128)(2,1)S(1)} collective-permute-done((bf16[1,4,16,512]{3,2,1,0:T(8,128)(2,1)S(1)}, bf16[1,4,16,512]{3,2,1,0:T(8,128)(2,1)S(1)}, u32[]{:S(2)}, u32[]{:S(2)}) %collective-permute-start.12) | collective-permute-done | bytes 65568 | tf_op jit(solution)/shard_map/ppermute | solution.py:434
  53.8 1.0 %shard_map.86 = bf16[4,4,4096]{2,1,0:T(4,128)(2,1)} custom-call(bf16[1,4,16,512]{3,2,1,0:T(8,128)(2,1)S(1)} %get-tuple-element.65.kept0_ref, bf16[1,4,16,512]{3,2,1,0:T(8,128)(2,1)S(1)} %get-tuple-element.72.kept1_ref, bf16[1,4,16,512]{3,2,1,0:T(8,128)(2,1)S(1)} %collective-permute-done.11.arrived0_ref, ...), custom_call_target="tpu_custom_call" | custom-call | tf_op jit(solution)/shard_map/pallas_call | solution.py:418
  (4 shorter events, 0.1 us)
Async XLA Ops:
  2.0 6.6 %collective-permute-start = (bf16[4,4,16,256]{3,2,1,0:T(8,128)(2,1)}, bf16[4,4,16,256]{3,2,1,0:T(8,128)(2,1)S(1)}, u32[]{:S(2)}, u32[]{:S(2)}) collective-permute-start(bf16[4,4,16,256]{3,2,1,0:T(8,128)(2,1)} %get-tuple-element.41), channel_id=1, source_target_pairs={{0,1},{1,0},{2,3},{3,2},{4,5},{5,4},{6,7},{7,6},{8,9},{9,8},{10,11... | collective-permute-start | bytes 393224 | tf_op jit(solution)/shard_map/ppermute | solution.py:434
  6.7 0.7 %copy-start.2 = (bf16[32,32]{1,0:T(8,128)(2,1)S(1)}, bf16[32,32]{1,0:T(8,128)(2,1)}, u32[]{:S(2)}) copy-start(bf16[32,32]{1,0:T(8,128)(2,1)} %scale_ref.1) | copy-start | bytes 6148
  6.7 1.9 %copy-start = (bf16[4,4,16,256]{3,2,1,0:T(8,128)(2,1)S(1)}, bf16[4,4,16,256]{3,2,1,0:T(8,128)(2,1)}, u32[]{:S(2)}) copy-start(bf16[4,4,16,256]{3,2,1,0:T(8,128)(2,1)} %get-tuple-element.40.refs_0_) | copy-start | bytes 393220
  6.7 1.9 %copy-start.1 = (s32[4,4]{1,0:T(4,128)S(1)}, s32[4,4]{1,0:T(4,128)}, u32[]{:S(2)}) copy-start(s32[4,4]{1,0:T(4,128)} %kind_ref.5) | copy-start | bytes 196
  14.7 14.6 %collective-permute-start.2 = (bf16[8,16,1024]{2,1,0:T(8,128)(2,1)S(1)}, bf16[8,16,1024]{2,1,0:T(8,128)(2,1)S(1)}, u32[]{:S(2)}, u32[]{:S(2)}) collective-permute-start(bf16[8,16,1024]{2,1,0:T(8,128)(2,1)S(1)} %get-tuple-element.54), channel_id=1, source_target_pairs={{0,1},{1,0},{2,3},{3,2},{4,5},{5,4},{6,7},{7,6},{8,9},{9,8},{10,11... | collective-permute-start | bytes 786440 | tf_op jit(solution)/shard_map/ppermute | solution.py:434
  19.9 5.6 %copy-start.4 = (s32[4,4,1]{1,2,0:T(1,128)S(1)}, s32[4,4,1]{1,2,0:T(1,128)}, u32[]{:S(2)}) copy-start(s32[4,4,1]{1,2,0:T(1,128)} %param.12) | copy-start | bytes 196
  19.9 5.6 %copy-start.3 = (s32[4,4]{1,0:T(4,128)S(1)}, s32[4,4]{1,0:T(4,128)}, u32[]{:S(2)}) copy-start(s32[4,4]{1,0:T(4,128)} %param.13) | copy-start | bytes 196
  20.0 9.3 %collective-permute-start.3 = (bf16[4,16,1024]{2,1,0:T(8,128)(2,1)S(1)}, bf16[4,16,1024]{2,1,0:T(8,128)(2,1)S(1)}, u32[]{:S(2)}, u32[]{:S(2)}) collective-permute-start(bf16[4,16,1024]{2,1,0:T(8,128)(2,1)S(1)} %get-tuple-element.56), channel_id=1, source_target_pairs={{0,1},{1,0},{2,3},{3,2},{4,5},{5,4},{6,7},{7,6},{8,9},{9,8},{10,11... | collective-permute-start | bytes 393224 | tf_op jit(solution)/shard_map/ppermute | solution.py:434
  23.8 5.5 %collective-permute-start.4 = (bf16[4,16,1024]{2,1,0:T(8,128)(2,1)S(1)}, bf16[4,16,1024]{2,1,0:T(8,128)(2,1)S(1)}, u32[]{:S(2)}, u32[]{:S(2)}) collective-permute-start(bf16[4,16,1024]{2,1,0:T(8,128)(2,1)S(1)} %get-tuple-element.58), channel_id=1, source_target_pairs={{0,1},{1,0},{2,3},{3,2},{4,5},{5,4},{6,7},{7,6},{8,9},{9,8},{10,11... | collective-permute-start | bytes 393224 | tf_op jit(solution)/shard_map/ppermute | solution.py:434
  25.7 3.5 %collective-permute-start.1 = (s32[16]{0:T(128)S(1)}, s32[16]{0:T(128)S(1)}, u32[]{:S(2)}, u32[]{:S(2)}) collective-permute-start(s32[16]{0:T(128)S(1)} %reshape.22), channel_id=1, source_target_pairs={{0,1},{1,0},{2,3},{3,2},{4,5},{5,4},{6,7},{7,6},{8,9},{9,8},{10,11... | collective-permute-start | bytes 200 | tf_op jit(solution)/shard_map/ppermute | solution.py:434
  30.2 2.0 %collective-permute-start.5 = (bf16[32,16,512]{2,1,0:T(8,128)(2,1)S(1)}, bf16[32,16,512]{2,1,0:T(8,128)(2,1)S(1)}, u32[]{:S(2)}, u32[]{:S(2)}) collective-permute-start(bf16[32,16,512]{2,1,0:T(8,128)(2,1)S(1)} %get-tuple-element.60), channel_id=1, source_target_pairs={{0,2},{2,0},{4,6},{6,4},{8,10},{10,8},{12,14},{14,12},{16,18},{18,... | collective-permute-start | bytes 1572872 | tf_op jit(solution)/shard_map/ppermute | solution.py:434
  31.2 2.7 %collective-permute-start.8 = (bf16[32,16,512]{2,1,0:T(8,128)(2,1)S(1)}, bf16[32,16,512]{2,1,0:T(8,128)(2,1)S(1)}, u32[]{:S(2)}, u32[]{:S(2)}) collective-permute-start(bf16[32,16,512]{2,1,0:T(8,128)(2,1)S(1)} %get-tuple-element.67), channel_id=1, source_target_pairs={{0,2},{2,0},{4,6},{6,4},{8,10},{10,8},{12,14},{14,12},{16,18},{18,... | collective-permute-start | bytes 1572872 | tf_op jit(solution)/shard_map/ppermute | solution.py:434
  32.3 8.4 %collective-permute-start.6 = (bf16[4,4,16,512]{3,2,1,0:T(8,128)(2,1)S(1)}, bf16[4,4,16,512]{3,2,1,0:T(8,128)(2,1)S(1)}, u32[]{:S(2)}, u32[]{:S(2)}) collective-permute-start(bf16[4,4,16,512]{3,2,1,0:T(8,128)(2,1)S(1)} %get-tuple-element.62), channel_id=1, source_target_pairs={{0,8},{2,10},{4,12},{6,14},{8,0},{10,2},{12,4},{14,6},{16,24},{18,... | collective-permute-start | bytes 786440 | tf_op jit(solution)/shard_map/ppermute | solution.py:434
  34.1 8.3 %collective-permute-start.9 = (bf16[4,4,16,512]{3,2,1,0:T(8,128)(2,1)S(1)}, bf16[4,4,16,512]{3,2,1,0:T(8,128)(2,1)S(1)}, u32[]{:S(2)}, u32[]{:S(2)}) collective-permute-start(bf16[4,4,16,512]{3,2,1,0:T(8,128)(2,1)S(1)} %get-tuple-element.69), channel_id=1, source_target_pairs={{0,4},{2,6},{4,0},{6,2},{8,12},{10,14},{12,8},{14,10},{16,20},{18,... | collective-permute-start | bytes 786440 | tf_op jit(solution)/shard_map/ppermute | solution.py:434
  40.8 5.0 %collective-permute-start.7 = (bf16[2,4,16,512]{3,2,1,0:T(8,128)(2,1)S(1)}, bf16[2,4,16,512]{3,2,1,0:T(8,128)(2,1)S(1)}, u32[]{:S(2)}, u32[]{:S(2)}) collective-permute-start(bf16[2,4,16,512]{3,2,1,0:T(8,128)(2,1)S(1)} %get-tuple-element.64), channel_id=1, source_target_pairs={{0,4},{2,6},{4,0},{6,2},{8,12},{10,14},{12,8},{14,10},{16,20},{18,... | collective-permute-start | bytes 393224 | tf_op jit(solution)/shard_map/ppermute | solution.py:434
  42.5 6.1 %collective-permute-start.10 = (bf16[2,4,16,512]{3,2,1,0:T(8,128)(2,1)S(1)}, bf16[2,4,16,512]{3,2,1,0:T(8,128)(2,1)S(1)}, u32[]{:S(2)}, u32[]{:S(2)}) collective-permute-start(bf16[2,4,16,512]{3,2,1,0:T(8,128)(2,1)S(1)} %get-tuple-element.71), channel_id=1, source_target_pairs={{0,8},{2,10},{4,12},{6,14},{8,0},{10,2},{12,4},{14,6},{16,24},{18,... | collective-permute-start | bytes 393224 | tf_op jit(solution)/shard_map/ppermute | solution.py:434
  45.9 6.9 %collective-permute-start.11 = (bf16[1,4,16,512]{3,2,1,0:T(8,128)(2,1)S(1)}, bf16[1,4,16,512]{3,2,1,0:T(8,128)(2,1)S(1)}, u32[]{:S(2)}, u32[]{:S(2)}) collective-permute-start(bf16[1,4,16,512]{3,2,1,0:T(8,128)(2,1)S(1)} %get-tuple-element.73), channel_id=1, source_target_pairs={{0,16},{2,18},{4,20},{6,22},{8,24},{10,26},{12,28},{14,30},{16,0},... | collective-permute-start | bytes 196616 | tf_op jit(solution)/shard_map/ppermute | solution.py:434
  48.6 5.2 %collective-permute-start.12 = (bf16[1,4,16,512]{3,2,1,0:T(8,128)(2,1)S(1)}, bf16[1,4,16,512]{3,2,1,0:T(8,128)(2,1)S(1)}, u32[]{:S(2)}, u32[]{:S(2)}) collective-permute-start(bf16[1,4,16,512]{3,2,1,0:T(8,128)(2,1)S(1)} %get-tuple-element.74), channel_id=1, source_target_pairs={{0,16},{2,18},{4,20},{6,22},{8,24},{10,26},{12,28},{14,30},{16,0},... | collective-permute-start | bytes 196616 | tf_op jit(solution)/shard_map/ppermute | solution.py:434
